TPU v7x, 32 devices: a whole 2x2x4 slice. The times are simulated.
32 devices in a mesh: groups: 2 (over y), ka: 16 (over z, x, core).
Axes of the slice: x: 2, y: 2, z: 4, core: 2. Of those that a mesh axis runs over, the one named last changes fastest.
Arguments:
- coeffs: bfloat16 [64, 32, 32, 1024], P(('groups', 'ka')), parts along dimension 0, may hold values from -6 to 6
- g_cond: bfloat16 [64, 2, 32, 32], P(('groups', 'ka')), parts along dimension 0, may hold values from -1 to 1
- g_val: bfloat16 [64, 2, 32, 32], P(('groups', 'ka')), parts along dimension 0, may hold values from -1 to 1
- k_plus_q: int32 [64], P(('groups', 'ka')), parts along dimension 0, may hold values from 0 to 31, as said below
- band_first: int32 [4, 2], P('groups'), parts along dimension 0, may hold values from 0 to 15
Outputs:
- coupling: float32 [2048, 2, 1024], P(('groups', 'ka')), parts along dimension 0
There are 2 independent parts, one for each index of `groups`. A program takes and returns all parts, laid end to end along the dimension named above; each array names one. Nothing has to cross between parts.
Inputs may be any that keep to these rules, and one draw needn't show every extreme that they name: Taking the k-points in aligned blocks of 2, k_plus_q[k] lies in the block of k or in the following block, the last block being followed by the first.
All inputs are finite; a program needn't handle non-finite values.
Results may differ from a plain program's by a relative error of at most 0.0029.
Values may be sent and summed in bfloat16 or wider, within the bound.
No kernel may reach another device: no remote copies, remote signals or barrier semaphores. Data moves between devices by JAX's collectives and lax.ppermute only.
A program may use at most 64 MiB of HBM per device.

v0:
```python
import functools
import math

import jax
import jax.numpy as jnp
from jax import lax
from jax.experimental import pallas as pl
from jax.experimental.pallas import tpu as pltpu
from jax.sharding import PartitionSpec as P

MIB = 1024 * 1024


def permute(x, target):
    size = lax.axis_size("ka")
    pairs = [(i, target(i)) for i in range(size)]
    return lax.ppermute(x, "ka", [(i, j % size) for i, j in pairs if j is not None])


def nt_dot(a, b):
    return lax.dot_general(a, b, (((1,), (1,)), ((), ())), preferred_element_type=jnp.float32)


def spread(rows, count, group, by_rest):
    row = lax.broadcasted_iota(jnp.int32, (rows, count), 0)
    col = lax.broadcasted_iota(jnp.int32, (rows, count), 1)
    return jnp.where((row % count if by_rest else row // group) == col, 1.0, 0.0).astype(jnp.bfloat16)


def products_kernel(first_ref, coeffs_ref, cond_ref, val_ref, out_ref, we_ref, wh_ref):
    _, bands_c, bands_v, tile = coeffs_ref.shape
    modes = cond_ref.shape[1]
    part_v, part_c = bands_v // 2, 8
    rows_e, rows_h = bands_c * part_v, part_c * bands_v

    @pl.when(pl.program_id(1) == 0)
    def _():
        take = spread(rows_e, bands_c, part_v, False)
        row = lax.broadcasted_iota(jnp.int32, (rows_e, rows_e), 0)
        col = lax.broadcasted_iota(jnp.int32, (rows_e, rows_e), 1)
        for m in range(modes):
            part = jnp.dot(take, cond_ref[0, m], preferred_element_type=jnp.float32)
            full = nt_dot(part.astype(jnp.bfloat16), take)
            keep = (row % part_v == col % part_v) & (row // part_v >= first_ref[m, 0])
            we_ref[m * rows_e:(m + 1) * rows_e, :] = jnp.where(keep, full, 0.0).astype(jnp.bfloat16)
        take = spread(rows_h, bands_v, 0, True)
        row = lax.broadcasted_iota(jnp.int32, (rows_h, rows_h), 0)
        col = lax.broadcasted_iota(jnp.int32, (rows_h, rows_h), 1)
        for m in range(modes):
            part = nt_dot(take, val_ref[0, m])
            full = nt_dot(part.astype(jnp.bfloat16), take)
            keep = (row // bands_v == col // bands_v) & (row % bands_v >= first_ref[m, 1])
            wh_ref[m * rows_h:(m + 1) * rows_h, :] = jnp.where(keep, full, 0.0).astype(jnp.bfloat16)

    electron = []
    for h in range(2):
        x = coeffs_ref[0, :, h * part_v:(h + 1) * part_v, :].reshape(rows_e, tile)
        e = jnp.dot(we_ref[...], x, preferred_element_type=jnp.float32)
        electron.append(e.reshape(modes, bands_c, part_v, tile))
    for q in range(bands_c // part_c):
        own = slice(q * part_c, (q + 1) * part_c)
        y = coeffs_ref[0, own].reshape(rows_h, tile)
        hole = jnp.dot(wh_ref[...], y, preferred_element_type=jnp.float32)
        hole = hole.reshape(modes, part_c, bands_v, tile)
        for m in range(modes):
            for h in range(2):
                cols = slice(h * part_v, (h + 1) * part_v)
                value = electron[h][m, own] - hole[m, :, cols]
                out_ref[0, m, own, cols, :] = value.astype(jnp.bfloat16)


def products_of(coeffs, g_cond, g_val, band_first):
    k_local, bands_c, bands_v, excitons = coeffs.shape
    modes = g_cond.shape[1]
    tile = 256
    rows_e, rows_h = bands_c * bands_v // 2, 8 * bands_v
    flops = 2 * k_local * modes * excitons * bands_c * bands_v * (rows_e + rows_h)
    out = pl.pallas_call(
        products_kernel,
        out_shape=jax.ShapeDtypeStruct((k_local, modes, bands_c, bands_v, excitons), jnp.bfloat16),
        grid=(k_local, excitons // tile),
        in_specs=[
            pl.BlockSpec(memory_space=pltpu.SMEM),
            pl.BlockSpec((1, bands_c, bands_v, tile), lambda k, s: (k, 0, 0, s)),
            pl.BlockSpec((1, modes, bands_c, bands_c), lambda k, s: (k, 0, 0, 0)),
            pl.BlockSpec((1, modes, bands_v, bands_v), lambda k, s: (k, 0, 0, 0)),
        ],
        out_specs=pl.BlockSpec((1, modes, bands_c, bands_v, tile), lambda k, s: (k, 0, 0, 0, s)),
        scratch_shapes=[
            pltpu.VMEM((modes * rows_e, rows_e), jnp.bfloat16),
            pltpu.VMEM((modes * rows_h, rows_h), jnp.bfloat16),
        ],
        compiler_params=pltpu.CompilerParams(vmem_limit_bytes=32 * MIB),
        cost_estimate=pl.CostEstimate(
            flops=flops, bytes_accessed=2 * coeffs.size * (1 + modes), transcendentals=0
        ),
    )(band_first, coeffs, g_cond, g_val)
    return out.reshape(k_local, modes, bands_c * bands_v, excitons)


def rows_kernel(adds, last, *refs):
    pick_ref, own_ref, sib_ref, next_ref, p_own_ref, p_sib_ref = refs[:6]
    arrived = refs[6:6 + adds]
    outs, left = refs[6 + adds:-1], refs[-1]
    k_local = own_ref.shape[0]

    @pl.when(pl.program_id(0) == 0)
    def _():
        for k in range(2 * k_local):
            which, place = pick_ref[2 * k], pick_ref[2 * k + 1]
            for source, ref in enumerate((own_ref, sib_ref, next_ref)):
                @pl.when(which == source)
                def _():
                    left[k] = ref[place].T

    total = None
    for k in range(2 * k_local):
        right = p_own_ref if k < k_local else p_sib_ref
        term = jnp.dot(left[k], right[k % k_local, 0], preferred_element_type=jnp.float32)
        total = term if total is None else total + term
    for ref in arrived:
        total = total + ref[...].astype(jnp.float32)
    if not last:
        outs[0][...] = total.astype(jnp.bfloat16)
        return
    half = total.shape[0] // 2
    low, high = total[:half], total[half:]
    core, first = pick_ref[4 * k_local + 1], pick_ref[4 * k_local + 2]
    outs[0][...] = jnp.where(core == 0, low, high)
    outs[1][...] = jnp.where(first == 0, low, high).astype(jnp.bfloat16)
    outs[2][...] = jnp.where(first == 0, high, low).astype(jnp.bfloat16)


def rows_of(pick, own, sib, following, p_own, p_sib, arrived, last, width):
    k_local, depth, excitons = own.shape
    modes = p_own.shape[1]
    tile = 512
    per_mode = excitons // tile
    columns = modes * excitons
    if last:
        half = width // 2
        outs = [((half, columns), jnp.float32)] + 2 * [((half, columns), jnp.bfloat16)]
    else:
        outs = [((width, columns), jnp.bfloat16)]
    block = lambda j, pick: (0, 0, pick[4 * k_local])
    right = pl.BlockSpec((k_local, 1, depth, tile), lambda j, pick: (0, j // per_mode, 0, j % per_mode))
    return pl.pallas_call(
        functools.partial(rows_kernel, len(arrived), last),
        out_shape=[jax.ShapeDtypeStruct(*o) for o in outs],
        grid_spec=pltpu.PrefetchScalarGridSpec(
            num_scalar_prefetch=1,
            grid=(modes * per_mode,),
            in_specs=[
                pl.BlockSpec((k_local, depth, width), block),
                pl.BlockSpec((k_local, depth, width), block),
                pl.BlockSpec((k_local, depth, width), lambda j, pick: (0, 0, 0)),
                right,
                right,
            ] + [pl.BlockSpec((width, tile), lambda j, pick: (0, j)) for _ in arrived],
            out_specs=[pl.BlockSpec((o[0][0], tile), lambda j, pick: (0, j)) for o in outs],
            scratch_shapes=[pltpu.VMEM((2 * k_local, width, depth), jnp.bfloat16)],
        ),
        compiler_params=pltpu.CompilerParams(vmem_limit_bytes=32 * MIB),
        cost_estimate=pl.CostEstimate(
            flops=4 * k_local * depth * width * columns,
            bytes_accessed=4 * k_local * depth * columns,
            transcendentals=0,
        ),
    )(pick, own, sib, following, p_own, p_sib, *arrived)


def on_two_by_four(coeffs, g_cond, g_val, k_plus_q, band_first, norm_factor):
    k_local, bands_c, bands_v, excitons = coeffs.shape
    modes = g_cond.shape[1]
    size = lax.axis_size("ka")
    chips = size // 2
    width = excitons // chips
    me = lax.axis_index("ka")
    core, x, z = me % 2, me // 2 % 2, me // 4
    flat = coeffs.reshape(k_local, bands_c * bands_v, excitons)

    offsets = jnp.mod(k_plus_q - me * k_local, k_local * size)
    small = jnp.concatenate(
        (g_cond.reshape(-1), g_val.reshape(-1), offsets.astype(jnp.bfloat16))
    )
    sib_small = permute(small, lambda i: i ^ 1)
    sib = permute(flat, lambda i: i ^ 1)

    def cut(array, block):
        return lax.dynamic_slice_in_dim(array, block * width, width, 2)

    behind_z = jnp.mod(me // 2 - 1, chips) // 2
    following = []
    for step in range(4):
        block = 2 * (behind_z ^ (3 - step))
        if step == 0:
            to_first = permute(cut(flat, block), lambda i: i - 2 if i % 2 == 0 else i)
            to_second = permute(cut(flat, block + 1), lambda i: i - 1 if i % 2 == 0 else i - 1)
            following.append(jnp.where(core == 0, to_first, to_second))
        else:
            sent = jnp.where(core == 0, cut(flat, block), cut(sib, block + 1))
            following.append(permute(sent, lambda i: i - 2))

    sib_cond = sib_small[:g_cond.size].reshape(g_cond.shape)
    sib_val = sib_small[g_cond.size:g_cond.size + g_val.size].reshape(g_val.shape)
    sib_offsets = sib_small[g_cond.size + g_val.size:].astype(jnp.int32)
    p_own = products_of(coeffs, g_cond, g_val, band_first)
    p_sib = products_of(sib.reshape(coeffs.shape), sib_cond, sib_val, band_first)

    places = jnp.concatenate((offsets + core * k_local, sib_offsets + (1 - core) * k_local))
    of_block = places // k_local
    which = jnp.where(of_block == 2, 2, of_block ^ core)
    picks = jnp.stack((which, places % k_local), 1).reshape(-1).astype(jnp.int32)
    keeper = core == x
    first = jnp.where(keeper, 1 - core, core)

    def rows(step, arrived, last=False):
        block = 2 * (z ^ (3 - step)) + core
        pick = jnp.concatenate((picks, jnp.stack((block, core, first)).astype(jnp.int32)))
        return rows_of(pick, flat, sib, following[step], p_own, p_sib, arrived, last, width)

    far = permute(rows(0, [])[0], lambda i: i ^ 4)
    pair = permute(rows(1, [far])[0], lambda i: i ^ 8)
    near = permute(rows(2, [])[0], lambda i: i ^ 4)
    mine, sent_a, sent_b = rows(3, [pair, near], True)
    is_keeper = lambda i: i % 2 == i // 2 % 2
    got_a = permute(sent_a, lambda i: i ^ 1 if is_keeper(i) else i ^ 2)
    got_b = permute(sent_b, lambda i: i if is_keeper(i) else i ^ 3)
    total = got_a.astype(jnp.float32) + jnp.where(keeper, mine, got_b.astype(jnp.float32))
    return (total * norm_factor).reshape(width // 2, modes, excitons)


def on_any(coeffs, g_cond, g_val, k_plus_q, band_first, norm_factor):
    k_local, bands_c, bands_v, excitons = coeffs.shape
    modes = g_cond.shape[1]
    size = lax.axis_size("ka")
    depth = bands_c * bands_v
    flat = coeffs.reshape(k_local, depth, excitons)
    blocks = jnp.concatenate((flat, permute(flat, lambda i: i - 1)), 0)
    offsets = jnp.mod(k_plus_q - lax.axis_index("ka") * k_local, k_local * size)
    products = products_of(coeffs, g_cond, g_val, band_first)
    partners = [
        lax.dynamic_index_in_dim(blocks, offsets[k], 0, keepdims=False) for k in range(k_local)
    ]
    running = jnp.einsum(
        "kds,kmdt->smt", jnp.stack(partners), products, preferred_element_type=jnp.float32
    )
    return lax.psum_scatter(running * norm_factor, "ka", scatter_dimension=0, tiled=True)


def shards(coeffs, g_cond, g_val, k_plus_q, band_first):
    k_local, bands_c, bands_v, excitons = coeffs.shape
    size = lax.axis_size("ka")
    norm_factor = 1.0 / math.sqrt(bands_c * bands_v * k_local * size)
    whole_tiles = excitons % (size // 2 * 128) == 0
    plan = on_two_by_four if size == 16 and whole_tiles else on_any
    return plan(coeffs, g_cond, g_val, k_plus_q, band_first, norm_factor)


def solution(mesh):
    in_specs = (
        P(("groups", "ka"), None, None, None),
        P(("groups", "ka"), None, None, None),
        P(("groups", "ka"), None, None, None),
        P(("groups", "ka")),
        P("groups", None),
    )
    out_specs = P(("groups", "ka"), None, None)
    return jax.shard_map(shards, mesh=mesh, in_specs=in_specs, out_specs=out_specs, check_vma=False)
```

profile of v0, /device:TPU:1, one launch (start us, length us, event | category | flops | bytes accessed | tf_op | source)
XLA Modules:
  0.0 137.3 jit_solution(7229715201443050243)
XLA Ops:
  0.0 0.1 collective-permute-start.1
  0.1 0.7 add_bitcast_fusion
  0.7 0.8 reshape.239
  1.6 0.9 reshape.240
  2.5 0.5 collective-permute-start
  3.0 2.2 %copy-done.3 = bf16[2,32,32,1024]{3,2,1,0:T(8,128)(2,1)S(1)} copy-done((bf16[2,32,32,1024]{3,2,1,0:T(8,128)(2,1)S(1)}, bf16[2,32,32,1024]{3,2,1,0:T(8,128)(2,1)}, u32[]{:S(2)}) %copy-start.3) | copy-done | bytes 4194328
  5.2 0.8 copy-done.6
  5.9 0.8 copy-done.7
  6.7 0.7 copy-done.8
  7.4 12.0 %shard_map.55 = bf16[2,2,32,32,1024]{4,3,2,1,0:T(8,128)(2,1)S(1)} custom-call(s32[2,2]{1,0:T(2,128)S(1)} %copy-done.8, bf16[2,32,32,1024]{3,2,1,0:T(8,128)(2,1)S(1)} %copy-done.3, bf16[2,2,32,32]{3,2,1,0:T(8,128)(2,1)S(1)} %copy-done.7, bf16[2,2,32,32]{3,2,1,0:T(8,128)(2,1)S(1)} %copy-done.6), custom_call_target="tpu_custom_call" | custom-call | flops 6442450944 | bytes 12582912 | tf_op jit(solution)/shard_map/pallas_call | solution.py:78
  19.3 3.3 %copy-done = bf16[2,2,32,32,1024]{4,3,2,1,0:T(8,128)(2,1)} copy-done((bf16[2,2,32,32,1024]{4,3,2,1,0:T(8,128)(2,1)}, bf16[2,2,32,32,1024]{4,3,2,1,0:T(8,128)(2,1)S(1)}, u32[]{:S(2)}) %copy-start) | copy-done | bytes 8388632
  22.6 0.1 compare_select_fusion.2
  22.7 0.1 copy.7
  22.8 0.1 reshape.241
  22.9 0.1 reshape.246.val_ref
  23.0 0.1 reshape.245.cond_ref
  23.1 0.1 add_add_fusion.2
  23.2 3.5 %dynamic-slice_select_fusion = (bf16[2,1024,128]{2,1,0:T(8,128)(2,1)}, bf16[2,1024,128]{2,1,0:T(8,128)(2,1)S(1)}, bf16[2,1024,128]{2,1,0:T(8,128)(2,1)S(1)}, bf1...) fusion(bf16[2,1024,1024]{2,1,0:T(8,128)(2,1)} %collective-permute-done.1.refs_2_, s32[]{:T(128)S(6)} %select_n.145, ...), kind=kLoop, calls=%fused_computation.1 | loop fusion | flops 786432 | bytes 6815777 | tf_op jit(solution)/shard_map/jit(_where)/select_n | solution.py:201
  26.7 5.3 %collective-permute-start.8 = (bf16[2,1024,128]{2,1,0:T(8,128)(2,1)}, bf16[2,1024,128]{2,1,0:T(8,128)(2,1)S(1)}, u32[]{:S(2)}, u32[]{:S(2)}) collective-permute-start(bf16[2,1024,128]{2,1,0:T(8,128)(2,1)} %get-tuple-element.15), channel_id=1, source_target_pairs={{0,14},{1,15},{2,0},{3,1},{4,2},{5,3},{6,4},{7,5},{8,6},{9,7},{10,... | collective-permute-start | bytes 1572872 | tf_op jit(solution)/shard_map/ppermute | solution.py:17
  31.9 0.3 collective-permute-start.3
  32.2 1.1 collective-permute-start.5
  33.2 0.7 collective-permute-start.4
  33.9 0.0 copy-start.4
  34.0 12.8 %shard_map.56 = bf16[2,2,32,32,1024]{4,3,2,1,0:T(8,128)(2,1)S(1)} custom-call(s32[2,2]{1,0:T(2,128)S(1)} %copy-done.9, bf16[2,32,32,1024]{3,2,1,0:T(8,128)(2,1)} %bitcast.7.coeffs_ref, bf16[2,2,32,32]{3,2,1,0:T(8,128)(2,1)S(1)} %reshape.245.cond_ref, bf16[2,2,32,32]{3,2,1,0:T(8,128)(2,1)S(1)} %reshape.246.val_ref), custom_call_target="tpu_custom_call" | custom-call | flops 6442450944 | bytes 12582912 | tf_op jit(solution)/shard_map/pallas_call | solution.py:78
  46.7 3.2 %copy-done.2 = bf16[2,2,32,32,1024]{4,3,2,1,0:T(8,128)(2,1)} copy-done((bf16[2,2,32,32,1024]{4,3,2,1,0:T(8,128)(2,1)}, bf16[2,2,32,32,1024]{4,3,2,1,0:T(8,128)(2,1)S(1)}, u32[]{:S(2)}) %copy-start.2) | copy-done | bytes 8388632
  50.0 8.2 %collective-permute-done.5 = bf16[2,1024,128]{2,1,0:T(8,128)(2,1)S(1)} collective-permute-done((bf16[2,1024,128]{2,1,0:T(8,128)(2,1)S(1)}, bf16[2,1024,128]{2,1,0:T(8,128)(2,1)S(1)}, u32[]{:S(2)}, u32[]{:S(2)}) %collective-permute-start.5) | collective-permute-done | bytes 524320 | tf_op jit(solution)/shard_map/ppermute | solution.py:17
  58.1 0.0 collective-permute-done.4
  58.1 0.1 broadcast_select_fusion.refs_3_
  58.2 7.3 %shard_map.57 = bf16[128,2048]{1,0:T(8,128)(2,1)S(1)} custom-call(s32[11]{0:T(128)S(1)} %get-tuple-element.24.refs_0_, bf16[2,1024,1024]{2,1,0:T(8,128)(2,1)S(1)} %bitcast.30, bf16[2,1024,1024]{2,1,0:T(8,128)(2,1)} %collective-permute-done.1.refs_2_, bf16[2,1024,128]{2,1,0:T(8,128)(2,1)S(1)} %broadcast_select_fusion.refs_3_, ...), custom_call_target="tpu_custom_call" | custom-call | flops 2147483648 | bytes 16777216 | tf_op jit(solution)/shard_map/pallas_call | solution.py:147
  65.5 1.6 %collective-permute-start.6 = (bf16[128,2048]{1,0:T(8,128)(2,1)S(1)}, bf16[128,2048]{1,0:T(8,128)(2,1)S(1)}, u32[]{:S(2)}, u32[]{:S(2)}) collective-permute-start(bf16[128,2048]{1,0:T(8,128)(2,1)S(1)} %shard_map.57), channel_id=1, source_target_pairs={{0,4},{1,5},{2,6},{3,7},{4,0},{5,1},{6,2},{7,3},{8,12},{9,13},{10,... | collective-permute-start | bytes 1572872 | tf_op jit(solution)/shard_map/ppermute | solution.py:17
  67.2 0.1 add_add_fusion.3
  67.2 5.8 %collective-permute-start.2 = (bf16[2,1024,128]{2,1,0:T(8,128)(2,1)S(1)}, bf16[2,1024,128]{2,1,0:T(8,128)(2,1)S(1)}, u32[]{:S(2)}, u32[]{:S(2)}) collective-permute-start(bf16[2,1024,128]{2,1,0:T(8,128)(2,1)S(1)} %get-tuple-element.17), channel_id=1, source_target_pairs={{0,14},{1,15},{2,0},{3,1},{4,2},{5,3},{6,4},{7,5},{8,6},{9,7},{10,... | collective-permute-start | bytes 1572872 | tf_op jit(solution)/shard_map/ppermute | solution.py:17
  73.1 0.0 collective-permute-done.8.refs_3_
  73.1 3.4 %copy-done.1 = bf16[2,2,32,32,1024]{4,3,2,1,0:T(8,128)(2,1)S(1)} copy-done((bf16[2,2,32,32,1024]{4,3,2,1,0:T(8,128)(2,1)S(1)}, bf16[2,2,32,32,1024]{4,3,2,1,0:T(8,128)(2,1)}, u32[]{:S(2)}) %copy-start.1) | copy-done | bytes 8388632
  76.5 2.2 %copy-done.5 = bf16[2,32,32,1024]{3,2,1,0:T(8,128)(2,1)S(1)} copy-done((bf16[2,32,32,1024]{3,2,1,0:T(8,128)(2,1)S(1)}, bf16[2,32,32,1024]{3,2,1,0:T(8,128)(2,1)}, u32[]{:S(2)}) %copy-start.5) | copy-done | bytes 4194328
  78.6 7.3 %shard_map.59 = bf16[128,2048]{1,0:T(8,128)(2,1)S(1)} custom-call(s32[11]{0:T(128)S(1)} %get-tuple-element.22.refs_0_, bf16[2,1024,1024]{2,1,0:T(8,128)(2,1)S(1)} %bitcast.31, bf16[2,1024,1024]{2,1,0:T(8,128)(2,1)} %collective-permute-done.1.refs_2_, bf16[2,1024,128]{2,1,0:T(8,128)(2,1)S(1)} %collective-permute-done.8.refs_3_, ...), custom_call_target="tpu_custom_call" | custom-call | flops 2147483648 | bytes 16777216 | tf_op jit(solution)/shard_map/pallas_call | solution.py:147
  86.0 0.1 collective-permute-start.9
  86.1 0.0 collective-permute-done.6.refs_6_
  86.1 7.3 %shard_map.58 = bf16[128,2048]{1,0:T(8,128)(2,1)S(1)} custom-call(s32[11]{0:T(128)S(1)} %get-tuple-element.23.refs_0_, bf16[2,1024,1024]{2,1,0:T(8,128)(2,1)S(1)} %bitcast.32, bf16[2,1024,1024]{2,1,0:T(8,128)(2,1)} %collective-permute-done.1.refs_2_, bf16[2,1024,128]{2,1,0:T(8,128)(2,1)S(1)} %collective-permute-done.3.refs_3_, ...), custom_call_target="tpu_custom_call" | custom-call | flops 2147483648 | bytes 16777216 | tf_op jit(solution)/shard_map/pallas_call | solution.py:147
  93.4 1.8 %collective-permute-start.7 = (bf16[128,2048]{1,0:T(8,128)(2,1)S(1)}, bf16[128,2048]{1,0:T(8,128)(2,1)S(1)}, u32[]{:S(2)}, u32[]{:S(2)}) collective-permute-start(bf16[128,2048]{1,0:T(8,128)(2,1)S(1)} %shard_map.58), channel_id=1, source_target_pairs={{0,8},{1,9},{2,10},{3,11},{4,12},{5,13},{6,14},{7,15},{8,0},{9,1},... | collective-permute-start | bytes 1572872 | tf_op jit(solution)/shard_map/ppermute | solution.py:17
  95.1 2.7 %collective-permute-done.9.refs_7_ = bf16[128,2048]{1,0:T(8,128)(2,1)S(1)} collective-permute-done((bf16[128,2048]{1,0:T(8,128)(2,1)S(1)}, bf16[128,2048]{1,0:T(8,128)(2,1)S(1)}, u32[]{:S(2)}, u32[]{:S(2)}) %collective-permute-start.9) | collective-permute-done | bytes 524320 | tf_op jit(solution)/shard_map/ppermute | solution.py:17
  97.8 11.3 %collective-permute-done.7.refs_6_ = bf16[128,2048]{1,0:T(8,128)(2,1)S(1)} collective-permute-done((bf16[128,2048]{1,0:T(8,128)(2,1)S(1)}, bf16[128,2048]{1,0:T(8,128)(2,1)S(1)}, u32[]{:S(2)}, u32[]{:S(2)}) %collective-permute-start.7) | collective-permute-done | bytes 524320 | tf_op jit(solution)/shard_map/ppermute | solution.py:17
  109.1 7.5 %shard_map.60 = (f32[64,2048]{1,0:T(8,128)S(1)}, bf16[64,2048]{1,0:T(8,128)(2,1)S(1)}, bf16[64,2048]{1,0:T(8,128)(2,1)S(1)}) custom-call(s32[11]{0:T(128)S(1)} %get-tuple-element.25.refs_0_, bf16[2,1024,1024]{2,1,0:T(8,128)(2,1)S(1)} %bitcast.33, bf16[2,1024,1024]{2,1,0:T(8,128)(2,1)} %collective-permute-done.1.refs_2_, ...), custom_call_target="tpu_custom_call" | custom-call | flops 2147483648 | bytes 16777216 | tf_op jit(solution)/shard_map/pallas_call | solution.py:147
  116.6 4.4 %collective-permute-start.10 = (bf16[64,2048]{1,0:T(8,128)(2,1)S(1)}, bf16[64,2048]{1,0:T(8,128)(2,1)S(1)}, u32[]{:S(2)}, u32[]{:S(2)}) collective-permute-start(bf16[64,2048]{1,0:T(8,128)(2,1)S(1)} %get-tuple-element.8), channel_id=1, source_target_pairs={{0,1},{1,3},{2,0},{3,2},{4,5},{5,7},{6,4},{7,6},{8,9},{9,11},{10,8... | collective-permute-start | bytes 786440 | tf_op jit(solution)/shard_map/ppermute | solution.py:17
  121.0 10.0 %collective-permute-start.11 = (bf16[64,2048]{1,0:T(8,128)(2,1)S(1)}, bf16[64,2048]{1,0:T(8,128)(2,1)S(1)}, u32[]{:S(2)}, u32[]{:S(2)}) collective-permute-start(bf16[64,2048]{1,0:T(8,128)(2,1)S(1)} %get-tuple-element.10), channel_id=1, source_target_pairs={{0,0},{1,2},{2,1},{3,3},{4,4},{5,6},{6,5},{7,7},{8,8},{9,10},{10,9... | collective-permute-start | bytes 786440 | tf_op jit(solution)/shard_map/ppermute | solution.py:17
  131.0 4.9 %collective-permute-done.11 = bf16[64,2048]{1,0:T(8,128)(2,1)S(1)} collective-permute-done((bf16[64,2048]{1,0:T(8,128)(2,1)S(1)}, bf16[64,2048]{1,0:T(8,128)(2,1)S(1)}, u32[]{:S(2)}, u32[]{:S(2)}) %collective-permute-start.11) | collective-permute-done | bytes 262176 | tf_op jit(solution)/shard_map/ppermute | solution.py:17
  136.0 0.1 add_multiply_fusion
  136.1 1.2 reshape.248
  (27 shorter events, 0.1 us)
Async XLA Ops:
  0.0 23.2 %collective-permute-start.1 = (bf16[2,1024,1024]{2,1,0:T(8,128)(2,1)}, bf16[2,1024,1024]{2,1,0:T(8,128)(2,1)}, u32[]{:S(2)}, u32[]{:S(2)}) collective-permute-start(bf16[2,1024,1024]{2,1,0:T(8,128)(2,1)} %bitcast.28), channel_id=1, source_target_pairs={{0,1},{1,0},{2,3},{3,2},{4,5},{5,4},{6,7},{7,6},{8,9},{9,8},{10,11... | collective-permute-start | bytes 12582920 | tf_op jit(solution)/shard_map/ppermute | solution.py:17
  2.5 20.1 %collective-permute-start = (bf16[8194]{0:T(1024)(128)(2,1)S(1)}, bf16[8194]{0:T(1024)(128)(2,1)S(1)}, u32[]{:S(2)}, u32[]{:S(2)}) collective-permute-start(bf16[8194]{0:T(1024)(128)(2,1)S(1)} %pad_maximum_fusion), channel_id=1, source_target_pairs={{0,1},{1,0},{2,3},{3,2},{4,5},{5,4},{6,7},{7,6},{8,9},{9,8},{10,11... | collective-permute-start | bytes 49172 | tf_op jit(solution)/shard_map/ppermute | solution.py:17
  3.0 2.2 %copy-start.3 = (bf16[2,32,32,1024]{3,2,1,0:T(8,128)(2,1)S(1)}, bf16[2,32,32,1024]{3,2,1,0:T(8,128)(2,1)}, u32[]{:S(2)}) copy-start(bf16[2,32,32,1024]{3,2,1,0:T(8,128)(2,1)} %coeffs_ref.1) | copy-start | bytes 12582916
  5.2 0.8 copy-start.6
  5.9 0.8 copy-start.7
  6.7 0.7 copy-start.8
  19.3 3.3 %copy-start = (bf16[2,2,32,32,1024]{4,3,2,1,0:T(8,128)(2,1)}, bf16[2,2,32,32,1024]{4,3,2,1,0:T(8,128)(2,1)S(1)}, u32[]{:S(2)}) copy-start(bf16[2,2,32,32,1024]{4,3,2,1,0:T(8,128)(2,1)S(1)} %shard_map.55) | copy-start | bytes 25165828
  22.6 11.3 %copy-start.9 = (s32[2,2]{1,0:T(2,128)S(1)}, s32[2,2]{1,0:T(2,128)}, u32[]{:S(2)}) copy-start(s32[2,2]{1,0:T(2,128)} %first_ref.3) | copy-start | bytes 52
  26.7 46.4 %collective-permute-start.8 = (bf16[2,1024,128]{2,1,0:T(8,128)(2,1)}, bf16[2,1024,128]{2,1,0:T(8,128)(2,1)S(1)}, u32[]{:S(2)}, u32[]{:S(2)}) collective-permute-start(bf16[2,1024,128]{2,1,0:T(8,128)(2,1)} %get-tuple-element.15), channel_id=1, source_target_pairs={{0,14},{1,15},{2,0},{3,1},{4,2},{5,3},{6,4},{7,5},{8,6},{9,7},{10,... | collective-permute-start | bytes 1572872 | tf_op jit(solution)/shard_map/ppermute | solution.py:17
  31.9 54.1 %collective-permute-start.3 = (bf16[2,1024,128]{2,1,0:T(8,128)(2,1)S(1)}, bf16[2,1024,128]{2,1,0:T(8,128)(2,1)S(1)}, u32[]{:S(2)}, u32[]{:S(2)}) collective-permute-start(bf16[2,1024,128]{2,1,0:T(8,128)(2,1)S(1)} %get-tuple-element.16), channel_id=1, source_target_pairs={{0,14},{1,15},{2,0},{3,1},{4,2},{5,3},{6,4},{7,5},{8,6},{9,7},{10,... | collective-permute-start | bytes 1572872 | tf_op jit(solution)/shard_map/ppermute | solution.py:17
  32.2 26.0 %collective-permute-start.5 = (bf16[2,1024,128]{2,1,0:T(8,128)(2,1)S(1)}, bf16[2,1024,128]{2,1,0:T(8,128)(2,1)S(1)}, u32[]{:S(2)}, u32[]{:S(2)}) collective-permute-start(bf16[2,1024,128]{2,1,0:T(8,128)(2,1)S(1)} %get-tuple-element.18), channel_id=1, source_target_pairs={{0,15},{1,0},{2,1},{3,2},{4,3},{5,4},{6,5},{7,6},{8,7},{9,8},{10,9... | collective-permute-start | bytes 1572872 | tf_op jit(solution)/shard_map/ppermute | solution.py:17
  33.2 24.9 %collective-permute-start.4 = (bf16[2,1024,128]{2,1,0:T(8,128)(2,1)S(1)}, bf16[2,1024,128]{2,1,0:T(8,128)(2,1)S(1)}, u32[]{:S(2)}, u32[]{:S(2)}) collective-permute-start(bf16[2,1024,128]{2,1,0:T(8,128)(2,1)S(1)} %get-tuple-element.19), channel_id=1, source_target_pairs={{0,14},{1,1},{2,0},{3,3},{4,2},{5,5},{6,4},{7,7},{8,6},{9,9},{10,8... | collective-permute-start | bytes 1572872 | tf_op jit(solution)/shard_map/ppermute | solution.py:17
  33.9 24.3 %slice-start = ((s8[8388608]{0:T(1024)(128)(4,1)}), s8[4194304]{0:T(1024)(128)(4,1)S(1)}, s32[]{:S(2)}) async-start(s8[8388608]{0:T(1024)(128)(4,1)} %bitcast.18), calls=%async_computation | async-start | bytes 8388608
  33.9 24.3 %slice-start.1 = ((s8[8388608]{0:T(1024)(128)(4,1)}), s8[4194304]{0:T(1024)(128)(4,1)S(1)}, s32[]{:S(2)}) async-start(s8[8388608]{0:T(1024)(128)(4,1)} %bitcast.18), calls=%async_computation.1 | async-start | bytes 8388608
  33.9 24.3 %copy-start.4 = (bf16[2,32,32,1024]{3,2,1,0:T(8,128)(2,1)S(1)}, bf16[2,32,32,1024]{3,2,1,0:T(8,128)(2,1)}, u32[]{:S(2)}) copy-start(bf16[2,32,32,1024]{3,2,1,0:T(8,128)(2,1)} %coeffs_ref.1) | copy-start | bytes 12582916
  46.7 3.2 %copy-start.2 = (bf16[2,2,32,32,1024]{4,3,2,1,0:T(8,128)(2,1)}, bf16[2,2,32,32,1024]{4,3,2,1,0:T(8,128)(2,1)S(1)}, u32[]{:S(2)}) copy-start(bf16[2,2,32,32,1024]{4,3,2,1,0:T(8,128)(2,1)S(1)} %shard_map.56) | copy-start | bytes 25165828
  65.5 20.5 %collective-permute-start.6 = (bf16[128,2048]{1,0:T(8,128)(2,1)S(1)}, bf16[128,2048]{1,0:T(8,128)(2,1)S(1)}, u32[]{:S(2)}, u32[]{:S(2)}) collective-permute-start(bf16[128,2048]{1,0:T(8,128)(2,1)S(1)} %shard_map.57), channel_id=1, source_target_pairs={{0,4},{1,5},{2,6},{3,7},{4,0},{5,1},{6,2},{7,3},{8,12},{9,13},{10,... | collective-permute-start | bytes 1572872 | tf_op jit(solution)/shard_map/ppermute | solution.py:17
  67.2 27.9 %collective-permute-start.2 = (bf16[2,1024,128]{2,1,0:T(8,128)(2,1)S(1)}, bf16[2,1024,128]{2,1,0:T(8,128)(2,1)S(1)}, u32[]{:S(2)}, u32[]{:S(2)}) collective-permute-start(bf16[2,1024,128]{2,1,0:T(8,128)(2,1)S(1)} %get-tuple-element.17), channel_id=1, source_target_pairs={{0,14},{1,15},{2,0},{3,1},{4,2},{5,3},{6,4},{7,5},{8,6},{9,7},{10,... | collective-permute-start | bytes 1572872 | tf_op jit(solution)/shard_map/ppermute | solution.py:17
  73.1 3.4 %copy-start.1 = (bf16[2,2,32,32,1024]{4,3,2,1,0:T(8,128)(2,1)S(1)}, bf16[2,2,32,32,1024]{4,3,2,1,0:T(8,128)(2,1)}, u32[]{:S(2)}) copy-start(bf16[2,2,32,32,1024]{4,3,2,1,0:T(8,128)(2,1)} %copy-done) | copy-start | bytes 25165828
  76.5 2.2 %copy-start.5 = (bf16[2,32,32,1024]{3,2,1,0:T(8,128)(2,1)S(1)}, bf16[2,32,32,1024]{3,2,1,0:T(8,128)(2,1)}, u32[]{:S(2)}) copy-start(bf16[2,32,32,1024]{3,2,1,0:T(8,128)(2,1)} %coeffs_ref.1) | copy-start | bytes 12582916
  86.0 11.9 %collective-permute-start.9 = (bf16[128,2048]{1,0:T(8,128)(2,1)S(1)}, bf16[128,2048]{1,0:T(8,128)(2,1)S(1)}, u32[]{:S(2)}, u32[]{:S(2)}) collective-permute-start(bf16[128,2048]{1,0:T(8,128)(2,1)S(1)} %shard_map.59), channel_id=1, source_target_pairs={{0,4},{1,5},{2,6},{3,7},{4,0},{5,1},{6,2},{7,3},{8,12},{9,13},{10,... | collective-permute-start | bytes 1572872 | tf_op jit(solution)/shard_map/ppermute | solution.py:17
  93.4 15.7 %collective-permute-start.7 = (bf16[128,2048]{1,0:T(8,128)(2,1)S(1)}, bf16[128,2048]{1,0:T(8,128)(2,1)S(1)}, u32[]{:S(2)}, u32[]{:S(2)}) collective-permute-start(bf16[128,2048]{1,0:T(8,128)(2,1)S(1)} %shard_map.58), channel_id=1, source_target_pairs={{0,8},{1,9},{2,10},{3,11},{4,12},{5,13},{6,14},{7,15},{8,0},{9,1},... | collective-permute-start | bytes 1572872 | tf_op jit(solution)/shard_map/ppermute | solution.py:17
  116.6 14.4 %collective-permute-start.10 = (bf16[64,2048]{1,0:T(8,128)(2,1)S(1)}, bf16[64,2048]{1,0:T(8,128)(2,1)S(1)}, u32[]{:S(2)}, u32[]{:S(2)}) collective-permute-start(bf16[64,2048]{1,0:T(8,128)(2,1)S(1)} %get-tuple-element.8), channel_id=1, source_target_pairs={{0,1},{1,3},{2,0},{3,2},{4,5},{5,7},{6,4},{7,6},{8,9},{9,11},{10,8... | collective-permute-start | bytes 786440 | tf_op jit(solution)/shard_map/ppermute | solution.py:17
  121.0 15.0 %collective-permute-start.11 = (bf16[64,2048]{1,0:T(8,128)(2,1)S(1)}, bf16[64,2048]{1,0:T(8,128)(2,1)S(1)}, u32[]{:S(2)}, u32[]{:S(2)}) collective-permute-start(bf16[64,2048]{1,0:T(8,128)(2,1)S(1)} %get-tuple-element.10), channel_id=1, source_target_pairs={{0,0},{1,2},{2,1},{3,3},{4,4},{5,6},{6,5},{7,7},{8,8},{9,10},{10,9... | collective-permute-start | bytes 786440 | tf_op jit(solution)/shard_map/ppermute | solution.py:17
where the time goes:
time: 138 us; the launch traced here: 137 us
  Pallas kernels  54.1 us (39%)
  starting transfers between devices  31.5 us (23%)
  waiting for transfers between devices  27.1 us (20%)
  local copies, waits for them, and re-layouts  19.7 us (14%)
  other arithmetic  4.58 us (3%)
    ppermute x12, starting transfers between devices, permute(): lax.ppermute(x, 'ka', [(i, j % size) for i, j in pairs if j is not None])  31.5 us
    pallas_call x4, Pallas kernels, rows_of(): pl.pallas_call(functools.partial(rows_kernel, len(arrived), last), out_sh...  29.4 us
    ppermute x12, waiting for transfers between devices, permute(): lax.ppermute(x, 'ka', [(i, j % size) for i, j in pairs if j is not None])  27.1 us
    pallas_call x2, Pallas kernels, products_of(): pl.pallas_call(products_kernel, out_shape=jax.ShapeDtypeStruct((k_local,...  24.7 us
    unnamed x24, local copies, waits for them, and re-layouts  16.5 us
    select_n x1, other arithmetic, on_two_by_four(): sent = jnp.where(core == 0, cut(flat, block), cut(sib, block + 1))  3.49 us
  transfers between devices with their start and end apart: 12, of which 4 were waited for; matrix products, arithmetic and copies ran while one was open for 2% of the time, Pallas kernels for 34%

commit v1 on v0

--- a/solution.py
+++ b/solution.py
@@ -98,136 +98,105 @@
     return out.reshape(k_local, modes, bands_c * bands_v, excitons)
 
 
-def rows_kernel(adds, last, *refs):
-    pick_ref, own_ref, sib_ref, next_ref, p_own_ref, p_sib_ref = refs[:6]
-    arrived = refs[6:6 + adds]
-    outs, left = refs[6 + adds:-1], refs[-1]
+def rows_kernel(pick_ref, own_ref, next_ref, right_ref, keep_ref, send_ref, left):
     k_local = own_ref.shape[0]
 
     @pl.when(pl.program_id(0) == 0)
     def _():
-        for k in range(2 * k_local):
-            which, place = pick_ref[2 * k], pick_ref[2 * k + 1]
-            for source, ref in enumerate((own_ref, sib_ref, next_ref)):
-                @pl.when(which == source)
-                def _():
-                    left[k] = ref[place].T
+        for k in range(k_local):
+            place = pick_ref[k]
+
+            @pl.when(place < k_local)
+            def _():
+                left[k] = own_ref[place].T
+
+            @pl.when(place >= k_local)
+            def _():
+                left[k] = next_ref[place - k_local].T
 
     total = None
-    for k in range(2 * k_local):
-        right = p_own_ref if k < k_local else p_sib_ref
-        term = jnp.dot(left[k], right[k % k_local, 0], preferred_element_type=jnp.float32)
+    for k in range(k_local):
+        term = jnp.dot(left[k], right_ref[k, 0], preferred_element_type=jnp.float32)
         total = term if total is None else total + term
-    for ref in arrived:
-        total = total + ref[...].astype(jnp.float32)
-    if not last:
-        outs[0][...] = total.astype(jnp.bfloat16)
-        return
-    half = total.shape[0] // 2
-    low, high = total[:half], total[half:]
-    core, first = pick_ref[4 * k_local + 1], pick_ref[4 * k_local + 2]
-    outs[0][...] = jnp.where(core == 0, low, high)
-    outs[1][...] = jnp.where(first == 0, low, high).astype(jnp.bfloat16)
-    outs[2][...] = jnp.where(first == 0, high, low).astype(jnp.bfloat16)
-
-
-def rows_of(pick, own, sib, following, p_own, p_sib, arrived, last, width):
+    core = pick_ref[k_local + 1]
+    width, tile = total.shape
+    parts = total.reshape(2, 2, width // 4, tile)
+    low, high = parts[:, 0].reshape(width // 2, tile), parts[:, 1].reshape(width // 2, tile)
+    keep_ref[...] = jnp.where(core == 0, low, high)
+    send_ref[...] = jnp.where(core == 0, high, low).astype(jnp.bfloat16)
+
+
+def rows_of(pick, own, following, products, width):
     k_local, depth, excitons = own.shape
-    modes = p_own.shape[1]
+    modes = products.shape[1]
     tile = 512
     per_mode = excitons // tile
     columns = modes * excitons
-    if last:
-        half = width // 2
-        outs = [((half, columns), jnp.float32)] + 2 * [((half, columns), jnp.bfloat16)]
-    else:
-        outs = [((width, columns), jnp.bfloat16)]
-    block = lambda j, pick: (0, 0, pick[4 * k_local])
-    right = pl.BlockSpec((k_local, 1, depth, tile), lambda j, pick: (0, j // per_mode, 0, j % per_mode))
     return pl.pallas_call(
-        functools.partial(rows_kernel, len(arrived), last),
-        out_shape=[jax.ShapeDtypeStruct(*o) for o in outs],
+        rows_kernel,
+        out_shape=[
+            jax.ShapeDtypeStruct((width // 2, columns), jnp.float32),
+            jax.ShapeDtypeStruct((width // 2, columns), jnp.bfloat16),
+        ],
         grid_spec=pltpu.PrefetchScalarGridSpec(
             num_scalar_prefetch=1,
             grid=(modes * per_mode,),
             in_specs=[
-                pl.BlockSpec((k_local, depth, width), block),
-                pl.BlockSpec((k_local, depth, width), block),
+                pl.BlockSpec((k_local, depth, width), lambda j, pick: (0, 0, pick[k_local])),
                 pl.BlockSpec((k_local, depth, width), lambda j, pick: (0, 0, 0)),
-                right,
-                right,
-            ] + [pl.BlockSpec((width, tile), lambda j, pick: (0, j)) for _ in arrived],
-            out_specs=[pl.BlockSpec((o[0][0], tile), lambda j, pick: (0, j)) for o in outs],
-            scratch_shapes=[pltpu.VMEM((2 * k_local, width, depth), jnp.bfloat16)],
+                pl.BlockSpec(
+                    (k_local, 1, depth, tile), lambda j, pick: (0, j // per_mode, 0, j % per_mode)
+                ),
+            ],
+            out_specs=[pl.BlockSpec((width // 2, tile), lambda j, pick: (0, j))] * 2,
+            scratch_shapes=[pltpu.VMEM((k_local, width, depth), jnp.bfloat16)],
         ),
         compiler_params=pltpu.CompilerParams(vmem_limit_bytes=32 * MIB),
         cost_estimate=pl.CostEstimate(
-            flops=4 * k_local * depth * width * columns,
-            bytes_accessed=4 * k_local * depth * columns,
+            flops=2 * k_local * depth * width * columns,
+            bytes_accessed=2 * k_local * depth * columns,
             transcendentals=0,
         ),
-    )(pick, own, sib, following, p_own, p_sib, *arrived)
+    )(pick, own, following, products)
 
 
 def on_two_by_four(coeffs, g_cond, g_val, k_plus_q, band_first, norm_factor):
     k_local, bands_c, bands_v, excitons = coeffs.shape
     modes = g_cond.shape[1]
     size = lax.axis_size("ka")
-    chips = size // 2
-    width = excitons // chips
+    width = excitons // 4
     me = lax.axis_index("ka")
-    core, x, z = me % 2, me // 2 % 2, me // 4
+    core, x, z = me & 1, me >> 1 & 1, me >> 2
     flat = coeffs.reshape(k_local, bands_c * bands_v, excitons)
 
-    offsets = jnp.mod(k_plus_q - me * k_local, k_local * size)
-    small = jnp.concatenate(
-        (g_cond.reshape(-1), g_val.reshape(-1), offsets.astype(jnp.bfloat16))
-    )
-    sib_small = permute(small, lambda i: i ^ 1)
-    sib = permute(flat, lambda i: i ^ 1)
-
-    def cut(array, block):
-        return lax.dynamic_slice_in_dim(array, block * width, width, 2)
-
-    behind_z = jnp.mod(me // 2 - 1, chips) // 2
-    following = []
+    behind_z = (me + size - 1) % size >> 2
+    following, source = [], flat
     for step in range(4):
-        block = 2 * (behind_z ^ (3 - step))
-        if step == 0:
-            to_first = permute(cut(flat, block), lambda i: i - 2 if i % 2 == 0 else i)
-            to_second = permute(cut(flat, block + 1), lambda i: i - 1 if i % 2 == 0 else i - 1)
-            following.append(jnp.where(core == 0, to_first, to_second))
-        else:
-            sent = jnp.where(core == 0, cut(flat, block), cut(sib, block + 1))
-            following.append(permute(sent, lambda i: i - 2))
-
-    sib_cond = sib_small[:g_cond.size].reshape(g_cond.shape)
-    sib_val = sib_small[g_cond.size:g_cond.size + g_val.size].reshape(g_val.shape)
-    sib_offsets = sib_small[g_cond.size + g_val.size:].astype(jnp.int32)
-    p_own = products_of(coeffs, g_cond, g_val, band_first)
-    p_sib = products_of(sib.reshape(coeffs.shape), sib_cond, sib_val, band_first)
-
-    places = jnp.concatenate((offsets + core * k_local, sib_offsets + (1 - core) * k_local))
-    of_block = places // k_local
-    which = jnp.where(of_block == 2, 2, of_block ^ core)
-    picks = jnp.stack((which, places % k_local), 1).reshape(-1).astype(jnp.int32)
-    keeper = core == x
-    first = jnp.where(keeper, 1 - core, core)
-
-    def rows(step, arrived, last=False):
-        block = 2 * (z ^ (3 - step)) + core
-        pick = jnp.concatenate((picks, jnp.stack((block, core, first)).astype(jnp.int32)))
-        return rows_of(pick, flat, sib, following[step], p_own, p_sib, arrived, last, width)
-
-    far = permute(rows(0, [])[0], lambda i: i ^ 4)
-    pair = permute(rows(1, [far])[0], lambda i: i ^ 8)
-    near = permute(rows(2, [])[0], lambda i: i ^ 4)
-    mine, sent_a, sent_b = rows(3, [pair, near], True)
-    is_keeper = lambda i: i % 2 == i // 2 % 2
-    got_a = permute(sent_a, lambda i: i ^ 1 if is_keeper(i) else i ^ 2)
-    got_b = permute(sent_b, lambda i: i if is_keeper(i) else i ^ 3)
-    total = got_a.astype(jnp.float32) + jnp.where(keeper, mine, got_b.astype(jnp.float32))
-    return (total * norm_factor).reshape(width // 2, modes, excitons)
+        piece = lax.dynamic_slice_in_dim(source, (behind_z ^ (3 - step)) * width, width, 2)
+        following.append(permute(piece, lambda i: i - 1))
+        source, piece = lax.optimization_barrier((source, piece))
+
+    products = products_of(coeffs, g_cond, g_val, band_first)
+    places = jnp.mod(k_plus_q - me * k_local, k_local * size)
+
+    def rows(step):
+        pick = jnp.concatenate((places, jnp.stack((z ^ (3 - step), core))))
+        keep, send = rows_of(pick, flat, following[step], products, width)
+        return keep, permute(send, lambda i: i ^ 1).astype(jnp.float32)
+
+    keep, other = rows(0)
+    far = permute((keep + other).astype(jnp.bfloat16), lambda i: i ^ 4)
+    keep, other = rows(1)
+    pair = permute((keep + other + far.astype(jnp.float32)).astype(jnp.bfloat16), lambda i: i ^ 8)
+    keep, other = rows(2)
+    near = permute((keep + other).astype(jnp.bfloat16), lambda i: i ^ 4)
+    keep, other = rows(3)
+    total = keep + other + near.astype(jnp.float32) + pair.astype(jnp.float32)
+    total = total.reshape(2, width // 4, modes * excitons)
+    mine = lax.dynamic_index_in_dim(total, x, 0, keepdims=False)
+    sent = lax.dynamic_index_in_dim(total, 1 - x, 0, keepdims=False).astype(jnp.bfloat16)
+    total = mine + permute(sent, lambda i: i ^ 2).astype(jnp.float32)
+    return (total * norm_factor).reshape(width // 4, modes, excitons)
 
 
 def on_any(coeffs, g_cond, g_val, k_plus_q, band_first, norm_factor):
@@ -252,7 +221,7 @@
     k_local, bands_c, bands_v, excitons = coeffs.shape
     size = lax.axis_size("ka")
     norm_factor = 1.0 / math.sqrt(bands_c * bands_v * k_local * size)
-    whole_tiles = excitons % (size // 2 * 128) == 0
+    whole_tiles = excitons % (4 * 128) == 0
     plan = on_two_by_four if size == 16 and whole_tiles else on_any
     return plan(coeffs, g_cond, g_val, k_plus_q, band_first, norm_factor)
 

time: 138 us -> 109 us (0.79)
  the two profiles are of different devices: /device:TPU:1 before, /device:TPU:0 now
where the time goes in v1:
time: 109 us; the launch traced here: 108 us
  waiting for transfers between devices  37.4 us (34%)
  Pallas kernels  32.7 us (30%)
  local copies, waits for them, and re-layouts  22.2 us (20%)
  starting transfers between devices  11.3 us (10%)
  other arithmetic  4.6 us (4%)
    ppermute x12, waiting for transfers between devices, permute(): lax.ppermute(x, 'ka', [(i, j % size) for i, j in pairs if j is not None])  37.4 us
    pallas_call x4, Pallas kernels, rows_of(): pl.pallas_call(rows_kernel, out_shape=[jax.ShapeDtypeStruct((width // 2,...  20.8 us
    pallas_call x1, Pallas kernels, products_of(): pl.pallas_call(products_kernel, out_shape=jax.ShapeDtypeStruct((k_local,...  12 us
    unnamed x22, local copies, waits for them, and re-layouts  11.7 us
    ppermute x12, starting transfers between devices, permute(): lax.ppermute(x, 'ka', [(i, j % size) for i, j in pairs if j is not None])  11.3 us
    dynamic_slice x4, local copies, waits for them, and re-layouts, on_two_by_four(): lax.dynamic_slice_in_dim(source, (behind_z ^ 3 - step) * width, width, 2)  9.28 us
  transfers between devices with their start and end apart: 12, of which 4 were waited for; matrix products, arithmetic and copies ran while one was open for 9% of the time, Pallas kernels for 30%

profile of v1, /device:TPU:0, one launch (start us, length us, event | category | flops | bytes accessed | tf_op | source)
XLA Modules:
  0.0 108.4 jit_solution(11948719475768329459)
XLA Ops:
  0.0 2.3 %constant_dynamic-slice_fusion.3 = bf16[2,1024,256]{2,1,0:T(8,128)(2,1)} fusion(bf16[2,1024,1024]{2,1,0:T(8,128)(2,1)} %bitcast.18, s32[]{:T(128)S(6)} %select_n.34), kind=kLoop, calls=%fused_computation.14 | loop fusion | bytes 2097156 | tf_op jit(solution)/shard_map/dynamic_slice | solution.py:175
  2.4 5.4 %collective-permute-start.7 = (bf16[2,1024,256]{2,1,0:T(8,128)(2,1)}, bf16[2,1024,256]{2,1,0:T(8,128)(2,1)S(1)}, u32[]{:S(2)}, u32[]{:S(2)}) collective-permute-start(bf16[2,1024,256]{2,1,0:T(8,128)(2,1)} %constant_dynamic-slice_fusion.3), channel_id=1, source_target_pairs={{0,15},{1,0},{2,1},{3,2},{4,3},{5,4},{6,5},{7,6},{8,7},{9,8},{10,9... | collective-permute-start | bytes 3145736 | tf_op jit(solution)/shard_map/ppermute | solution.py:17
  7.8 2.3 %constant_dynamic-slice_fusion.2 = bf16[2,1024,256]{2,1,0:T(8,128)(2,1)} fusion(bf16[2,1024,1024]{2,1,0:T(8,128)(2,1)} %bitcast.19, s32[]{:T(128)S(6)} %select_n.35), kind=kLoop, calls=%fused_computation.13 | loop fusion | bytes 2097156 | tf_op jit(solution)/shard_map/dynamic_slice | solution.py:175
  10.1 0.7 collective-permute-start.5
  10.8 2.3 %constant_dynamic-slice_fusion.1 = bf16[2,1024,256]{2,1,0:T(8,128)(2,1)} fusion(bf16[2,1024,1024]{2,1,0:T(8,128)(2,1)} %bitcast.20, s32[]{:T(128)S(6)} %select_n.36), kind=kLoop, calls=%fused_computation.12 | loop fusion | bytes 2097156 | tf_op jit(solution)/shard_map/dynamic_slice | solution.py:175
  13.0 0.0 collective-permute-start.2
  13.1 2.4 %constant_dynamic-slice_fusion = bf16[2,1024,256]{2,1,0:T(8,128)(2,1)} fusion(bf16[2,1024,1024]{2,1,0:T(8,128)(2,1)} %bitcast.21, s32[]{:T(128)S(6)} %select_n.37), kind=kLoop, calls=%fused_computation.11 | loop fusion | bytes 2097156 | tf_op jit(solution)/shard_map/dynamic_slice | solution.py:175
  15.4 0.6 collective-permute-start
  16.1 0.1 add_add_fusion.3.pick_ref
  16.2 0.0 copy-start.2
  16.2 2.2 %copy-done.2 = bf16[2,32,32,1024]{3,2,1,0:T(8,128)(2,1)S(1)} copy-done((bf16[2,32,32,1024]{3,2,1,0:T(8,128)(2,1)S(1)}, bf16[2,32,32,1024]{3,2,1,0:T(8,128)(2,1)}, u32[]{:S(2)}) %copy-start.2) | copy-done | bytes 4194328
  18.4 12.0 %shard_map.55 = bf16[2,2,32,32,1024]{4,3,2,1,0:T(8,128)(2,1)S(1)} custom-call(s32[2,2]{1,0:T(2,128)S(1)} %copy-done.8, bf16[2,32,32,1024]{3,2,1,0:T(8,128)(2,1)S(1)} %copy-done.2, bf16[2,2,32,32]{3,2,1,0:T(8,128)(2,1)S(1)} %copy-done.6, bf16[2,2,32,32]{3,2,1,0:T(8,128)(2,1)S(1)} %copy-done.7), custom_call_target="tpu_custom_call" | custom-call | flops 6442450944 | bytes 12582912 | tf_op jit(solution)/shard_map/pallas_call | solution.py:78
  30.3 0.0 collective-permute-done.7.next_ref
  30.4 1.1 copy-done.4
  31.4 2.0 %copy-done.5 = bf16[2,1024,256]{2,1,0:T(8,128)(2,1)S(1)} copy-done((bf16[2,1024,256]{2,1,0:T(8,128)(2,1)S(1)}, bf16[2,1024,256]{2,1,0:T(8,128)(2,1)}, u32[]{:S(2)}) %copy-start.5) | copy-done | bytes 1048600
  33.5 5.4 %shard_map.59 = (f32[128,2048]{1,0:T(8,128)S(1)}, bf16[128,2048]{1,0:T(8,128)(2,1)}) custom-call(s32[4]{0:T(128)S(1)} %add_add_fusion.3.pick_ref, bf16[2,1024,1024]{2,1,0:T(8,128)(2,1)S(1)} %bitcast.22, bf16[2,1024,256]{2,1,0:T(8,128)(2,1)S(1)} %copy-done.5, bf16[2,2,1024,1024]{3,2,1,0:T(8,128)(2,1)S(1)} %bitcast.14), custom_call_target="tpu_custom_call" | custom-call | flops 2147483648 | bytes 8388608 | tf_op jit(solution)/shard_map/pallas_call | solution.py:135
  38.8 0.0 collective-permute-start.8
  38.8 0.1 add_add_fusion
  38.9 0.0 collective-permute-done.5.next_ref
  38.9 3.4 %copy-done.1 = bf16[2,2,32,32,1024]{4,3,2,1,0:T(8,128)(2,1)S(1)} copy-done((bf16[2,2,32,32,1024]{4,3,2,1,0:T(8,128)(2,1)S(1)}, bf16[2,2,32,32,1024]{4,3,2,1,0:T(8,128)(2,1)}, u32[]{:S(2)}) %copy-start.1) | copy-done | bytes 8388632
  42.3 2.2 %copy-done.3 = bf16[2,32,32,1024]{3,2,1,0:T(8,128)(2,1)S(1)} copy-done((bf16[2,32,32,1024]{3,2,1,0:T(8,128)(2,1)S(1)}, bf16[2,32,32,1024]{3,2,1,0:T(8,128)(2,1)}, u32[]{:S(2)}) %copy-start.3) | copy-done | bytes 4194328
  44.5 4.8 %shard_map.58 = (f32[128,2048]{1,0:T(8,128)S(1)}, bf16[128,2048]{1,0:T(8,128)(2,1)S(1)}) custom-call(s32[4]{0:T(128)S(1)} %get-tuple-element.29.pick_ref, bf16[2,1024,1024]{2,1,0:T(8,128)(2,1)S(1)} %bitcast.23, bf16[2,1024,256]{2,1,0:T(8,128)(2,1)S(1)} %collective-permute-done.5.next_ref, bf16[2,2,1024,1024]{3,2,1,0:T(8,128)(2,1)S(1)} %bitcast.15), custom_call_target="tpu_custom_call" | custom-call | flops 2147483648 | bytes 8388608 | tf_op jit(solution)/shard_map/pallas_call | solution.py:135
  49.3 0.6 collective-permute-start.6
  49.8 0.0 collective-permute-done.2.next_ref
  49.8 5.8 %shard_map.57 = (f32[128,2048]{1,0:T(8,128)S(1)}, bf16[128,2048]{1,0:T(8,128)(2,1)S(1)}) custom-call(s32[4]{0:T(128)S(1)} %get-tuple-element.28.pick_ref, bf16[2,1024,1024]{2,1,0:T(8,128)(2,1)S(1)} %bitcast.24, bf16[2,1024,256]{2,1,0:T(8,128)(2,1)} %collective-permute-done.2.next_ref, bf16[2,2,1024,1024]{3,2,1,0:T(8,128)(2,1)S(1)} %bitcast.16), custom_call_target="tpu_custom_call" | custom-call | flops 2147483648 | bytes 8388608 | tf_op jit(solution)/shard_map/pallas_call | solution.py:135
  55.7 0.1 collective-permute-start.3
  55.8 0.0 collective-permute-done.8
  55.8 1.2 %add_convert_fusion.1 = bf16[128,2048]{1,0:T(8,128)(2,1)S(1)} fusion(f32[128,2048]{1,0:T(8,128)S(1)} %get-tuple-element.25, bf16[128,2048]{1,0:T(8,128)(2,1)} %collective-permute-done.8), kind=kLoop, calls=%fused_computation.2 | loop fusion | flops 786432 | bytes 2097152 | tf_op jit(solution)/shard_map/convert_element_type | solution.py:188
  56.9 0.1 collective-permute-start.9
  57.0 0.0 collective-permute-done.next_ref
  57.0 4.8 %shard_map.56 = (f32[128,2048]{1,0:T(8,128)S(1)}, bf16[128,2048]{1,0:T(8,128)(2,1)S(1)}) custom-call(s32[4]{0:T(128)S(1)} %get-tuple-element.27.pick_ref, bf16[2,1024,1024]{2,1,0:T(8,128)(2,1)S(1)} %bitcast.25, bf16[2,1024,256]{2,1,0:T(8,128)(2,1)S(1)} %collective-permute-done.next_ref, bf16[2,2,1024,1024]{3,2,1,0:T(8,128)(2,1)S(1)} %bitcast.17), custom_call_target="tpu_custom_call" | custom-call | flops 2147483648 | bytes 8388608 | tf_op jit(solution)/shard_map/pallas_call | solution.py:135
  61.8 0.6 collective-permute-start.1
  62.4 0.0 collective-permute-done.3
  62.4 0.9 add_convert_fusion.2
  63.3 1.7 %collective-permute-start.4 = (bf16[128,2048]{1,0:T(8,128)(2,1)}, bf16[128,2048]{1,0:T(8,128)(2,1)S(1)}, u32[]{:S(2)}, u32[]{:S(2)}) collective-permute-start(bf16[128,2048]{1,0:T(8,128)(2,1)} %add_convert_fusion.2), channel_id=1, source_target_pairs={{0,4},{1,5},{2,6},{3,7},{4,0},{5,1},{6,2},{7,3},{8,12},{9,13},{10,... | collective-permute-start | bytes 1572872 | tf_op jit(solution)/shard_map/ppermute | solution.py:17
  65.0 0.0 collective-permute-done.6
  65.0 6.7 %collective-permute-done.9 = bf16[128,2048]{1,0:T(8,128)(2,1)S(1)} collective-permute-done((bf16[128,2048]{1,0:T(8,128)(2,1)S(1)}, bf16[128,2048]{1,0:T(8,128)(2,1)S(1)}, u32[]{:S(2)}, u32[]{:S(2)}) %collective-permute-start.9) | collective-permute-done | bytes 524320 | tf_op jit(solution)/shard_map/ppermute | solution.py:17
  71.7 1.0 add_convert_fusion
  72.7 0.0 collective-permute-start.10
  72.7 0.0 collective-permute-done.1
  72.7 15.6 %collective-permute-done.4 = bf16[128,2048]{1,0:T(8,128)(2,1)S(1)} collective-permute-done((bf16[128,2048]{1,0:T(8,128)(2,1)}, bf16[128,2048]{1,0:T(8,128)(2,1)S(1)}, u32[]{:S(2)}, u32[]{:S(2)}) %collective-permute-start.4) | collective-permute-done | bytes 524320 | tf_op jit(solution)/shard_map/ppermute | solution.py:17
  88.3 9.9 %collective-permute-done.10 = bf16[128,2048]{1,0:T(8,128)(2,1)S(1)} collective-permute-done((bf16[128,2048]{1,0:T(8,128)(2,1)}, bf16[128,2048]{1,0:T(8,128)(2,1)S(1)}, u32[]{:S(2)}, u32[]{:S(2)}) %collective-permute-start.10) | collective-permute-done | bytes 524320 | tf_op jit(solution)/shard_map/ppermute | solution.py:17
  98.2 0.8 copy-done.9
  99.0 1.3 %convert_add_fusion = f32[128,2048]{1,0:T(8,128)S(1)} fusion(bf16[128,2048]{1,0:T(8,128)(2,1)} %copy-done.9, bf16[128,2048]{1,0:T(8,128)(2,1)S(1)} %collective-permute-done.4, f32[128,2048]{1,0:T(8,128)S(1)} %get-tuple-element.19, bf16[128,2048]{1,0:T(8,128)(2,1)S(1)} %collective-permute-done.1), kind=kLoop, calls=%fused_computation | loop fusion | flops 1572864 | bytes 3670016 | tf_op jit(solution)/shard_map/add | solution.py:194
  100.4 1.6 %collective-permute-start.11 = (bf16[64,2048]{1,0:T(8,128)(2,1)S(1)}, bf16[64,2048]{1,0:T(8,128)(2,1)S(1)}, u32[]{:S(2)}, u32[]{:S(2)}) collective-permute-start(bf16[64,2048]{1,0:T(8,128)(2,1)S(1)} %fusion.1), channel_id=1, source_target_pairs={{0,2},{1,3},{2,0},{3,1},{4,6},{5,7},{6,4},{7,5},{8,10},{9,11},{10,... | collective-permute-start | bytes 786440 | tf_op jit(solution)/shard_map/ppermute | solution.py:17
  102.0 5.1 %collective-permute-done.11 = bf16[64,2048]{1,0:T(8,128)(2,1)S(1)} collective-permute-done((bf16[64,2048]{1,0:T(8,128)(2,1)S(1)}, bf16[64,2048]{1,0:T(8,128)(2,1)S(1)}, u32[]{:S(2)}, u32[]{:S(2)}) %collective-permute-start.11) | collective-permute-done | bytes 262176 | tf_op jit(solution)/shard_map/ppermute | solution.py:17
  107.1 0.1 fusion
  107.2 1.2 %reshape.16 = f32[64,2,1024]{2,1,0:T(2,128)} reshape(f32[64,2048]{1,0:T(8,128)S(1)} %fusion) | data formatting | bytes 1048576 | tf_op jit(solution)/shard_map/reshape | solution.py:199
  (17 shorter events, 0.1 us)
Async XLA Ops:
  0.0 16.1 %copy-start.10 = (s32[2]{0:T(128)S(1)}, s32[2]{0:T(128)}, u32[]{:S(2)}) copy-start(s32[2]{0:T(128)} %param.8) | copy-start | bytes 28
  0.0 16.2 %copy-start.6 = (bf16[2,2,32,32]{3,2,1,0:T(8,128)(2,1)S(1)}, bf16[2,2,32,32]{3,2,1,0:T(8,128)(2,1)}, u32[]{:S(2)}) copy-start(bf16[2,2,32,32]{3,2,1,0:T(8,128)(2,1)} %cond_ref.1) | copy-start | bytes 24580
  0.0 16.2 %copy-start.7 = (bf16[2,2,32,32]{3,2,1,0:T(8,128)(2,1)S(1)}, bf16[2,2,32,32]{3,2,1,0:T(8,128)(2,1)}, u32[]{:S(2)}) copy-start(bf16[2,2,32,32]{3,2,1,0:T(8,128)(2,1)} %val_ref.1) | copy-start | bytes 24580
  0.0 16.2 %copy-start.8 = (s32[2,2]{1,0:T(2,128)S(1)}, s32[2,2]{1,0:T(2,128)}, u32[]{:S(2)}) copy-start(s32[2,2]{1,0:T(2,128)} %first_ref.1) | copy-start | bytes 52
  2.4 28.0 %collective-permute-start.7 = (bf16[2,1024,256]{2,1,0:T(8,128)(2,1)}, bf16[2,1024,256]{2,1,0:T(8,128)(2,1)S(1)}, u32[]{:S(2)}, u32[]{:S(2)}) collective-permute-start(bf16[2,1024,256]{2,1,0:T(8,128)(2,1)} %constant_dynamic-slice_fusion.3), channel_id=1, source_target_pairs={{0,15},{1,0},{2,1},{3,2},{4,3},{5,4},{6,5},{7,6},{8,7},{9,8},{10,9... | collective-permute-start | bytes 3145736 | tf_op jit(solution)/shard_map/ppermute | solution.py:17
  10.1 28.8 %collective-permute-start.5 = (bf16[2,1024,256]{2,1,0:T(8,128)(2,1)}, bf16[2,1024,256]{2,1,0:T(8,128)(2,1)S(1)}, u32[]{:S(2)}, u32[]{:S(2)}) collective-permute-start(bf16[2,1024,256]{2,1,0:T(8,128)(2,1)} %constant_dynamic-slice_fusion.2), channel_id=1, source_target_pairs={{0,15},{1,0},{2,1},{3,2},{4,3},{5,4},{6,5},{7,6},{8,7},{9,8},{10,9... | collective-permute-start | bytes 3145736 | tf_op jit(solution)/shard_map/ppermute | solution.py:17
  13.0 36.8 %collective-permute-start.2 = (bf16[2,1024,256]{2,1,0:T(8,128)(2,1)}, bf16[2,1024,256]{2,1,0:T(8,128)(2,1)}, u32[]{:S(2)}, u32[]{:S(2)}) collective-permute-start(bf16[2,1024,256]{2,1,0:T(8,128)(2,1)} %constant_dynamic-slice_fusion.1), channel_id=1, source_target_pairs={{0,15},{1,0},{2,1},{3,2},{4,3},{5,4},{6,5},{7,6},{8,7},{9,8},{10,9... | collective-permute-start | bytes 3145736 | tf_op jit(solution)/shard_map/ppermute | solution.py:17
  15.4 41.6 %collective-permute-start = (bf16[2,1024,256]{2,1,0:T(8,128)(2,1)}, bf16[2,1024,256]{2,1,0:T(8,128)(2,1)S(1)}, u32[]{:S(2)}, u32[]{:S(2)}) collective-permute-start(bf16[2,1024,256]{2,1,0:T(8,128)(2,1)} %constant_dynamic-slice_fusion), channel_id=1, source_target_pairs={{0,15},{1,0},{2,1},{3,2},{4,3},{5,4},{6,5},{7,6},{8,7},{9,8},{10,9... | collective-permute-start | bytes 3145736 | tf_op jit(solution)/shard_map/ppermute | solution.py:17
  16.2 2.2 %copy-start.2 = (bf16[2,32,32,1024]{3,2,1,0:T(8,128)(2,1)S(1)}, bf16[2,32,32,1024]{3,2,1,0:T(8,128)(2,1)}, u32[]{:S(2)}) copy-start(bf16[2,32,32,1024]{3,2,1,0:T(8,128)(2,1)} %coeffs_ref.1) | copy-start | bytes 12582916
  30.3 8.5 %copy-start = (bf16[2,2,32,32,1024]{4,3,2,1,0:T(8,128)(2,1)}, bf16[2,2,32,32,1024]{4,3,2,1,0:T(8,128)(2,1)S(1)}, u32[]{:S(2)}) copy-start(bf16[2,2,32,32,1024]{4,3,2,1,0:T(8,128)(2,1)S(1)} %shard_map.55) | copy-start | bytes 25165828
  30.3 1.1 %copy-start.4 = (bf16[2,1024,256]{2,1,0:T(8,128)(2,1)}, bf16[2,1024,256]{2,1,0:T(8,128)(2,1)S(1)}, u32[]{:S(2)}) copy-start(bf16[2,1024,256]{2,1,0:T(8,128)(2,1)S(1)} %collective-permute-done.7.next_ref) | copy-start | bytes 3145732
  31.4 2.0 %copy-start.5 = (bf16[2,1024,256]{2,1,0:T(8,128)(2,1)S(1)}, bf16[2,1024,256]{2,1,0:T(8,128)(2,1)}, u32[]{:S(2)}) copy-start(bf16[2,1024,256]{2,1,0:T(8,128)(2,1)} %copy-done.4) | copy-start | bytes 3145732
  38.8 17.0 %collective-permute-start.8 = (bf16[128,2048]{1,0:T(8,128)(2,1)}, bf16[128,2048]{1,0:T(8,128)(2,1)}, u32[]{:S(2)}, u32[]{:S(2)}) collective-permute-start(bf16[128,2048]{1,0:T(8,128)(2,1)} %get-tuple-element.26), channel_id=1, source_target_pairs={{0,1},{1,0},{2,3},{3,2},{4,5},{5,4},{6,7},{7,6},{8,9},{9,8},{10,11... | collective-permute-start | bytes 1572872 | tf_op jit(solution)/shard_map/ppermute | solution.py:17
  38.9 3.4 %copy-start.1 = (bf16[2,2,32,32,1024]{4,3,2,1,0:T(8,128)(2,1)S(1)}, bf16[2,2,32,32,1024]{4,3,2,1,0:T(8,128)(2,1)}, u32[]{:S(2)}) copy-start(bf16[2,2,32,32,1024]{4,3,2,1,0:T(8,128)(2,1)} %copy-done) | copy-start | bytes 25165828
  42.3 2.2 %copy-start.3 = (bf16[2,32,32,1024]{3,2,1,0:T(8,128)(2,1)S(1)}, bf16[2,32,32,1024]{3,2,1,0:T(8,128)(2,1)}, u32[]{:S(2)}) copy-start(bf16[2,32,32,1024]{3,2,1,0:T(8,128)(2,1)} %coeffs_ref.1) | copy-start | bytes 12582916
  49.3 15.8 %collective-permute-start.6 = (bf16[128,2048]{1,0:T(8,128)(2,1)S(1)}, bf16[128,2048]{1,0:T(8,128)(2,1)S(1)}, u32[]{:S(2)}, u32[]{:S(2)}) collective-permute-start(bf16[128,2048]{1,0:T(8,128)(2,1)S(1)} %get-tuple-element.24), channel_id=1, source_target_pairs={{0,1},{1,0},{2,3},{3,2},{4,5},{5,4},{6,7},{7,6},{8,9},{9,8},{10,11... | collective-permute-start | bytes 1572872 | tf_op jit(solution)/shard_map/ppermute | solution.py:17
  55.7 6.7 %collective-permute-start.3 = (bf16[128,2048]{1,0:T(8,128)(2,1)S(1)}, bf16[128,2048]{1,0:T(8,128)(2,1)S(1)}, u32[]{:S(2)}, u32[]{:S(2)}) collective-permute-start(bf16[128,2048]{1,0:T(8,128)(2,1)S(1)} %get-tuple-element.22), channel_id=1, source_target_pairs={{0,1},{1,0},{2,3},{3,2},{4,5},{5,4},{6,7},{7,6},{8,9},{9,8},{10,11... | collective-permute-start | bytes 1572872 | tf_op jit(solution)/shard_map/ppermute | solution.py:17
  56.9 14.8 %collective-permute-start.9 = (bf16[128,2048]{1,0:T(8,128)(2,1)S(1)}, bf16[128,2048]{1,0:T(8,128)(2,1)S(1)}, u32[]{:S(2)}, u32[]{:S(2)}) collective-permute-start(bf16[128,2048]{1,0:T(8,128)(2,1)S(1)} %add_convert_fusion.1), channel_id=1, source_target_pairs={{0,4},{1,5},{2,6},{3,7},{4,0},{5,1},{6,2},{7,3},{8,12},{9,13},{10,... | collective-permute-start | bytes 1572872 | tf_op jit(solution)/shard_map/ppermute | solution.py:17
  61.8 10.9 %collective-permute-start.1 = (bf16[128,2048]{1,0:T(8,128)(2,1)S(1)}, bf16[128,2048]{1,0:T(8,128)(2,1)S(1)}, u32[]{:S(2)}, u32[]{:S(2)}) collective-permute-start(bf16[128,2048]{1,0:T(8,128)(2,1)S(1)} %get-tuple-element.20), channel_id=1, source_target_pairs={{0,1},{1,0},{2,3},{3,2},{4,5},{5,4},{6,7},{7,6},{8,9},{9,8},{10,11... | collective-permute-start | bytes 1572872 | tf_op jit(solution)/shard_map/ppermute | solution.py:17
  63.3 25.0 %collective-permute-start.4 = (bf16[128,2048]{1,0:T(8,128)(2,1)}, bf16[128,2048]{1,0:T(8,128)(2,1)S(1)}, u32[]{:S(2)}, u32[]{:S(2)}) collective-permute-start(bf16[128,2048]{1,0:T(8,128)(2,1)} %add_convert_fusion.2), channel_id=1, source_target_pairs={{0,4},{1,5},{2,6},{3,7},{4,0},{5,1},{6,2},{7,3},{8,12},{9,13},{10,... | collective-permute-start | bytes 1572872 | tf_op jit(solution)/shard_map/ppermute | solution.py:17
  72.7 25.5 %collective-permute-start.10 = (bf16[128,2048]{1,0:T(8,128)(2,1)}, bf16[128,2048]{1,0:T(8,128)(2,1)S(1)}, u32[]{:S(2)}, u32[]{:S(2)}) collective-permute-start(bf16[128,2048]{1,0:T(8,128)(2,1)} %add_convert_fusion), channel_id=1, source_target_pairs={{0,8},{1,9},{2,10},{3,11},{4,12},{5,13},{6,14},{7,15},{8,0},{9,1},... | collective-permute-start | bytes 1572872 | tf_op jit(solution)/shard_map/ppermute | solution.py:17
  98.2 0.8 copy-start.9
  100.4 6.7 %collective-permute-start.11 = (bf16[64,2048]{1,0:T(8,128)(2,1)S(1)}, bf16[64,2048]{1,0:T(8,128)(2,1)S(1)}, u32[]{:S(2)}, u32[]{:S(2)}) collective-permute-start(bf16[64,2048]{1,0:T(8,128)(2,1)S(1)} %fusion.1), channel_id=1, source_target_pairs={{0,2},{1,3},{2,0},{3,1},{4,6},{5,7},{6,4},{7,5},{8,10},{9,11},{10,... | collective-permute-start | bytes 786440 | tf_op jit(solution)/shard_map/ppermute | solution.py:17

commit v2 on v1

v2 whole, which is shorter than its diff:
```python
import functools
import math

import jax
import jax.numpy as jnp
from jax import lax
from jax.experimental import pallas as pl
from jax.experimental.pallas import tpu as pltpu
from jax.sharding import PartitionSpec as P

VMEM = 60 * 1024 * 1024


def permute(x, target):
    size = lax.axis_size("ka")
    pairs = [(i, target(i)) for i in range(size)]
    return lax.ppermute(x, "ka", [(i, j % size) for i, j in pairs if j is not None])


def nt_dot(a, b):
    return lax.dot_general(a, b, (((1,), (1,)), ((), ())), preferred_element_type=jnp.float32)


def iotas(rows, cols):
    shape = (rows, cols)
    return lax.broadcasted_iota(jnp.int32, shape, 0), lax.broadcasted_iota(jnp.int32, shape, 1)


def ones_where(condition):
    return jnp.where(condition, 1.0, 0.0).astype(jnp.bfloat16)


PART_C, PART_V = 8, 16


def fill_weights(first_ref, cond_ref, val_ref, we_ref, wh_ref):
    _, modes, bands_c, _ = cond_ref.shape
    bands_v = val_ref.shape[2]
    rows_e, part = bands_c * PART_V, PART_C * PART_V
    row, col = iotas(rows_e, bands_c)
    take = ones_where(row // PART_V == col)
    row, col = iotas(rows_e, rows_e)
    for m in range(modes):
        half = jnp.dot(take, cond_ref[0, m], preferred_element_type=jnp.float32)
        full = nt_dot(half.astype(jnp.bfloat16), take)
        keep = (row % PART_V == col % PART_V) & (row // PART_V >= first_ref[m, 0])
        full = jnp.where(keep, full, 0.0).astype(jnp.bfloat16)
        for q in range(bands_c // PART_C):
            we_ref[q, m * part:(m + 1) * part, :] = full[q * part:(q + 1) * part]
    row, col = iotas(PART_C * bands_v, bands_v)
    take_cols = ones_where(row % bands_v == col)
    for h in range(bands_v // PART_V):
        row, col = iotas(part, bands_v)
        take = ones_where(row % PART_V + h * PART_V == col)
        row, col = iotas(part, PART_C * bands_v)
        for m in range(modes):
            half = nt_dot(take, val_ref[0, m])
            full = nt_dot(half.astype(jnp.bfloat16), take_cols)
            keep = (row // PART_V == col // bands_v) & (
                row % PART_V + h * PART_V >= first_ref[m, 1]
            )
            wh_ref[h, m * part:(m + 1) * part, :] = jnp.where(keep, -full, 0.0).astype(jnp.bfloat16)


def products_kernel(order_ref, first_ref, coeffs_ref, cond_ref, val_ref, out_ref, *refs):
    *turned, we_ref, wh_ref = refs
    _, bands_c, bands_v, tile = coeffs_ref.shape
    modes = cond_ref.shape[1]

    @pl.when(pl.program_id(1) == 0)
    def _():
        fill_weights(first_ref, cond_ref, val_ref, we_ref, wh_ref)

    if turned:
        block = coeffs_ref[0].reshape(bands_c * bands_v, tile).T
        turned[0][0, 0] = block
        for step in range(1, len(turned)):
            @pl.when(pl.program_id(1) == step)
            def _():
                turned[step][0] = block

    for h in range(bands_v // PART_V):
        own_v = slice(h * PART_V, (h + 1) * PART_V)
        x = coeffs_ref[0, :, own_v, :].reshape(bands_c * PART_V, tile)
        for q in range(bands_c // PART_C):
            own_c = slice(q * PART_C, (q + 1) * PART_C)
            y = coeffs_ref[0, own_c].reshape(PART_C * bands_v, tile)
            left = jnp.concatenate((we_ref[q], wh_ref[h]), 1)
            value = jnp.dot(left, jnp.concatenate((x, y), 0), preferred_element_type=jnp.float32)
            value = value.reshape(modes, PART_C, PART_V, tile).astype(jnp.bfloat16)
            out_ref[0, :, own_c, own_v, :] = value


def products_of(coeffs, g_cond, g_val, band_first, order=None):
    k_local, bands_c, bands_v, excitons = coeffs.shape
    modes = g_cond.shape[1]
    tile = 256
    tiles, depth = excitons // tile, bands_c * bands_v
    rows_e, rows_h = bands_c * PART_V, PART_C * bands_v
    rows = modes * PART_C * PART_V
    out_shape = [jax.ShapeDtypeStruct((k_local, modes, bands_c, bands_v, excitons), jnp.bfloat16)]
    out_specs = [
        pl.BlockSpec(
            (1, modes, bands_c, bands_v, tile), lambda k, s, order: (k, 0, 0, 0, order[s])
        )
    ]
    if order is None:
        order = jnp.arange(tiles, dtype=jnp.int32)
    else:
        out_shape += [jax.ShapeDtypeStruct((tiles, k_local, tile, depth), jnp.bfloat16)]
        out_specs += [pl.BlockSpec((1, 1, tile, depth), lambda k, s, order: (order[s], k, 0, 0))]
        out_shape += [jax.ShapeDtypeStruct((k_local, tile, depth), jnp.bfloat16)] * (tiles - 1)
        out_specs += [pl.BlockSpec((1, tile, depth), lambda k, s, order: (k, 0, 0))] * (tiles - 1)
    return pl.pallas_call(
        products_kernel,
        out_shape=out_shape,
        grid_spec=pltpu.PrefetchScalarGridSpec(
            num_scalar_prefetch=1,
            grid=(k_local, tiles),
            in_specs=[
                pl.BlockSpec(memory_space=pltpu.SMEM),
                pl.BlockSpec((1, bands_c, bands_v, tile), lambda k, s, order: (k, 0, 0, order[s])),
                pl.BlockSpec((1, modes, bands_c, bands_c), lambda k, s, order: (k, 0, 0, 0)),
                pl.BlockSpec((1, modes, bands_v, bands_v), lambda k, s, order: (k, 0, 0, 0)),
            ],
            out_specs=out_specs,
            scratch_shapes=[
                pltpu.VMEM((bands_c // PART_C, rows, rows_e), jnp.bfloat16),
                pltpu.VMEM((bands_v // PART_V, rows, rows_h), jnp.bfloat16),
            ],
        ),
        compiler_params=pltpu.CompilerParams(vmem_limit_bytes=VMEM),
        cost_estimate=pl.CostEstimate(
            flops=2 * k_local * modes * excitons * depth * (rows_e + rows_h),
            bytes_accessed=2 * coeffs.size * (3 + modes),
            transcendentals=0,
        ),
    )(order, band_first, coeffs, g_cond, g_val)


def turn_kernel(block_ref, coeffs_ref, out_ref):
    out_ref[0] = coeffs_ref[0].T


def turned_piece(flat, block, width):
    k_local, depth, _ = flat.shape
    parts = 2
    return pl.pallas_call(
        turn_kernel,
        out_shape=jax.ShapeDtypeStruct((k_local, width, depth), jnp.bfloat16),
        grid_spec=pltpu.PrefetchScalarGridSpec(
            num_scalar_prefetch=1,
            grid=(k_local, parts),
            in_specs=[
                pl.BlockSpec((1, depth // parts, width), lambda k, d, block: (k, d, block[0]))
            ],
            out_specs=pl.BlockSpec((1, width, depth // parts), lambda k, d, block: (k, 0, d)),
        ),
        compiler_params=pltpu.CompilerParams(vmem_limit_bytes=VMEM),
        cost_estimate=pl.CostEstimate(
            flops=0, bytes_accessed=4 * k_local * depth * width, transcendentals=0
        ),
    )(block, flat)


def rows_kernel(pick_ref, own_ref, next_ref, right_ref, keep_ref, send_ref, left):
    _, k_local, width, depth = own_ref.shape

    @pl.when(pl.program_id(0) == 0)
    def _():
        for k in range(k_local):
            place = pick_ref[k]

            @pl.when(place < k_local)
            def _():
                left[:, k * depth:(k + 1) * depth] = own_ref[0, place]

            @pl.when(place >= k_local)
            def _():
                left[:, k * depth:(k + 1) * depth] = next_ref[place - k_local]

    tile = right_ref.shape[3]
    right = right_ref[:, 0].reshape(k_local * depth, tile)
    total = jnp.dot(left[...], right, preferred_element_type=jnp.float32)
    core = pick_ref[k_local + 1]
    parts = total.reshape(2, 2, width // 4, tile)
    low, high = parts[:, 0].reshape(width // 2, tile), parts[:, 1].reshape(width // 2, tile)
    keep_ref[...] = jnp.where(core == 0, low, high)
    send_ref[...] = jnp.where(core == 0, high, low).astype(jnp.bfloat16)


def rows_of(pick, own, following, products):
    _, k_local, width, depth = own.shape
    modes, excitons = products.shape[1], products.shape[3]
    tile = 512
    per_mode = excitons // tile
    columns = modes * excitons
    return pl.pallas_call(
        rows_kernel,
        out_shape=[
            jax.ShapeDtypeStruct((width // 2, columns), jnp.float32),
            jax.ShapeDtypeStruct((width // 2, columns), jnp.bfloat16),
        ],
        grid_spec=pltpu.PrefetchScalarGridSpec(
            num_scalar_prefetch=1,
            grid=(modes * per_mode,),
            in_specs=[
                pl.BlockSpec(
                    (1, k_local, width, depth), lambda j, pick: (pick[k_local], 0, 0, 0)
                ),
                pl.BlockSpec((k_local, width, depth), lambda j, pick: (0, 0, 0)),
                pl.BlockSpec(
                    (k_local, 1, depth, tile), lambda j, pick: (0, j // per_mode, 0, j % per_mode)
                ),
            ],
            out_specs=[pl.BlockSpec((width // 2, tile), lambda j, pick: (0, j))] * 2,
            scratch_shapes=[pltpu.VMEM((width, k_local * depth), jnp.bfloat16)],
        ),
        compiler_params=pltpu.CompilerParams(vmem_limit_bytes=VMEM),
        cost_estimate=pl.CostEstimate(
            flops=2 * k_local * depth * width * columns,
            bytes_accessed=2 * k_local * depth * columns,
            transcendentals=0,
        ),
    )(pick, own, following, products)


def on_two_by_four(coeffs, g_cond, g_val, k_plus_q, band_first, norm_factor):
    k_local, bands_c, bands_v, excitons = coeffs.shape
    modes = g_cond.shape[1]
    size = lax.axis_size("ka")
    width = excitons // 4
    me = lax.axis_index("ka")
    core, x, z = me & 1, me >> 1 & 1, me >> 2
    flat = coeffs.reshape(k_local, bands_c * bands_v, excitons)

    behind_z = (me + size - 1) % size >> 2
    order = behind_z ^ jnp.arange(3, -1, -1, dtype=jnp.int32)
    pieces = [turned_piece(flat, order[:1], width)]
    following = [permute(pieces[0], lambda i: i - 1)]
    products, own, *pieces = products_of(coeffs, g_cond, g_val, band_first, order)
    products = products.reshape(k_local, modes, bands_c * bands_v, excitons)
    following += [permute(piece, lambda i: i - 1) for piece in pieces]
    places = jnp.mod(k_plus_q - me * k_local, k_local * size)
    picks = [jnp.concatenate((places, jnp.stack((z ^ (3 - step), core)))) for step in range(4)]

    def rows(step):
        keep, send = rows_of(picks[step], own, following[step], products)
        return keep, permute(send, lambda i: i ^ 1).astype(jnp.float32)

    keep, other = rows(0)
    send = (keep + other).astype(jnp.bfloat16)
    send, picks[1] = lax.optimization_barrier((send, picks[1]))
    far = permute(send, lambda i: i ^ 4)
    keep, other = rows(1)
    pair = permute((keep + other + far.astype(jnp.float32)).astype(jnp.bfloat16), lambda i: i ^ 8)
    keep, other = rows(2)
    near = permute((keep + other).astype(jnp.bfloat16), lambda i: i ^ 4)
    keep, other = rows(3)
    total = keep + other + near.astype(jnp.float32) + pair.astype(jnp.float32)
    total = total.reshape(2, width // 4, modes * excitons)
    mine = lax.dynamic_index_in_dim(total, x, 0, keepdims=False)
    sent = lax.dynamic_index_in_dim(total, 1 - x, 0, keepdims=False).astype(jnp.bfloat16)
    total = mine + permute(sent, lambda i: i ^ 2).astype(jnp.float32)
    return (total * norm_factor).reshape(width // 4, modes, excitons)


def on_any(coeffs, g_cond, g_val, k_plus_q, band_first, norm_factor):
    k_local, bands_c, bands_v, excitons = coeffs.shape
    modes = g_cond.shape[1]
    size = lax.axis_size("ka")
    depth = bands_c * bands_v
    flat = coeffs.reshape(k_local, depth, excitons)
    blocks = jnp.concatenate((flat, permute(flat, lambda i: i - 1)), 0)
    offsets = jnp.mod(k_plus_q - lax.axis_index("ka") * k_local, k_local * size)
    products = products_of(coeffs, g_cond, g_val, band_first)[0]
    products = products.reshape(k_local, modes, depth, excitons)
    partners = [
        lax.dynamic_index_in_dim(blocks, offsets[k], 0, keepdims=False) for k in range(k_local)
    ]
    running = jnp.einsum(
        "kds,kmdt->smt", jnp.stack(partners), products, preferred_element_type=jnp.float32
    )
    return lax.psum_scatter(running * norm_factor, "ka", scatter_dimension=0, tiled=True)


def shards(coeffs, g_cond, g_val, k_plus_q, band_first):
    k_local, bands_c, bands_v, excitons = coeffs.shape
    size = lax.axis_size("ka")
    norm_factor = 1.0 / math.sqrt(bands_c * bands_v * k_local * size)
    whole_tiles = excitons % (4 * 128) == 0
    plan = on_two_by_four if size == 16 and whole_tiles else on_any
    return plan(coeffs, g_cond, g_val, k_plus_q, band_first, norm_factor)


def solution(mesh):
    in_specs = (
        P(("groups", "ka"), None, None, None),
        P(("groups", "ka"), None, None, None),
        P(("groups", "ka"), None, None, None),
        P(("groups", "ka")),
        P("groups", None),
    )
    out_specs = P(("groups", "ka"), None, None)
    return jax.shard_map(shards, mesh=mesh, in_specs=in_specs, out_specs=out_specs, check_vma=False)
```

time: 109 us -> 115 us (1.055)
  Pallas kernels: 32.7 us -> 51.8 us
  local copies, waits for them, and re-layouts: 22.2 us -> 4.2 us
  other arithmetic: 4.6 us -> 8.1 us
    pallas_call x4, Pallas kernels: 20.8 us -> 31.7 us  [rows_of(): pl.pallas_call(rows_kernel, out_shape=[jax.ShapeDtypeStruct((width // 2,...]
    dynamic_slice x4 -> x0, local copies, waits for them, and re-layouts: 9.28 us -> none  [on_two_by_four(): lax.dynamic_slice_in_dim(source, (behind_z ^ 3 - step) * width, width, 2)]
    unnamed x22 -> x16, local copies, waits for them, and re-layouts: 11.7 us -> 2.93 us
    pallas_call x1 -> x2, Pallas kernels: 12 us -> 20.1 us  [the longest x1 15.8 us: products_of(): pl.pallas_call(products_kernel, out_shape=out_shape, grid_spec=pltpu.Pref...]
  transfers between devices with their start and end apart: 12 -> 12, of which waited for: 4 -> 7; matrix products, arithmetic and copies ran while one was open for 9% -> 5% of each run, Pallas kernels for 30% -> 42%
where the time goes in v2:
time: 115 us; the launch traced here: 114 us
  Pallas kernels  51.8 us (45%)
  waiting for transfers between devices  37.8 us (33%)
  starting transfers between devices  11.8 us (10%)
  other arithmetic  8.1 us (7%)
  local copies, waits for them, and re-layouts  4.2 us (4%)
    ppermute x12, waiting for transfers between devices, permute(): lax.ppermute(x, 'ka', [(i, j % size) for i, j in pairs if j is not None])  37.8 us
    pallas_call x4, Pallas kernels, rows_of(): pl.pallas_call(rows_kernel, out_shape=[jax.ShapeDtypeStruct((width // 2,...  31.7 us
    pallas_call x1, Pallas kernels, products_of(): pl.pallas_call(products_kernel, out_shape=out_shape, grid_spec=pltpu.Pref...  15.8 us
    ppermute x12, starting transfers between devices, permute(): lax.ppermute(x, 'ka', [(i, j % size) for i, j in pairs if j is not None])  11.8 us
    pallas_call x1, Pallas kernels, turned_piece(): pl.pallas_call(turn_kernel, out_shape=jax.ShapeDtypeStruct((k_local, widt...  4.3 us
    unnamed x16, local copies, waits for them, and re-layouts  2.93 us
  transfers between devices with their start and end apart: 12, of which 7 were waited for; matrix products, arithmetic and copies ran while one was open for 5% of the time, Pallas kernels for 42%

profile of v2, /device:TPU:0, one launch (start us, length us, event | category | flops | bytes accessed | tf_op | source)
XLA Modules:
  0.0 113.8 jit_solution(13774496172508145129)
XLA Ops:
  0.0 0.5 add_xor_fusion.order_ref
  0.5 4.3 %shard_map.58 = bf16[2,256,1024]{2,1,0:T(8,128)(2,1)} custom-call(s32[1]{0:T(128)} %bitcast.22, bf16[2,1024,1024]{2,1,0:T(8,128)(2,1)} %bitcast.19), custom_call_target="tpu_custom_call" | custom-call | bytes 2097152 | tf_op jit(solution)/shard_map/pallas_call | solution.py:148
  4.8 0.0 copy-start.7
  4.8 5.4 %collective-permute-start.5 = (bf16[2,256,1024]{2,1,0:T(8,128)(2,1)}, bf16[2,256,1024]{2,1,0:T(8,128)(2,1)S(1)}, u32[]{:S(2)}, u32[]{:S(2)}) collective-permute-start(bf16[2,256,1024]{2,1,0:T(8,128)(2,1)} %shard_map.58), channel_id=1, source_target_pairs={{0,15},{1,0},{2,1},{3,2},{4,3},{5,4},{6,5},{7,6},{8,7},{9,8},{10,9... | collective-permute-start | bytes 3145736 | tf_op jit(solution)/shard_map/ppermute | solution.py:17
  10.2 15.8 %shard_map.55 = (bf16[2,2,32,32,1024]{4,3,2,1,0:T(8,128)(2,1)}, bf16[4,2,256,1024]{3,2,1,0:T(8,128)(2,1)}, bf16[2,256,1024]{2,1,0:T(8,128)(2,1)}, bf16[2,256,1024]{2,1,0:T(8,128)(2,1)}, bf16[2,256,1024]{2,1,0:T(8,128)(2,1)}) custom-call(s32[4]{0:T(128)} %add_xor_fusion.order_ref, s32[2,2]{1,0:T(2,128)} %first_ref.1, bf16[2,32,32,1024]{3,2,1,0:T(8,128)(2,1)} %coeffs_ref.1, ...), custom_call_target="tpu_custom_call" | custom-call | flops 6442450944 | bytes 20971520 | tf_op jit(solution)/shard_map/pallas_call | solution.py:114
  26.0 0.7 collective-permute-start.2
  26.8 0.1 collective-permute-start.7
  26.9 0.0 copy-done.7
  26.9 0.7 add_add_fusion
  27.6 0.0 collective-permute-done.5.next_ref
  27.6 1.0 copy-done.6
  28.6 7.8 %shard_map.59 = (f32[128,2048]{1,0:T(8,128)}, bf16[128,2048]{1,0:T(8,128)(2,1)}) custom-call(s32[4]{0:T(128)} %get-tuple-element.37.pick_ref, bf16[4,2,256,1024]{3,2,1,0:T(8,128)(2,1)} %get-tuple-element.20.own_ref, bf16[2,256,1024]{2,1,0:T(8,128)(2,1)} %copy-done.6, bf16[2,2,1024,1024]{3,2,1,0:T(8,128)(2,1)} %bitcast.15), custom_call_target="tpu_custom_call" | custom-call | flops 2147483648 | bytes 8388608 | tf_op jit(solution)/shard_map/pallas_call | solution.py:198
  36.4 0.4 collective-permute-start.6
  36.8 0.9 collective-permute-start
  37.7 0.6 add_add_fusion.3.pick_ref
  38.3 1.1 collective-permute-done.2.next_ref
  39.4 8.0 %shard_map.57 = (f32[128,2048]{1,0:T(8,128)}, bf16[128,2048]{1,0:T(8,128)(2,1)}) custom-call(s32[4]{0:T(128)} %get-tuple-element.36.pick_ref, bf16[4,2,256,1024]{3,2,1,0:T(8,128)(2,1)} %get-tuple-element.20.own_ref, bf16[2,256,1024]{2,1,0:T(8,128)(2,1)} %collective-permute-done.2.next_ref, bf16[2,2,1024,1024]{3,2,1,0:T(8,128)(2,1)} %bitcast.16), custom_call_target="tpu_custom_call" | custom-call | flops 2147483648 | bytes 8388608 | tf_op jit(solution)/shard_map/pallas_call | solution.py:198
  47.4 0.0 collective-permute-start.3
  47.4 0.0 collective-permute-done.6
  47.4 0.0 copy-done.3
  47.4 0.9 add_convert_fusion.1
  48.3 2.3 %collective-permute-done.7.next_ref = bf16[2,256,1024]{2,1,0:T(8,128)(2,1)S(1)} collective-permute-done((bf16[2,256,1024]{2,1,0:T(8,128)(2,1)}, bf16[2,256,1024]{2,1,0:T(8,128)(2,1)S(1)}, u32[]{:S(2)}, u32[]{:S(2)}) %collective-permute-start.7) | collective-permute-done | bytes 1048608 | tf_op jit(solution)/shard_map/ppermute | solution.py:17
  50.6 1.0 copy-done.4
  51.6 7.9 %shard_map.60 = (f32[128,2048]{1,0:T(8,128)}, bf16[128,2048]{1,0:T(8,128)(2,1)}) custom-call(s32[4]{0:T(128)} %add_add_fusion.3.pick_ref, bf16[4,2,256,1024]{3,2,1,0:T(8,128)(2,1)} %get-tuple-element.20.own_ref, bf16[2,256,1024]{2,1,0:T(8,128)(2,1)} %copy-done.4, bf16[2,2,1024,1024]{3,2,1,0:T(8,128)(2,1)} %bitcast.17), custom_call_target="tpu_custom_call" | custom-call | flops 2147483648 | bytes 8388608 | tf_op jit(solution)/shard_map/pallas_call | solution.py:198
  59.5 0.0 collective-permute-start.8
  59.5 0.1 collective-permute-start.9
  59.5 3.5 %collective-permute-done.next_ref = bf16[2,256,1024]{2,1,0:T(8,128)(2,1)S(1)} collective-permute-done((bf16[2,256,1024]{2,1,0:T(8,128)(2,1)}, bf16[2,256,1024]{2,1,0:T(8,128)(2,1)S(1)}, u32[]{:S(2)}, u32[]{:S(2)}) %collective-permute-start) | collective-permute-done | bytes 1048608 | tf_op jit(solution)/shard_map/ppermute | solution.py:17
  63.0 1.0 copy-done.5
  64.0 8.0 %shard_map.56 = (f32[128,2048]{1,0:T(8,128)}, bf16[128,2048]{1,0:T(8,128)(2,1)}) custom-call(s32[4]{0:T(128)} %get-tuple-element.35.pick_ref, bf16[4,2,256,1024]{3,2,1,0:T(8,128)(2,1)} %get-tuple-element.20.own_ref, bf16[2,256,1024]{2,1,0:T(8,128)(2,1)} %copy-done.5, bf16[2,2,1024,1024]{3,2,1,0:T(8,128)(2,1)} %bitcast.18), custom_call_target="tpu_custom_call" | custom-call | flops 2147483648 | bytes 8388608 | tf_op jit(solution)/shard_map/pallas_call | solution.py:198
  72.0 0.0 collective-permute-start.1
  72.0 0.0 collective-permute-done.3
  72.0 0.0 copy-done.1
  72.0 2.0 %add_convert_fusion.2 = bf16[128,2048]{1,0:T(8,128)(2,1)} fusion(f32[128,2048]{1,0:T(8,128)S(1)} %copy-done.1, bf16[128,2048]{1,0:T(8,128)(2,1)} %collective-permute-done.3), kind=kLoop, calls=%fused_computation.3 | loop fusion | flops 786432 | bytes 2097152 | tf_op jit(solution)/shard_map/convert_element_type | solution.py:258
  74.0 0.0 collective-permute-start.4
  74.0 0.0 collective-permute-done.8
  74.0 0.1 collective-permute-done.9
  74.1 0.0 copy-done.2
  74.1 2.0 %add_convert_fusion = bf16[128,2048]{1,0:T(8,128)(2,1)} fusion(bf16[128,2048]{1,0:T(8,128)(2,1)} %collective-permute-done.9, f32[128,2048]{1,0:T(8,128)S(1)} %copy-done.2, bf16[128,2048]{1,0:T(8,128)(2,1)S(1)} %collective-permute-done.8), kind=kLoop, calls=%fused_computation.1 | loop fusion | flops 1310720 | bytes 2621440 | tf_op jit(solution)/shard_map/convert_element_type | solution.py:256
  76.2 1.4 %collective-permute-start.10 = (bf16[128,2048]{1,0:T(8,128)(2,1)}, bf16[128,2048]{1,0:T(8,128)(2,1)S(1)}, u32[]{:S(2)}, u32[]{:S(2)}) collective-permute-start(bf16[128,2048]{1,0:T(8,128)(2,1)} %add_convert_fusion), channel_id=1, source_target_pairs={{0,8},{1,9},{2,10},{3,11},{4,12},{5,13},{6,14},{7,15},{8,0},{9,1},... | collective-permute-start | bytes 1572872 | tf_op jit(solution)/shard_map/ppermute | solution.py:17
  77.6 0.0 collective-permute-done.1
  77.6 17.4 %collective-permute-done.4 = bf16[128,2048]{1,0:T(8,128)(2,1)S(1)} collective-permute-done((bf16[128,2048]{1,0:T(8,128)(2,1)}, bf16[128,2048]{1,0:T(8,128)(2,1)S(1)}, u32[]{:S(2)}, u32[]{:S(2)}) %collective-permute-start.4) | collective-permute-done | bytes 524320 | tf_op jit(solution)/shard_map/ppermute | solution.py:17
  95.0 7.7 %collective-permute-done.10 = bf16[128,2048]{1,0:T(8,128)(2,1)S(1)} collective-permute-done((bf16[128,2048]{1,0:T(8,128)(2,1)}, bf16[128,2048]{1,0:T(8,128)(2,1)S(1)}, u32[]{:S(2)}, u32[]{:S(2)}) %collective-permute-start.10) | collective-permute-done | bytes 524320 | tf_op jit(solution)/shard_map/ppermute | solution.py:17
  102.7 0.0 copy-done
  102.7 1.3 %convert_add_fusion = f32[128,2048]{1,0:T(8,128)S(1)} fusion(bf16[128,2048]{1,0:T(8,128)(2,1)S(1)} %collective-permute-done.10, bf16[128,2048]{1,0:T(8,128)(2,1)S(1)} %collective-permute-done.4, f32[128,2048]{1,0:T(8,128)S(1)} %copy-done, bf16[128,2048]{1,0:T(8,128)(2,1)} %collective-permute-done.1), kind=kLoop, calls=%fused_computation | loop fusion | flops 1572864 | bytes 3670016 | tf_op jit(solution)/shard_map/add | solution.py:260
  104.1 2.7 %collective-permute-start.11 = (bf16[64,2048]{1,0:T(8,128)(2,1)S(1)}, bf16[64,2048]{1,0:T(8,128)(2,1)S(1)}, u32[]{:S(2)}, u32[]{:S(2)}) collective-permute-start(bf16[64,2048]{1,0:T(8,128)(2,1)S(1)} %fusion.1), channel_id=1, source_target_pairs={{0,2},{1,3},{2,0},{3,1},{4,6},{5,7},{6,4},{7,5},{8,10},{9,11},{10,... | collective-permute-start | bytes 786440 | tf_op jit(solution)/shard_map/ppermute | solution.py:17
  106.8 5.7 %collective-permute-done.11 = bf16[64,2048]{1,0:T(8,128)(2,1)S(1)} collective-permute-done((bf16[64,2048]{1,0:T(8,128)(2,1)S(1)}, bf16[64,2048]{1,0:T(8,128)(2,1)S(1)}, u32[]{:S(2)}, u32[]{:S(2)}) %collective-permute-start.11) | collective-permute-done | bytes 262176 | tf_op jit(solution)/shard_map/ppermute | solution.py:17
  112.5 0.1 fusion
  112.6 1.2 %reshape.16 = f32[64,2,1024]{2,1,0:T(2,128)} reshape(f32[64,2048]{1,0:T(8,128)S(1)} %fusion) | data formatting | bytes 1048576 | tf_op jit(solution)/shard_map/reshape | solution.py:265
  (9 shorter events, 0.1 us)
Async XLA Ops:
  4.8 22.1 %copy-start.7 = (s32[2]{0:T(128)S(1)}, s32[2]{0:T(128)}, u32[]{:S(2)}) copy-start(s32[2]{0:T(128)} %param.8) | copy-start | bytes 28
  4.8 22.8 %collective-permute-start.5 = (bf16[2,256,1024]{2,1,0:T(8,128)(2,1)}, bf16[2,256,1024]{2,1,0:T(8,128)(2,1)S(1)}, u32[]{:S(2)}, u32[]{:S(2)}) collective-permute-start(bf16[2,256,1024]{2,1,0:T(8,128)(2,1)} %shard_map.58), channel_id=1, source_target_pairs={{0,15},{1,0},{2,1},{3,2},{4,3},{5,4},{6,5},{7,6},{8,7},{9,8},{10,9... | collective-permute-start | bytes 3145736 | tf_op jit(solution)/shard_map/ppermute | solution.py:17
  26.0 13.4 %collective-permute-start.2 = (bf16[2,256,1024]{2,1,0:T(8,128)(2,1)}, bf16[2,256,1024]{2,1,0:T(8,128)(2,1)}, u32[]{:S(2)}, u32[]{:S(2)}) collective-permute-start(bf16[2,256,1024]{2,1,0:T(8,128)(2,1)} %get-tuple-element.25), channel_id=1, source_target_pairs={{0,15},{1,0},{2,1},{3,2},{4,3},{5,4},{6,5},{7,6},{8,7},{9,8},{10,9... | collective-permute-start | bytes 3145736 | tf_op jit(solution)/shard_map/ppermute | solution.py:17
  26.8 23.9 %collective-permute-start.7 = (bf16[2,256,1024]{2,1,0:T(8,128)(2,1)}, bf16[2,256,1024]{2,1,0:T(8,128)(2,1)S(1)}, u32[]{:S(2)}, u32[]{:S(2)}) collective-permute-start(bf16[2,256,1024]{2,1,0:T(8,128)(2,1)} %get-tuple-element.31), channel_id=1, source_target_pairs={{0,15},{1,0},{2,1},{3,2},{4,3},{5,4},{6,5},{7,6},{8,7},{9,8},{10,9... | collective-permute-start | bytes 3145736 | tf_op jit(solution)/shard_map/ppermute | solution.py:17
  27.6 1.0 copy-start.6
  36.4 11.0 %collective-permute-start.6 = (bf16[128,2048]{1,0:T(8,128)(2,1)}, bf16[128,2048]{1,0:T(8,128)(2,1)S(1)}, u32[]{:S(2)}, u32[]{:S(2)}) collective-permute-start(bf16[128,2048]{1,0:T(8,128)(2,1)} %get-tuple-element.29), channel_id=1, source_target_pairs={{0,1},{1,0},{2,3},{3,2},{4,5},{5,4},{6,7},{7,6},{8,9},{9,8},{10,11... | collective-permute-start | bytes 1572872 | tf_op jit(solution)/shard_map/ppermute | solution.py:17
  36.8 26.2 %collective-permute-start = (bf16[2,256,1024]{2,1,0:T(8,128)(2,1)}, bf16[2,256,1024]{2,1,0:T(8,128)(2,1)S(1)}, u32[]{:S(2)}, u32[]{:S(2)}) collective-permute-start(bf16[2,256,1024]{2,1,0:T(8,128)(2,1)} %get-tuple-element.21), channel_id=1, source_target_pairs={{0,15},{1,0},{2,1},{3,2},{4,3},{5,4},{6,5},{7,6},{8,7},{9,8},{10,9... | collective-permute-start | bytes 3145736 | tf_op jit(solution)/shard_map/ppermute | solution.py:17
  39.4 8.0 %copy-start.3 = (f32[128,2048]{1,0:T(8,128)S(1)}, f32[128,2048]{1,0:T(8,128)}, u32[]{:S(2)}) copy-start(f32[128,2048]{1,0:T(8,128)} %get-tuple-element.28) | copy-start | bytes 3145732
  47.4 24.6 %collective-permute-start.3 = (bf16[128,2048]{1,0:T(8,128)(2,1)}, bf16[128,2048]{1,0:T(8,128)(2,1)}, u32[]{:S(2)}, u32[]{:S(2)}) collective-permute-start(bf16[128,2048]{1,0:T(8,128)(2,1)} %get-tuple-element.27), channel_id=1, source_target_pairs={{0,1},{1,0},{2,3},{3,2},{4,5},{5,4},{6,7},{7,6},{8,9},{9,8},{10,11... | collective-permute-start | bytes 1572872 | tf_op jit(solution)/shard_map/ppermute | solution.py:17
  50.6 1.0 copy-start.4
  59.5 14.6 %collective-permute-start.8 = (bf16[128,2048]{1,0:T(8,128)(2,1)}, bf16[128,2048]{1,0:T(8,128)(2,1)S(1)}, u32[]{:S(2)}, u32[]{:S(2)}) collective-permute-start(bf16[128,2048]{1,0:T(8,128)(2,1)} %get-tuple-element.33), channel_id=1, source_target_pairs={{0,1},{1,0},{2,3},{3,2},{4,5},{5,4},{6,7},{7,6},{8,9},{9,8},{10,11... | collective-permute-start | bytes 1572872 | tf_op jit(solution)/shard_map/ppermute | solution.py:17
  59.5 14.7 %collective-permute-start.9 = (bf16[128,2048]{1,0:T(8,128)(2,1)}, bf16[128,2048]{1,0:T(8,128)(2,1)}, u32[]{:S(2)}, u32[]{:S(2)}) collective-permute-start(bf16[128,2048]{1,0:T(8,128)(2,1)} %add_convert_fusion.1), channel_id=1, source_target_pairs={{0,4},{1,5},{2,6},{3,7},{4,0},{5,1},{6,2},{7,3},{8,12},{9,13},{10,... | collective-permute-start | bytes 1572872 | tf_op jit(solution)/shard_map/ppermute | solution.py:17
  63.0 1.0 copy-start.5
  64.0 8.0 %copy-start.1 = (f32[128,2048]{1,0:T(8,128)S(1)}, f32[128,2048]{1,0:T(8,128)}, u32[]{:S(2)}) copy-start(f32[128,2048]{1,0:T(8,128)} %get-tuple-element.26) | copy-start | bytes 3145732
  64.0 10.2 %copy-start.2 = (f32[128,2048]{1,0:T(8,128)S(1)}, f32[128,2048]{1,0:T(8,128)}, u32[]{:S(2)}) copy-start(f32[128,2048]{1,0:T(8,128)} %get-tuple-element.32) | copy-start | bytes 3145732
  72.0 30.7 %copy-start = (f32[128,2048]{1,0:T(8,128)S(1)}, f32[128,2048]{1,0:T(8,128)}, u32[]{:S(2)}) copy-start(f32[128,2048]{1,0:T(8,128)} %get-tuple-element.23) | copy-start | bytes 3145732
  72.0 5.6 %collective-permute-start.1 = (bf16[128,2048]{1,0:T(8,128)(2,1)}, bf16[128,2048]{1,0:T(8,128)(2,1)}, u32[]{:S(2)}, u32[]{:S(2)}) collective-permute-start(bf16[128,2048]{1,0:T(8,128)(2,1)} %get-tuple-element.24), channel_id=1, source_target_pairs={{0,1},{1,0},{2,3},{3,2},{4,5},{5,4},{6,7},{7,6},{8,9},{9,8},{10,11... | collective-permute-start | bytes 1572872 | tf_op jit(solution)/shard_map/ppermute | solution.py:17
  74.0 21.0 %collective-permute-start.4 = (bf16[128,2048]{1,0:T(8,128)(2,1)}, bf16[128,2048]{1,0:T(8,128)(2,1)S(1)}, u32[]{:S(2)}, u32[]{:S(2)}) collective-permute-start(bf16[128,2048]{1,0:T(8,128)(2,1)} %add_convert_fusion.2), channel_id=1, source_target_pairs={{0,4},{1,5},{2,6},{3,7},{4,0},{5,1},{6,2},{7,3},{8,12},{9,13},{10,... | collective-permute-start | bytes 1572872 | tf_op jit(solution)/shard_map/ppermute | solution.py:17
  76.2 26.5 %collective-permute-start.10 = (bf16[128,2048]{1,0:T(8,128)(2,1)}, bf16[128,2048]{1,0:T(8,128)(2,1)S(1)}, u32[]{:S(2)}, u32[]{:S(2)}) collective-permute-start(bf16[128,2048]{1,0:T(8,128)(2,1)} %add_convert_fusion), channel_id=1, source_target_pairs={{0,8},{1,9},{2,10},{3,11},{4,12},{5,13},{6,14},{7,15},{8,0},{9,1},... | collective-permute-start | bytes 1572872 | tf_op jit(solution)/shard_map/ppermute | solution.py:17
  104.1 8.5 %collective-permute-start.11 = (bf16[64,2048]{1,0:T(8,128)(2,1)S(1)}, bf16[64,2048]{1,0:T(8,128)(2,1)S(1)}, u32[]{:S(2)}, u32[]{:S(2)}) collective-permute-start(bf16[64,2048]{1,0:T(8,128)(2,1)S(1)} %fusion.1), channel_id=1, source_target_pairs={{0,2},{1,3},{2,0},{3,1},{4,6},{5,7},{6,4},{7,5},{8,10},{9,11},{10,... | collective-permute-start | bytes 786440 | tf_op jit(solution)/shard_map/ppermute | solution.py:17

commit v3 on v2

--- a/solution.py
+++ b/solution.py
@@ -8,7 +8,7 @@
 from jax.experimental.pallas import tpu as pltpu
 from jax.sharding import PartitionSpec as P
 
-VMEM = 60 * 1024 * 1024
+VMEM = 16 * 1024 * 1024
 
 
 def permute(x, target):
@@ -62,32 +62,54 @@
             wh_ref[h, m * part:(m + 1) * part, :] = jnp.where(keep, -full, 0.0).astype(jnp.bfloat16)
 
 
+def tile_copy(order_ref, coeffs_ref, held, sems, step, tiles, tile):
+    columns = pl.ds(pl.multiple_of(order_ref[step % tiles] * tile, tile), tile)
+    slot = step % 2
+    return pltpu.make_async_copy(
+        coeffs_ref.at[step // tiles, :, :, columns], held.at[slot], sems.at[slot]
+    )
+
+
 def products_kernel(order_ref, first_ref, coeffs_ref, cond_ref, val_ref, out_ref, *refs):
-    *turned, we_ref, wh_ref = refs
-    _, bands_c, bands_v, tile = coeffs_ref.shape
-    modes = cond_ref.shape[1]
-
-    @pl.when(pl.program_id(1) == 0)
+    *turned, we_ref, wh_ref, held, sems = refs
+    _, bands_c, bands_v, tile = held.shape
+    k, s, tiles = pl.program_id(0), pl.program_id(1), pl.num_programs(1)
+    step = k * tiles + s
+    copy = functools.partial(
+        tile_copy, order_ref, coeffs_ref, held, sems, tiles=tiles, tile=tile
+    )
+
+    @pl.when(step == 0)
+    def _():
+        copy(step=step).start()
+
+    @pl.when(step + 1 < tiles * pl.num_programs(0))
+    def _():
+        copy(step=step + 1).start()
+
+    @pl.when(s == 0)
     def _():
         fill_weights(first_ref, cond_ref, val_ref, we_ref, wh_ref)
 
+    copy(step=step).wait()
+    block_ref = held.at[step % 2]
     if turned:
-        block = coeffs_ref[0].reshape(bands_c * bands_v, tile).T
+        block = block_ref[...].reshape(bands_c * bands_v, tile).T
         turned[0][0, 0] = block
-        for step in range(1, len(turned)):
-            @pl.when(pl.program_id(1) == step)
+        for place in range(1, len(turned)):
+            @pl.when(s == place)
             def _():
-                turned[step][0] = block
+                turned[place][0] = block
 
     for h in range(bands_v // PART_V):
         own_v = slice(h * PART_V, (h + 1) * PART_V)
-        x = coeffs_ref[0, :, own_v, :].reshape(bands_c * PART_V, tile)
+        x = block_ref[:, own_v, :].reshape(bands_c * PART_V, tile)
         for q in range(bands_c // PART_C):
             own_c = slice(q * PART_C, (q + 1) * PART_C)
-            y = coeffs_ref[0, own_c].reshape(PART_C * bands_v, tile)
+            y = block_ref[own_c].reshape(PART_C * bands_v, tile)
             left = jnp.concatenate((we_ref[q], wh_ref[h]), 1)
             value = jnp.dot(left, jnp.concatenate((x, y), 0), preferred_element_type=jnp.float32)
-            value = value.reshape(modes, PART_C, PART_V, tile).astype(jnp.bfloat16)
+            value = value.reshape(-1, PART_C, PART_V, tile).astype(jnp.bfloat16)
             out_ref[0, :, own_c, own_v, :] = value
 
 
@@ -119,7 +141,7 @@
             grid=(k_local, tiles),
             in_specs=[
                 pl.BlockSpec(memory_space=pltpu.SMEM),
-                pl.BlockSpec((1, bands_c, bands_v, tile), lambda k, s, order: (k, 0, 0, order[s])),
+                pl.BlockSpec(memory_space=pltpu.HBM),
                 pl.BlockSpec((1, modes, bands_c, bands_c), lambda k, s, order: (k, 0, 0, 0)),
                 pl.BlockSpec((1, modes, bands_v, bands_v), lambda k, s, order: (k, 0, 0, 0)),
             ],
@@ -127,6 +149,8 @@
             scratch_shapes=[
                 pltpu.VMEM((bands_c // PART_C, rows, rows_e), jnp.bfloat16),
                 pltpu.VMEM((bands_v // PART_V, rows, rows_h), jnp.bfloat16),
+                pltpu.VMEM((2, bands_c, bands_v, tile), jnp.bfloat16),
+                pltpu.SemaphoreType.DMA((2,)),
             ],
         ),
         compiler_params=pltpu.CompilerParams(vmem_limit_bytes=VMEM),
@@ -138,8 +162,20 @@
     )(order, band_first, coeffs, g_cond, g_val)
 
 
-def turn_kernel(block_ref, coeffs_ref, out_ref):
-    out_ref[0] = coeffs_ref[0].T
+def turn_kernel(block_ref, coeffs_ref, out_ref, held, sems):
+    k_local, parts, rows, width = held.shape
+    columns = pl.ds(pl.multiple_of(block_ref[0] * width, width), width)
+    copies = {}
+    for k in range(k_local):
+        for p in range(parts):
+            copies[k, p] = pltpu.make_async_copy(
+                coeffs_ref.at[k, pl.ds(p * rows, rows), columns], held.at[k, p], sems.at[k, p]
+            )
+            copies[k, p].start()
+    for k in range(k_local):
+        for p in range(parts):
+            copies[k, p].wait()
+            out_ref[k, :, p * rows:(p + 1) * rows] = held[k, p].T
 
 
 def turned_piece(flat, block, width):
@@ -148,14 +184,15 @@
     return pl.pallas_call(
         turn_kernel,
         out_shape=jax.ShapeDtypeStruct((k_local, width, depth), jnp.bfloat16),
-        grid_spec=pltpu.PrefetchScalarGridSpec(
-            num_scalar_prefetch=1,
-            grid=(k_local, parts),
-            in_specs=[
-                pl.BlockSpec((1, depth // parts, width), lambda k, d, block: (k, d, block[0]))
-            ],
-            out_specs=pl.BlockSpec((1, width, depth // parts), lambda k, d, block: (k, 0, d)),
-        ),
+        in_specs=[
+            pl.BlockSpec(memory_space=pltpu.SMEM),
+            pl.BlockSpec(memory_space=pltpu.HBM),
+        ],
+        out_specs=pl.BlockSpec(memory_space=pltpu.VMEM),
+        scratch_shapes=[
+            pltpu.VMEM((k_local, parts, depth // parts, width), jnp.bfloat16),
+            pltpu.SemaphoreType.DMA((k_local, parts)),
+        ],
         compiler_params=pltpu.CompilerParams(vmem_limit_bytes=VMEM),
         cost_estimate=pl.CostEstimate(
             flops=0, bytes_accessed=4 * k_local * depth * width, transcendentals=0
@@ -165,35 +202,35 @@
 
 def rows_kernel(pick_ref, own_ref, next_ref, right_ref, keep_ref, send_ref, left):
     _, k_local, width, depth = own_ref.shape
-
-    @pl.when(pl.program_id(0) == 0)
-    def _():
-        for k in range(k_local):
-            place = pick_ref[k]
-
-            @pl.when(place < k_local)
-            def _():
-                left[:, k * depth:(k + 1) * depth] = own_ref[0, place]
-
-            @pl.when(place >= k_local)
-            def _():
-                left[:, k * depth:(k + 1) * depth] = next_ref[place - k_local]
-
-    tile = right_ref.shape[3]
-    right = right_ref[:, 0].reshape(k_local * depth, tile)
-    total = jnp.dot(left[...], right, preferred_element_type=jnp.float32)
-    core = pick_ref[k_local + 1]
-    parts = total.reshape(2, 2, width // 4, tile)
-    low, high = parts[:, 0].reshape(width // 2, tile), parts[:, 1].reshape(width // 2, tile)
-    keep_ref[...] = jnp.where(core == 0, low, high)
-    send_ref[...] = jnp.where(core == 0, high, low).astype(jnp.bfloat16)
+    _, modes, _, excitons = right_ref.shape
+    block, core = pick_ref[k_local], pick_ref[k_local + 1]
+    for k in range(k_local):
+        place = pick_ref[k]
+
+        @pl.when(place < k_local)
+        def _():
+            left[:, k * depth:(k + 1) * depth] = own_ref[block, place]
+
+        @pl.when(place >= k_local)
+        def _():
+            left[:, k * depth:(k + 1) * depth] = next_ref[place - k_local]
+
+    tile = 512
+    for m in range(modes):
+        for s in range(0, excitons, tile):
+            right = right_ref[:, m, :, s:s + tile].reshape(k_local * depth, tile)
+            total = jnp.dot(left[...], right, preferred_element_type=jnp.float32)
+            parts = total.reshape(2, 2, width // 4, tile)
+            low = parts[:, 0].reshape(width // 2, tile)
+            high = parts[:, 1].reshape(width // 2, tile)
+            columns = slice(m * excitons + s, m * excitons + s + tile)
+            keep_ref[:, columns] = jnp.where(core == 0, low, high)
+            send_ref[:, columns] = jnp.where(core == 0, high, low).astype(jnp.bfloat16)
 
 
 def rows_of(pick, own, following, products):
     _, k_local, width, depth = own.shape
     modes, excitons = products.shape[1], products.shape[3]
-    tile = 512
-    per_mode = excitons // tile
     columns = modes * excitons
     return pl.pallas_call(
         rows_kernel,
@@ -201,21 +238,10 @@
             jax.ShapeDtypeStruct((width // 2, columns), jnp.float32),
             jax.ShapeDtypeStruct((width // 2, columns), jnp.bfloat16),
         ],
-        grid_spec=pltpu.PrefetchScalarGridSpec(
-            num_scalar_prefetch=1,
-            grid=(modes * per_mode,),
-            in_specs=[
-                pl.BlockSpec(
-                    (1, k_local, width, depth), lambda j, pick: (pick[k_local], 0, 0, 0)
-                ),
-                pl.BlockSpec((k_local, width, depth), lambda j, pick: (0, 0, 0)),
-                pl.BlockSpec(
-                    (k_local, 1, depth, tile), lambda j, pick: (0, j // per_mode, 0, j % per_mode)
-                ),
-            ],
-            out_specs=[pl.BlockSpec((width // 2, tile), lambda j, pick: (0, j))] * 2,
-            scratch_shapes=[pltpu.VMEM((width, k_local * depth), jnp.bfloat16)],
-        ),
+        in_specs=[pl.BlockSpec(memory_space=pltpu.SMEM)]
+        + [pl.BlockSpec(memory_space=pltpu.VMEM)] * 3,
+        out_specs=[pl.BlockSpec(memory_space=pltpu.VMEM)] * 2,
+        scratch_shapes=[pltpu.VMEM((width, k_local * depth), jnp.bfloat16)],
         compiler_params=pltpu.CompilerParams(vmem_limit_bytes=VMEM),
         cost_estimate=pl.CostEstimate(
             flops=2 * k_local * depth * width * columns,
@@ -244,19 +270,21 @@
     places = jnp.mod(k_plus_q - me * k_local, k_local * size)
     picks = [jnp.concatenate((places, jnp.stack((z ^ (3 - step), core)))) for step in range(4)]
 
-    def rows(step):
-        keep, send = rows_of(picks[step], own, following[step], products)
+    def rows(step, after):
+        pick, _ = lax.optimization_barrier((picks[step], after))
+        keep, send = rows_of(pick, own, following[step], products)
         return keep, permute(send, lambda i: i ^ 1).astype(jnp.float32)
 
-    keep, other = rows(0)
-    send = (keep + other).astype(jnp.bfloat16)
-    send, picks[1] = lax.optimization_barrier((send, picks[1]))
-    far = permute(send, lambda i: i ^ 4)
-    keep, other = rows(1)
-    pair = permute((keep + other + far.astype(jnp.float32)).astype(jnp.bfloat16), lambda i: i ^ 8)
-    keep, other = rows(2)
-    near = permute((keep + other).astype(jnp.bfloat16), lambda i: i ^ 4)
-    keep, other = rows(3)
+    keep, other = rows(0, products)
+    send_far = (keep + other).astype(jnp.bfloat16)
+    far = permute(send_far, lambda i: i ^ 4)
+    keep_1, other_1 = rows(1, send_far)
+    keep, other = rows(2, keep_1)
+    send_pair = (keep_1 + other_1 + far.astype(jnp.float32)).astype(jnp.bfloat16)
+    pair = permute(send_pair, lambda i: i ^ 8)
+    send_near = (keep + other).astype(jnp.bfloat16)
+    near = permute(send_near, lambda i: i ^ 4)
+    keep, other = rows(3, (send_pair, send_near))
     total = keep + other + near.astype(jnp.float32) + pair.astype(jnp.float32)
     total = total.reshape(2, width // 4, modes * excitons)
     mine = lax.dynamic_index_in_dim(total, x, 0, keepdims=False)

time: 115 us -> 111 us (0.965)
  Pallas kernels: 51.8 us -> 29.5 us
  local copies, waits for them, and re-layouts: 4.2 us -> 19.9 us
  starting transfers between devices: 11.8 us -> 14.2 us
  other arithmetic: 8.1 us -> 5.71 us
  waiting for transfers between devices: 37.8 us -> 40.1 us
    pallas_call x4, Pallas kernels: 31.7 us -> 12.7 us  [rows_of(): pl.pallas_call(rows_kernel, out_shape=[jax.ShapeDtypeStruct((width // 2,...]
    unnamed x16 -> x24, local copies, waits for them, and re-layouts: 2.93 us -> 18.6 us
    pallas_call x1, Pallas kernels: 4.3 us -> 0.72 us  [turned_piece(): pl.pallas_call(turn_kernel, out_shape=jax.ShapeDtypeStruct((k_local, widt...]
    ppermute x12, starting transfers between devices: 11.8 us -> 14.2 us  [permute(): lax.ppermute(x, 'ka', [(i, j % size) for i, j in pairs if j is not None])]
    ppermute x12, waiting for transfers between devices: 37.8 us -> 40.1 us  [permute(): lax.ppermute(x, 'ka', [(i, j % size) for i, j in pairs if j is not None])]
  transfers between devices with their start and end apart: 12 -> 12, of which waited for: 7 -> 7; matrix products, arithmetic and copies ran while one was open for 5% -> 4% of each run, Pallas kernels for 42% -> 26%
where the time goes in v3:
time: 111 us; the launch traced here: 110 us
  waiting for transfers between devices  40.1 us (36%)
  Pallas kernels  29.5 us (27%)
  local copies, waits for them, and re-layouts  19.9 us (18%)
  starting transfers between devices  14.2 us (13%)
  other arithmetic  5.71 us (5%)
    ppermute x12, waiting for transfers between devices, permute(): lax.ppermute(x, 'ka', [(i, j % size) for i, j in pairs if j is not None])  40.1 us
    unnamed x24, local copies, waits for them, and re-layouts  18.6 us
    pallas_call x1, Pallas kernels, products_of(): pl.pallas_call(products_kernel, out_shape=out_shape, grid_spec=pltpu.Pref...  16.1 us
    ppermute x12, starting transfers between devices, permute(): lax.ppermute(x, 'ka', [(i, j % size) for i, j in pairs if j is not None])  14.2 us
    pallas_call x4, Pallas kernels, rows_of(): pl.pallas_call(rows_kernel, out_shape=[jax.ShapeDtypeStruct((width // 2,...  12.7 us
  transfers between devices with their start and end apart: 12, of which 7 were waited for; matrix products, arithmetic and copies ran while one was open for 4% of the time, Pallas kernels for 26%

profile of v3, /device:TPU:0, one launch (start us, length us, event | category | flops | bytes accessed | tf_op | source)
XLA Modules:
  0.0 109.6 jit_solution(2865967681939306094)
XLA Ops:
  0.0 2.2 %copy-done.6 = bf16[2,32,32,1024]{3,2,1,0:T(8,128)(2,1)S(1)} copy-done((bf16[2,32,32,1024]{3,2,1,0:T(8,128)(2,1)S(1)}, bf16[2,32,32,1024]{3,2,1,0:T(8,128)(2,1)}, u32[]{:S(2)}) %copy-start.6) | copy-done | bytes 4194328
  2.2 0.7 shard_map.56
  3.0 0.0 copy-start.11
  3.0 5.5 %collective-permute-start = (bf16[2,256,1024]{2,1,0:T(8,128)(2,1)S(1)}, bf16[2,256,1024]{2,1,0:T(8,128)(2,1)S(1)}, u32[]{:S(2)}, u32[]{:S(2)}) collective-permute-start(bf16[2,256,1024]{2,1,0:T(8,128)(2,1)S(1)} %shard_map.56), channel_id=1, source_target_pairs={{0,15},{1,0},{2,1},{3,2},{4,3},{5,4},{6,5},{7,6},{8,7},{9,8},{10,9... | collective-permute-start | bytes 3145736 | tf_op jit(solution)/shard_map/ppermute | solution.py:17
  8.4 0.0 copy-done.9
  8.4 16.1 %shard_map.55 = (bf16[2,2,32,32,1024]{4,3,2,1,0:T(8,128)(2,1)S(1)}, bf16[4,2,256,1024]{3,2,1,0:T(8,128)(2,1)S(1)}, bf16[2,256,1024]{2,1,0:T(8,128)(2,1)}, bf16[2...) custom-call(s32[4]{0:T(128)S(1)} %add_xor_fusion.order_ref, s32[2,2]{1,0:T(2,128)S(1)} %copy-done.10, ...), custom_call_target="tpu_custom_call" | custom-call | flops 6442450944 | bytes 20971520 | tf_op jit(solution)/shard_map/pallas_call | solution.py:136
  24.6 0.0 copy-start
  24.6 3.3 %copy-done = bf16[2,2,32,32,1024]{4,3,2,1,0:T(8,128)(2,1)} copy-done((bf16[2,2,32,32,1024]{4,3,2,1,0:T(8,128)(2,1)}, bf16[2,2,32,32,1024]{4,3,2,1,0:T(8,128)(2,1)S(1)}, u32[]{:S(2)}) %copy-start) | copy-done | bytes 8388632
  27.8 2.0 %copy-done.3 = bf16[4,2,256,1024]{3,2,1,0:T(8,128)(2,1)} copy-done((bf16[4,2,256,1024]{3,2,1,0:T(8,128)(2,1)}, bf16[4,2,256,1024]{3,2,1,0:T(8,128)(2,1)S(1)}, u32[]{:S(2)}) %copy-start.3) | copy-done | bytes 4194328
  29.8 1.4 %collective-permute-start.2 = (bf16[2,256,1024]{2,1,0:T(8,128)(2,1)}, bf16[2,256,1024]{2,1,0:T(8,128)(2,1)S(1)}, u32[]{:S(2)}, u32[]{:S(2)}) collective-permute-start(bf16[2,256,1024]{2,1,0:T(8,128)(2,1)} %get-tuple-element.28), channel_id=1, source_target_pairs={{0,15},{1,0},{2,1},{3,2},{4,3},{5,4},{6,5},{7,6},{8,7},{9,8},{10,9... | collective-permute-start | bytes 3145736 | tf_op jit(solution)/shard_map/ppermute | solution.py:17
  31.2 0.1 add_add_fusion
  31.3 0.0 collective-permute-done.next_ref
  31.3 3.4 %copy-done.1 = bf16[2,2,32,32,1024]{4,3,2,1,0:T(8,128)(2,1)S(1)} copy-done((bf16[2,2,32,32,1024]{4,3,2,1,0:T(8,128)(2,1)S(1)}, bf16[2,2,32,32,1024]{4,3,2,1,0:T(8,128)(2,1)}, u32[]{:S(2)}) %copy-start.1) | copy-done | bytes 8388632
  34.7 2.2 %copy-done.4 = bf16[4,2,256,1024]{3,2,1,0:T(8,128)(2,1)S(1)} copy-done((bf16[4,2,256,1024]{3,2,1,0:T(8,128)(2,1)S(1)}, bf16[4,2,256,1024]{3,2,1,0:T(8,128)(2,1)}, u32[]{:S(2)}) %copy-start.4) | copy-done | bytes 4194328
  36.9 3.0 %shard_map.57 = (f32[128,2048]{1,0:T(8,128)S(1)}, bf16[128,2048]{1,0:T(8,128)(2,1)S(1)}) custom-call(s32[4]{0:T(128)S(1)} %get-tuple-element.23.pick_ref, bf16[4,2,256,1024]{3,2,1,0:T(8,128)(2,1)S(1)} %copy-done.4, bf16[2,256,1024]{2,1,0:T(8,128)(2,1)S(1)} %collective-permute-done.next_ref, bf16[2,2,1024,1024]{3,2,1,0:T(8,128)(2,1)S(1)} %bitcast.15), custom_call_target="tpu_custom_call" | custom-call | flops 2147483648 | bytes 8388608 | tf_op jit(solution)/shard_map/pallas_call | solution.py:235
  39.8 0.1 collective-permute-start.1
  39.9 0.7 collective-permute-start.5
  40.6 1.3 %collective-permute-done.1 = bf16[128,2048]{1,0:T(8,128)(2,1)S(1)} collective-permute-done((bf16[128,2048]{1,0:T(8,128)(2,1)S(1)}, bf16[128,2048]{1,0:T(8,128)(2,1)S(1)}, u32[]{:S(2)}, u32[]{:S(2)}) %collective-permute-start.1) | collective-permute-done | bytes 524320 | tf_op jit(solution)/shard_map/ppermute | solution.py:17
  41.9 0.9 add_convert_fusion.2
  42.8 0.0 collective-permute-start.4
  42.8 1.1 collective-permute-done.2.next_ref
  43.9 3.8 %shard_map.58 = (f32[128,2048]{1,0:T(8,128)S(1)}, bf16[128,2048]{1,0:T(8,128)(2,1)}) custom-call(s32[4]{0:T(128)S(1)} %get-tuple-element.27.pick_ref, bf16[4,2,256,1024]{3,2,1,0:T(8,128)(2,1)S(1)} %copy-done.4, bf16[2,256,1024]{2,1,0:T(8,128)(2,1)S(1)} %collective-permute-done.2.next_ref, bf16[2,2,1024,1024]{3,2,1,0:T(8,128)(2,1)S(1)} %bitcast.16), custom_call_target="tpu_custom_call" | custom-call | flops 2147483648 | bytes 8388608 | tf_op jit(solution)/shard_map/pallas_call | solution.py:235
  47.7 0.0 collective-permute-start.3
  47.7 4.5 %collective-permute-start.7 = (bf16[2,256,1024]{2,1,0:T(8,128)(2,1)}, bf16[2,256,1024]{2,1,0:T(8,128)(2,1)S(1)}, u32[]{:S(2)}, u32[]{:S(2)}) collective-permute-start(bf16[2,256,1024]{2,1,0:T(8,128)(2,1)} %get-tuple-element.36), channel_id=1, source_target_pairs={{0,15},{1,0},{2,1},{3,2},{4,3},{5,4},{6,5},{7,6},{8,7},{9,8},{10,9... | collective-permute-start | bytes 3145736 | tf_op jit(solution)/shard_map/ppermute | solution.py:17
  52.2 0.1 add_add_fusion.3.pick_ref
  52.3 8.4 %collective-permute-done.5.next_ref = bf16[2,256,1024]{2,1,0:T(8,128)(2,1)S(1)} collective-permute-done((bf16[2,256,1024]{2,1,0:T(8,128)(2,1)}, bf16[2,256,1024]{2,1,0:T(8,128)(2,1)S(1)}, u32[]{:S(2)}, u32[]{:S(2)}) %collective-permute-start.5) | collective-permute-done | bytes 1048608 | tf_op jit(solution)/shard_map/ppermute | solution.py:17
  60.7 3.4 %copy-done.2 = bf16[2,2,32,32,1024]{4,3,2,1,0:T(8,128)(2,1)S(1)} copy-done((bf16[2,2,32,32,1024]{4,3,2,1,0:T(8,128)(2,1)S(1)}, bf16[2,2,32,32,1024]{4,3,2,1,0:T(8,128)(2,1)}, u32[]{:S(2)}) %copy-start.2) | copy-done | bytes 8388632
  64.1 2.2 %copy-done.5 = bf16[4,2,256,1024]{3,2,1,0:T(8,128)(2,1)S(1)} copy-done((bf16[4,2,256,1024]{3,2,1,0:T(8,128)(2,1)S(1)}, bf16[4,2,256,1024]{3,2,1,0:T(8,128)(2,1)}, u32[]{:S(2)}) %copy-start.5) | copy-done | bytes 4194328
  66.2 3.0 %shard_map.59 = (f32[128,2048]{1,0:T(8,128)S(1)}, bf16[128,2048]{1,0:T(8,128)(2,1)S(1)}) custom-call(s32[4]{0:T(128)S(1)} %add_add_fusion.3.pick_ref, bf16[4,2,256,1024]{3,2,1,0:T(8,128)(2,1)S(1)} %copy-done.5, bf16[2,256,1024]{2,1,0:T(8,128)(2,1)S(1)} %collective-permute-done.5.next_ref, bf16[2,2,1024,1024]{3,2,1,0:T(8,128)(2,1)S(1)} %bitcast.17), custom_call_target="tpu_custom_call" | custom-call | flops 2147483648 | bytes 8388608 | tf_op jit(solution)/shard_map/pallas_call | solution.py:235
  69.2 0.1 collective-permute-start.6
  69.3 0.0 collective-permute-done.4
  69.3 0.0 collective-permute-done.3
  69.3 2.2 %add_convert_fusion.1 = bf16[128,2048]{1,0:T(8,128)(2,1)} fusion(bf16[128,2048]{1,0:T(8,128)(2,1)} %collective-permute-done.4, f32[128,2048]{1,0:T(8,128)S(1)} %get-tuple-element.29, bf16[128,2048]{1,0:T(8,128)(2,1)} %collective-permute-done.3), kind=kLoop, calls=%fused_computation.2 | loop fusion | flops 1310720 | bytes 2621440 | tf_op jit(solution)/shard_map/convert_element_type | solution.py:283
  71.5 0.0 collective-permute-start.10
  71.5 0.0 collective-permute-done.6
  71.5 0.9 add_convert_fusion
  72.4 1.8 %collective-permute-start.9 = (bf16[128,2048]{1,0:T(8,128)(2,1)}, bf16[128,2048]{1,0:T(8,128)(2,1)}, u32[]{:S(2)}, u32[]{:S(2)}) collective-permute-start(bf16[128,2048]{1,0:T(8,128)(2,1)} %add_convert_fusion), channel_id=1, source_target_pairs={{0,4},{1,5},{2,6},{3,7},{4,0},{5,1},{6,2},{7,3},{8,12},{9,13},{10,... | collective-permute-start | bytes 1572872 | tf_op jit(solution)/shard_map/ppermute | solution.py:17
  74.2 8.1 %collective-permute-done.7.next_ref = bf16[2,256,1024]{2,1,0:T(8,128)(2,1)S(1)} collective-permute-done((bf16[2,256,1024]{2,1,0:T(8,128)(2,1)}, bf16[2,256,1024]{2,1,0:T(8,128)(2,1)S(1)}, u32[]{:S(2)}, u32[]{:S(2)}) %collective-permute-start.7) | collective-permute-done | bytes 1048608 | tf_op jit(solution)/shard_map/ppermute | solution.py:17
  82.3 3.0 %shard_map.60 = (f32[128,2048]{1,0:T(8,128)S(1)}, bf16[128,2048]{1,0:T(8,128)(2,1)S(1)}) custom-call(s32[4]{0:T(128)S(1)} %get-tuple-element.35.pick_ref, bf16[4,2,256,1024]{3,2,1,0:T(8,128)(2,1)S(1)} %copy-done.5, bf16[2,256,1024]{2,1,0:T(8,128)(2,1)S(1)} %collective-permute-done.7.next_ref, bf16[2,2,1024,1024]{3,2,1,0:T(8,128)(2,1)S(1)} %bitcast.18), custom_call_target="tpu_custom_call" | custom-call | flops 2147483648 | bytes 8388608 | tf_op jit(solution)/shard_map/pallas_call | solution.py:235
  85.3 0.1 collective-permute-start.8
  85.4 12.0 %collective-permute-done.10 = bf16[128,2048]{1,0:T(8,128)(2,1)S(1)} collective-permute-done((bf16[128,2048]{1,0:T(8,128)(2,1)}, bf16[128,2048]{1,0:T(8,128)(2,1)S(1)}, u32[]{:S(2)}, u32[]{:S(2)}) %collective-permute-start.10) | collective-permute-done | bytes 524320 | tf_op jit(solution)/shard_map/ppermute | solution.py:17
  97.4 2.7 %collective-permute-done.9 = bf16[128,2048]{1,0:T(8,128)(2,1)} collective-permute-done((bf16[128,2048]{1,0:T(8,128)(2,1)}, bf16[128,2048]{1,0:T(8,128)(2,1)}, u32[]{:S(2)}, u32[]{:S(2)}) %collective-permute-start.9) | collective-permute-done | bytes 524320 | tf_op jit(solution)/shard_map/ppermute | solution.py:17
  100.0 0.0 collective-permute-done.8
  100.0 1.5 %convert_add_fusion = f32[128,2048]{1,0:T(8,128)S(1)} fusion(bf16[128,2048]{1,0:T(8,128)(2,1)S(1)} %collective-permute-done.10, bf16[128,2048]{1,0:T(8,128)(2,1)} %collective-permute-done.9, f32[128,2048]{1,0:T(8,128)S(1)} %get-tuple-element.37, bf16[128,2048]{1,0:T(8,128)(2,1)} %collective-permute-done.8), kind=kLoop, calls=%fused_computation | loop fusion | flops 1572864 | bytes 3670016 | tf_op jit(solution)/shard_map/add | solution.py:288
  101.6 0.1 collective-permute-start.11
  101.6 6.6 %collective-permute-done.11 = bf16[64,2048]{1,0:T(8,128)(2,1)S(1)} collective-permute-done((bf16[64,2048]{1,0:T(8,128)(2,1)S(1)}, bf16[64,2048]{1,0:T(8,128)(2,1)S(1)}, u32[]{:S(2)}, u32[]{:S(2)}) %collective-permute-start.11) | collective-permute-done | bytes 262176 | tf_op jit(solution)/shard_map/ppermute | solution.py:17
  108.3 0.1 fusion
  108.3 1.2 %reshape.16 = f32[64,2,1024]{2,1,0:T(2,128)} reshape(f32[64,2048]{1,0:T(8,128)S(1)} %fusion) | data formatting | bytes 1048576 | tf_op jit(solution)/shard_map/reshape | solution.py:293
  (17 shorter events, 0.1 us)
Async XLA Ops:
  0.0 8.4 %copy-start.10 = (s32[2,2]{1,0:T(2,128)S(1)}, s32[2,2]{1,0:T(2,128)}, u32[]{:S(2)}) copy-start(s32[2,2]{1,0:T(2,128)} %first_ref.1) | copy-start | bytes 52
  0.0 8.4 %copy-start.8 = (bf16[2,2,32,32]{3,2,1,0:T(8,128)(2,1)S(1)}, bf16[2,2,32,32]{3,2,1,0:T(8,128)(2,1)}, u32[]{:S(2)}) copy-start(bf16[2,2,32,32]{3,2,1,0:T(8,128)(2,1)} %cond_ref.1) | copy-start | bytes 24580
  0.0 2.2 %copy-start.6 = (bf16[2,32,32,1024]{3,2,1,0:T(8,128)(2,1)S(1)}, bf16[2,32,32,1024]{3,2,1,0:T(8,128)(2,1)}, u32[]{:S(2)}) copy-start(bf16[2,32,32,1024]{3,2,1,0:T(8,128)(2,1)} %coeffs_ref.1) | copy-start | bytes 12582916
  2.2 6.2 %copy-start.7 = (bf16[2,32,32,1024]{3,2,1,0:T(8,128)(2,1)S(1)}, bf16[2,32,32,1024]{3,2,1,0:T(8,128)(2,1)}, u32[]{:S(2)}) copy-start(bf16[2,32,32,1024]{3,2,1,0:T(8,128)(2,1)} %coeffs_ref.1) | copy-start | bytes 12582916
  2.2 6.2 %copy-start.9 = (bf16[2,2,32,32]{3,2,1,0:T(8,128)(2,1)S(1)}, bf16[2,2,32,32]{3,2,1,0:T(8,128)(2,1)}, u32[]{:S(2)}) copy-start(bf16[2,2,32,32]{3,2,1,0:T(8,128)(2,1)} %val_ref.1) | copy-start | bytes 24580
  3.0 28.2 %copy-start.11 = (s32[2]{0:T(128)S(1)}, s32[2]{0:T(128)}, u32[]{:S(2)}) copy-start(s32[2]{0:T(128)} %param.8) | copy-start | bytes 28
  3.0 28.3 %collective-permute-start = (bf16[2,256,1024]{2,1,0:T(8,128)(2,1)S(1)}, bf16[2,256,1024]{2,1,0:T(8,128)(2,1)S(1)}, u32[]{:S(2)}, u32[]{:S(2)}) collective-permute-start(bf16[2,256,1024]{2,1,0:T(8,128)(2,1)S(1)} %shard_map.56), channel_id=1, source_target_pairs={{0,15},{1,0},{2,1},{3,2},{4,3},{5,4},{6,5},{7,6},{8,7},{9,8},{10,9... | collective-permute-start | bytes 3145736 | tf_op jit(solution)/shard_map/ppermute | solution.py:17
  24.6 3.3 %copy-start = (bf16[2,2,32,32,1024]{4,3,2,1,0:T(8,128)(2,1)}, bf16[2,2,32,32,1024]{4,3,2,1,0:T(8,128)(2,1)S(1)}, u32[]{:S(2)}) copy-start(bf16[2,2,32,32,1024]{4,3,2,1,0:T(8,128)(2,1)S(1)} %get-tuple-element.22) | copy-start | bytes 25165828
  27.8 2.0 %copy-start.3 = (bf16[4,2,256,1024]{3,2,1,0:T(8,128)(2,1)}, bf16[4,2,256,1024]{3,2,1,0:T(8,128)(2,1)S(1)}, u32[]{:S(2)}) copy-start(bf16[4,2,256,1024]{3,2,1,0:T(8,128)(2,1)S(1)} %get-tuple-element.24.own_ref) | copy-start | bytes 12582916
  29.8 14.1 %collective-permute-start.2 = (bf16[2,256,1024]{2,1,0:T(8,128)(2,1)}, bf16[2,256,1024]{2,1,0:T(8,128)(2,1)S(1)}, u32[]{:S(2)}, u32[]{:S(2)}) collective-permute-start(bf16[2,256,1024]{2,1,0:T(8,128)(2,1)} %get-tuple-element.28), channel_id=1, source_target_pairs={{0,15},{1,0},{2,1},{3,2},{4,3},{5,4},{6,5},{7,6},{8,7},{9,8},{10,9... | collective-permute-start | bytes 3145736 | tf_op jit(solution)/shard_map/ppermute | solution.py:17
  31.3 3.4 %copy-start.1 = (bf16[2,2,32,32,1024]{4,3,2,1,0:T(8,128)(2,1)S(1)}, bf16[2,2,32,32,1024]{4,3,2,1,0:T(8,128)(2,1)}, u32[]{:S(2)}) copy-start(bf16[2,2,32,32,1024]{4,3,2,1,0:T(8,128)(2,1)} %copy-done) | copy-start | bytes 25165828
  34.7 2.2 %copy-start.4 = (bf16[4,2,256,1024]{3,2,1,0:T(8,128)(2,1)S(1)}, bf16[4,2,256,1024]{3,2,1,0:T(8,128)(2,1)}, u32[]{:S(2)}) copy-start(bf16[4,2,256,1024]{3,2,1,0:T(8,128)(2,1)} %copy-done.3) | copy-start | bytes 12582916
  39.8 2.1 %collective-permute-start.1 = (bf16[128,2048]{1,0:T(8,128)(2,1)S(1)}, bf16[128,2048]{1,0:T(8,128)(2,1)S(1)}, u32[]{:S(2)}, u32[]{:S(2)}) collective-permute-start(bf16[128,2048]{1,0:T(8,128)(2,1)S(1)} %get-tuple-element.26), channel_id=1, source_target_pairs={{0,1},{1,0},{2,3},{3,2},{4,5},{5,4},{6,7},{7,6},{8,9},{9,8},{10,11... | collective-permute-start | bytes 1572872 | tf_op jit(solution)/shard_map/ppermute | solution.py:17
  39.9 20.8 %collective-permute-start.5 = (bf16[2,256,1024]{2,1,0:T(8,128)(2,1)}, bf16[2,256,1024]{2,1,0:T(8,128)(2,1)S(1)}, u32[]{:S(2)}, u32[]{:S(2)}) collective-permute-start(bf16[2,256,1024]{2,1,0:T(8,128)(2,1)} %get-tuple-element.32), channel_id=1, source_target_pairs={{0,15},{1,0},{2,1},{3,2},{4,3},{5,4},{6,5},{7,6},{8,7},{9,8},{10,9... | collective-permute-start | bytes 3145736 | tf_op jit(solution)/shard_map/ppermute | solution.py:17
  42.8 26.5 %collective-permute-start.4 = (bf16[128,2048]{1,0:T(8,128)(2,1)}, bf16[128,2048]{1,0:T(8,128)(2,1)}, u32[]{:S(2)}, u32[]{:S(2)}) collective-permute-start(bf16[128,2048]{1,0:T(8,128)(2,1)} %add_convert_fusion.2), channel_id=1, source_target_pairs={{0,4},{1,5},{2,6},{3,7},{4,0},{5,1},{6,2},{7,3},{8,12},{9,13},{10,... | collective-permute-start | bytes 1572872 | tf_op jit(solution)/shard_map/ppermute | solution.py:17
  47.7 21.6 %collective-permute-start.3 = (bf16[128,2048]{1,0:T(8,128)(2,1)}, bf16[128,2048]{1,0:T(8,128)(2,1)}, u32[]{:S(2)}, u32[]{:S(2)}) collective-permute-start(bf16[128,2048]{1,0:T(8,128)(2,1)} %get-tuple-element.30), channel_id=1, source_target_pairs={{0,1},{1,0},{2,3},{3,2},{4,5},{5,4},{6,7},{7,6},{8,9},{9,8},{10,11... | collective-permute-start | bytes 1572872 | tf_op jit(solution)/shard_map/ppermute | solution.py:17
  47.7 34.7 %collective-permute-start.7 = (bf16[2,256,1024]{2,1,0:T(8,128)(2,1)}, bf16[2,256,1024]{2,1,0:T(8,128)(2,1)S(1)}, u32[]{:S(2)}, u32[]{:S(2)}) collective-permute-start(bf16[2,256,1024]{2,1,0:T(8,128)(2,1)} %get-tuple-element.36), channel_id=1, source_target_pairs={{0,15},{1,0},{2,1},{3,2},{4,3},{5,4},{6,5},{7,6},{8,7},{9,8},{10,9... | collective-permute-start | bytes 3145736 | tf_op jit(solution)/shard_map/ppermute | solution.py:17
  60.7 3.4 %copy-start.2 = (bf16[2,2,32,32,1024]{4,3,2,1,0:T(8,128)(2,1)S(1)}, bf16[2,2,32,32,1024]{4,3,2,1,0:T(8,128)(2,1)}, u32[]{:S(2)}) copy-start(bf16[2,2,32,32,1024]{4,3,2,1,0:T(8,128)(2,1)} %copy-done) | copy-start | bytes 25165828
  64.1 2.2 %copy-start.5 = (bf16[4,2,256,1024]{3,2,1,0:T(8,128)(2,1)S(1)}, bf16[4,2,256,1024]{3,2,1,0:T(8,128)(2,1)}, u32[]{:S(2)}) copy-start(bf16[4,2,256,1024]{3,2,1,0:T(8,128)(2,1)} %copy-done.3) | copy-start | bytes 12582916
  69.2 2.3 %collective-permute-start.6 = (bf16[128,2048]{1,0:T(8,128)(2,1)S(1)}, bf16[128,2048]{1,0:T(8,128)(2,1)S(1)}, u32[]{:S(2)}, u32[]{:S(2)}) collective-permute-start(bf16[128,2048]{1,0:T(8,128)(2,1)S(1)} %get-tuple-element.34), channel_id=1, source_target_pairs={{0,1},{1,0},{2,3},{3,2},{4,5},{5,4},{6,7},{7,6},{8,9},{9,8},{10,11... | collective-permute-start | bytes 1572872 | tf_op jit(solution)/shard_map/ppermute | solution.py:17
  71.5 25.9 %collective-permute-start.10 = (bf16[128,2048]{1,0:T(8,128)(2,1)}, bf16[128,2048]{1,0:T(8,128)(2,1)S(1)}, u32[]{:S(2)}, u32[]{:S(2)}) collective-permute-start(bf16[128,2048]{1,0:T(8,128)(2,1)} %add_convert_fusion.1), channel_id=1, source_target_pairs={{0,8},{1,9},{2,10},{3,11},{4,12},{5,13},{6,14},{7,15},{8,0},{9,1},... | collective-permute-start | bytes 1572872 | tf_op jit(solution)/shard_map/ppermute | solution.py:17
  72.4 27.6 %collective-permute-start.9 = (bf16[128,2048]{1,0:T(8,128)(2,1)}, bf16[128,2048]{1,0:T(8,128)(2,1)}, u32[]{:S(2)}, u32[]{:S(2)}) collective-permute-start(bf16[128,2048]{1,0:T(8,128)(2,1)} %add_convert_fusion), channel_id=1, source_target_pairs={{0,4},{1,5},{2,6},{3,7},{4,0},{5,1},{6,2},{7,3},{8,12},{9,13},{10,... | collective-permute-start | bytes 1572872 | tf_op jit(solution)/shard_map/ppermute | solution.py:17
  85.3 14.7 %collective-permute-start.8 = (bf16[128,2048]{1,0:T(8,128)(2,1)S(1)}, bf16[128,2048]{1,0:T(8,128)(2,1)}, u32[]{:S(2)}, u32[]{:S(2)}) collective-permute-start(bf16[128,2048]{1,0:T(8,128)(2,1)S(1)} %get-tuple-element.38), channel_id=1, source_target_pairs={{0,1},{1,0},{2,3},{3,2},{4,5},{5,4},{6,7},{7,6},{8,9},{9,8},{10,11... | collective-permute-start | bytes 1572872 | tf_op jit(solution)/shard_map/ppermute | solution.py:17
  101.6 6.7 %collective-permute-start.11 = (bf16[64,2048]{1,0:T(8,128)(2,1)S(1)}, bf16[64,2048]{1,0:T(8,128)(2,1)S(1)}, u32[]{:S(2)}, u32[]{:S(2)}) collective-permute-start(bf16[64,2048]{1,0:T(8,128)(2,1)S(1)} %fusion.1), channel_id=1, source_target_pairs={{0,2},{1,3},{2,0},{3,1},{4,6},{5,7},{6,4},{7,5},{8,10},{9,11},{10,... | collective-permute-start | bytes 786440 | tf_op jit(solution)/shard_map/ppermute | solution.py:17

commit v4 on v1

v4 whole, which is shorter than its diff:
```python
import functools
import math

import jax
import jax.numpy as jnp
from jax import lax
from jax.experimental import pallas as pl
from jax.experimental.pallas import tpu as pltpu
from jax.sharding import PartitionSpec as P

MIB = 1024 * 1024


def permute(x, target):
    size = lax.axis_size("ka")
    pairs = [(i, target(i)) for i in range(size)]
    return lax.ppermute(x, "ka", [(i, j % size) for i, j in pairs if j is not None])


def nt_dot(a, b):
    return lax.dot_general(a, b, (((1,), (1,)), ((), ())), preferred_element_type=jnp.float32)


def iotas(rows, cols):
    shape = (rows, cols)
    return lax.broadcasted_iota(jnp.int32, shape, 0), lax.broadcasted_iota(jnp.int32, shape, 1)


def ones_where(condition):
    return jnp.where(condition, 1.0, 0.0).astype(jnp.bfloat16)


PART_C, PART_V = 8, 16


def fill_weights(first_ref, cond_ref, val_ref, we_ref, wh_ref):
    _, modes, bands_c, _ = cond_ref.shape
    bands_v = val_ref.shape[2]
    rows_e, rows_h = bands_c * PART_V, PART_C * bands_v
    row, col = iotas(rows_e, bands_c)
    take = ones_where(row // PART_V == col)
    row, col = iotas(rows_e, rows_e)
    for m in range(modes):
        half = jnp.dot(take, cond_ref[0, m], preferred_element_type=jnp.float32)
        full = nt_dot(half.astype(jnp.bfloat16), take)
        keep = (row % PART_V == col % PART_V) & (row // PART_V >= first_ref[m, 0])
        we_ref[m * rows_e:(m + 1) * rows_e, :] = jnp.where(keep, full, 0.0).astype(jnp.bfloat16)
    row, col = iotas(rows_h, bands_v)
    take = ones_where(row % bands_v == col)
    row, col = iotas(rows_h, rows_h)
    for m in range(modes):
        half = nt_dot(take, val_ref[0, m])
        full = nt_dot(half.astype(jnp.bfloat16), take)
        keep = (row // bands_v == col // bands_v) & (row % bands_v >= first_ref[m, 1])
        wh_ref[m * rows_h:(m + 1) * rows_h, :] = jnp.where(keep, full, 0.0).astype(jnp.bfloat16)


def products_kernel(first_ref, coeffs_ref, cond_ref, val_ref, out_ref, we_ref, wh_ref):
    _, bands_c, bands_v, tile = coeffs_ref.shape
    modes = cond_ref.shape[1]
    rows_e, rows_h = bands_c * PART_V, PART_C * bands_v

    @pl.when(pl.program_id(1) == 0)
    def _():
        fill_weights(first_ref, cond_ref, val_ref, we_ref, wh_ref)

    electron = []
    for h in range(bands_v // PART_V):
        x = coeffs_ref[0, :, h * PART_V:(h + 1) * PART_V, :].reshape(rows_e, tile)
        e = jnp.dot(we_ref[...], x, preferred_element_type=jnp.float32)
        electron.append(e.reshape(modes, bands_c, PART_V, tile))
    for q in range(bands_c // PART_C):
        own = slice(q * PART_C, (q + 1) * PART_C)
        y = coeffs_ref[0, own].reshape(rows_h, tile)
        hole = jnp.dot(wh_ref[...], y, preferred_element_type=jnp.float32)
        hole = hole.reshape(modes, PART_C, bands_v, tile)
        for m in range(modes):
            for h in range(bands_v // PART_V):
                cols = slice(h * PART_V, (h + 1) * PART_V)
                value = electron[h][m, own] - hole[m, :, cols]
                out_ref[0, m, own, cols, :] = value.astype(jnp.bfloat16)


def products_of(coeffs, g_cond, g_val, band_first):
    k_local, bands_c, bands_v, excitons = coeffs.shape
    modes = g_cond.shape[1]
    tile = 256
    rows_e, rows_h = bands_c * PART_V, PART_C * bands_v
    depth = bands_c * bands_v
    return pl.pallas_call(
        products_kernel,
        out_shape=jax.ShapeDtypeStruct((k_local, modes, bands_c, bands_v, excitons), jnp.bfloat16),
        grid=(k_local, excitons // tile),
        in_specs=[
            pl.BlockSpec(memory_space=pltpu.SMEM),
            pl.BlockSpec((1, bands_c, bands_v, tile), lambda k, s: (k, 0, 0, s)),
            pl.BlockSpec((1, modes, bands_c, bands_c), lambda k, s: (k, 0, 0, 0)),
            pl.BlockSpec((1, modes, bands_v, bands_v), lambda k, s: (k, 0, 0, 0)),
        ],
        out_specs=pl.BlockSpec((1, modes, bands_c, bands_v, tile), lambda k, s: (k, 0, 0, 0, s)),
        scratch_shapes=[
            pltpu.VMEM((modes * rows_e, rows_e), jnp.bfloat16),
            pltpu.VMEM((modes * rows_h, rows_h), jnp.bfloat16),
        ],
        compiler_params=pltpu.CompilerParams(vmem_limit_bytes=60 * MIB),
        cost_estimate=pl.CostEstimate(
            flops=2 * k_local * modes * excitons * depth * (rows_e + rows_h),
            bytes_accessed=2 * coeffs.size * (1 + modes),
            transcendentals=0,
        ),
    )(band_first, coeffs, g_cond, g_val)


def turn_kernel(blocks_ref, coeffs_ref, *refs):
    *out_refs, held, sems = refs
    pieces, k_local, parts, rows, width = held.shape

    def copy(i, k, p):
        columns = pl.ds(pl.multiple_of(blocks_ref[i] * width, width), width)
        source = coeffs_ref.at[k, pl.ds(p * rows, rows), columns]
        return pltpu.make_async_copy(source, held.at[i, k, p], sems.at[i, k, p])

    steps = [(i, k, p) for i in range(pieces) for k in range(k_local) for p in range(parts)]
    for step in steps:
        copy(*step).start()
    for step in steps:
        i, k, p = step
        copy(*step).wait()
        out_refs[i][k, :, p * rows:(p + 1) * rows] = held[i, k, p].T


def turned_pieces(flat, blocks, width):
    k_local, depth, _ = flat.shape
    pieces, parts = blocks.shape[0], 2
    return pl.pallas_call(
        turn_kernel,
        out_shape=[jax.ShapeDtypeStruct((k_local, width, depth), jnp.bfloat16)] * pieces,
        in_specs=[
            pl.BlockSpec(memory_space=pltpu.SMEM),
            pl.BlockSpec(memory_space=pl.ANY),
        ],
        out_specs=[pl.BlockSpec(memory_space=pltpu.VMEM)] * pieces,
        scratch_shapes=[
            pltpu.VMEM((pieces, k_local, parts, depth // parts, width), jnp.bfloat16),
            pltpu.SemaphoreType.DMA((pieces, k_local, parts)),
        ],
        compiler_params=pltpu.CompilerParams(vmem_limit_bytes=60 * MIB),
        cost_estimate=pl.CostEstimate(
            flops=0, bytes_accessed=4 * pieces * k_local * depth * width, transcendentals=0
        ),
    )(blocks, flat)


def rows_kernel(pick_ref, own_ref, next_ref, right_ref, keep_ref, send_ref, *refs):
    own_held, next_held, held, left, own_sems, next_sems, sems = refs
    k_local, depth, width = own_held.shape
    tiles, _, _, tile = held.shape
    per_mode = right_ref.shape[3] // tile
    core = pick_ref[k_local + 1]
    columns = pl.ds(pl.multiple_of(pick_ref[k_local] * width, width), width)
    near = [pick_ref[k] < k_local for k in range(k_local)]

    def copy_own(k):
        source = own_ref.at[jnp.minimum(pick_ref[k], k_local - 1), :, columns]
        return pltpu.make_async_copy(source, own_held.at[k], own_sems.at[k])

    def copy_next(k):
        source = next_ref.at[jnp.maximum(pick_ref[k] - k_local, 0)]
        return pltpu.make_async_copy(source, next_held.at[k], next_sems.at[k])

    def copy_right(t, k):
        source = right_ref.at[k, t // per_mode, :, pl.ds(t % per_mode * tile, tile)]
        return pltpu.make_async_copy(source, held.at[t, k], sems.at[t, k])

    for k in range(k_local):
        copy_own(k).start()
        copy_next(k).start()
    for t in range(tiles):
        for k in range(k_local):
            copy_right(t, k).start()
    for k in range(k_local):
        copy_own(k).wait()
        copy_next(k).wait()

        @pl.when(near[k])
        def _():
            left[:, k * depth:(k + 1) * depth] = own_held[k].T

        @pl.when(jnp.logical_not(near[k]))
        def _():
            left[:, k * depth:(k + 1) * depth] = next_held[k]

    for t in range(tiles):
        for k in range(k_local):
            copy_right(t, k).wait()
        right = held[t].reshape(k_local * depth, tile)
        total = jnp.dot(left[...], right, preferred_element_type=jnp.float32)
        parts = total.reshape(2, 2, width // 4, tile)
        low = parts[:, 0].reshape(width // 2, tile)
        high = parts[:, 1].reshape(width // 2, tile)
        place = slice(t * tile, (t + 1) * tile)
        keep_ref[:, place] = jnp.where(core == 0, low, high)
        send_ref[:, place] = jnp.where(core == 0, high, low).astype(jnp.bfloat16)


def rows_of(pick, own, following, products):
    k_local, width, depth = following.shape
    modes, excitons = products.shape[1], products.shape[3]
    columns, tile = modes * excitons, 512
    tiles = columns // tile
    return pl.pallas_call(
        rows_kernel,
        out_shape=[
            jax.ShapeDtypeStruct((width // 2, columns), jnp.float32),
            jax.ShapeDtypeStruct((width // 2, columns), jnp.bfloat16),
        ],
        in_specs=[pl.BlockSpec(memory_space=pltpu.SMEM)]
        + [pl.BlockSpec(memory_space=pl.ANY)] * 3,
        out_specs=[pl.BlockSpec(memory_space=pltpu.VMEM)] * 2,
        scratch_shapes=[
            pltpu.VMEM((k_local, depth, width), jnp.bfloat16),
            pltpu.VMEM((k_local, width, depth), jnp.bfloat16),
            pltpu.VMEM((tiles, k_local, depth, tile), jnp.bfloat16),
            pltpu.VMEM((width, k_local * depth), jnp.bfloat16),
            pltpu.SemaphoreType.DMA((k_local,)),
            pltpu.SemaphoreType.DMA((k_local,)),
            pltpu.SemaphoreType.DMA((tiles, k_local)),
        ],
        compiler_params=pltpu.CompilerParams(vmem_limit_bytes=50 * MIB),
        cost_estimate=pl.CostEstimate(
            flops=2 * k_local * depth * width * columns,
            bytes_accessed=2 * k_local * depth * columns,
            transcendentals=0,
        ),
    )(pick, own, following, products)


def on_two_by_four(coeffs, g_cond, g_val, k_plus_q, band_first, norm_factor):
    k_local, bands_c, bands_v, excitons = coeffs.shape
    modes = g_cond.shape[1]
    size = lax.axis_size("ka")
    width = excitons // 4
    me = lax.axis_index("ka")
    core, x, z = me & 1, me >> 1 & 1, me >> 2
    flat = coeffs.reshape(k_local, bands_c * bands_v, excitons)

    behind_z = (me + size - 1) % size >> 2
    order = behind_z ^ jnp.arange(3, -1, -1, dtype=jnp.int32)
    pieces = turned_pieces(flat, order[:1], width)
    others, _ = lax.optimization_barrier((order[1:], pieces))
    pieces += turned_pieces(flat, others, width)
    following = [permute(piece, lambda i: i - 1) for piece in pieces]
    products = products_of(coeffs, g_cond, g_val, band_first)
    products = products.reshape(k_local, modes, bands_c * bands_v, excitons)
    places = jnp.mod(k_plus_q - me * k_local, k_local * size)
    picks = [jnp.concatenate((places, jnp.stack((z ^ (3 - step), core)))) for step in range(4)]

    def rows(step, after):
        pick, _ = lax.optimization_barrier((picks[step], after))
        keep, send = rows_of(pick, flat, following[step], products)
        return keep, permute(send, lambda i: i ^ 1).astype(jnp.float32)

    keep, other = rows(0, products)
    send_far = (keep + other).astype(jnp.bfloat16)
    far = permute(send_far, lambda i: i ^ 4)
    keep_1, other_1 = rows(1, send_far)
    keep, other = rows(2, keep_1)
    send_pair = (keep_1 + other_1 + far.astype(jnp.float32)).astype(jnp.bfloat16)
    pair = permute(send_pair, lambda i: i ^ 8)
    send_near = (keep + other).astype(jnp.bfloat16)
    near = permute(send_near, lambda i: i ^ 4)
    keep, other = rows(3, (send_pair, send_near))
    total = keep + other + near.astype(jnp.float32) + pair.astype(jnp.float32)
    total = total.reshape(2, width // 4, modes * excitons)
    mine = lax.dynamic_index_in_dim(total, x, 0, keepdims=False)
    sent = lax.dynamic_index_in_dim(total, 1 - x, 0, keepdims=False).astype(jnp.bfloat16)
    total = mine + permute(sent, lambda i: i ^ 2).astype(jnp.float32)
    return (total * norm_factor).reshape(width // 4, modes, excitons)


def on_any(coeffs, g_cond, g_val, k_plus_q, band_first, norm_factor):
    k_local, bands_c, bands_v, excitons = coeffs.shape
    modes = g_cond.shape[1]
    size = lax.axis_size("ka")
    depth = bands_c * bands_v
    flat = coeffs.reshape(k_local, depth, excitons)
    blocks = jnp.concatenate((flat, permute(flat, lambda i: i - 1)), 0)
    offsets = jnp.mod(k_plus_q - lax.axis_index("ka") * k_local, k_local * size)
    products = products_of(coeffs, g_cond, g_val, band_first)
    products = products.reshape(k_local, modes, depth, excitons)
    partners = [
        lax.dynamic_index_in_dim(blocks, offsets[k], 0, keepdims=False) for k in range(k_local)
    ]
    running = jnp.einsum(
        "kds,kmdt->smt", jnp.stack(partners), products, preferred_element_type=jnp.float32
    )
    return lax.psum_scatter(running * norm_factor, "ka", scatter_dimension=0, tiled=True)


def shards(coeffs, g_cond, g_val, k_plus_q, band_first):
    k_local, bands_c, bands_v, excitons = coeffs.shape
    size = lax.axis_size("ka")
    norm_factor = 1.0 / math.sqrt(bands_c * bands_v * k_local * size)
    whole_tiles = excitons % (4 * 128) == 0
    plan = on_two_by_four if size == 16 and whole_tiles else on_any
    return plan(coeffs, g_cond, g_val, k_plus_q, band_first, norm_factor)


def solution(mesh):
    in_specs = (
        P(("groups", "ka"), None, None, None),
        P(("groups", "ka"), None, None, None),
        P(("groups", "ka"), None, None, None),
        P(("groups", "ka")),
        P("groups", None),
    )
    out_specs = P(("groups", "ka"), None, None)
    return jax.shard_map(shards, mesh=mesh, in_specs=in_specs, out_specs=out_specs, check_vma=False)
```

time: 109 us -> 104 us (0.954)
  local copies, waits for them, and re-layouts: 22.2 us -> 2.59 us
  Pallas kernels: 32.7 us -> 43.9 us
  starting transfers between devices: 11.3 us -> 13 us
  other arithmetic: 4.6 us -> 6.26 us
    unnamed x22 -> x2, local copies, waits for them, and re-layouts: 11.7 us -> 0.01 us
    dynamic_slice x4 -> x0, local copies, waits for them, and re-layouts: 9.28 us -> none  [on_two_by_four(): lax.dynamic_slice_in_dim(source, (behind_z ^ 3 - step) * width, width, 2)]
    pallas_call x0 -> x2, Pallas kernels: none -> 7.92 us  [turned_pieces(): pl.pallas_call(turn_kernel, out_shape=[jax.ShapeDtypeStruct((k_local, wid...]
    pallas_call x4, Pallas kernels: 20.8 us -> 22.6 us  [rows_of(): pl.pallas_call(rows_kernel, out_shape=[jax.ShapeDtypeStruct((width // 2,...]
    ppermute x12, starting transfers between devices: 11.3 us -> 13 us  [permute(): lax.ppermute(x, 'ka', [(i, j % size) for i, j in pairs if j is not None])]
    pallas_call x1, Pallas kernels: 12 us -> 13.4 us  [products_of(): pl.pallas_call(products_kernel, out_shape=jax.ShapeDtypeStruct((k_local,...]
    slice x0 -> x1, local copies, waits for them, and re-layouts: none -> 1.31 us  [on_two_by_four(): others, _ = lax.optimization_barrier((order[1:], pieces))]
  transfers between devices with their start and end apart: 12 -> 12, of which waited for: 4 -> 7; matrix products, arithmetic and copies ran while one was open for 9% -> 5% of each run, Pallas kernels for 30% -> 40%
where the time goes in v4:
time: 104 us; the launch traced here: 102 us
  Pallas kernels  43.9 us (42%)
  waiting for transfers between devices  36.6 us (35%)
  starting transfers between devices  13 us (12%)
  other arithmetic  6.26 us (6%)
  local copies, waits for them, and re-layouts  2.59 us (2%)
    ppermute x12, waiting for transfers between devices, permute(): lax.ppermute(x, 'ka', [(i, j % size) for i, j in pairs if j is not None])  36.6 us
    pallas_call x4, Pallas kernels, rows_of(): pl.pallas_call(rows_kernel, out_shape=[jax.ShapeDtypeStruct((width // 2,...  22.6 us
    pallas_call x1, Pallas kernels, products_of(): pl.pallas_call(products_kernel, out_shape=jax.ShapeDtypeStruct((k_local,...  13.4 us
    ppermute x12, starting transfers between devices, permute(): lax.ppermute(x, 'ka', [(i, j % size) for i, j in pairs if j is not None])  13 us
    pallas_call x2, Pallas kernels, turned_pieces(): pl.pallas_call(turn_kernel, out_shape=[jax.ShapeDtypeStruct((k_local, wid...  7.92 us
    convert_element_type x1, other arithmetic, on_two_by_four(): (keep_1 + other_1 + far.astype(jnp.float32)).astype(jnp.bfloat16)  2.21 us
  transfers between devices with their start and end apart: 12, of which 7 were waited for; matrix products, arithmetic and copies ran while one was open for 5% of the time, Pallas kernels for 40%

profile of v4, /device:TPU:0, one launch (start us, length us, event | category | flops | bytes accessed | tf_op | source)
XLA Modules:
  0.0 102.5 jit_solution(6640071160081141315)
XLA Ops:
  0.0 0.0 copy-start
  0.0 0.5 add_xor_fusion
  0.5 3.1 %shard_map.56 = bf16[2,256,1024]{2,1,0:T(8,128)(2,1)} custom-call(s32[1]{0:T(128)} %bitcast.27, bf16[2,1024,1024]{2,1,0:T(8,128)(2,1)} %bitcast.15), custom_call_target="tpu_custom_call" | custom-call | bytes 2097152 | tf_op jit(solution)/shard_map/pallas_call | solution.py:135
  3.6 5.5 %collective-permute-start = (bf16[2,256,1024]{2,1,0:T(8,128)(2,1)}, bf16[2,256,1024]{2,1,0:T(8,128)(2,1)S(1)}, u32[]{:S(2)}, u32[]{:S(2)}) collective-permute-start(bf16[2,256,1024]{2,1,0:T(8,128)(2,1)} %shard_map.56), channel_id=1, source_target_pairs={{0,15},{1,0},{2,1},{3,2},{4,3},{5,4},{6,5},{7,6},{8,7},{9,8},{10,9... | collective-permute-start | bytes 3145736 | tf_op jit(solution)/shard_map/ppermute | solution.py:17
  9.1 1.3 %slice.7.blocks_ref = s32[3]{0:T(128)} slice(s32[4]{0:T(128)} %add_xor_fusion), slice={[1:4]} | slice | bytes 24 | tf_op jit(solution)/shard_map/slice | solution.py:250
  10.4 4.8 %shard_map.58 = (bf16[2,256,1024]{2,1,0:T(8,128)(2,1)}, bf16[2,256,1024]{2,1,0:T(8,128)(2,1)}, bf16[2,256,1024]{2,1,0:T(8,128)(2,1)}) custom-call(s32[3]{0:T(128)} %slice.7.blocks_ref, bf16[2,1024,1024]{2,1,0:T(8,128)(2,1)} %bitcast.16), custom_call_target="tpu_custom_call" | custom-call | bytes 6291456 | tf_op jit(solution)/shard_map/pallas_call | solution.py:135
  15.2 0.7 collective-permute-start.2
  16.0 0.0 copy-done
  16.0 0.1 add_add_fusion
  16.1 13.4 %shard_map.55 = bf16[2,2,32,32,1024]{4,3,2,1,0:T(8,128)(2,1)} custom-call(s32[2,2]{1,0:T(2,128)} %first_ref.1, bf16[2,32,32,1024]{3,2,1,0:T(8,128)(2,1)} %coeffs_ref.1, bf16[2,2,32,32]{3,2,1,0:T(8,128)(2,1)} %cond_ref.1, bf16[2,2,32,32]{3,2,1,0:T(8,128)(2,1)} %val_ref.1), custom_call_target="tpu_custom_call" | custom-call | flops 6442450944 | bytes 12582912 | tf_op jit(solution)/shard_map/pallas_call | solution.py:90
  29.4 0.0 collective-permute-done.next_ref
  29.4 5.5 %shard_map.57 = (f32[128,2048]{1,0:T(8,128)S(1)}, bf16[128,2048]{1,0:T(8,128)(2,1)S(1)}) custom-call(s32[4]{0:T(128)S(1)} %get-tuple-element.21.pick_ref, bf16[2,1024,1024]{2,1,0:T(8,128)(2,1)} %bitcast.17, bf16[2,256,1024]{2,1,0:T(8,128)(2,1)S(1)} %collective-permute-done.next_ref, bf16[2,2,1024,1024]{3,2,1,0:T(8,128)(2,1)} %bitcast.21), custom_call_target="tpu_custom_call" | custom-call | flops 2147483648 | bytes 8388608 | tf_op jit(solution)/shard_map/pallas_call | solution.py:211
  34.9 0.1 collective-permute-start.1
  35.0 0.6 collective-permute-start.5
  35.6 1.4 %collective-permute-done.1 = bf16[128,2048]{1,0:T(8,128)(2,1)S(1)} collective-permute-done((bf16[128,2048]{1,0:T(8,128)(2,1)S(1)}, bf16[128,2048]{1,0:T(8,128)(2,1)S(1)}, u32[]{:S(2)}, u32[]{:S(2)}) %collective-permute-start.1) | collective-permute-done | bytes 524320 | tf_op jit(solution)/shard_map/ppermute | solution.py:17
  37.0 0.9 add_convert_fusion.2
  37.9 0.0 collective-permute-start.4
  37.9 0.0 collective-permute-done.2.next_ref
  37.9 6.3 %shard_map.59 = (f32[128,2048]{1,0:T(8,128)S(1)}, bf16[128,2048]{1,0:T(8,128)(2,1)}) custom-call(s32[4]{0:T(128)S(1)} %get-tuple-element.24.pick_ref, bf16[2,1024,1024]{2,1,0:T(8,128)(2,1)} %bitcast.18, bf16[2,256,1024]{2,1,0:T(8,128)(2,1)S(1)} %collective-permute-done.2.next_ref, bf16[2,2,1024,1024]{3,2,1,0:T(8,128)(2,1)} %bitcast.22), custom_call_target="tpu_custom_call" | custom-call | flops 2147483648 | bytes 8388608 | tf_op jit(solution)/shard_map/pallas_call | solution.py:211
  44.2 0.2 collective-permute-start.3
  44.4 0.9 collective-permute-start.7
  45.3 0.1 add_add_fusion.3.pick_ref
  45.3 8.5 %collective-permute-done.5.next_ref = bf16[2,256,1024]{2,1,0:T(8,128)(2,1)S(1)} collective-permute-done((bf16[2,256,1024]{2,1,0:T(8,128)(2,1)}, bf16[2,256,1024]{2,1,0:T(8,128)(2,1)S(1)}, u32[]{:S(2)}, u32[]{:S(2)}) %collective-permute-start.5) | collective-permute-done | bytes 1048608 | tf_op jit(solution)/shard_map/ppermute | solution.py:17
  53.8 5.4 %shard_map.60 = (f32[128,2048]{1,0:T(8,128)S(1)}, bf16[128,2048]{1,0:T(8,128)(2,1)S(1)}) custom-call(s32[4]{0:T(128)S(1)} %add_add_fusion.3.pick_ref, bf16[2,1024,1024]{2,1,0:T(8,128)(2,1)} %bitcast.19, bf16[2,256,1024]{2,1,0:T(8,128)(2,1)S(1)} %collective-permute-done.5.next_ref, bf16[2,2,1024,1024]{3,2,1,0:T(8,128)(2,1)} %bitcast.23), custom_call_target="tpu_custom_call" | custom-call | flops 2147483648 | bytes 8388608 | tf_op jit(solution)/shard_map/pallas_call | solution.py:211
  59.3 0.1 collective-permute-start.6
  59.4 0.1 collective-permute-done.4
  59.4 0.0 collective-permute-done.3
  59.4 2.2 %add_convert_fusion.1 = bf16[128,2048]{1,0:T(8,128)(2,1)} fusion(bf16[128,2048]{1,0:T(8,128)(2,1)} %collective-permute-done.4, f32[128,2048]{1,0:T(8,128)S(1)} %get-tuple-element.27, bf16[128,2048]{1,0:T(8,128)(2,1)} %collective-permute-done.3), kind=kLoop, calls=%fused_computation.2 | loop fusion | flops 1310720 | bytes 2621440 | tf_op jit(solution)/shard_map/convert_element_type | solution.py:268
  61.7 2.4 %collective-permute-start.10 = (bf16[128,2048]{1,0:T(8,128)(2,1)}, bf16[128,2048]{1,0:T(8,128)(2,1)S(1)}, u32[]{:S(2)}, u32[]{:S(2)}) collective-permute-start(bf16[128,2048]{1,0:T(8,128)(2,1)} %add_convert_fusion.1), channel_id=1, source_target_pairs={{0,8},{1,9},{2,10},{3,11},{4,12},{5,13},{6,14},{7,15},{8,0},{9,1},... | collective-permute-start | bytes 1572872 | tf_op jit(solution)/shard_map/ppermute | solution.py:17
  64.0 0.0 collective-permute-done.6
  64.0 0.9 add_convert_fusion
  65.0 2.5 %collective-permute-start.9 = (bf16[128,2048]{1,0:T(8,128)(2,1)}, bf16[128,2048]{1,0:T(8,128)(2,1)}, u32[]{:S(2)}, u32[]{:S(2)}) collective-permute-start(bf16[128,2048]{1,0:T(8,128)(2,1)} %add_convert_fusion), channel_id=1, source_target_pairs={{0,4},{1,5},{2,6},{3,7},{4,0},{5,1},{6,2},{7,3},{8,12},{9,13},{10,... | collective-permute-start | bytes 1572872 | tf_op jit(solution)/shard_map/ppermute | solution.py:17
  67.4 9.4 %collective-permute-done.7.next_ref = bf16[2,256,1024]{2,1,0:T(8,128)(2,1)S(1)} collective-permute-done((bf16[2,256,1024]{2,1,0:T(8,128)(2,1)}, bf16[2,256,1024]{2,1,0:T(8,128)(2,1)S(1)}, u32[]{:S(2)}, u32[]{:S(2)}) %collective-permute-start.7) | collective-permute-done | bytes 1048608 | tf_op jit(solution)/shard_map/ppermute | solution.py:17
  76.9 5.4 %shard_map.61 = (f32[128,2048]{1,0:T(8,128)S(1)}, bf16[128,2048]{1,0:T(8,128)(2,1)S(1)}) custom-call(s32[4]{0:T(128)S(1)} %get-tuple-element.33.pick_ref, bf16[2,1024,1024]{2,1,0:T(8,128)(2,1)} %bitcast.20, bf16[2,256,1024]{2,1,0:T(8,128)(2,1)S(1)} %collective-permute-done.7.next_ref, bf16[2,2,1024,1024]{3,2,1,0:T(8,128)(2,1)} %bitcast.24), custom_call_target="tpu_custom_call" | custom-call | flops 2147483648 | bytes 8388608 | tf_op jit(solution)/shard_map/pallas_call | solution.py:211
  82.3 0.1 collective-permute-start.8
  82.4 6.0 %collective-permute-done.10 = bf16[128,2048]{1,0:T(8,128)(2,1)S(1)} collective-permute-done((bf16[128,2048]{1,0:T(8,128)(2,1)}, bf16[128,2048]{1,0:T(8,128)(2,1)S(1)}, u32[]{:S(2)}, u32[]{:S(2)}) %collective-permute-start.10) | collective-permute-done | bytes 524320 | tf_op jit(solution)/shard_map/ppermute | solution.py:17
  88.4 4.8 %collective-permute-done.9 = bf16[128,2048]{1,0:T(8,128)(2,1)} collective-permute-done((bf16[128,2048]{1,0:T(8,128)(2,1)}, bf16[128,2048]{1,0:T(8,128)(2,1)}, u32[]{:S(2)}, u32[]{:S(2)}) %collective-permute-start.9) | collective-permute-done | bytes 524320 | tf_op jit(solution)/shard_map/ppermute | solution.py:17
  93.2 0.0 collective-permute-done.8
  93.2 1.5 %convert_add_fusion = f32[128,2048]{1,0:T(8,128)S(1)} fusion(bf16[128,2048]{1,0:T(8,128)(2,1)S(1)} %collective-permute-done.10, bf16[128,2048]{1,0:T(8,128)(2,1)} %collective-permute-done.9, f32[128,2048]{1,0:T(8,128)S(1)} %get-tuple-element.35, bf16[128,2048]{1,0:T(8,128)(2,1)} %collective-permute-done.8), kind=kLoop, calls=%fused_computation | loop fusion | flops 1572864 | bytes 3670016 | tf_op jit(solution)/shard_map/add | solution.py:273
  94.7 0.1 collective-permute-start.11
  94.8 6.4 %collective-permute-done.11 = bf16[64,2048]{1,0:T(8,128)(2,1)S(1)} collective-permute-done((bf16[64,2048]{1,0:T(8,128)(2,1)S(1)}, bf16[64,2048]{1,0:T(8,128)(2,1)S(1)}, u32[]{:S(2)}, u32[]{:S(2)}) %collective-permute-start.11) | collective-permute-done | bytes 262176 | tf_op jit(solution)/shard_map/ppermute | solution.py:17
  101.2 0.1 fusion
  101.2 1.2 %reshape.16 = f32[64,2,1024]{2,1,0:T(2,128)} reshape(f32[64,2048]{1,0:T(8,128)S(1)} %fusion) | data formatting | bytes 1048576 | tf_op jit(solution)/shard_map/reshape | solution.py:278
  (2 shorter events, 0.0 us)
Async XLA Ops:
  0.0 16.0 %copy-start = (s32[2]{0:T(128)S(1)}, s32[2]{0:T(128)}, u32[]{:S(2)}) copy-start(s32[2]{0:T(128)} %param.8) | copy-start | bytes 28
  3.6 25.8 %collective-permute-start = (bf16[2,256,1024]{2,1,0:T(8,128)(2,1)}, bf16[2,256,1024]{2,1,0:T(8,128)(2,1)S(1)}, u32[]{:S(2)}, u32[]{:S(2)}) collective-permute-start(bf16[2,256,1024]{2,1,0:T(8,128)(2,1)} %shard_map.56), channel_id=1, source_target_pairs={{0,15},{1,0},{2,1},{3,2},{4,3},{5,4},{6,5},{7,6},{8,7},{9,8},{10,9... | collective-permute-start | bytes 3145736 | tf_op jit(solution)/shard_map/ppermute | solution.py:17
  15.2 22.7 %collective-permute-start.2 = (bf16[2,256,1024]{2,1,0:T(8,128)(2,1)}, bf16[2,256,1024]{2,1,0:T(8,128)(2,1)S(1)}, u32[]{:S(2)}, u32[]{:S(2)}) collective-permute-start(bf16[2,256,1024]{2,1,0:T(8,128)(2,1)} %get-tuple-element.26), channel_id=1, source_target_pairs={{0,15},{1,0},{2,1},{3,2},{4,3},{5,4},{6,5},{7,6},{8,7},{9,8},{10,9... | collective-permute-start | bytes 3145736 | tf_op jit(solution)/shard_map/ppermute | solution.py:17
  34.9 2.1 %collective-permute-start.1 = (bf16[128,2048]{1,0:T(8,128)(2,1)S(1)}, bf16[128,2048]{1,0:T(8,128)(2,1)S(1)}, u32[]{:S(2)}, u32[]{:S(2)}) collective-permute-start(bf16[128,2048]{1,0:T(8,128)(2,1)S(1)} %get-tuple-element.23), channel_id=1, source_target_pairs={{0,1},{1,0},{2,3},{3,2},{4,5},{5,4},{6,7},{7,6},{8,9},{9,8},{10,11... | collective-permute-start | bytes 1572872 | tf_op jit(solution)/shard_map/ppermute | solution.py:17
  35.0 18.8 %collective-permute-start.5 = (bf16[2,256,1024]{2,1,0:T(8,128)(2,1)}, bf16[2,256,1024]{2,1,0:T(8,128)(2,1)S(1)}, u32[]{:S(2)}, u32[]{:S(2)}) collective-permute-start(bf16[2,256,1024]{2,1,0:T(8,128)(2,1)} %get-tuple-element.30), channel_id=1, source_target_pairs={{0,15},{1,0},{2,1},{3,2},{4,3},{5,4},{6,5},{7,6},{8,7},{9,8},{10,9... | collective-permute-start | bytes 3145736 | tf_op jit(solution)/shard_map/ppermute | solution.py:17
  37.9 21.6 %collective-permute-start.4 = (bf16[128,2048]{1,0:T(8,128)(2,1)}, bf16[128,2048]{1,0:T(8,128)(2,1)}, u32[]{:S(2)}, u32[]{:S(2)}) collective-permute-start(bf16[128,2048]{1,0:T(8,128)(2,1)} %add_convert_fusion.2), channel_id=1, source_target_pairs={{0,4},{1,5},{2,6},{3,7},{4,0},{5,1},{6,2},{7,3},{8,12},{9,13},{10,... | collective-permute-start | bytes 1572872 | tf_op jit(solution)/shard_map/ppermute | solution.py:17
  44.2 15.2 %collective-permute-start.3 = (bf16[128,2048]{1,0:T(8,128)(2,1)}, bf16[128,2048]{1,0:T(8,128)(2,1)}, u32[]{:S(2)}, u32[]{:S(2)}) collective-permute-start(bf16[128,2048]{1,0:T(8,128)(2,1)} %get-tuple-element.28), channel_id=1, source_target_pairs={{0,1},{1,0},{2,3},{3,2},{4,5},{5,4},{6,7},{7,6},{8,9},{9,8},{10,11... | collective-permute-start | bytes 1572872 | tf_op jit(solution)/shard_map/ppermute | solution.py:17
  44.4 32.4 %collective-permute-start.7 = (bf16[2,256,1024]{2,1,0:T(8,128)(2,1)}, bf16[2,256,1024]{2,1,0:T(8,128)(2,1)S(1)}, u32[]{:S(2)}, u32[]{:S(2)}) collective-permute-start(bf16[2,256,1024]{2,1,0:T(8,128)(2,1)} %get-tuple-element.34), channel_id=1, source_target_pairs={{0,15},{1,0},{2,1},{3,2},{4,3},{5,4},{6,5},{7,6},{8,7},{9,8},{10,9... | collective-permute-start | bytes 3145736 | tf_op jit(solution)/shard_map/ppermute | solution.py:17
  59.3 4.7 %collective-permute-start.6 = (bf16[128,2048]{1,0:T(8,128)(2,1)S(1)}, bf16[128,2048]{1,0:T(8,128)(2,1)S(1)}, u32[]{:S(2)}, u32[]{:S(2)}) collective-permute-start(bf16[128,2048]{1,0:T(8,128)(2,1)S(1)} %get-tuple-element.32), channel_id=1, source_target_pairs={{0,1},{1,0},{2,3},{3,2},{4,5},{5,4},{6,7},{7,6},{8,9},{9,8},{10,11... | collective-permute-start | bytes 1572872 | tf_op jit(solution)/shard_map/ppermute | solution.py:17
  61.7 26.8 %collective-permute-start.10 = (bf16[128,2048]{1,0:T(8,128)(2,1)}, bf16[128,2048]{1,0:T(8,128)(2,1)S(1)}, u32[]{:S(2)}, u32[]{:S(2)}) collective-permute-start(bf16[128,2048]{1,0:T(8,128)(2,1)} %add_convert_fusion.1), channel_id=1, source_target_pairs={{0,8},{1,9},{2,10},{3,11},{4,12},{5,13},{6,14},{7,15},{8,0},{9,1},... | collective-permute-start | bytes 1572872 | tf_op jit(solution)/shard_map/ppermute | solution.py:17
  65.0 28.2 %collective-permute-start.9 = (bf16[128,2048]{1,0:T(8,128)(2,1)}, bf16[128,2048]{1,0:T(8,128)(2,1)}, u32[]{:S(2)}, u32[]{:S(2)}) collective-permute-start(bf16[128,2048]{1,0:T(8,128)(2,1)} %add_convert_fusion), channel_id=1, source_target_pairs={{0,4},{1,5},{2,6},{3,7},{4,0},{5,1},{6,2},{7,3},{8,12},{9,13},{10,... | collective-permute-start | bytes 1572872 | tf_op jit(solution)/shard_map/ppermute | solution.py:17
  82.3 10.9 %collective-permute-start.8 = (bf16[128,2048]{1,0:T(8,128)(2,1)S(1)}, bf16[128,2048]{1,0:T(8,128)(2,1)}, u32[]{:S(2)}, u32[]{:S(2)}) collective-permute-start(bf16[128,2048]{1,0:T(8,128)(2,1)S(1)} %get-tuple-element.36), channel_id=1, source_target_pairs={{0,1},{1,0},{2,3},{3,2},{4,5},{5,4},{6,7},{7,6},{8,9},{9,8},{10,11... | collective-permute-start | bytes 1572872 | tf_op jit(solution)/shard_map/ppermute | solution.py:17
  94.7 6.4 %collective-permute-start.11 = (bf16[64,2048]{1,0:T(8,128)(2,1)S(1)}, bf16[64,2048]{1,0:T(8,128)(2,1)S(1)}, u32[]{:S(2)}, u32[]{:S(2)}) collective-permute-start(bf16[64,2048]{1,0:T(8,128)(2,1)S(1)} %fusion.1), channel_id=1, source_target_pairs={{0,2},{1,3},{2,0},{3,1},{4,6},{5,7},{6,4},{7,5},{8,10},{9,11},{10,... | collective-permute-start | bytes 786440 | tf_op jit(solution)/shard_map/ppermute | solution.py:17

commit v5 on v4

--- a/solution.py
+++ b/solution.py
@@ -111,12 +111,12 @@
     )(band_first, coeffs, g_cond, g_val)
 
 
-def turn_kernel(blocks_ref, coeffs_ref, *refs):
+def turn_kernel(first, order_ref, coeffs_ref, *refs):
     *out_refs, held, sems = refs
     pieces, k_local, parts, rows, width = held.shape
 
     def copy(i, k, p):
-        columns = pl.ds(pl.multiple_of(blocks_ref[i] * width, width), width)
+        columns = pl.ds(pl.multiple_of(order_ref[first + i] * width, width), width)
         source = coeffs_ref.at[k, pl.ds(p * rows, rows), columns]
         return pltpu.make_async_copy(source, held.at[i, k, p], sems.at[i, k, p])
 
@@ -129,11 +129,11 @@
         out_refs[i][k, :, p * rows:(p + 1) * rows] = held[i, k, p].T
 
 
-def turned_pieces(flat, blocks, width):
+def turned_pieces(flat, order, first, pieces, width):
     k_local, depth, _ = flat.shape
-    pieces, parts = blocks.shape[0], 2
+    parts = 2
     return pl.pallas_call(
-        turn_kernel,
+        functools.partial(turn_kernel, first),
         out_shape=[jax.ShapeDtypeStruct((k_local, width, depth), jnp.bfloat16)] * pieces,
         in_specs=[
             pl.BlockSpec(memory_space=pltpu.SMEM),
@@ -148,15 +148,15 @@
         cost_estimate=pl.CostEstimate(
             flops=0, bytes_accessed=4 * pieces * k_local * depth * width, transcendentals=0
         ),
-    )(blocks, flat)
-
-
-def rows_kernel(pick_ref, own_ref, next_ref, right_ref, keep_ref, send_ref, *refs):
+    )(order, flat)
+
+
+def rows_kernel(pick_ref, own_ref, next_ref, right_ref, mine_ref, other_ref, send_ref, *refs):
     own_held, next_held, held, left, own_sems, next_sems, sems = refs
     k_local, depth, width = own_held.shape
     tiles, _, _, tile = held.shape
     per_mode = right_ref.shape[3] // tile
-    core = pick_ref[k_local + 1]
+    core, x = pick_ref[k_local + 1], pick_ref[k_local + 2]
     columns = pl.ds(pl.multiple_of(pick_ref[k_local] * width, width), width)
     near = [pick_ref[k] < k_local for k in range(k_local)]
 
@@ -196,11 +196,13 @@
         right = held[t].reshape(k_local * depth, tile)
         total = jnp.dot(left[...], right, preferred_element_type=jnp.float32)
         parts = total.reshape(2, 2, width // 4, tile)
-        low = parts[:, 0].reshape(width // 2, tile)
-        high = parts[:, 1].reshape(width // 2, tile)
+        mine = jnp.where(x == 0, parts[0], parts[1])
+        other = jnp.where(x == 0, parts[1], parts[0])
         place = slice(t * tile, (t + 1) * tile)
-        keep_ref[:, place] = jnp.where(core == 0, low, high)
-        send_ref[:, place] = jnp.where(core == 0, high, low).astype(jnp.bfloat16)
+        mine_ref[:, place] = jnp.where(core == 0, mine[0], mine[1])
+        other_ref[:, place] = jnp.where(core == 0, other[0], other[1])
+        send_ref[:width // 4, place] = jnp.where(core == 0, mine[1], mine[0]).astype(jnp.bfloat16)
+        send_ref[width // 4:, place] = jnp.where(core == 0, other[1], other[0]).astype(jnp.bfloat16)
 
 
 def rows_of(pick, own, following, products):
@@ -211,12 +213,13 @@
     return pl.pallas_call(
         rows_kernel,
         out_shape=[
-            jax.ShapeDtypeStruct((width // 2, columns), jnp.float32),
+            jax.ShapeDtypeStruct((width // 4, columns), jnp.float32),
+            jax.ShapeDtypeStruct((width // 4, columns), jnp.float32),
             jax.ShapeDtypeStruct((width // 2, columns), jnp.bfloat16),
         ],
         in_specs=[pl.BlockSpec(memory_space=pltpu.SMEM)]
         + [pl.BlockSpec(memory_space=pl.ANY)] * 3,
-        out_specs=[pl.BlockSpec(memory_space=pltpu.VMEM)] * 2,
+        out_specs=[pl.BlockSpec(memory_space=pltpu.VMEM)] * 3,
         scratch_shapes=[
             pltpu.VMEM((k_local, depth, width), jnp.bfloat16),
             pltpu.VMEM((k_local, width, depth), jnp.bfloat16),
@@ -246,35 +249,44 @@
 
     behind_z = (me + size - 1) % size >> 2
     order = behind_z ^ jnp.arange(3, -1, -1, dtype=jnp.int32)
-    pieces = turned_pieces(flat, order[:1], width)
-    others, _ = lax.optimization_barrier((order[1:], pieces))
-    pieces += turned_pieces(flat, others, width)
+    pieces = turned_pieces(flat, order, 0, 1, width)
+    order, _ = lax.optimization_barrier((order, pieces))
+    pieces += turned_pieces(flat, order, 1, 3, width)
     following = [permute(piece, lambda i: i - 1) for piece in pieces]
     products = products_of(coeffs, g_cond, g_val, band_first)
     products = products.reshape(k_local, modes, bands_c * bands_v, excitons)
     places = jnp.mod(k_plus_q - me * k_local, k_local * size)
-    picks = [jnp.concatenate((places, jnp.stack((z ^ (3 - step), core)))) for step in range(4)]
 
     def rows(step, after):
-        pick, _ = lax.optimization_barrier((picks[step], after))
-        keep, send = rows_of(pick, flat, following[step], products)
-        return keep, permute(send, lambda i: i ^ 1).astype(jnp.float32)
-
-    keep, other = rows(0, products)
-    send_far = (keep + other).astype(jnp.bfloat16)
-    far = permute(send_far, lambda i: i ^ 4)
-    keep_1, other_1 = rows(1, send_far)
-    keep, other = rows(2, keep_1)
-    send_pair = (keep_1 + other_1 + far.astype(jnp.float32)).astype(jnp.bfloat16)
-    pair = permute(send_pair, lambda i: i ^ 8)
-    send_near = (keep + other).astype(jnp.bfloat16)
-    near = permute(send_near, lambda i: i ^ 4)
-    keep, other = rows(3, (send_pair, send_near))
-    total = keep + other + near.astype(jnp.float32) + pair.astype(jnp.float32)
-    total = total.reshape(2, width // 4, modes * excitons)
-    mine = lax.dynamic_index_in_dim(total, x, 0, keepdims=False)
-    sent = lax.dynamic_index_in_dim(total, 1 - x, 0, keepdims=False).astype(jnp.bfloat16)
-    total = mine + permute(sent, lambda i: i ^ 2).astype(jnp.float32)
+        pick = jnp.concatenate((places, jnp.stack((z ^ (3 - step), core, x))))
+        pick, _ = lax.optimization_barrier((pick, after))
+        mine, other, send = rows_of(pick, flat, following[step], products)
+        return mine, other, permute(send, lambda i: i ^ 1)
+
+    def for_x(step, from_core):
+        return (step[1] + from_core[width // 4:].astype(jnp.float32)).astype(jnp.bfloat16)
+
+    steps = [rows(0, products)]
+    for step in (1, 2):
+        steps.append(rows(step, steps[-1][0]))
+    from_cores = [step[2] for step in steps]
+    from_cores, following[3] = lax.optimization_barrier((from_cores, following[3]))
+    sends = [for_x(*both) for both in zip(steps, from_cores)]
+    steps.append(rows(3, sends))
+    from_cores.append(steps[3][2])
+    sends.append(for_x(steps[3], from_cores[3]))
+
+    def summed(step):
+        from_x = permute(sends[step], lambda i: i ^ 2).astype(jnp.float32)
+        return steps[step][0] + from_cores[step][:width // 4].astype(jnp.float32) + from_x
+
+    def over(value, bit):
+        return permute(value.astype(jnp.bfloat16), lambda i: i ^ bit).astype(jnp.float32)
+
+    far = over(summed(0), 4)
+    pair = over(summed(1) + far, 8)
+    near = over(summed(2), 4)
+    total = summed(3) + near + pair
     return (total * norm_factor).reshape(width // 4, modes, excitons)
 
 

time: 104 us -> 91.3 us (0.88); the launches traced: 102 us -> 90.9 us
  waiting for transfers between devices: 36.6 us -> 28.3 us
  other arithmetic: 6.26 us -> 1.34 us
  Pallas kernels: 43.9 us -> 45.5 us
  starting transfers between devices: 13 us -> 14.4 us
  local copies, waits for them, and re-layouts: 2.59 us -> 1.24 us
    ppermute x12 -> x15, waiting for transfers between devices: 36.6 us -> 28.3 us  [permute(): lax.ppermute(x, 'ka', [(i, j % size) for i, j in pairs if j is not None])]
    convert_element_type x3 -> x7, other arithmetic: 4.04 us -> 0.49 us  [the longest x3 0.3 us: over(): value.astype(jnp.bfloat16)]
    pallas_call x6, Pallas kernels: 30.6 us -> 32.1 us  [the longest x4 24 us: rows_of(): pl.pallas_call(rows_kernel, out_shape=[jax.ShapeDtypeStruct((width // 4,...]
    add x1 -> x0, other arithmetic: 1.48 us -> none  [on_two_by_four(): total = keep + other + near.astype(jnp.float32) + pair.astype(jnp.float32)]
    ppermute x12 -> x15, starting transfers between devices: 13 us -> 14.4 us  [permute(): lax.ppermute(x, 'ka', [(i, j % size) for i, j in pairs if j is not None])]
    slice x1 -> x0, local copies, waits for them, and re-layouts: 1.31 us -> none  [on_two_by_four(): others, _ = lax.optimization_barrier((order[1:], pieces))]
  transfers between devices with their start and end apart: 12 -> 15, of which waited for: 7 -> 6; matrix products, arithmetic and copies ran while one was open for 5% -> 1% of each run, Pallas kernels for 40% -> 46%
where the time goes in v5:
time: 91.3 us; the launch traced here: 90.9 us
  Pallas kernels  45.5 us (50%)
  waiting for transfers between devices  28.3 us (31%)
  starting transfers between devices  14.4 us (16%)
  other arithmetic  1.34 us (1%)
  local copies, waits for them, and re-layouts  1.24 us (1%)
    ppermute x15, waiting for transfers between devices, permute(): lax.ppermute(x, 'ka', [(i, j % size) for i, j in pairs if j is not None])  28.3 us
    pallas_call x4, Pallas kernels, rows_of(): pl.pallas_call(rows_kernel, out_shape=[jax.ShapeDtypeStruct((width // 4,...  24 us
    ppermute x15, starting transfers between devices, permute(): lax.ppermute(x, 'ka', [(i, j % size) for i, j in pairs if j is not None])  14.4 us
    pallas_call x1, Pallas kernels, products_of(): pl.pallas_call(products_kernel, out_shape=jax.ShapeDtypeStruct((k_local,...  13.4 us
    pallas_call x2, Pallas kernels, turned_pieces(): pl.pallas_call(functools.partial(turn_kernel, first), out_shape=[jax.Shap...  8.1 us
  transfers between devices with their start and end apart: 15, of which 6 were waited for; matrix products, arithmetic and copies ran while one was open for 1% of the time, Pallas kernels for 46%

profile of v5, /device:TPU:0, one launch (start us, length us, event | category | flops | bytes accessed | tf_op | source)
XLA Modules:
  0.0 90.9 jit_solution(1175199852759360506)
XLA Ops:
  0.0 0.0 copy-start
  0.0 0.5 add_xor_fusion.order_ref
  0.5 3.2 %shard_map.56 = bf16[2,256,1024]{2,1,0:T(8,128)(2,1)} custom-call(s32[4]{0:T(128)} %add_xor_fusion.order_ref, bf16[2,1024,1024]{2,1,0:T(8,128)(2,1)} %bitcast.8), custom_call_target="tpu_custom_call" | custom-call | bytes 2097152 | tf_op jit(solution)/shard_map/pallas_call | solution.py:135
  3.7 5.5 %collective-permute-start = (bf16[2,256,1024]{2,1,0:T(8,128)(2,1)}, bf16[2,256,1024]{2,1,0:T(8,128)(2,1)}, u32[]{:S(2)}, u32[]{:S(2)}) collective-permute-start(bf16[2,256,1024]{2,1,0:T(8,128)(2,1)} %shard_map.56), channel_id=1, source_target_pairs={{0,15},{1,0},{2,1},{3,2},{4,3},{5,4},{6,5},{7,6},{8,7},{9,8},{10,9... | collective-permute-start | bytes 3145736 | tf_op jit(solution)/shard_map/ppermute | solution.py:17
  9.2 4.9 %shard_map.58 = (bf16[2,256,1024]{2,1,0:T(8,128)(2,1)}, bf16[2,256,1024]{2,1,0:T(8,128)(2,1)}, bf16[2,256,1024]{2,1,0:T(8,128)(2,1)}) custom-call(s32[4]{0:T(128)} %add_xor_fusion.order_ref, bf16[2,1024,1024]{2,1,0:T(8,128)(2,1)} %bitcast.9), custom_call_target="tpu_custom_call" | custom-call | bytes 6291456 | tf_op jit(solution)/shard_map/pallas_call | solution.py:135
  14.1 0.7 collective-permute-start.2
  14.8 0.1 collective-permute-start.4
  14.9 0.6 collective-permute-start.6
  15.5 0.0 copy-done
  15.5 0.1 add_add_fusion
  15.6 13.4 %shard_map.55 = bf16[2,2,32,32,1024]{4,3,2,1,0:T(8,128)(2,1)} custom-call(s32[2,2]{1,0:T(2,128)} %first_ref.1, bf16[2,32,32,1024]{3,2,1,0:T(8,128)(2,1)} %coeffs_ref.1, bf16[2,2,32,32]{3,2,1,0:T(8,128)(2,1)} %cond_ref.1, bf16[2,2,32,32]{3,2,1,0:T(8,128)(2,1)} %val_ref.1), custom_call_target="tpu_custom_call" | custom-call | flops 6442450944 | bytes 12582912 | tf_op jit(solution)/shard_map/pallas_call | solution.py:90
  29.0 0.1 add_add_fusion.3
  29.0 0.0 collective-permute-done.next_ref
  29.0 7.5 %shard_map.57 = (f32[64,2048]{1,0:T(8,128)S(1)}, f32[64,2048]{1,0:T(8,128)S(1)}, bf16[128,2048]{1,0:T(8,128)(2,1)S(1)}) custom-call(s32[5]{0:T(128)S(1)} %get-tuple-element.29.pick_ref, bf16[2,1024,1024]{2,1,0:T(8,128)(2,1)} %bitcast.10, bf16[2,256,1024]{2,1,0:T(8,128)(2,1)} %collective-permute-done.next_ref, bf16[2,2,1024,1024]{3,2,1,0:T(8,128)(2,1)} %bitcast.14), custom_call_target="tpu_custom_call" | custom-call | flops 2147483648 | bytes 8388608 | tf_op jit(solution)/shard_map/pallas_call | solution.py:213
  36.5 0.0 collective-permute-done.2.next_ref
  36.5 5.5 %shard_map.59 = (f32[64,2048]{1,0:T(8,128)S(1)}, f32[64,2048]{1,0:T(8,128)S(1)}, bf16[128,2048]{1,0:T(8,128)(2,1)S(1)}) custom-call(s32[5]{0:T(128)S(1)} %get-tuple-element.33.pick_ref, bf16[2,1024,1024]{2,1,0:T(8,128)(2,1)} %bitcast.11, bf16[2,256,1024]{2,1,0:T(8,128)(2,1)S(1)} %collective-permute-done.2.next_ref, bf16[2,2,1024,1024]{3,2,1,0:T(8,128)(2,1)} %bitcast.15), custom_call_target="tpu_custom_call" | custom-call | flops 2147483648 | bytes 8388608 | tf_op jit(solution)/shard_map/pallas_call | solution.py:213
  42.1 2.2 %collective-permute-done.4.next_ref = bf16[2,256,1024]{2,1,0:T(8,128)(2,1)S(1)} collective-permute-done((bf16[2,256,1024]{2,1,0:T(8,128)(2,1)}, bf16[2,256,1024]{2,1,0:T(8,128)(2,1)S(1)}, u32[]{:S(2)}, u32[]{:S(2)}) %collective-permute-start.4) | collective-permute-done | bytes 1048608 | tf_op jit(solution)/shard_map/ppermute | solution.py:17
  44.3 5.5 %shard_map.60 = (f32[64,2048]{1,0:T(8,128)S(1)}, f32[64,2048]{1,0:T(8,128)S(1)}, bf16[128,2048]{1,0:T(8,128)(2,1)S(1)}) custom-call(s32[5]{0:T(128)S(1)} %get-tuple-element.38.pick_ref, bf16[2,1024,1024]{2,1,0:T(8,128)(2,1)} %bitcast.12, bf16[2,256,1024]{2,1,0:T(8,128)(2,1)S(1)} %collective-permute-done.4.next_ref, bf16[2,2,1024,1024]{3,2,1,0:T(8,128)(2,1)} %bitcast.16), custom_call_target="tpu_custom_call" | custom-call | flops 2147483648 | bytes 8388608 | tf_op jit(solution)/shard_map/pallas_call | solution.py:213
  49.8 0.1 collective-permute-start.5
  49.9 0.5 collective-permute-start.3
  50.4 0.1 collective-permute-start.1
  50.5 5.1 %collective-permute-done.6.next_ref = bf16[2,256,1024]{2,1,0:T(8,128)(2,1)S(1)} collective-permute-done((bf16[2,256,1024]{2,1,0:T(8,128)(2,1)}, bf16[2,256,1024]{2,1,0:T(8,128)(2,1)S(1)}, u32[]{:S(2)}, u32[]{:S(2)}) %collective-permute-start.6) | collective-permute-done | bytes 1048608 | tf_op jit(solution)/shard_map/ppermute | solution.py:17
  55.5 0.0 collective-permute-done.5
  55.6 0.0 collective-permute-done.3
  55.6 0.0 collective-permute-done.1
  55.6 0.1 collective-permute-start.12
  55.8 2.1 %collective-permute-start.11 = (bf16[64,2048]{1,0:T(8,128)(2,1)S(1)}, bf16[64,2048]{1,0:T(8,128)(2,1)S(1)}, u32[]{:S(2)}, u32[]{:S(2)}) collective-permute-start(bf16[64,2048]{1,0:T(8,128)(2,1)S(1)} %add_convert_fusion.5), channel_id=1, source_target_pairs={{0,2},{1,3},{2,0},{3,1},{4,6},{5,7},{6,4},{7,5},{8,10},{9,11},{10,... | collective-permute-start | bytes 786440 | tf_op jit(solution)/shard_map/ppermute | solution.py:17
  57.9 0.1 collective-permute-start.9
  58.0 5.5 %shard_map.61 = (f32[64,2048]{1,0:T(8,128)S(1)}, f32[64,2048]{1,0:T(8,128)S(1)}, bf16[128,2048]{1,0:T(8,128)(2,1)S(1)}) custom-call(s32[5]{0:T(128)S(1)} %get-tuple-element.47.pick_ref, bf16[2,1024,1024]{2,1,0:T(8,128)(2,1)} %bitcast.13, bf16[2,256,1024]{2,1,0:T(8,128)(2,1)S(1)} %collective-permute-done.6.next_ref, bf16[2,2,1024,1024]{3,2,1,0:T(8,128)(2,1)} %bitcast.17), custom_call_target="tpu_custom_call" | custom-call | flops 2147483648 | bytes 8388608 | tf_op jit(solution)/shard_map/pallas_call | solution.py:213
  63.4 0.1 collective-permute-start.7
  63.5 1.4 %collective-permute-done.12 = bf16[64,2048]{1,0:T(8,128)(2,1)S(1)} collective-permute-done((bf16[64,2048]{1,0:T(8,128)(2,1)S(1)}, bf16[64,2048]{1,0:T(8,128)(2,1)S(1)}, u32[]{:S(2)}, u32[]{:S(2)}) %collective-permute-start.12) | collective-permute-done | bytes 262176 | tf_op jit(solution)/shard_map/ppermute | solution.py:17
  64.9 0.1 add_convert_fusion.1
  65.0 0.1 collective-permute-start.13
  65.1 8.3 %collective-permute-done.9 = bf16[64,2048]{1,0:T(8,128)(2,1)S(1)} collective-permute-done((bf16[64,2048]{1,0:T(8,128)(2,1)S(1)}, bf16[64,2048]{1,0:T(8,128)(2,1)S(1)}, u32[]{:S(2)}, u32[]{:S(2)}) %collective-permute-start.9) | collective-permute-done | bytes 262176 | tf_op jit(solution)/shard_map/ppermute | solution.py:17
  73.4 0.1 add_convert_fusion.2
  73.5 0.7 collective-permute-start.10
  74.2 0.0 collective-permute-done.11
  74.2 0.0 collective-permute-done.13
  74.2 0.1 add_convert_fusion
  74.4 1.5 %collective-permute-start.14 = (bf16[64,2048]{1,0:T(8,128)(2,1)S(1)}, bf16[64,2048]{1,0:T(8,128)(2,1)S(1)}, u32[]{:S(2)}, u32[]{:S(2)}) collective-permute-start(bf16[64,2048]{1,0:T(8,128)(2,1)S(1)} %add_convert_fusion), channel_id=1, source_target_pairs={{0,8},{1,9},{2,10},{3,11},{4,12},{5,13},{6,14},{7,15},{8,0},{9,1},... | collective-permute-start | bytes 786440 | tf_op jit(solution)/shard_map/ppermute | solution.py:17
  75.9 0.0 collective-permute-done.7
  75.9 2.4 %collective-permute-start.8 = (bf16[64,2048]{1,0:T(8,128)(2,1)S(1)}, bf16[64,2048]{1,0:T(8,128)(2,1)S(1)}, u32[]{:S(2)}, u32[]{:S(2)}) collective-permute-start(bf16[64,2048]{1,0:T(8,128)(2,1)S(1)} %add_convert_fusion.3), channel_id=1, source_target_pairs={{0,2},{1,3},{2,0},{3,1},{4,6},{5,7},{6,4},{7,5},{8,10},{9,11},{10,... | collective-permute-start | bytes 786440 | tf_op jit(solution)/shard_map/ppermute | solution.py:17
  78.3 7.9 %collective-permute-done.10 = bf16[64,2048]{1,0:T(8,128)(2,1)S(1)} collective-permute-done((bf16[64,2048]{1,0:T(8,128)(2,1)S(1)}, bf16[64,2048]{1,0:T(8,128)(2,1)S(1)}, u32[]{:S(2)}, u32[]{:S(2)}) %collective-permute-start.10) | collective-permute-done | bytes 262176 | tf_op jit(solution)/shard_map/ppermute | solution.py:17
  86.2 3.4 %collective-permute-done.14 = bf16[64,2048]{1,0:T(8,128)(2,1)S(1)} collective-permute-done((bf16[64,2048]{1,0:T(8,128)(2,1)S(1)}, bf16[64,2048]{1,0:T(8,128)(2,1)S(1)}, u32[]{:S(2)}, u32[]{:S(2)}) %collective-permute-start.14) | collective-permute-done | bytes 262176 | tf_op jit(solution)/shard_map/ppermute | solution.py:17
  89.5 0.0 collective-permute-done.8
  89.5 0.2 add_multiply_fusion
  89.7 1.2 %reshape.11 = f32[64,2,1024]{2,1,0:T(2,128)} reshape(f32[64,2048]{1,0:T(8,128)S(1)} %add_multiply_fusion) | data formatting | bytes 1048576 | tf_op jit(solution)/shard_map/reshape | solution.py:290
  (5 shorter events, 0.2 us)
Async XLA Ops:
  0.0 15.5 %copy-start = (s32[2]{0:T(128)S(1)}, s32[2]{0:T(128)}, u32[]{:S(2)}) copy-start(s32[2]{0:T(128)} %param.8) | copy-start | bytes 28
  3.7 25.3 %collective-permute-start = (bf16[2,256,1024]{2,1,0:T(8,128)(2,1)}, bf16[2,256,1024]{2,1,0:T(8,128)(2,1)}, u32[]{:S(2)}, u32[]{:S(2)}) collective-permute-start(bf16[2,256,1024]{2,1,0:T(8,128)(2,1)} %shard_map.56), channel_id=1, source_target_pairs={{0,15},{1,0},{2,1},{3,2},{4,3},{5,4},{6,5},{7,6},{8,7},{9,8},{10,9... | collective-permute-start | bytes 3145736 | tf_op jit(solution)/shard_map/ppermute | solution.py:17
  14.1 22.4 %collective-permute-start.2 = (bf16[2,256,1024]{2,1,0:T(8,128)(2,1)}, bf16[2,256,1024]{2,1,0:T(8,128)(2,1)S(1)}, u32[]{:S(2)}, u32[]{:S(2)}) collective-permute-start(bf16[2,256,1024]{2,1,0:T(8,128)(2,1)} %get-tuple-element.35), channel_id=1, source_target_pairs={{0,15},{1,0},{2,1},{3,2},{4,3},{5,4},{6,5},{7,6},{8,7},{9,8},{10,9... | collective-permute-start | bytes 3145736 | tf_op jit(solution)/shard_map/ppermute | solution.py:17
  14.8 29.5 %collective-permute-start.4 = (bf16[2,256,1024]{2,1,0:T(8,128)(2,1)}, bf16[2,256,1024]{2,1,0:T(8,128)(2,1)S(1)}, u32[]{:S(2)}, u32[]{:S(2)}) collective-permute-start(bf16[2,256,1024]{2,1,0:T(8,128)(2,1)} %get-tuple-element.39), channel_id=1, source_target_pairs={{0,15},{1,0},{2,1},{3,2},{4,3},{5,4},{6,5},{7,6},{8,7},{9,8},{10,9... | collective-permute-start | bytes 3145736 | tf_op jit(solution)/shard_map/ppermute | solution.py:17
  14.9 40.6 %collective-permute-start.6 = (bf16[2,256,1024]{2,1,0:T(8,128)(2,1)}, bf16[2,256,1024]{2,1,0:T(8,128)(2,1)S(1)}, u32[]{:S(2)}, u32[]{:S(2)}) collective-permute-start(bf16[2,256,1024]{2,1,0:T(8,128)(2,1)} %get-tuple-element.41), channel_id=1, source_target_pairs={{0,15},{1,0},{2,1},{3,2},{4,3},{5,4},{6,5},{7,6},{8,7},{9,8},{10,9... | collective-permute-start | bytes 3145736 | tf_op jit(solution)/shard_map/ppermute | solution.py:17
  49.8 5.7 %collective-permute-start.5 = (bf16[128,2048]{1,0:T(8,128)(2,1)S(1)}, bf16[128,2048]{1,0:T(8,128)(2,1)S(1)}, u32[]{:S(2)}, u32[]{:S(2)}) collective-permute-start(bf16[128,2048]{1,0:T(8,128)(2,1)S(1)} %get-tuple-element.40), channel_id=1, source_target_pairs={{0,1},{1,0},{2,3},{3,2},{4,5},{5,4},{6,7},{7,6},{8,9},{9,8},{10,11... | collective-permute-start | bytes 1572872 | tf_op jit(solution)/shard_map/ppermute | solution.py:17
  49.9 5.7 %collective-permute-start.3 = (bf16[128,2048]{1,0:T(8,128)(2,1)S(1)}, bf16[128,2048]{1,0:T(8,128)(2,1)S(1)}, u32[]{:S(2)}, u32[]{:S(2)}) collective-permute-start(bf16[128,2048]{1,0:T(8,128)(2,1)S(1)} %get-tuple-element.36), channel_id=1, source_target_pairs={{0,1},{1,0},{2,3},{3,2},{4,5},{5,4},{6,7},{7,6},{8,9},{9,8},{10,11... | collective-permute-start | bytes 1572872 | tf_op jit(solution)/shard_map/ppermute | solution.py:17
  50.4 5.2 %collective-permute-start.1 = (bf16[128,2048]{1,0:T(8,128)(2,1)S(1)}, bf16[128,2048]{1,0:T(8,128)(2,1)S(1)}, u32[]{:S(2)}, u32[]{:S(2)}) collective-permute-start(bf16[128,2048]{1,0:T(8,128)(2,1)S(1)} %get-tuple-element.31), channel_id=1, source_target_pairs={{0,1},{1,0},{2,3},{3,2},{4,5},{5,4},{6,7},{7,6},{8,9},{9,8},{10,11... | collective-permute-start | bytes 1572872 | tf_op jit(solution)/shard_map/ppermute | solution.py:17
  55.6 9.3 %collective-permute-start.12 = (bf16[64,2048]{1,0:T(8,128)(2,1)S(1)}, bf16[64,2048]{1,0:T(8,128)(2,1)S(1)}, u32[]{:S(2)}, u32[]{:S(2)}) collective-permute-start(bf16[64,2048]{1,0:T(8,128)(2,1)S(1)} %add_convert_fusion.6), channel_id=1, source_target_pairs={{0,2},{1,3},{2,0},{3,1},{4,6},{5,7},{6,4},{7,5},{8,10},{9,11},{10,... | collective-permute-start | bytes 786440 | tf_op jit(solution)/shard_map/ppermute | solution.py:17
  55.8 18.5 %collective-permute-start.11 = (bf16[64,2048]{1,0:T(8,128)(2,1)S(1)}, bf16[64,2048]{1,0:T(8,128)(2,1)S(1)}, u32[]{:S(2)}, u32[]{:S(2)}) collective-permute-start(bf16[64,2048]{1,0:T(8,128)(2,1)S(1)} %add_convert_fusion.5), channel_id=1, source_target_pairs={{0,2},{1,3},{2,0},{3,1},{4,6},{5,7},{6,4},{7,5},{8,10},{9,11},{10,... | collective-permute-start | bytes 786440 | tf_op jit(solution)/shard_map/ppermute | solution.py:17
  57.9 15.6 %collective-permute-start.9 = (bf16[64,2048]{1,0:T(8,128)(2,1)S(1)}, bf16[64,2048]{1,0:T(8,128)(2,1)S(1)}, u32[]{:S(2)}, u32[]{:S(2)}) collective-permute-start(bf16[64,2048]{1,0:T(8,128)(2,1)S(1)} %add_convert_fusion.4), channel_id=1, source_target_pairs={{0,2},{1,3},{2,0},{3,1},{4,6},{5,7},{6,4},{7,5},{8,10},{9,11},{10,... | collective-permute-start | bytes 786440 | tf_op jit(solution)/shard_map/ppermute | solution.py:17
  63.4 12.4 %collective-permute-start.7 = (bf16[128,2048]{1,0:T(8,128)(2,1)S(1)}, bf16[128,2048]{1,0:T(8,128)(2,1)S(1)}, u32[]{:S(2)}, u32[]{:S(2)}) collective-permute-start(bf16[128,2048]{1,0:T(8,128)(2,1)S(1)} %get-tuple-element.50), channel_id=1, source_target_pairs={{0,1},{1,0},{2,3},{3,2},{4,5},{5,4},{6,7},{7,6},{8,9},{9,8},{10,11... | collective-permute-start | bytes 1572872 | tf_op jit(solution)/shard_map/ppermute | solution.py:17
  65.0 9.2 %collective-permute-start.13 = (bf16[64,2048]{1,0:T(8,128)(2,1)S(1)}, bf16[64,2048]{1,0:T(8,128)(2,1)S(1)}, u32[]{:S(2)}, u32[]{:S(2)}) collective-permute-start(bf16[64,2048]{1,0:T(8,128)(2,1)S(1)} %add_convert_fusion.1), channel_id=1, source_target_pairs={{0,4},{1,5},{2,6},{3,7},{4,0},{5,1},{6,2},{7,3},{8,12},{9,13},{10,... | collective-permute-start | bytes 786440 | tf_op jit(solution)/shard_map/ppermute | solution.py:17
  73.5 12.6 %collective-permute-start.10 = (bf16[64,2048]{1,0:T(8,128)(2,1)S(1)}, bf16[64,2048]{1,0:T(8,128)(2,1)S(1)}, u32[]{:S(2)}, u32[]{:S(2)}) collective-permute-start(bf16[64,2048]{1,0:T(8,128)(2,1)S(1)} %add_convert_fusion.2), channel_id=1, source_target_pairs={{0,4},{1,5},{2,6},{3,7},{4,0},{5,1},{6,2},{7,3},{8,12},{9,13},{10,... | collective-permute-start | bytes 786440 | tf_op jit(solution)/shard_map/ppermute | solution.py:17
  74.4 15.1 %collective-permute-start.14 = (bf16[64,2048]{1,0:T(8,128)(2,1)S(1)}, bf16[64,2048]{1,0:T(8,128)(2,1)S(1)}, u32[]{:S(2)}, u32[]{:S(2)}) collective-permute-start(bf16[64,2048]{1,0:T(8,128)(2,1)S(1)} %add_convert_fusion), channel_id=1, source_target_pairs={{0,8},{1,9},{2,10},{3,11},{4,12},{5,13},{6,14},{7,15},{8,0},{9,1},... | collective-permute-start | bytes 786440 | tf_op jit(solution)/shard_map/ppermute | solution.py:17
  75.9 13.6 %collective-permute-start.8 = (bf16[64,2048]{1,0:T(8,128)(2,1)S(1)}, bf16[64,2048]{1,0:T(8,128)(2,1)S(1)}, u32[]{:S(2)}, u32[]{:S(2)}) collective-permute-start(bf16[64,2048]{1,0:T(8,128)(2,1)S(1)} %add_convert_fusion.3), channel_id=1, source_target_pairs={{0,2},{1,3},{2,0},{3,1},{4,6},{5,7},{6,4},{7,5},{8,10},{9,11},{10,... | collective-permute-start | bytes 786440 | tf_op jit(solution)/shard_map/ppermute | solution.py:17

commit v6 on v5

--- a/solution.py
+++ b/solution.py
@@ -266,27 +266,34 @@
     def for_x(step, from_core):
         return (step[1] + from_core[width // 4:].astype(jnp.float32)).astype(jnp.bfloat16)
 
-    steps = [rows(0, products)]
-    for step in (1, 2):
-        steps.append(rows(step, steps[-1][0]))
-    from_cores = [step[2] for step in steps]
-    from_cores, following[3] = lax.optimization_barrier((from_cores, following[3]))
-    sends = [for_x(*both) for both in zip(steps, from_cores)]
-    steps.append(rows(3, sends))
-    from_cores.append(steps[3][2])
-    sends.append(for_x(steps[3], from_cores[3]))
-
-    def summed(step):
-        from_x = permute(sends[step], lambda i: i ^ 2).astype(jnp.float32)
-        return steps[step][0] + from_cores[step][:width // 4].astype(jnp.float32) + from_x
+    def from_x(send):
+        return permute(send, lambda i: i ^ 2).astype(jnp.float32)
+
+    def own_sum(step, from_core, across):
+        return step[0] + from_core[:width // 4].astype(jnp.float32) + across
 
     def over(value, bit):
-        return permute(value.astype(jnp.bfloat16), lambda i: i ^ bit).astype(jnp.float32)
-
-    far = over(summed(0), 4)
-    pair = over(summed(1) + far, 8)
-    near = over(summed(2), 4)
-    total = summed(3) + near + pair
+        return permute(value, lambda i: i ^ bit).astype(jnp.float32)
+
+    step_0 = rows(0, products)
+    step_1 = rows(1, step_0[0])
+    core_0, following[2], _ = lax.optimization_barrier((step_0[2], following[2], step_1[0]))
+    send_0 = for_x(step_0, core_0)
+    across_0 = from_x(send_0)
+    step_2 = rows(2, (step_1[0], send_0))
+    core_1, core_2, following[3] = lax.optimization_barrier((step_1[2], step_2[2], following[3]))
+    send_1, send_2 = for_x(step_1, core_1), for_x(step_2, core_2)
+    across_1, across_2 = from_x(send_1), from_x(send_2)
+    far = own_sum(step_0, core_0, across_0).astype(jnp.bfloat16)
+    step_3 = rows(3, (send_1, send_2, far))
+    far = over(far, 4)
+    pair = (own_sum(step_1, core_1, across_1) + far).astype(jnp.bfloat16)
+    send_3 = for_x(step_3, step_3[2])
+    across_2, _ = lax.optimization_barrier((across_2, (pair, send_3)))
+    pair = over(pair, 8)
+    near = over(own_sum(step_2, core_2, across_2).astype(jnp.bfloat16), 4)
+    across_3 = from_x(send_3)
+    total = own_sum(step_3, step_3[2], across_3) + near + pair
     return (total * norm_factor).reshape(width // 4, modes, excitons)
 
 

time: 91.3 us -> 93.8 us (1.027)
  starting transfers between devices: 14.4 us -> 17.7 us
  waiting for transfers between devices: 28.3 us -> 25.2 us
  other arithmetic: 1.34 us -> 3.32 us
  local copies, waits for them, and re-layouts: 1.24 us -> 2.87 us
  Pallas kernels: 45.5 us -> 44.1 us
    ppermute x15, starting transfers between devices: 14.4 us -> 17.7 us  [permute(): lax.ppermute(x, 'ka', [(i, j % size) for i, j in pairs if j is not None])]
    ppermute x15, waiting for transfers between devices: 28.3 us -> 25.2 us  [permute(): lax.ppermute(x, 'ka', [(i, j % size) for i, j in pairs if j is not None])]
    unnamed x2 -> x10, local copies, waits for them, and re-layouts: 0.01 us -> 1.64 us
    pallas_call x4, Pallas kernels: 24 us -> 22.7 us  [rows_of(): pl.pallas_call(rows_kernel, out_shape=[jax.ShapeDtypeStruct((width // 4,...]
    convert_element_type x3 -> x4, other arithmetic: 0.3 us -> 1.3 us  [the longest x1 1.04 us: on_two_by_four(): far = own_sum(step_0, core_0, across_0).astype(jnp.bfloat16)]
    convert_element_type x4, other arithmetic: 0.19 us -> 1.16 us  [for_x(): (step[1] + from_core[width // 4:].astype(jnp.float32)).astype(jnp.bfloat16)]
  transfers between devices with their start and end apart: 15 -> 15, of which waited for: 6 -> 6; matrix products, arithmetic and copies ran while one was open for 1% -> 3% of each run, Pallas kernels for 46% -> 44%
where the time goes in v6:
time: 93.8 us; the launch traced here: 93.4 us
  Pallas kernels  44.1 us (47%)
  waiting for transfers between devices  25.2 us (27%)
  starting transfers between devices  17.7 us (19%)
  other arithmetic  3.32 us (4%)
  local copies, waits for them, and re-layouts  2.87 us (3%)
    ppermute x15, waiting for transfers between devices, permute(): lax.ppermute(x, 'ka', [(i, j % size) for i, j in pairs if j is not None])  25.2 us
    pallas_call x4, Pallas kernels, rows_of(): pl.pallas_call(rows_kernel, out_shape=[jax.ShapeDtypeStruct((width // 4,...  22.7 us
    ppermute x15, starting transfers between devices, permute(): lax.ppermute(x, 'ka', [(i, j % size) for i, j in pairs if j is not None])  17.7 us
    pallas_call x1, Pallas kernels, products_of(): pl.pallas_call(products_kernel, out_shape=jax.ShapeDtypeStruct((k_local,...  13.4 us
    pallas_call x2, Pallas kernels, turned_pieces(): pl.pallas_call(functools.partial(turn_kernel, first), out_shape=[jax.Shap...  8.02 us
  transfers between devices with their start and end apart: 15, of which 6 were waited for; matrix products, arithmetic and copies ran while one was open for 3% of the time, Pallas kernels for 44%

profile of v6, /device:TPU:0, one launch (start us, length us, event | category | flops | bytes accessed | tf_op | source)
XLA Modules:
  0.0 93.4 jit_solution(15200196317208010680)
XLA Ops:
  0.0 0.5 add_xor_fusion.order_ref
  0.5 3.2 %shard_map.56 = bf16[2,256,1024]{2,1,0:T(8,128)(2,1)} custom-call(s32[4]{0:T(128)} %add_xor_fusion.order_ref, bf16[2,1024,1024]{2,1,0:T(8,128)(2,1)} %bitcast.8), custom_call_target="tpu_custom_call" | custom-call | bytes 2097152 | tf_op jit(solution)/shard_map/pallas_call | solution.py:135
  3.7 5.5 %collective-permute-start = (bf16[2,256,1024]{2,1,0:T(8,128)(2,1)}, bf16[2,256,1024]{2,1,0:T(8,128)(2,1)S(1)}, u32[]{:S(2)}, u32[]{:S(2)}) collective-permute-start(bf16[2,256,1024]{2,1,0:T(8,128)(2,1)} %shard_map.56), channel_id=1, source_target_pairs={{0,15},{1,0},{2,1},{3,2},{4,3},{5,4},{6,5},{7,6},{8,7},{9,8},{10,9... | collective-permute-start | bytes 3145736 | tf_op jit(solution)/shard_map/ppermute | solution.py:17
  9.1 4.9 %shard_map.58 = (bf16[2,256,1024]{2,1,0:T(8,128)(2,1)}, bf16[2,256,1024]{2,1,0:T(8,128)(2,1)}, bf16[2,256,1024]{2,1,0:T(8,128)(2,1)}) custom-call(s32[4]{0:T(128)} %add_xor_fusion.order_ref, bf16[2,1024,1024]{2,1,0:T(8,128)(2,1)} %bitcast.9), custom_call_target="tpu_custom_call" | custom-call | bytes 6291456 | tf_op jit(solution)/shard_map/pallas_call | solution.py:135
  14.0 0.7 collective-permute-start.1
  14.8 0.1 collective-permute-start.4
  14.8 13.4 %shard_map.55 = bf16[2,2,32,32,1024]{4,3,2,1,0:T(8,128)(2,1)} custom-call(s32[2,2]{1,0:T(2,128)} %first_ref.1, bf16[2,32,32,1024]{3,2,1,0:T(8,128)(2,1)} %coeffs_ref.1, bf16[2,2,32,32]{3,2,1,0:T(8,128)(2,1)} %cond_ref.1, bf16[2,2,32,32]{3,2,1,0:T(8,128)(2,1)} %val_ref.1), custom_call_target="tpu_custom_call" | custom-call | flops 6442450944 | bytes 12582912 | tf_op jit(solution)/shard_map/pallas_call | solution.py:90
  28.2 0.1 add_add_fusion.3
  28.3 0.0 collective-permute-done.next_ref
  28.3 6.3 %shard_map.57 = (f32[64,2048]{1,0:T(8,128)S(1)}, f32[64,2048]{1,0:T(8,128)S(1)}, bf16[128,2048]{1,0:T(8,128)(2,1)}) custom-call(s32[5]{0:T(128)S(1)} %get-tuple-element.31.pick_ref, bf16[2,1024,1024]{2,1,0:T(8,128)(2,1)} %bitcast.10, bf16[2,256,1024]{2,1,0:T(8,128)(2,1)S(1)} %collective-permute-done.next_ref, bf16[2,2,1024,1024]{3,2,1,0:T(8,128)(2,1)} %bitcast.14), custom_call_target="tpu_custom_call" | custom-call | flops 2147483648 | bytes 8388608 | tf_op jit(solution)/shard_map/pallas_call | solution.py:213
  34.6 0.8 copy-done
  35.4 0.8 copy-done.2
  36.2 0.4 collective-permute-start.3
  36.7 0.9 %collective-permute-start.6 = (bf16[2,256,1024]{2,1,0:T(8,128)(2,1)}, bf16[2,256,1024]{2,1,0:T(8,128)(2,1)S(1)}, u32[]{:S(2)}, u32[]{:S(2)}) collective-permute-start(bf16[2,256,1024]{2,1,0:T(8,128)(2,1)} %get-tuple-element.46), channel_id=1, source_target_pairs={{0,15},{1,0},{2,1},{3,2},{4,3},{5,4},{6,5},{7,6},{8,7},{9,8},{10,9... | collective-permute-start | bytes 3145736 | tf_op jit(solution)/shard_map/ppermute | solution.py:17
  37.6 0.1 add_add_fusion
  37.7 0.0 collective-permute-done.1.next_ref
  37.7 5.5 %shard_map.59 = (f32[64,2048]{1,0:T(8,128)S(1)}, f32[64,2048]{1,0:T(8,128)S(1)}, bf16[128,2048]{1,0:T(8,128)(2,1)S(1)}) custom-call(s32[5]{0:T(128)S(1)} %get-tuple-element.33.pick_ref, bf16[2,1024,1024]{2,1,0:T(8,128)(2,1)} %bitcast.11, bf16[2,256,1024]{2,1,0:T(8,128)(2,1)S(1)} %collective-permute-done.1.next_ref, bf16[2,2,1024,1024]{3,2,1,0:T(8,128)(2,1)} %bitcast.15), custom_call_target="tpu_custom_call" | custom-call | flops 2147483648 | bytes 8388608 | tf_op jit(solution)/shard_map/pallas_call | solution.py:213
  43.2 1.0 %collective-permute-done.4.next_ref = bf16[2,256,1024]{2,1,0:T(8,128)(2,1)S(1)} collective-permute-done((bf16[2,256,1024]{2,1,0:T(8,128)(2,1)}, bf16[2,256,1024]{2,1,0:T(8,128)(2,1)S(1)}, u32[]{:S(2)}, u32[]{:S(2)}) %collective-permute-start.4) | collective-permute-done | bytes 1048608 | tf_op jit(solution)/shard_map/ppermute | solution.py:17
  44.2 0.0 collective-permute-done.3
  44.3 1.0 %add_convert_fusion.6 = bf16[64,2048]{1,0:T(8,128)(2,1)S(1)} fusion(f32[64,2048]{1,0:T(8,128)S(1)} %copy-done.3, bf16[128,2048]{1,0:T(8,128)(2,1)} %collective-permute-done.3), kind=kLoop, calls=%fused_computation.7 | loop fusion | flops 393216 | bytes 1048576 | tf_op jit(solution)/shard_map/convert_element_type | solution.py:267
  45.3 0.1 collective-permute-start.7
  45.3 0.1 collective-permute-start.2
  45.4 5.5 %shard_map.60 = (f32[64,2048]{1,0:T(8,128)S(1)}, f32[64,2048]{1,0:T(8,128)S(1)}, bf16[128,2048]{1,0:T(8,128)(2,1)S(1)}) custom-call(s32[5]{0:T(128)S(1)} %get-tuple-element.43.pick_ref, bf16[2,1024,1024]{2,1,0:T(8,128)(2,1)} %bitcast.12, bf16[2,256,1024]{2,1,0:T(8,128)(2,1)S(1)} %collective-permute-done.4.next_ref, bf16[2,2,1024,1024]{3,2,1,0:T(8,128)(2,1)} %bitcast.16), custom_call_target="tpu_custom_call" | custom-call | flops 2147483648 | bytes 8388608 | tf_op jit(solution)/shard_map/pallas_call | solution.py:213
  50.9 0.6 collective-permute-start.5
  51.5 7.5 %collective-permute-done.7 = bf16[64,2048]{1,0:T(8,128)(2,1)S(1)} collective-permute-done((bf16[64,2048]{1,0:T(8,128)(2,1)S(1)}, bf16[64,2048]{1,0:T(8,128)(2,1)S(1)}, u32[]{:S(2)}, u32[]{:S(2)}) %collective-permute-start.7) | collective-permute-done | bytes 262176 | tf_op jit(solution)/shard_map/ppermute | solution.py:17
  59.0 1.0 %add_convert_fusion.3 = bf16[64,2048]{1,0:T(8,128)(2,1)S(1)} fusion(bf16[64,2048]{1,0:T(8,128)(2,1)S(1)} %collective-permute-done.7, f32[64,2048]{1,0:T(8,128)S(1)} %copy-done.1, bf16[128,2048]{1,0:T(8,128)(2,1)} %collective-permute-done.3), kind=kLoop, calls=%fused_computation.4 | loop fusion | flops 655360 | bytes 1310720 | tf_op jit(solution)/shard_map/convert_element_type | solution.py:287
  60.0 1.6 %collective-permute-start.12 = (bf16[64,2048]{1,0:T(8,128)(2,1)S(1)}, bf16[64,2048]{1,0:T(8,128)(2,1)S(1)}, u32[]{:S(2)}, u32[]{:S(2)}) collective-permute-start(bf16[64,2048]{1,0:T(8,128)(2,1)S(1)} %add_convert_fusion.3), channel_id=1, source_target_pairs={{0,4},{1,5},{2,6},{3,7},{4,0},{5,1},{6,2},{7,3},{8,12},{9,13},{10,... | collective-permute-start | bytes 786440 | tf_op jit(solution)/shard_map/ppermute | solution.py:17
  61.7 0.0 collective-permute-done.6.next_ref
  61.7 0.0 collective-permute-done.2
  61.7 0.0 collective-permute-done.5
  61.7 0.1 add_convert_fusion.5
  61.7 2.4 %collective-permute-start.11 = (bf16[64,2048]{1,0:T(8,128)(2,1)S(1)}, bf16[64,2048]{1,0:T(8,128)(2,1)S(1)}, u32[]{:S(2)}, u32[]{:S(2)}) collective-permute-start(bf16[64,2048]{1,0:T(8,128)(2,1)S(1)} %add_convert_fusion.5), channel_id=1, source_target_pairs={{0,2},{1,3},{2,0},{3,1},{4,6},{5,7},{6,4},{7,5},{8,10},{9,11},{10,... | collective-permute-start | bytes 786440 | tf_op jit(solution)/shard_map/ppermute | solution.py:17
  64.2 5.5 %shard_map.61 = (f32[64,2048]{1,0:T(8,128)S(1)}, f32[64,2048]{1,0:T(8,128)S(1)}, bf16[128,2048]{1,0:T(8,128)(2,1)S(1)}) custom-call(s32[5]{0:T(128)S(1)} %get-tuple-element.50.pick_ref, bf16[2,1024,1024]{2,1,0:T(8,128)(2,1)} %bitcast.13, bf16[2,256,1024]{2,1,0:T(8,128)(2,1)S(1)} %collective-permute-done.6.next_ref, bf16[2,2,1024,1024]{3,2,1,0:T(8,128)(2,1)} %bitcast.17), custom_call_target="tpu_custom_call" | custom-call | flops 2147483648 | bytes 8388608 | tf_op jit(solution)/shard_map/pallas_call | solution.py:213
  69.7 0.1 collective-permute-start.8
  69.8 0.1 collective-permute-start.10
  69.9 0.0 collective-permute-done.12
  69.9 0.6 collective-permute-done.11
  70.5 0.1 add_convert_fusion.1
  70.6 4.4 %collective-permute-start.14 = (bf16[64,2048]{1,0:T(8,128)(2,1)S(1)}, bf16[64,2048]{1,0:T(8,128)(2,1)S(1)}, u32[]{:S(2)}, u32[]{:S(2)}) collective-permute-start(bf16[64,2048]{1,0:T(8,128)(2,1)S(1)} %add_convert_fusion.1), channel_id=1, source_target_pairs={{0,8},{1,9},{2,10},{3,11},{4,12},{5,13},{6,14},{7,15},{8,0},{9,1},... | collective-permute-start | bytes 786440 | tf_op jit(solution)/shard_map/ppermute | solution.py:17
  75.0 3.5 %collective-permute-done.10 = bf16[64,2048]{1,0:T(8,128)(2,1)S(1)} collective-permute-done((bf16[64,2048]{1,0:T(8,128)(2,1)S(1)}, bf16[64,2048]{1,0:T(8,128)(2,1)S(1)}, u32[]{:S(2)}, u32[]{:S(2)}) %collective-permute-start.10) | collective-permute-done | bytes 262176 | tf_op jit(solution)/shard_map/ppermute | solution.py:17
  78.6 0.1 add_convert_fusion
  78.7 0.5 collective-permute-start.13
  79.2 0.3 collective-permute-start.9
  79.5 7.0 %collective-permute-done.14 = bf16[64,2048]{1,0:T(8,128)(2,1)S(1)} collective-permute-done((bf16[64,2048]{1,0:T(8,128)(2,1)S(1)}, bf16[64,2048]{1,0:T(8,128)(2,1)S(1)}, u32[]{:S(2)}, u32[]{:S(2)}) %collective-permute-start.14) | collective-permute-done | bytes 262176 | tf_op jit(solution)/shard_map/ppermute | solution.py:17
  86.5 5.5 %collective-permute-done.13 = bf16[64,2048]{1,0:T(8,128)(2,1)S(1)} collective-permute-done((bf16[64,2048]{1,0:T(8,128)(2,1)S(1)}, bf16[64,2048]{1,0:T(8,128)(2,1)S(1)}, u32[]{:S(2)}, u32[]{:S(2)}) %collective-permute-start.13) | collective-permute-done | bytes 262176 | tf_op jit(solution)/shard_map/ppermute | solution.py:17
  92.0 0.0 collective-permute-done.9
  92.0 0.2 add_multiply_fusion
  92.2 1.2 %reshape.11 = f32[64,2,1024]{2,1,0:T(2,128)} reshape(f32[64,2048]{1,0:T(8,128)S(1)} %add_multiply_fusion) | data formatting | bytes 1048576 | tf_op jit(solution)/shard_map/reshape | solution.py:297
  (13 shorter events, 0.2 us)
Async XLA Ops:
  3.7 24.6 %collective-permute-start = (bf16[2,256,1024]{2,1,0:T(8,128)(2,1)}, bf16[2,256,1024]{2,1,0:T(8,128)(2,1)S(1)}, u32[]{:S(2)}, u32[]{:S(2)}) collective-permute-start(bf16[2,256,1024]{2,1,0:T(8,128)(2,1)} %shard_map.56), channel_id=1, source_target_pairs={{0,15},{1,0},{2,1},{3,2},{4,3},{5,4},{6,5},{7,6},{8,7},{9,8},{10,9... | collective-permute-start | bytes 3145736 | tf_op jit(solution)/shard_map/ppermute | solution.py:17
  14.0 23.7 %collective-permute-start.1 = (bf16[2,256,1024]{2,1,0:T(8,128)(2,1)}, bf16[2,256,1024]{2,1,0:T(8,128)(2,1)S(1)}, u32[]{:S(2)}, u32[]{:S(2)}) collective-permute-start(bf16[2,256,1024]{2,1,0:T(8,128)(2,1)} %get-tuple-element.35), channel_id=1, source_target_pairs={{0,15},{1,0},{2,1},{3,2},{4,3},{5,4},{6,5},{7,6},{8,7},{9,8},{10,9... | collective-permute-start | bytes 3145736 | tf_op jit(solution)/shard_map/ppermute | solution.py:17
  14.8 13.5 %copy-start.4 = (s32[2]{0:T(128)S(1)}, s32[2]{0:T(128)}, u32[]{:S(2)}) copy-start(s32[2]{0:T(128)} %param.8) | copy-start | bytes 28
  14.8 29.5 %collective-permute-start.4 = (bf16[2,256,1024]{2,1,0:T(8,128)(2,1)}, bf16[2,256,1024]{2,1,0:T(8,128)(2,1)S(1)}, u32[]{:S(2)}, u32[]{:S(2)}) collective-permute-start(bf16[2,256,1024]{2,1,0:T(8,128)(2,1)} %get-tuple-element.41), channel_id=1, source_target_pairs={{0,15},{1,0},{2,1},{3,2},{4,3},{5,4},{6,5},{7,6},{8,7},{9,8},{10,9... | collective-permute-start | bytes 3145736 | tf_op jit(solution)/shard_map/ppermute | solution.py:17
  34.6 0.8 copy-start
  35.4 0.8 copy-start.2
  36.2 8.0 %collective-permute-start.3 = (bf16[128,2048]{1,0:T(8,128)(2,1)}, bf16[128,2048]{1,0:T(8,128)(2,1)}, u32[]{:S(2)}, u32[]{:S(2)}) collective-permute-start(bf16[128,2048]{1,0:T(8,128)(2,1)} %get-tuple-element.40), channel_id=1, source_target_pairs={{0,1},{1,0},{2,3},{3,2},{4,5},{5,4},{6,7},{7,6},{8,9},{9,8},{10,11... | collective-permute-start | bytes 1572872 | tf_op jit(solution)/shard_map/ppermute | solution.py:17
  36.7 25.0 %collective-permute-start.6 = (bf16[2,256,1024]{2,1,0:T(8,128)(2,1)}, bf16[2,256,1024]{2,1,0:T(8,128)(2,1)S(1)}, u32[]{:S(2)}, u32[]{:S(2)}) collective-permute-start(bf16[2,256,1024]{2,1,0:T(8,128)(2,1)} %get-tuple-element.46), channel_id=1, source_target_pairs={{0,15},{1,0},{2,1},{3,2},{4,3},{5,4},{6,5},{7,6},{8,7},{9,8},{10,9... | collective-permute-start | bytes 3145736 | tf_op jit(solution)/shard_map/ppermute | solution.py:17
  37.6 6.7 %copy-start.3 = (f32[64,2048]{1,0:T(8,128)S(1)}, f32[64,2048]{1,0:T(8,128)}, u32[]{:S(2)}) copy-start(f32[64,2048]{1,0:T(8,128)} %copy-done.2) | copy-start | bytes 1572868
  43.2 15.8 %copy-start.1 = (f32[64,2048]{1,0:T(8,128)S(1)}, f32[64,2048]{1,0:T(8,128)}, u32[]{:S(2)}) copy-start(f32[64,2048]{1,0:T(8,128)} %copy-done) | copy-start | bytes 1572868
  45.3 13.7 %collective-permute-start.7 = (bf16[64,2048]{1,0:T(8,128)(2,1)S(1)}, bf16[64,2048]{1,0:T(8,128)(2,1)S(1)}, u32[]{:S(2)}, u32[]{:S(2)}) collective-permute-start(bf16[64,2048]{1,0:T(8,128)(2,1)S(1)} %add_convert_fusion.6), channel_id=1, source_target_pairs={{0,2},{1,3},{2,0},{3,1},{4,6},{5,7},{6,4},{7,5},{8,10},{9,11},{10,... | collective-permute-start | bytes 786440 | tf_op jit(solution)/shard_map/ppermute | solution.py:17
  45.3 16.3 %collective-permute-start.2 = (bf16[128,2048]{1,0:T(8,128)(2,1)S(1)}, bf16[128,2048]{1,0:T(8,128)(2,1)S(1)}, u32[]{:S(2)}, u32[]{:S(2)}) collective-permute-start(bf16[128,2048]{1,0:T(8,128)(2,1)S(1)} %get-tuple-element.37), channel_id=1, source_target_pairs={{0,1},{1,0},{2,3},{3,2},{4,5},{5,4},{6,7},{7,6},{8,9},{9,8},{10,11... | collective-permute-start | bytes 1572872 | tf_op jit(solution)/shard_map/ppermute | solution.py:17
  50.9 10.8 %collective-permute-start.5 = (bf16[128,2048]{1,0:T(8,128)(2,1)S(1)}, bf16[128,2048]{1,0:T(8,128)(2,1)S(1)}, u32[]{:S(2)}, u32[]{:S(2)}) collective-permute-start(bf16[128,2048]{1,0:T(8,128)(2,1)S(1)} %get-tuple-element.45), channel_id=1, source_target_pairs={{0,1},{1,0},{2,3},{3,2},{4,5},{5,4},{6,7},{7,6},{8,9},{9,8},{10,11... | collective-permute-start | bytes 1572872 | tf_op jit(solution)/shard_map/ppermute | solution.py:17
  60.0 9.8 %collective-permute-start.12 = (bf16[64,2048]{1,0:T(8,128)(2,1)S(1)}, bf16[64,2048]{1,0:T(8,128)(2,1)S(1)}, u32[]{:S(2)}, u32[]{:S(2)}) collective-permute-start(bf16[64,2048]{1,0:T(8,128)(2,1)S(1)} %add_convert_fusion.3), channel_id=1, source_target_pairs={{0,4},{1,5},{2,6},{3,7},{4,0},{5,1},{6,2},{7,3},{8,12},{9,13},{10,... | collective-permute-start | bytes 786440 | tf_op jit(solution)/shard_map/ppermute | solution.py:17
  61.7 8.7 %collective-permute-start.11 = (bf16[64,2048]{1,0:T(8,128)(2,1)S(1)}, bf16[64,2048]{1,0:T(8,128)(2,1)S(1)}, u32[]{:S(2)}, u32[]{:S(2)}) collective-permute-start(bf16[64,2048]{1,0:T(8,128)(2,1)S(1)} %add_convert_fusion.5), channel_id=1, source_target_pairs={{0,2},{1,3},{2,0},{3,1},{4,6},{5,7},{6,4},{7,5},{8,10},{9,11},{10,... | collective-permute-start | bytes 786440 | tf_op jit(solution)/shard_map/ppermute | solution.py:17
  69.7 8.8 %collective-permute-start.8 = (bf16[128,2048]{1,0:T(8,128)(2,1)S(1)}, bf16[128,2048]{1,0:T(8,128)(2,1)S(1)}, u32[]{:S(2)}, u32[]{:S(2)}) collective-permute-start(bf16[128,2048]{1,0:T(8,128)(2,1)S(1)} %get-tuple-element.53), channel_id=1, source_target_pairs={{0,1},{1,0},{2,3},{3,2},{4,5},{5,4},{6,7},{7,6},{8,9},{9,8},{10,11... | collective-permute-start | bytes 1572872 | tf_op jit(solution)/shard_map/ppermute | solution.py:17
  69.8 8.7 %collective-permute-start.10 = (bf16[64,2048]{1,0:T(8,128)(2,1)S(1)}, bf16[64,2048]{1,0:T(8,128)(2,1)S(1)}, u32[]{:S(2)}, u32[]{:S(2)}) collective-permute-start(bf16[64,2048]{1,0:T(8,128)(2,1)S(1)} %add_convert_fusion.4), channel_id=1, source_target_pairs={{0,2},{1,3},{2,0},{3,1},{4,6},{5,7},{6,4},{7,5},{8,10},{9,11},{10,... | collective-permute-start | bytes 786440 | tf_op jit(solution)/shard_map/ppermute | solution.py:17
  70.6 15.9 %collective-permute-start.14 = (bf16[64,2048]{1,0:T(8,128)(2,1)S(1)}, bf16[64,2048]{1,0:T(8,128)(2,1)S(1)}, u32[]{:S(2)}, u32[]{:S(2)}) collective-permute-start(bf16[64,2048]{1,0:T(8,128)(2,1)S(1)} %add_convert_fusion.1), channel_id=1, source_target_pairs={{0,8},{1,9},{2,10},{3,11},{4,12},{5,13},{6,14},{7,15},{8,0},{9,1},... | collective-permute-start | bytes 786440 | tf_op jit(solution)/shard_map/ppermute | solution.py:17
  78.7 13.3 %collective-permute-start.13 = (bf16[64,2048]{1,0:T(8,128)(2,1)S(1)}, bf16[64,2048]{1,0:T(8,128)(2,1)S(1)}, u32[]{:S(2)}, u32[]{:S(2)}) collective-permute-start(bf16[64,2048]{1,0:T(8,128)(2,1)S(1)} %add_convert_fusion), channel_id=1, source_target_pairs={{0,4},{1,5},{2,6},{3,7},{4,0},{5,1},{6,2},{7,3},{8,12},{9,13},{10,... | collective-permute-start | bytes 786440 | tf_op jit(solution)/shard_map/ppermute | solution.py:17
  79.2 12.8 %collective-permute-start.9 = (bf16[64,2048]{1,0:T(8,128)(2,1)S(1)}, bf16[64,2048]{1,0:T(8,128)(2,1)S(1)}, u32[]{:S(2)}, u32[]{:S(2)}) collective-permute-start(bf16[64,2048]{1,0:T(8,128)(2,1)S(1)} %add_convert_fusion.2), channel_id=1, source_target_pairs={{0,2},{1,3},{2,0},{3,1},{4,6},{5,7},{6,4},{7,5},{8,10},{9,11},{10,... | collective-permute-start | bytes 786440 | tf_op jit(solution)/shard_map/ppermute | solution.py:17

commit v7 on v6

--- a/solution.py
+++ b/solution.py
@@ -78,7 +78,7 @@
             for h in range(bands_v // PART_V):
                 cols = slice(h * PART_V, (h + 1) * PART_V)
                 value = electron[h][m, own] - hole[m, :, cols]
-                out_ref[0, m, own, cols, :] = value.astype(jnp.bfloat16)
+                out_ref[0, m, 0, own, cols, :] = value.astype(jnp.bfloat16)
 
 
 def products_of(coeffs, g_cond, g_val, band_first):
@@ -89,7 +89,9 @@
     depth = bands_c * bands_v
     return pl.pallas_call(
         products_kernel,
-        out_shape=jax.ShapeDtypeStruct((k_local, modes, bands_c, bands_v, excitons), jnp.bfloat16),
+        out_shape=jax.ShapeDtypeStruct(
+            (k_local, modes, excitons // tile, bands_c, bands_v, tile), jnp.bfloat16
+        ),
         grid=(k_local, excitons // tile),
         in_specs=[
             pl.BlockSpec(memory_space=pltpu.SMEM),
@@ -97,7 +99,9 @@
             pl.BlockSpec((1, modes, bands_c, bands_c), lambda k, s: (k, 0, 0, 0)),
             pl.BlockSpec((1, modes, bands_v, bands_v), lambda k, s: (k, 0, 0, 0)),
         ],
-        out_specs=pl.BlockSpec((1, modes, bands_c, bands_v, tile), lambda k, s: (k, 0, 0, 0, s)),
+        out_specs=pl.BlockSpec(
+            (1, modes, 1, bands_c, bands_v, tile), lambda k, s: (k, 0, s, 0, 0, 0)
+        ),
         scratch_shapes=[
             pltpu.VMEM((modes * rows_e, rows_e), jnp.bfloat16),
             pltpu.VMEM((modes * rows_h, rows_h), jnp.bfloat16),
@@ -155,7 +159,6 @@
     own_held, next_held, held, left, own_sems, next_sems, sems = refs
     k_local, depth, width = own_held.shape
     tiles, _, _, tile = held.shape
-    per_mode = right_ref.shape[3] // tile
     core, x = pick_ref[k_local + 1], pick_ref[k_local + 2]
     columns = pl.ds(pl.multiple_of(pick_ref[k_local] * width, width), width)
     near = [pick_ref[k] < k_local for k in range(k_local)]
@@ -169,8 +172,7 @@
         return pltpu.make_async_copy(source, next_held.at[k], next_sems.at[k])
 
     def copy_right(t, k):
-        source = right_ref.at[k, t // per_mode, :, pl.ds(t % per_mode * tile, tile)]
-        return pltpu.make_async_copy(source, held.at[t, k], sems.at[t, k])
+        return pltpu.make_async_copy(right_ref.at[k, t], held.at[t, k], sems.at[t, k])
 
     for k in range(k_local):
         copy_own(k).start()
@@ -207,9 +209,8 @@
 
 def rows_of(pick, own, following, products):
     k_local, width, depth = following.shape
-    modes, excitons = products.shape[1], products.shape[3]
-    columns, tile = modes * excitons, 512
-    tiles = columns // tile
+    _, tiles, _, tile = products.shape
+    columns = tiles * tile
     return pl.pallas_call(
         rows_kernel,
         out_shape=[
@@ -254,7 +255,7 @@
     pieces += turned_pieces(flat, order, 1, 3, width)
     following = [permute(piece, lambda i: i - 1) for piece in pieces]
     products = products_of(coeffs, g_cond, g_val, band_first)
-    products = products.reshape(k_local, modes, bands_c * bands_v, excitons)
+    products = products.reshape(k_local, -1, bands_c * bands_v, products.shape[-1])
     places = jnp.mod(k_plus_q - me * k_local, k_local * size)
 
     def rows(step, after):
@@ -277,16 +278,18 @@
 
     step_0 = rows(0, products)
     step_1 = rows(1, step_0[0])
-    core_0, following[2], _ = lax.optimization_barrier((step_0[2], following[2], step_1[0]))
-    send_0 = for_x(step_0, core_0)
-    across_0 = from_x(send_0)
-    step_2 = rows(2, (step_1[0], send_0))
-    core_1, core_2, following[3] = lax.optimization_barrier((step_1[2], step_2[2], following[3]))
-    send_1, send_2 = for_x(step_1, core_1), for_x(step_2, core_2)
-    across_1, across_2 = from_x(send_1), from_x(send_2)
+    step_2 = rows(2, step_1[0])
+    core_0, core_1, core_2, following[3] = lax.optimization_barrier(
+        (step_0[2], step_1[2], step_2[2], following[3])
+    )
+    send_0, send_1 = for_x(step_0, core_0), for_x(step_1, core_1)
+    across_0, across_1 = from_x(send_0), from_x(send_1)
+    across_0, _ = lax.optimization_barrier((across_0, send_1))
     far = own_sum(step_0, core_0, across_0).astype(jnp.bfloat16)
-    step_3 = rows(3, (send_1, send_2, far))
+    step_3 = rows(3, far)
     far = over(far, 4)
+    send_2, _ = lax.optimization_barrier((for_x(step_2, core_2), step_3[0]))
+    across_2 = from_x(send_2)
     pair = (own_sum(step_1, core_1, across_1) + far).astype(jnp.bfloat16)
     send_3 = for_x(step_3, step_3[2])
     across_2, _ = lax.optimization_barrier((across_2, (pair, send_3)))
@@ -306,7 +309,8 @@
     blocks = jnp.concatenate((flat, permute(flat, lambda i: i - 1)), 0)
     offsets = jnp.mod(k_plus_q - lax.axis_index("ka") * k_local, k_local * size)
     products = products_of(coeffs, g_cond, g_val, band_first)
-    products = products.reshape(k_local, modes, depth, excitons)
+    products = products.reshape(k_local, modes, -1, depth, products.shape[-1])
+    products = jnp.moveaxis(products, 2, 3).reshape(k_local, modes, depth, excitons)
     partners = [
         lax.dynamic_index_in_dim(blocks, offsets[k], 0, keepdims=False) for k in range(k_local)
     ]

time: 93.8 us -> 98.9 us (1.054)
  Pallas kernels: 44.1 us -> 55.3 us
  other arithmetic: 3.32 us -> 1.4 us
  starting transfers between devices: 17.7 us -> 16 us
  local copies, waits for them, and re-layouts: 2.87 us -> 1.24 us
    pallas_call x4, Pallas kernels: 22.7 us -> 33.9 us  [rows_of(): pl.pallas_call(rows_kernel, out_shape=[jax.ShapeDtypeStruct((width // 4,...]
    ppermute x15, starting transfers between devices: 17.7 us -> 16 us  [permute(): lax.ppermute(x, 'ka', [(i, j % size) for i, j in pairs if j is not None])]
    unnamed x10 -> x2, local copies, waits for them, and re-layouts: 1.64 us -> 0.01 us
  transfers between devices with their start and end apart: 15 -> 15, of which waited for: 6 -> 7; matrix products, arithmetic and copies ran while one was open for 3% -> 1% of each run, Pallas kernels for 44% -> 53%
where the time goes in v7:
time: 98.9 us; the launch traced here: 98.7 us
  Pallas kernels  55.3 us (56%)
  waiting for transfers between devices  24.7 us (25%)
  starting transfers between devices  16 us (16%)
  other arithmetic  1.4 us (1%)
  local copies, waits for them, and re-layouts  1.24 us (1%)
    pallas_call x4, Pallas kernels, rows_of(): pl.pallas_call(rows_kernel, out_shape=[jax.ShapeDtypeStruct((width // 4,...  33.9 us
    ppermute x15, waiting for transfers between devices, permute(): lax.ppermute(x, 'ka', [(i, j % size) for i, j in pairs if j is not None])  24.7 us
    ppermute x15, starting transfers between devices, permute(): lax.ppermute(x, 'ka', [(i, j % size) for i, j in pairs if j is not None])  16 us
    pallas_call x1, Pallas kernels, products_of(): pl.pallas_call(products_kernel, out_shape=jax.ShapeDtypeStruct((k_local,...  13.3 us
    pallas_call x2, Pallas kernels, turned_pieces(): pl.pallas_call(functools.partial(turn_kernel, first), out_shape=[jax.Shap...  8.1 us
  transfers between devices with their start and end apart: 15, of which 7 were waited for; matrix products, arithmetic and copies ran while one was open for 1% of the time, Pallas kernels for 53%

profile of v7, /device:TPU:0, one launch (start us, length us, event | category | flops | bytes accessed | tf_op | source)
XLA Modules:
  0.0 98.7 jit_solution(3305148506730243192)
XLA Ops:
  0.0 0.0 copy-start
  0.0 0.5 add_xor_fusion.order_ref
  0.5 3.2 %shard_map.56 = bf16[2,256,1024]{2,1,0:T(8,128)(2,1)} custom-call(s32[4]{0:T(128)} %add_xor_fusion.order_ref, bf16[2,1024,1024]{2,1,0:T(8,128)(2,1)} %bitcast.8), custom_call_target="tpu_custom_call" | custom-call | bytes 2097152 | tf_op jit(solution)/shard_map/pallas_call | solution.py:139
  3.7 5.5 %collective-permute-start = (bf16[2,256,1024]{2,1,0:T(8,128)(2,1)}, bf16[2,256,1024]{2,1,0:T(8,128)(2,1)}, u32[]{:S(2)}, u32[]{:S(2)}) collective-permute-start(bf16[2,256,1024]{2,1,0:T(8,128)(2,1)} %shard_map.56), channel_id=1, source_target_pairs={{0,15},{1,0},{2,1},{3,2},{4,3},{5,4},{6,5},{7,6},{8,7},{9,8},{10,9... | collective-permute-start | bytes 3145736 | tf_op jit(solution)/shard_map/ppermute | solution.py:17
  9.2 4.9 %shard_map.58 = (bf16[2,256,1024]{2,1,0:T(8,128)(2,1)}, bf16[2,256,1024]{2,1,0:T(8,128)(2,1)}, bf16[2,256,1024]{2,1,0:T(8,128)(2,1)}) custom-call(s32[4]{0:T(128)} %add_xor_fusion.order_ref, bf16[2,1024,1024]{2,1,0:T(8,128)(2,1)} %bitcast.9), custom_call_target="tpu_custom_call" | custom-call | bytes 6291456 | tf_op jit(solution)/shard_map/pallas_call | solution.py:139
  14.1 0.7 collective-permute-start.2
  14.8 0.1 collective-permute-start.4
  14.9 0.6 collective-permute-start.6
  15.5 0.0 copy-done
  15.5 0.1 add_add_fusion
  15.6 13.3 %shard_map.55 = bf16[2,2,4,32,32,256]{5,4,3,2,1,0:T(8,128)(2,1)} custom-call(s32[2,2]{1,0:T(2,128)} %first_ref.1, bf16[2,32,32,1024]{3,2,1,0:T(8,128)(2,1)} %coeffs_ref.1, bf16[2,2,32,32]{3,2,1,0:T(8,128)(2,1)} %cond_ref.1, bf16[2,2,32,32]{3,2,1,0:T(8,128)(2,1)} %val_ref.1), custom_call_target="tpu_custom_call" | custom-call | flops 6442450944 | bytes 12582912 | tf_op jit(solution)/shard_map/pallas_call | solution.py:90
  28.9 0.1 add_add_fusion.3
  28.9 0.0 collective-permute-done.next_ref
  29.0 10.3 %shard_map.57 = (f32[64,2048]{1,0:T(8,128)S(1)}, f32[64,2048]{1,0:T(8,128)S(1)}, bf16[128,2048]{1,0:T(8,128)(2,1)S(1)}) custom-call(s32[5]{0:T(128)S(1)} %get-tuple-element.32.pick_ref, bf16[2,1024,1024]{2,1,0:T(8,128)(2,1)} %bitcast.10, bf16[2,256,1024]{2,1,0:T(8,128)(2,1)} %collective-permute-done.next_ref, bf16[2,8,1024,256]{3,2,1,0:T(8,128)(2,1)} %bitcast.14), custom_call_target="tpu_custom_call" | custom-call | flops 2147483648 | bytes 8388608 | tf_op jit(solution)/shard_map/pallas_call | solution.py:214
  39.3 0.0 collective-permute-done.2.next_ref
  39.3 7.8 %shard_map.59 = (f32[64,2048]{1,0:T(8,128)S(1)}, f32[64,2048]{1,0:T(8,128)S(1)}, bf16[128,2048]{1,0:T(8,128)(2,1)S(1)}) custom-call(s32[5]{0:T(128)S(1)} %get-tuple-element.35.pick_ref, bf16[2,1024,1024]{2,1,0:T(8,128)(2,1)} %bitcast.11, bf16[2,256,1024]{2,1,0:T(8,128)(2,1)S(1)} %collective-permute-done.2.next_ref, bf16[2,8,1024,256]{3,2,1,0:T(8,128)(2,1)} %bitcast.15), custom_call_target="tpu_custom_call" | custom-call | flops 2147483648 | bytes 8388608 | tf_op jit(solution)/shard_map/pallas_call | solution.py:214
  47.1 0.0 collective-permute-done.4.next_ref
  47.2 7.9 %shard_map.60 = (f32[64,2048]{1,0:T(8,128)S(1)}, f32[64,2048]{1,0:T(8,128)S(1)}, bf16[128,2048]{1,0:T(8,128)(2,1)S(1)}) custom-call(s32[5]{0:T(128)S(1)} %get-tuple-element.40.pick_ref, bf16[2,1024,1024]{2,1,0:T(8,128)(2,1)} %bitcast.12, bf16[2,256,1024]{2,1,0:T(8,128)(2,1)S(1)} %collective-permute-done.4.next_ref, bf16[2,8,1024,256]{3,2,1,0:T(8,128)(2,1)} %bitcast.16), custom_call_target="tpu_custom_call" | custom-call | flops 2147483648 | bytes 8388608 | tf_op jit(solution)/shard_map/pallas_call | solution.py:214
  55.1 0.2 collective-permute-start.5
  55.2 0.4 collective-permute-start.3
  55.7 0.1 collective-permute-start.1
  55.7 0.0 collective-permute-done.6.next_ref
  55.7 1.3 %collective-permute-done.5 = bf16[128,2048]{1,0:T(8,128)(2,1)S(1)} collective-permute-done((bf16[128,2048]{1,0:T(8,128)(2,1)S(1)}, bf16[128,2048]{1,0:T(8,128)(2,1)S(1)}, u32[]{:S(2)}, u32[]{:S(2)}) %collective-permute-start.5) | collective-permute-done | bytes 524320 | tf_op jit(solution)/shard_map/ppermute | solution.py:17
  57.1 0.7 collective-permute-done.3
  57.8 0.7 collective-permute-done.1
  58.6 1.3 %collective-permute-start.7 = (bf16[64,2048]{1,0:T(8,128)(2,1)S(1)}, bf16[64,2048]{1,0:T(8,128)(2,1)S(1)}, u32[]{:S(2)}, u32[]{:S(2)}) collective-permute-start(bf16[64,2048]{1,0:T(8,128)(2,1)S(1)} %add_convert_fusion.6), channel_id=1, source_target_pairs={{0,2},{1,3},{2,0},{3,1},{4,6},{5,7},{6,4},{7,5},{8,10},{9,11},{10,... | collective-permute-start | bytes 786440 | tf_op jit(solution)/shard_map/ppermute | solution.py:17
  60.0 0.8 collective-permute-start.11
  60.8 7.0 %collective-permute-done.7 = bf16[64,2048]{1,0:T(8,128)(2,1)S(1)} collective-permute-done((bf16[64,2048]{1,0:T(8,128)(2,1)S(1)}, bf16[64,2048]{1,0:T(8,128)(2,1)S(1)}, u32[]{:S(2)}, u32[]{:S(2)}) %collective-permute-start.7) | collective-permute-done | bytes 262176 | tf_op jit(solution)/shard_map/ppermute | solution.py:17
  67.9 0.1 add_convert_fusion.4
  67.9 0.1 collective-permute-start.12
  68.0 7.8 %shard_map.61 = (f32[64,2048]{1,0:T(8,128)S(1)}, f32[64,2048]{1,0:T(8,128)S(1)}, bf16[128,2048]{1,0:T(8,128)(2,1)S(1)}) custom-call(s32[5]{0:T(128)S(1)} %get-tuple-element.49.pick_ref, bf16[2,1024,1024]{2,1,0:T(8,128)(2,1)} %bitcast.13, bf16[2,256,1024]{2,1,0:T(8,128)(2,1)S(1)} %collective-permute-done.6.next_ref, bf16[2,8,1024,256]{3,2,1,0:T(8,128)(2,1)} %bitcast.17), custom_call_target="tpu_custom_call" | custom-call | flops 2147483648 | bytes 8388608 | tf_op jit(solution)/shard_map/pallas_call | solution.py:214
  75.9 0.1 collective-permute-start.8
  75.9 0.1 add_convert_fusion.2
  76.0 1.3 %collective-permute-start.10 = (bf16[64,2048]{1,0:T(8,128)(2,1)S(1)}, bf16[64,2048]{1,0:T(8,128)(2,1)S(1)}, u32[]{:S(2)}, u32[]{:S(2)}) collective-permute-start(bf16[64,2048]{1,0:T(8,128)(2,1)S(1)} %add_convert_fusion.2), channel_id=1, source_target_pairs={{0,2},{1,3},{2,0},{3,1},{4,6},{5,7},{6,4},{7,5},{8,10},{9,11},{10,... | collective-permute-start | bytes 786440 | tf_op jit(solution)/shard_map/ppermute | solution.py:17
  77.3 0.0 collective-permute-done.11
  77.3 0.0 collective-permute-done.12
  77.3 0.1 add_convert_fusion.1
  77.4 1.5 %collective-permute-start.14 = (bf16[64,2048]{1,0:T(8,128)(2,1)S(1)}, bf16[64,2048]{1,0:T(8,128)(2,1)S(1)}, u32[]{:S(2)}, u32[]{:S(2)}) collective-permute-start(bf16[64,2048]{1,0:T(8,128)(2,1)S(1)} %add_convert_fusion.1), channel_id=1, source_target_pairs={{0,8},{1,9},{2,10},{3,11},{4,12},{5,13},{6,14},{7,15},{8,0},{9,1},... | collective-permute-start | bytes 786440 | tf_op jit(solution)/shard_map/ppermute | solution.py:17
  79.0 5.8 %collective-permute-done.10 = bf16[64,2048]{1,0:T(8,128)(2,1)S(1)} collective-permute-done((bf16[64,2048]{1,0:T(8,128)(2,1)S(1)}, bf16[64,2048]{1,0:T(8,128)(2,1)S(1)}, u32[]{:S(2)}, u32[]{:S(2)}) %collective-permute-start.10) | collective-permute-done | bytes 262176 | tf_op jit(solution)/shard_map/ppermute | solution.py:17
  84.8 0.0 collective-permute-done.8
  84.9 0.1 add_convert_fusion
  85.0 2.1 %collective-permute-start.13 = (bf16[64,2048]{1,0:T(8,128)(2,1)S(1)}, bf16[64,2048]{1,0:T(8,128)(2,1)S(1)}, u32[]{:S(2)}, u32[]{:S(2)}) collective-permute-start(bf16[64,2048]{1,0:T(8,128)(2,1)S(1)} %add_convert_fusion), channel_id=1, source_target_pairs={{0,4},{1,5},{2,6},{3,7},{4,0},{5,1},{6,2},{7,3},{8,12},{9,13},{10,... | collective-permute-start | bytes 786440 | tf_op jit(solution)/shard_map/ppermute | solution.py:17
  87.1 1.2 %collective-permute-start.9 = (bf16[64,2048]{1,0:T(8,128)(2,1)S(1)}, bf16[64,2048]{1,0:T(8,128)(2,1)S(1)}, u32[]{:S(2)}, u32[]{:S(2)}) collective-permute-start(bf16[64,2048]{1,0:T(8,128)(2,1)S(1)} %add_convert_fusion.3), channel_id=1, source_target_pairs={{0,2},{1,3},{2,0},{3,1},{4,6},{5,7},{6,4},{7,5},{8,10},{9,11},{10,... | collective-permute-start | bytes 786440 | tf_op jit(solution)/shard_map/ppermute | solution.py:17
  88.3 4.3 %collective-permute-done.14 = bf16[64,2048]{1,0:T(8,128)(2,1)S(1)} collective-permute-done((bf16[64,2048]{1,0:T(8,128)(2,1)S(1)}, bf16[64,2048]{1,0:T(8,128)(2,1)S(1)}, u32[]{:S(2)}, u32[]{:S(2)}) %collective-permute-start.14) | collective-permute-done | bytes 262176 | tf_op jit(solution)/shard_map/ppermute | solution.py:17
  92.6 4.8 %collective-permute-done.13 = bf16[64,2048]{1,0:T(8,128)(2,1)S(1)} collective-permute-done((bf16[64,2048]{1,0:T(8,128)(2,1)S(1)}, bf16[64,2048]{1,0:T(8,128)(2,1)S(1)}, u32[]{:S(2)}, u32[]{:S(2)}) %collective-permute-start.13) | collective-permute-done | bytes 262176 | tf_op jit(solution)/shard_map/ppermute | solution.py:17
  97.3 0.0 collective-permute-done.9
  97.3 0.2 add_multiply_fusion
  97.5 1.2 %reshape.11 = f32[64,2,1024]{2,1,0:T(2,128)} reshape(f32[64,2048]{1,0:T(8,128)S(1)} %add_multiply_fusion) | data formatting | bytes 1048576 | tf_op jit(solution)/shard_map/reshape | solution.py:300
  (6 shorter events, 0.2 us)
Async XLA Ops:
  0.0 15.5 %copy-start = (s32[2]{0:T(128)S(1)}, s32[2]{0:T(128)}, u32[]{:S(2)}) copy-start(s32[2]{0:T(128)} %param.8) | copy-start | bytes 28
  3.7 25.2 %collective-permute-start = (bf16[2,256,1024]{2,1,0:T(8,128)(2,1)}, bf16[2,256,1024]{2,1,0:T(8,128)(2,1)}, u32[]{:S(2)}, u32[]{:S(2)}) collective-permute-start(bf16[2,256,1024]{2,1,0:T(8,128)(2,1)} %shard_map.56), channel_id=1, source_target_pairs={{0,15},{1,0},{2,1},{3,2},{4,3},{5,4},{6,5},{7,6},{8,7},{9,8},{10,9... | collective-permute-start | bytes 3145736 | tf_op jit(solution)/shard_map/ppermute | solution.py:17
  14.1 25.2 %collective-permute-start.2 = (bf16[2,256,1024]{2,1,0:T(8,128)(2,1)}, bf16[2,256,1024]{2,1,0:T(8,128)(2,1)S(1)}, u32[]{:S(2)}, u32[]{:S(2)}) collective-permute-start(bf16[2,256,1024]{2,1,0:T(8,128)(2,1)} %get-tuple-element.37), channel_id=1, source_target_pairs={{0,15},{1,0},{2,1},{3,2},{4,3},{5,4},{6,5},{7,6},{8,7},{9,8},{10,9... | collective-permute-start | bytes 3145736 | tf_op jit(solution)/shard_map/ppermute | solution.py:17
  14.8 32.3 %collective-permute-start.4 = (bf16[2,256,1024]{2,1,0:T(8,128)(2,1)}, bf16[2,256,1024]{2,1,0:T(8,128)(2,1)S(1)}, u32[]{:S(2)}, u32[]{:S(2)}) collective-permute-start(bf16[2,256,1024]{2,1,0:T(8,128)(2,1)} %get-tuple-element.41), channel_id=1, source_target_pairs={{0,15},{1,0},{2,1},{3,2},{4,3},{5,4},{6,5},{7,6},{8,7},{9,8},{10,9... | collective-permute-start | bytes 3145736 | tf_op jit(solution)/shard_map/ppermute | solution.py:17
  14.9 40.8 %collective-permute-start.6 = (bf16[2,256,1024]{2,1,0:T(8,128)(2,1)}, bf16[2,256,1024]{2,1,0:T(8,128)(2,1)S(1)}, u32[]{:S(2)}, u32[]{:S(2)}) collective-permute-start(bf16[2,256,1024]{2,1,0:T(8,128)(2,1)} %get-tuple-element.43), channel_id=1, source_target_pairs={{0,15},{1,0},{2,1},{3,2},{4,3},{5,4},{6,5},{7,6},{8,7},{9,8},{10,9... | collective-permute-start | bytes 3145736 | tf_op jit(solution)/shard_map/ppermute | solution.py:17
  55.1 2.0 %collective-permute-start.5 = (bf16[128,2048]{1,0:T(8,128)(2,1)S(1)}, bf16[128,2048]{1,0:T(8,128)(2,1)S(1)}, u32[]{:S(2)}, u32[]{:S(2)}) collective-permute-start(bf16[128,2048]{1,0:T(8,128)(2,1)S(1)} %get-tuple-element.42), channel_id=1, source_target_pairs={{0,1},{1,0},{2,3},{3,2},{4,5},{5,4},{6,7},{7,6},{8,9},{9,8},{10,11... | collective-permute-start | bytes 1572872 | tf_op jit(solution)/shard_map/ppermute | solution.py:17
  55.2 2.6 %collective-permute-start.3 = (bf16[128,2048]{1,0:T(8,128)(2,1)S(1)}, bf16[128,2048]{1,0:T(8,128)(2,1)S(1)}, u32[]{:S(2)}, u32[]{:S(2)}) collective-permute-start(bf16[128,2048]{1,0:T(8,128)(2,1)S(1)} %get-tuple-element.38), channel_id=1, source_target_pairs={{0,1},{1,0},{2,3},{3,2},{4,5},{5,4},{6,7},{7,6},{8,9},{9,8},{10,11... | collective-permute-start | bytes 1572872 | tf_op jit(solution)/shard_map/ppermute | solution.py:17
  55.7 2.9 %collective-permute-start.1 = (bf16[128,2048]{1,0:T(8,128)(2,1)S(1)}, bf16[128,2048]{1,0:T(8,128)(2,1)S(1)}, u32[]{:S(2)}, u32[]{:S(2)}) collective-permute-start(bf16[128,2048]{1,0:T(8,128)(2,1)S(1)} %get-tuple-element.34), channel_id=1, source_target_pairs={{0,1},{1,0},{2,3},{3,2},{4,5},{5,4},{6,7},{7,6},{8,9},{9,8},{10,11... | collective-permute-start | bytes 1572872 | tf_op jit(solution)/shard_map/ppermute | solution.py:17
  58.6 9.2 %collective-permute-start.7 = (bf16[64,2048]{1,0:T(8,128)(2,1)S(1)}, bf16[64,2048]{1,0:T(8,128)(2,1)S(1)}, u32[]{:S(2)}, u32[]{:S(2)}) collective-permute-start(bf16[64,2048]{1,0:T(8,128)(2,1)S(1)} %add_convert_fusion.6), channel_id=1, source_target_pairs={{0,2},{1,3},{2,0},{3,1},{4,6},{5,7},{6,4},{7,5},{8,10},{9,11},{10,... | collective-permute-start | bytes 786440 | tf_op jit(solution)/shard_map/ppermute | solution.py:17
  60.0 17.3 %collective-permute-start.11 = (bf16[64,2048]{1,0:T(8,128)(2,1)S(1)}, bf16[64,2048]{1,0:T(8,128)(2,1)S(1)}, u32[]{:S(2)}, u32[]{:S(2)}) collective-permute-start(bf16[64,2048]{1,0:T(8,128)(2,1)S(1)} %add_convert_fusion.5), channel_id=1, source_target_pairs={{0,2},{1,3},{2,0},{3,1},{4,6},{5,7},{6,4},{7,5},{8,10},{9,11},{10,... | collective-permute-start | bytes 786440 | tf_op jit(solution)/shard_map/ppermute | solution.py:17
  67.9 9.4 %collective-permute-start.12 = (bf16[64,2048]{1,0:T(8,128)(2,1)S(1)}, bf16[64,2048]{1,0:T(8,128)(2,1)S(1)}, u32[]{:S(2)}, u32[]{:S(2)}) collective-permute-start(bf16[64,2048]{1,0:T(8,128)(2,1)S(1)} %add_convert_fusion.4), channel_id=1, source_target_pairs={{0,4},{1,5},{2,6},{3,7},{4,0},{5,1},{6,2},{7,3},{8,12},{9,13},{10,... | collective-permute-start | bytes 786440 | tf_op jit(solution)/shard_map/ppermute | solution.py:17
  75.9 9.0 %collective-permute-start.8 = (bf16[128,2048]{1,0:T(8,128)(2,1)S(1)}, bf16[128,2048]{1,0:T(8,128)(2,1)S(1)}, u32[]{:S(2)}, u32[]{:S(2)}) collective-permute-start(bf16[128,2048]{1,0:T(8,128)(2,1)S(1)} %get-tuple-element.52), channel_id=1, source_target_pairs={{0,1},{1,0},{2,3},{3,2},{4,5},{5,4},{6,7},{7,6},{8,9},{9,8},{10,11... | collective-permute-start | bytes 1572872 | tf_op jit(solution)/shard_map/ppermute | solution.py:17
  76.0 8.8 %collective-permute-start.10 = (bf16[64,2048]{1,0:T(8,128)(2,1)S(1)}, bf16[64,2048]{1,0:T(8,128)(2,1)S(1)}, u32[]{:S(2)}, u32[]{:S(2)}) collective-permute-start(bf16[64,2048]{1,0:T(8,128)(2,1)S(1)} %add_convert_fusion.2), channel_id=1, source_target_pairs={{0,2},{1,3},{2,0},{3,1},{4,6},{5,7},{6,4},{7,5},{8,10},{9,11},{10,... | collective-permute-start | bytes 786440 | tf_op jit(solution)/shard_map/ppermute | solution.py:17
  77.4 15.1 %collective-permute-start.14 = (bf16[64,2048]{1,0:T(8,128)(2,1)S(1)}, bf16[64,2048]{1,0:T(8,128)(2,1)S(1)}, u32[]{:S(2)}, u32[]{:S(2)}) collective-permute-start(bf16[64,2048]{1,0:T(8,128)(2,1)S(1)} %add_convert_fusion.1), channel_id=1, source_target_pairs={{0,8},{1,9},{2,10},{3,11},{4,12},{5,13},{6,14},{7,15},{8,0},{9,1},... | collective-permute-start | bytes 786440 | tf_op jit(solution)/shard_map/ppermute | solution.py:17
  85.0 12.3 %collective-permute-start.13 = (bf16[64,2048]{1,0:T(8,128)(2,1)S(1)}, bf16[64,2048]{1,0:T(8,128)(2,1)S(1)}, u32[]{:S(2)}, u32[]{:S(2)}) collective-permute-start(bf16[64,2048]{1,0:T(8,128)(2,1)S(1)} %add_convert_fusion), channel_id=1, source_target_pairs={{0,4},{1,5},{2,6},{3,7},{4,0},{5,1},{6,2},{7,3},{8,12},{9,13},{10,... | collective-permute-start | bytes 786440 | tf_op jit(solution)/shard_map/ppermute | solution.py:17
  87.1 10.3 %collective-permute-start.9 = (bf16[64,2048]{1,0:T(8,128)(2,1)S(1)}, bf16[64,2048]{1,0:T(8,128)(2,1)S(1)}, u32[]{:S(2)}, u32[]{:S(2)}) collective-permute-start(bf16[64,2048]{1,0:T(8,128)(2,1)S(1)} %add_convert_fusion.3), channel_id=1, source_target_pairs={{0,2},{1,3},{2,0},{3,1},{4,6},{5,7},{6,4},{7,5},{8,10},{9,11},{10,... | collective-permute-start | bytes 786440 | tf_op jit(solution)/shard_map/ppermute | solution.py:17

commit v8 on v6

--- a/solution.py
+++ b/solution.py
@@ -175,7 +175,8 @@
     for k in range(k_local):
         copy_own(k).start()
         copy_next(k).start()
-    for t in range(tiles):
+    ahead = 2
+    for t in range(ahead):
         for k in range(k_local):
             copy_right(t, k).start()
     for k in range(k_local):
@@ -193,6 +194,9 @@
     for t in range(tiles):
         for k in range(k_local):
             copy_right(t, k).wait()
+        if t + ahead < tiles:
+            for k in range(k_local):
+                copy_right(t + ahead, k).start()
         right = held[t].reshape(k_local * depth, tile)
         total = jnp.dot(left[...], right, preferred_element_type=jnp.float32)
         parts = total.reshape(2, 2, width // 4, tile)
@@ -277,16 +281,18 @@
 
     step_0 = rows(0, products)
     step_1 = rows(1, step_0[0])
-    core_0, following[2], _ = lax.optimization_barrier((step_0[2], following[2], step_1[0]))
-    send_0 = for_x(step_0, core_0)
-    across_0 = from_x(send_0)
-    step_2 = rows(2, (step_1[0], send_0))
-    core_1, core_2, following[3] = lax.optimization_barrier((step_1[2], step_2[2], following[3]))
-    send_1, send_2 = for_x(step_1, core_1), for_x(step_2, core_2)
-    across_1, across_2 = from_x(send_1), from_x(send_2)
+    step_2 = rows(2, step_1[0])
+    core_0, core_1, core_2, following[3] = lax.optimization_barrier(
+        (step_0[2], step_1[2], step_2[2], following[3])
+    )
+    send_0, send_1 = for_x(step_0, core_0), for_x(step_1, core_1)
+    across_0, across_1 = from_x(send_0), from_x(send_1)
+    across_0, _ = lax.optimization_barrier((across_0, send_1))
     far = own_sum(step_0, core_0, across_0).astype(jnp.bfloat16)
-    step_3 = rows(3, (send_1, send_2, far))
+    step_3 = rows(3, far)
     far = over(far, 4)
+    send_2, _ = lax.optimization_barrier((for_x(step_2, core_2), step_3[0]))
+    across_2 = from_x(send_2)
     pair = (own_sum(step_1, core_1, across_1) + far).astype(jnp.bfloat16)
     send_3 = for_x(step_3, step_3[2])
     across_2, _ = lax.optimization_barrier((across_2, (pair, send_3)))

time: 93.8 us -> 95.4 us (1.017)
  waiting for transfers between devices: 25.2 us -> 29.7 us
  other arithmetic: 3.32 us -> 1.41 us
  local copies, waits for them, and re-layouts: 2.87 us -> 1.24 us
  Pallas kernels: 44.1 us -> 45.3 us
    ppermute x15, waiting for transfers between devices: 25.2 us -> 29.7 us  [permute(): lax.ppermute(x, 'ka', [(i, j % size) for i, j in pairs if j is not None])]
    unnamed x10 -> x2, local copies, waits for them, and re-layouts: 1.64 us -> 0.01 us
    pallas_call x4, Pallas kernels: 22.7 us -> 23.8 us  [rows_of(): pl.pallas_call(rows_kernel, out_shape=[jax.ShapeDtypeStruct((width // 4,...]
    convert_element_type x1, other arithmetic: 1.04 us -> 0.07 us  [on_two_by_four(): far = own_sum(step_0, core_0, across_0).astype(jnp.bfloat16)]
  transfers between devices with their start and end apart: 15 -> 15, of which waited for: 6 -> 6; matrix products, arithmetic and copies ran while one was open for 3% -> 1% of each run, Pallas kernels for 44% -> 44%
where the time goes in v8:
time: 95.4 us; the launch traced here: 94.9 us
  Pallas kernels  45.3 us (47%)
  waiting for transfers between devices  29.7 us (31%)
  starting transfers between devices  17.1 us (18%)
  other arithmetic  1.41 us (1%)
  local copies, waits for them, and re-layouts  1.24 us (1%)
    ppermute x15, waiting for transfers between devices, permute(): lax.ppermute(x, 'ka', [(i, j % size) for i, j in pairs if j is not None])  29.7 us
    pallas_call x4, Pallas kernels, rows_of(): pl.pallas_call(rows_kernel, out_shape=[jax.ShapeDtypeStruct((width // 4,...  23.8 us
    ppermute x15, starting transfers between devices, permute(): lax.ppermute(x, 'ka', [(i, j % size) for i, j in pairs if j is not None])  17.1 us
    pallas_call x1, Pallas kernels, products_of(): pl.pallas_call(products_kernel, out_shape=jax.ShapeDtypeStruct((k_local,...  13.4 us
    pallas_call x2, Pallas kernels, turned_pieces(): pl.pallas_call(functools.partial(turn_kernel, first), out_shape=[jax.Shap...  8.1 us
  transfers between devices with their start and end apart: 15, of which 6 were waited for; matrix products, arithmetic and copies ran while one was open for 1% of the time, Pallas kernels for 44%

profile of v8, /device:TPU:0, one launch (start us, length us, event | category | flops | bytes accessed | tf_op | source)
XLA Modules:
  0.0 94.9 jit_solution(6383596108648438997)
XLA Ops:
  0.0 0.0 copy-start
  0.0 0.5 add_xor_fusion.order_ref
  0.5 3.2 %shard_map.56 = bf16[2,256,1024]{2,1,0:T(8,128)(2,1)} custom-call(s32[4]{0:T(128)} %add_xor_fusion.order_ref, bf16[2,1024,1024]{2,1,0:T(8,128)(2,1)} %bitcast.8), custom_call_target="tpu_custom_call" | custom-call | bytes 2097152 | tf_op jit(solution)/shard_map/pallas_call | solution.py:135
  3.7 5.5 %collective-permute-start = (bf16[2,256,1024]{2,1,0:T(8,128)(2,1)}, bf16[2,256,1024]{2,1,0:T(8,128)(2,1)}, u32[]{:S(2)}, u32[]{:S(2)}) collective-permute-start(bf16[2,256,1024]{2,1,0:T(8,128)(2,1)} %shard_map.56), channel_id=1, source_target_pairs={{0,15},{1,0},{2,1},{3,2},{4,3},{5,4},{6,5},{7,6},{8,7},{9,8},{10,9... | collective-permute-start | bytes 3145736 | tf_op jit(solution)/shard_map/ppermute | solution.py:17
  9.2 4.9 %shard_map.58 = (bf16[2,256,1024]{2,1,0:T(8,128)(2,1)}, bf16[2,256,1024]{2,1,0:T(8,128)(2,1)}, bf16[2,256,1024]{2,1,0:T(8,128)(2,1)}) custom-call(s32[4]{0:T(128)} %add_xor_fusion.order_ref, bf16[2,1024,1024]{2,1,0:T(8,128)(2,1)} %bitcast.9), custom_call_target="tpu_custom_call" | custom-call | bytes 6291456 | tf_op jit(solution)/shard_map/pallas_call | solution.py:135
  14.1 0.7 collective-permute-start.2
  14.8 0.1 collective-permute-start.4
  14.9 0.6 collective-permute-start.6
  15.5 0.0 copy-done
  15.5 0.1 add_add_fusion
  15.6 13.4 %shard_map.55 = bf16[2,2,32,32,1024]{4,3,2,1,0:T(8,128)(2,1)} custom-call(s32[2,2]{1,0:T(2,128)} %first_ref.1, bf16[2,32,32,1024]{3,2,1,0:T(8,128)(2,1)} %coeffs_ref.1, bf16[2,2,32,32]{3,2,1,0:T(8,128)(2,1)} %cond_ref.1, bf16[2,2,32,32]{3,2,1,0:T(8,128)(2,1)} %val_ref.1), custom_call_target="tpu_custom_call" | custom-call | flops 6442450944 | bytes 12582912 | tf_op jit(solution)/shard_map/pallas_call | solution.py:90
  29.0 0.1 add_add_fusion.3
  29.0 0.0 collective-permute-done.next_ref
  29.0 6.7 %shard_map.57 = (f32[64,2048]{1,0:T(8,128)S(1)}, f32[64,2048]{1,0:T(8,128)S(1)}, bf16[128,2048]{1,0:T(8,128)(2,1)S(1)}) custom-call(s32[5]{0:T(128)S(1)} %get-tuple-element.32.pick_ref, bf16[2,1024,1024]{2,1,0:T(8,128)(2,1)} %bitcast.10, bf16[2,256,1024]{2,1,0:T(8,128)(2,1)} %collective-permute-done.next_ref, bf16[2,2,1024,1024]{3,2,1,0:T(8,128)(2,1)} %bitcast.14), custom_call_target="tpu_custom_call" | custom-call | flops 2147483648 | bytes 8388608 | tf_op jit(solution)/shard_map/pallas_call | solution.py:217
  35.8 0.0 collective-permute-done.2.next_ref
  35.8 5.7 %shard_map.59 = (f32[64,2048]{1,0:T(8,128)S(1)}, f32[64,2048]{1,0:T(8,128)S(1)}, bf16[128,2048]{1,0:T(8,128)(2,1)S(1)}) custom-call(s32[5]{0:T(128)S(1)} %get-tuple-element.35.pick_ref, bf16[2,1024,1024]{2,1,0:T(8,128)(2,1)} %bitcast.11, bf16[2,256,1024]{2,1,0:T(8,128)(2,1)S(1)} %collective-permute-done.2.next_ref, bf16[2,2,1024,1024]{3,2,1,0:T(8,128)(2,1)} %bitcast.15), custom_call_target="tpu_custom_call" | custom-call | flops 2147483648 | bytes 8388608 | tf_op jit(solution)/shard_map/pallas_call | solution.py:217
  41.5 2.8 %collective-permute-done.4.next_ref = bf16[2,256,1024]{2,1,0:T(8,128)(2,1)S(1)} collective-permute-done((bf16[2,256,1024]{2,1,0:T(8,128)(2,1)}, bf16[2,256,1024]{2,1,0:T(8,128)(2,1)S(1)}, u32[]{:S(2)}, u32[]{:S(2)}) %collective-permute-start.4) | collective-permute-done | bytes 1048608 | tf_op jit(solution)/shard_map/ppermute | solution.py:17
  44.3 5.7 %shard_map.60 = (f32[64,2048]{1,0:T(8,128)S(1)}, f32[64,2048]{1,0:T(8,128)S(1)}, bf16[128,2048]{1,0:T(8,128)(2,1)S(1)}) custom-call(s32[5]{0:T(128)S(1)} %get-tuple-element.40.pick_ref, bf16[2,1024,1024]{2,1,0:T(8,128)(2,1)} %bitcast.12, bf16[2,256,1024]{2,1,0:T(8,128)(2,1)S(1)} %collective-permute-done.4.next_ref, bf16[2,2,1024,1024]{3,2,1,0:T(8,128)(2,1)} %bitcast.16), custom_call_target="tpu_custom_call" | custom-call | flops 2147483648 | bytes 8388608 | tf_op jit(solution)/shard_map/pallas_call | solution.py:217
  50.0 0.1 collective-permute-start.5
  50.1 0.5 collective-permute-start.3
  50.6 0.1 collective-permute-start.1
  50.7 4.9 %collective-permute-done.6.next_ref = bf16[2,256,1024]{2,1,0:T(8,128)(2,1)S(1)} collective-permute-done((bf16[2,256,1024]{2,1,0:T(8,128)(2,1)}, bf16[2,256,1024]{2,1,0:T(8,128)(2,1)S(1)}, u32[]{:S(2)}, u32[]{:S(2)}) %collective-permute-start.6) | collective-permute-done | bytes 1048608 | tf_op jit(solution)/shard_map/ppermute | solution.py:17
  55.5 0.0 collective-permute-done.5
  55.6 0.0 collective-permute-done.3
  55.6 0.0 collective-permute-done.1
  55.6 0.1 collective-permute-start.7
  55.8 2.1 %collective-permute-start.11 = (bf16[64,2048]{1,0:T(8,128)(2,1)S(1)}, bf16[64,2048]{1,0:T(8,128)(2,1)S(1)}, u32[]{:S(2)}, u32[]{:S(2)}) collective-permute-start(bf16[64,2048]{1,0:T(8,128)(2,1)S(1)} %add_convert_fusion.5), channel_id=1, source_target_pairs={{0,2},{1,3},{2,0},{3,1},{4,6},{5,7},{6,4},{7,5},{8,10},{9,11},{10,... | collective-permute-start | bytes 786440 | tf_op jit(solution)/shard_map/ppermute | solution.py:17
  57.8 7.1 %collective-permute-done.7 = bf16[64,2048]{1,0:T(8,128)(2,1)S(1)} collective-permute-done((bf16[64,2048]{1,0:T(8,128)(2,1)S(1)}, bf16[64,2048]{1,0:T(8,128)(2,1)S(1)}, u32[]{:S(2)}, u32[]{:S(2)}) %collective-permute-start.7) | collective-permute-done | bytes 262176 | tf_op jit(solution)/shard_map/ppermute | solution.py:17
  65.0 0.1 add_convert_fusion.4
  65.0 0.1 collective-permute-start.12
  65.1 5.7 %shard_map.61 = (f32[64,2048]{1,0:T(8,128)S(1)}, f32[64,2048]{1,0:T(8,128)S(1)}, bf16[128,2048]{1,0:T(8,128)(2,1)S(1)}) custom-call(s32[5]{0:T(128)S(1)} %get-tuple-element.49.pick_ref, bf16[2,1024,1024]{2,1,0:T(8,128)(2,1)} %bitcast.13, bf16[2,256,1024]{2,1,0:T(8,128)(2,1)S(1)} %collective-permute-done.6.next_ref, bf16[2,2,1024,1024]{3,2,1,0:T(8,128)(2,1)} %bitcast.17), custom_call_target="tpu_custom_call" | custom-call | flops 2147483648 | bytes 8388608 | tf_op jit(solution)/shard_map/pallas_call | solution.py:217
  70.8 0.1 collective-permute-start.8
  70.9 0.1 add_convert_fusion.2
  71.0 0.5 collective-permute-start.10
  71.5 0.0 collective-permute-done.11
  71.5 0.0 collective-permute-done.12
  71.5 0.1 add_convert_fusion.1
  71.6 4.5 %collective-permute-start.14 = (bf16[64,2048]{1,0:T(8,128)(2,1)S(1)}, bf16[64,2048]{1,0:T(8,128)(2,1)S(1)}, u32[]{:S(2)}, u32[]{:S(2)}) collective-permute-start(bf16[64,2048]{1,0:T(8,128)(2,1)S(1)} %add_convert_fusion.1), channel_id=1, source_target_pairs={{0,8},{1,9},{2,10},{3,11},{4,12},{5,13},{6,14},{7,15},{8,0},{9,1},... | collective-permute-start | bytes 786440 | tf_op jit(solution)/shard_map/ppermute | solution.py:17
  76.1 3.7 %collective-permute-done.10 = bf16[64,2048]{1,0:T(8,128)(2,1)S(1)} collective-permute-done((bf16[64,2048]{1,0:T(8,128)(2,1)S(1)}, bf16[64,2048]{1,0:T(8,128)(2,1)S(1)}, u32[]{:S(2)}, u32[]{:S(2)}) %collective-permute-start.10) | collective-permute-done | bytes 262176 | tf_op jit(solution)/shard_map/ppermute | solution.py:17
  79.8 0.0 collective-permute-done.8
  79.9 0.1 add_convert_fusion
  80.0 2.1 %collective-permute-start.13 = (bf16[64,2048]{1,0:T(8,128)(2,1)S(1)}, bf16[64,2048]{1,0:T(8,128)(2,1)S(1)}, u32[]{:S(2)}, u32[]{:S(2)}) collective-permute-start(bf16[64,2048]{1,0:T(8,128)(2,1)S(1)} %add_convert_fusion), channel_id=1, source_target_pairs={{0,4},{1,5},{2,6},{3,7},{4,0},{5,1},{6,2},{7,3},{8,12},{9,13},{10,... | collective-permute-start | bytes 786440 | tf_op jit(solution)/shard_map/ppermute | solution.py:17
  82.1 0.3 collective-permute-start.9
  82.3 5.7 %collective-permute-done.14 = bf16[64,2048]{1,0:T(8,128)(2,1)S(1)} collective-permute-done((bf16[64,2048]{1,0:T(8,128)(2,1)S(1)}, bf16[64,2048]{1,0:T(8,128)(2,1)S(1)}, u32[]{:S(2)}, u32[]{:S(2)}) %collective-permute-start.14) | collective-permute-done | bytes 262176 | tf_op jit(solution)/shard_map/ppermute | solution.py:17
  88.0 5.5 %collective-permute-done.13 = bf16[64,2048]{1,0:T(8,128)(2,1)S(1)} collective-permute-done((bf16[64,2048]{1,0:T(8,128)(2,1)S(1)}, bf16[64,2048]{1,0:T(8,128)(2,1)S(1)}, u32[]{:S(2)}, u32[]{:S(2)}) %collective-permute-start.13) | collective-permute-done | bytes 262176 | tf_op jit(solution)/shard_map/ppermute | solution.py:17
  93.5 0.0 collective-permute-done.9
  93.5 0.2 add_multiply_fusion
  93.7 1.2 %reshape.11 = f32[64,2,1024]{2,1,0:T(2,128)} reshape(f32[64,2048]{1,0:T(8,128)S(1)} %add_multiply_fusion) | data formatting | bytes 1048576 | tf_op jit(solution)/shard_map/reshape | solution.py:303
  (6 shorter events, 0.2 us)
Async XLA Ops:
  0.0 15.5 %copy-start = (s32[2]{0:T(128)S(1)}, s32[2]{0:T(128)}, u32[]{:S(2)}) copy-start(s32[2]{0:T(128)} %param.8) | copy-start | bytes 28
  3.7 25.3 %collective-permute-start = (bf16[2,256,1024]{2,1,0:T(8,128)(2,1)}, bf16[2,256,1024]{2,1,0:T(8,128)(2,1)}, u32[]{:S(2)}, u32[]{:S(2)}) collective-permute-start(bf16[2,256,1024]{2,1,0:T(8,128)(2,1)} %shard_map.56), channel_id=1, source_target_pairs={{0,15},{1,0},{2,1},{3,2},{4,3},{5,4},{6,5},{7,6},{8,7},{9,8},{10,9... | collective-permute-start | bytes 3145736 | tf_op jit(solution)/shard_map/ppermute | solution.py:17
  14.1 21.7 %collective-permute-start.2 = (bf16[2,256,1024]{2,1,0:T(8,128)(2,1)}, bf16[2,256,1024]{2,1,0:T(8,128)(2,1)S(1)}, u32[]{:S(2)}, u32[]{:S(2)}) collective-permute-start(bf16[2,256,1024]{2,1,0:T(8,128)(2,1)} %get-tuple-element.37), channel_id=1, source_target_pairs={{0,15},{1,0},{2,1},{3,2},{4,3},{5,4},{6,5},{7,6},{8,7},{9,8},{10,9... | collective-permute-start | bytes 3145736 | tf_op jit(solution)/shard_map/ppermute | solution.py:17
  14.8 29.5 %collective-permute-start.4 = (bf16[2,256,1024]{2,1,0:T(8,128)(2,1)}, bf16[2,256,1024]{2,1,0:T(8,128)(2,1)S(1)}, u32[]{:S(2)}, u32[]{:S(2)}) collective-permute-start(bf16[2,256,1024]{2,1,0:T(8,128)(2,1)} %get-tuple-element.41), channel_id=1, source_target_pairs={{0,15},{1,0},{2,1},{3,2},{4,3},{5,4},{6,5},{7,6},{8,7},{9,8},{10,9... | collective-permute-start | bytes 3145736 | tf_op jit(solution)/shard_map/ppermute | solution.py:17
  14.9 40.6 %collective-permute-start.6 = (bf16[2,256,1024]{2,1,0:T(8,128)(2,1)}, bf16[2,256,1024]{2,1,0:T(8,128)(2,1)S(1)}, u32[]{:S(2)}, u32[]{:S(2)}) collective-permute-start(bf16[2,256,1024]{2,1,0:T(8,128)(2,1)} %get-tuple-element.43), channel_id=1, source_target_pairs={{0,15},{1,0},{2,1},{3,2},{4,3},{5,4},{6,5},{7,6},{8,7},{9,8},{10,9... | collective-permute-start | bytes 3145736 | tf_op jit(solution)/shard_map/ppermute | solution.py:17
  50.0 5.5 %collective-permute-start.5 = (bf16[128,2048]{1,0:T(8,128)(2,1)S(1)}, bf16[128,2048]{1,0:T(8,128)(2,1)S(1)}, u32[]{:S(2)}, u32[]{:S(2)}) collective-permute-start(bf16[128,2048]{1,0:T(8,128)(2,1)S(1)} %get-tuple-element.42), channel_id=1, source_target_pairs={{0,1},{1,0},{2,3},{3,2},{4,5},{5,4},{6,7},{7,6},{8,9},{9,8},{10,11... | collective-permute-start | bytes 1572872 | tf_op jit(solution)/shard_map/ppermute | solution.py:17
  50.1 5.5 %collective-permute-start.3 = (bf16[128,2048]{1,0:T(8,128)(2,1)S(1)}, bf16[128,2048]{1,0:T(8,128)(2,1)S(1)}, u32[]{:S(2)}, u32[]{:S(2)}) collective-permute-start(bf16[128,2048]{1,0:T(8,128)(2,1)S(1)} %get-tuple-element.38), channel_id=1, source_target_pairs={{0,1},{1,0},{2,3},{3,2},{4,5},{5,4},{6,7},{7,6},{8,9},{9,8},{10,11... | collective-permute-start | bytes 1572872 | tf_op jit(solution)/shard_map/ppermute | solution.py:17
  50.6 5.0 %collective-permute-start.1 = (bf16[128,2048]{1,0:T(8,128)(2,1)S(1)}, bf16[128,2048]{1,0:T(8,128)(2,1)S(1)}, u32[]{:S(2)}, u32[]{:S(2)}) collective-permute-start(bf16[128,2048]{1,0:T(8,128)(2,1)S(1)} %get-tuple-element.34), channel_id=1, source_target_pairs={{0,1},{1,0},{2,3},{3,2},{4,5},{5,4},{6,7},{7,6},{8,9},{9,8},{10,11... | collective-permute-start | bytes 1572872 | tf_op jit(solution)/shard_map/ppermute | solution.py:17
  55.6 9.3 %collective-permute-start.7 = (bf16[64,2048]{1,0:T(8,128)(2,1)S(1)}, bf16[64,2048]{1,0:T(8,128)(2,1)S(1)}, u32[]{:S(2)}, u32[]{:S(2)}) collective-permute-start(bf16[64,2048]{1,0:T(8,128)(2,1)S(1)} %add_convert_fusion.6), channel_id=1, source_target_pairs={{0,2},{1,3},{2,0},{3,1},{4,6},{5,7},{6,4},{7,5},{8,10},{9,11},{10,... | collective-permute-start | bytes 786440 | tf_op jit(solution)/shard_map/ppermute | solution.py:17
  55.8 15.8 %collective-permute-start.11 = (bf16[64,2048]{1,0:T(8,128)(2,1)S(1)}, bf16[64,2048]{1,0:T(8,128)(2,1)S(1)}, u32[]{:S(2)}, u32[]{:S(2)}) collective-permute-start(bf16[64,2048]{1,0:T(8,128)(2,1)S(1)} %add_convert_fusion.5), channel_id=1, source_target_pairs={{0,2},{1,3},{2,0},{3,1},{4,6},{5,7},{6,4},{7,5},{8,10},{9,11},{10,... | collective-permute-start | bytes 786440 | tf_op jit(solution)/shard_map/ppermute | solution.py:17
  65.0 6.5 %collective-permute-start.12 = (bf16[64,2048]{1,0:T(8,128)(2,1)S(1)}, bf16[64,2048]{1,0:T(8,128)(2,1)S(1)}, u32[]{:S(2)}, u32[]{:S(2)}) collective-permute-start(bf16[64,2048]{1,0:T(8,128)(2,1)S(1)} %add_convert_fusion.4), channel_id=1, source_target_pairs={{0,4},{1,5},{2,6},{3,7},{4,0},{5,1},{6,2},{7,3},{8,12},{9,13},{10,... | collective-permute-start | bytes 786440 | tf_op jit(solution)/shard_map/ppermute | solution.py:17
  70.8 9.0 %collective-permute-start.8 = (bf16[128,2048]{1,0:T(8,128)(2,1)S(1)}, bf16[128,2048]{1,0:T(8,128)(2,1)S(1)}, u32[]{:S(2)}, u32[]{:S(2)}) collective-permute-start(bf16[128,2048]{1,0:T(8,128)(2,1)S(1)} %get-tuple-element.52), channel_id=1, source_target_pairs={{0,1},{1,0},{2,3},{3,2},{4,5},{5,4},{6,7},{7,6},{8,9},{9,8},{10,11... | collective-permute-start | bytes 1572872 | tf_op jit(solution)/shard_map/ppermute | solution.py:17
  71.0 8.8 %collective-permute-start.10 = (bf16[64,2048]{1,0:T(8,128)(2,1)S(1)}, bf16[64,2048]{1,0:T(8,128)(2,1)S(1)}, u32[]{:S(2)}, u32[]{:S(2)}) collective-permute-start(bf16[64,2048]{1,0:T(8,128)(2,1)S(1)} %add_convert_fusion.2), channel_id=1, source_target_pairs={{0,2},{1,3},{2,0},{3,1},{4,6},{5,7},{6,4},{7,5},{8,10},{9,11},{10,... | collective-permute-start | bytes 786440 | tf_op jit(solution)/shard_map/ppermute | solution.py:17
  71.6 16.4 %collective-permute-start.14 = (bf16[64,2048]{1,0:T(8,128)(2,1)S(1)}, bf16[64,2048]{1,0:T(8,128)(2,1)S(1)}, u32[]{:S(2)}, u32[]{:S(2)}) collective-permute-start(bf16[64,2048]{1,0:T(8,128)(2,1)S(1)} %add_convert_fusion.1), channel_id=1, source_target_pairs={{0,8},{1,9},{2,10},{3,11},{4,12},{5,13},{6,14},{7,15},{8,0},{9,1},... | collective-permute-start | bytes 786440 | tf_op jit(solution)/shard_map/ppermute | solution.py:17
  80.0 13.6 %collective-permute-start.13 = (bf16[64,2048]{1,0:T(8,128)(2,1)S(1)}, bf16[64,2048]{1,0:T(8,128)(2,1)S(1)}, u32[]{:S(2)}, u32[]{:S(2)}) collective-permute-start(bf16[64,2048]{1,0:T(8,128)(2,1)S(1)} %add_convert_fusion), channel_id=1, source_target_pairs={{0,4},{1,5},{2,6},{3,7},{4,0},{5,1},{6,2},{7,3},{8,12},{9,13},{10,... | collective-permute-start | bytes 786440 | tf_op jit(solution)/shard_map/ppermute | solution.py:17
  82.1 11.5 %collective-permute-start.9 = (bf16[64,2048]{1,0:T(8,128)(2,1)S(1)}, bf16[64,2048]{1,0:T(8,128)(2,1)S(1)}, u32[]{:S(2)}, u32[]{:S(2)}) collective-permute-start(bf16[64,2048]{1,0:T(8,128)(2,1)S(1)} %add_convert_fusion.3), channel_id=1, source_target_pairs={{0,2},{1,3},{2,0},{3,1},{4,6},{5,7},{6,4},{7,5},{8,10},{9,11},{10,... | collective-permute-start | bytes 786440 | tf_op jit(solution)/shard_map/ppermute | solution.py:17

commit v9 on v8

--- a/solution.py
+++ b/solution.py
@@ -111,12 +111,14 @@
     )(band_first, coeffs, g_cond, g_val)
 
 
-def turn_kernel(first, order_ref, coeffs_ref, *refs):
+def turn_kernel(first, coeffs_ref, *refs):
     *out_refs, held, sems = refs
     pieces, k_local, parts, rows, width = held.shape
+    size = lax.axis_size("ka")
+    behind_z = lax.shift_right_logical(lax.rem(lax.axis_index("ka") + size - 1, size), 2)
 
     def copy(i, k, p):
-        columns = pl.ds(pl.multiple_of(order_ref[first + i] * width, width), width)
+        columns = pl.ds(pl.multiple_of((behind_z ^ (3 - first - i)) * width, width), width)
         source = coeffs_ref.at[k, pl.ds(p * rows, rows), columns]
         return pltpu.make_async_copy(source, held.at[i, k, p], sems.at[i, k, p])
 
@@ -129,16 +131,13 @@
         out_refs[i][k, :, p * rows:(p + 1) * rows] = held[i, k, p].T
 
 
-def turned_pieces(flat, order, first, pieces, width):
+def turned_pieces(flat, first, pieces, width):
     k_local, depth, _ = flat.shape
     parts = 2
     return pl.pallas_call(
         functools.partial(turn_kernel, first),
         out_shape=[jax.ShapeDtypeStruct((k_local, width, depth), jnp.bfloat16)] * pieces,
-        in_specs=[
-            pl.BlockSpec(memory_space=pltpu.SMEM),
-            pl.BlockSpec(memory_space=pl.ANY),
-        ],
+        in_specs=[pl.BlockSpec(memory_space=pl.ANY)],
         out_specs=[pl.BlockSpec(memory_space=pltpu.VMEM)] * pieces,
         scratch_shapes=[
             pltpu.VMEM((pieces, k_local, parts, depth // parts, width), jnp.bfloat16),
@@ -148,7 +147,7 @@
         cost_estimate=pl.CostEstimate(
             flops=0, bytes_accessed=4 * pieces * k_local * depth * width, transcendentals=0
         ),
-    )(order, flat)
+    )(flat)
 
 
 def rows_kernel(pick_ref, own_ref, next_ref, right_ref, mine_ref, other_ref, send_ref, *refs):
@@ -175,8 +174,7 @@
     for k in range(k_local):
         copy_own(k).start()
         copy_next(k).start()
-    ahead = 2
-    for t in range(ahead):
+    for t in range(tiles):
         for k in range(k_local):
             copy_right(t, k).start()
     for k in range(k_local):
@@ -194,9 +192,6 @@
     for t in range(tiles):
         for k in range(k_local):
             copy_right(t, k).wait()
-        if t + ahead < tiles:
-            for k in range(k_local):
-                copy_right(t + ahead, k).start()
         right = held[t].reshape(k_local * depth, tile)
         total = jnp.dot(left[...], right, preferred_element_type=jnp.float32)
         parts = total.reshape(2, 2, width // 4, tile)
@@ -242,6 +237,32 @@
     )(pick, own, following, products)
 
 
+def close_kernel(factor, mine_ref, core_ref, across_ref, near_ref, pair_ref, out_ref):
+    _, modes, excitons = out_ref.shape
+    total = mine_ref[...]
+    for ref in (core_ref, across_ref, near_ref, pair_ref):
+        total = total + ref[...].astype(jnp.float32)
+    total = total * factor
+    for m in range(modes):
+        out_ref[:, m, :] = total[:, m * excitons:(m + 1) * excitons]
+
+
+def closed(mine, from_core, across, near, pair, modes, factor):
+    rows, columns = mine.shape
+    step = 16
+    part = pl.BlockSpec((step, columns), lambda i: (i, 0))
+    return pl.pallas_call(
+        functools.partial(close_kernel, factor),
+        out_shape=jax.ShapeDtypeStruct((rows, modes, columns // modes), jnp.float32),
+        grid=(rows // step,),
+        in_specs=[part] * 5,
+        out_specs=pl.BlockSpec((step, modes, columns // modes), lambda i: (i, 0, 0)),
+        cost_estimate=pl.CostEstimate(
+            flops=5 * mine.size, bytes_accessed=16 * mine.size, transcendentals=0
+        ),
+    )(mine, from_core, across, near, pair)
+
+
 def on_two_by_four(coeffs, g_cond, g_val, k_plus_q, band_first, norm_factor):
     k_local, bands_c, bands_v, excitons = coeffs.shape
     modes = g_cond.shape[1]
@@ -251,11 +272,9 @@
     core, x, z = me & 1, me >> 1 & 1, me >> 2
     flat = coeffs.reshape(k_local, bands_c * bands_v, excitons)
 
-    behind_z = (me + size - 1) % size >> 2
-    order = behind_z ^ jnp.arange(3, -1, -1, dtype=jnp.int32)
-    pieces = turned_pieces(flat, order, 0, 1, width)
-    order, _ = lax.optimization_barrier((order, pieces))
-    pieces += turned_pieces(flat, order, 1, 3, width)
+    pieces = turned_pieces(flat, 0, 1, width)
+    rest, _ = lax.optimization_barrier((flat, pieces))
+    pieces += turned_pieces(rest, 1, 3, width)
     following = [permute(piece, lambda i: i - 1) for piece in pieces]
     products = products_of(coeffs, g_cond, g_val, band_first)
     products = products.reshape(k_local, modes, bands_c * bands_v, excitons)
@@ -271,13 +290,13 @@
         return (step[1] + from_core[width // 4:].astype(jnp.float32)).astype(jnp.bfloat16)
 
     def from_x(send):
-        return permute(send, lambda i: i ^ 2).astype(jnp.float32)
-
-    def own_sum(step, from_core, across):
-        return step[0] + from_core[:width // 4].astype(jnp.float32) + across
+        return permute(send, lambda i: i ^ 2)
+
+    def own_sum(mine, from_core, across):
+        return mine + from_core[:width // 4].astype(jnp.float32) + across.astype(jnp.float32)
 
     def over(value, bit):
-        return permute(value, lambda i: i ^ bit).astype(jnp.float32)
+        return permute(value.astype(jnp.bfloat16), lambda i: i ^ bit)
 
     step_0 = rows(0, products)
     step_1 = rows(1, step_0[0])
@@ -285,22 +304,18 @@
     core_0, core_1, core_2, following[3] = lax.optimization_barrier(
         (step_0[2], step_1[2], step_2[2], following[3])
     )
-    send_0, send_1 = for_x(step_0, core_0), for_x(step_1, core_1)
-    across_0, across_1 = from_x(send_0), from_x(send_1)
-    across_0, _ = lax.optimization_barrier((across_0, send_1))
-    far = own_sum(step_0, core_0, across_0).astype(jnp.bfloat16)
-    step_3 = rows(3, far)
+    send_0, send_1, send_2 = for_x(step_0, core_0), for_x(step_1, core_1), for_x(step_2, core_2)
+    across_0, across_1, across_2 = from_x(send_0), from_x(send_1), from_x(send_2)
+    mine_3, other_3, core_3 = rows(3, (send_0, send_1, send_2))
+    far = own_sum(step_0[0], core_0, across_0)
     far = over(far, 4)
-    send_2, _ = lax.optimization_barrier((for_x(step_2, core_2), step_3[0]))
-    across_2 = from_x(send_2)
-    pair = (own_sum(step_1, core_1, across_1) + far).astype(jnp.bfloat16)
-    send_3 = for_x(step_3, step_3[2])
-    across_2, _ = lax.optimization_barrier((across_2, (pair, send_3)))
+    send_3 = for_x((mine_3, other_3), core_3)
+    across_3 = from_x(send_3)
+    pair = own_sum(step_1[0], core_1, across_1) + far.astype(jnp.float32)
+    mine_2, _ = lax.optimization_barrier((step_2[0], pair))
     pair = over(pair, 8)
-    near = over(own_sum(step_2, core_2, across_2).astype(jnp.bfloat16), 4)
-    across_3 = from_x(send_3)
-    total = own_sum(step_3, step_3[2], across_3) + near + pair
-    return (total * norm_factor).reshape(width // 4, modes, excitons)
+    near = over(own_sum(mine_2, core_2, across_2), 4)
+    return closed(mine_3, core_3, across_3, near, pair, modes, norm_factor)
 
 
 def on_any(coeffs, g_cond, g_val, k_plus_q, band_first, norm_factor):

time: 95.4 us -> 92.6 us (0.971)
  starting transfers between devices: 17.1 us -> 14.7 us
  Pallas kernels: 45.3 us -> 47.3 us
  waiting for transfers between devices: 29.7 us -> 28.5 us
    pallas_call x0 -> x1, Pallas kernels: none -> 3.45 us  [closed(): pl.pallas_call(functools.partial(close_kernel, factor), out_shape=jax.Sha...]
    ppermute x15, starting transfers between devices: 17.1 us -> 14.7 us  [permute(): lax.ppermute(x, 'ka', [(i, j % size) for i, j in pairs if j is not None])]
    pallas_call x2, Pallas kernels: 8.1 us -> 6.67 us  [turned_pieces(): pl.pallas_call(functools.partial(turn_kernel, first), out_shape=[jax.Shap...]
    reshape x1 -> x0, local copies, waits for them, and re-layouts: 1.23 us -> none  [on_two_by_four(): return (total * norm_factor).reshape(width // 4, modes, excitons)]
    ppermute x15, waiting for transfers between devices: 29.7 us -> 28.5 us  [permute(): lax.ppermute(x, 'ka', [(i, j % size) for i, j in pairs if j is not None])]
  transfers between devices with their start and end apart: 15 -> 15, of which waited for: 6 -> 6; matrix products, arithmetic and copies ran while one was open for 1% -> 1% of each run, Pallas kernels for 44% -> 45%
where the time goes in v9:
time: 92.6 us; the launch traced here: 92.2 us
  Pallas kernels  47.3 us (51%)
  waiting for transfers between devices  28.5 us (31%)
  starting transfers between devices  14.7 us (16%)
    ppermute x15, waiting for transfers between devices, permute(): lax.ppermute(x, 'ka', [(i, j % size) for i, j in pairs if j is not None])  28.5 us
    pallas_call x4, Pallas kernels, rows_of(): pl.pallas_call(rows_kernel, out_shape=[jax.ShapeDtypeStruct((width // 4,...  23.8 us
    ppermute x15, starting transfers between devices, permute(): lax.ppermute(x, 'ka', [(i, j % size) for i, j in pairs if j is not None])  14.7 us
    pallas_call x1, Pallas kernels, products_of(): pl.pallas_call(products_kernel, out_shape=jax.ShapeDtypeStruct((k_local,...  13.4 us
    pallas_call x2, Pallas kernels, turned_pieces(): pl.pallas_call(functools.partial(turn_kernel, first), out_shape=[jax.Shap...  6.67 us
    pallas_call x1, Pallas kernels, closed(): pl.pallas_call(functools.partial(close_kernel, factor), out_shape=jax.Sha...  3.45 us
  transfers between devices with their start and end apart: 15, of which 6 were waited for; matrix products, arithmetic and copies ran while one was open for 1% of the time, Pallas kernels for 45%

profile of v9, /device:TPU:0, one launch (start us, length us, event | category | flops | bytes accessed | tf_op | source)
XLA Modules:
  0.0 92.2 jit_solution(16110114821794708317)
XLA Ops:
  0.0 2.5 %shard_map.56 = bf16[2,256,1024]{2,1,0:T(8,128)(2,1)} custom-call(bf16[2,1024,1024]{2,1,0:T(8,128)(2,1)} %bitcast.8), custom_call_target="tpu_custom_call" | custom-call | bytes 2097152 | tf_op jit(solution)/shard_map/pallas_call | solution.py:137
  2.5 5.5 %collective-permute-start = (bf16[2,256,1024]{2,1,0:T(8,128)(2,1)}, bf16[2,256,1024]{2,1,0:T(8,128)(2,1)}, u32[]{:S(2)}, u32[]{:S(2)}) collective-permute-start(bf16[2,256,1024]{2,1,0:T(8,128)(2,1)} %shard_map.56), channel_id=1, source_target_pairs={{0,15},{1,0},{2,1},{3,2},{4,3},{5,4},{6,5},{7,6},{8,7},{9,8},{10,9... | collective-permute-start | bytes 3145736 | tf_op jit(solution)/shard_map/ppermute | solution.py:17
  8.0 4.2 %shard_map.58 = (bf16[2,256,1024]{2,1,0:T(8,128)(2,1)}, bf16[2,256,1024]{2,1,0:T(8,128)(2,1)}, bf16[2,256,1024]{2,1,0:T(8,128)(2,1)}) custom-call(bf16[2,1024,1024]{2,1,0:T(8,128)(2,1)} %bitcast.9), custom_call_target="tpu_custom_call" | custom-call | bytes 6291456 | tf_op jit(solution)/shard_map/pallas_call | solution.py:137
  12.2 0.7 collective-permute-start.2
  12.9 0.1 collective-permute-start.4
  13.0 0.6 collective-permute-start.6
  13.5 0.0 copy-done.5
  13.6 0.1 add_add_fusion.3
  13.6 13.4 %shard_map.55 = bf16[2,2,32,32,1024]{4,3,2,1,0:T(8,128)(2,1)} custom-call(s32[2,2]{1,0:T(2,128)} %first_ref.1, bf16[2,32,32,1024]{3,2,1,0:T(8,128)(2,1)} %coeffs_ref.1, bf16[2,2,32,32]{3,2,1,0:T(8,128)(2,1)} %cond_ref.1, bf16[2,2,32,32]{3,2,1,0:T(8,128)(2,1)} %val_ref.1), custom_call_target="tpu_custom_call" | custom-call | flops 6442450944 | bytes 12582912 | tf_op jit(solution)/shard_map/pallas_call | solution.py:90
  27.0 0.1 add_add_fusion.2
  27.1 0.0 collective-permute-done.next_ref
  27.1 7.4 %shard_map.57 = (f32[64,2048]{1,0:T(8,128)S(1)}, f32[64,2048]{1,0:T(8,128)S(1)}, bf16[128,2048]{1,0:T(8,128)(2,1)S(1)}) custom-call(s32[5]{0:T(128)S(1)} %get-tuple-element.30.pick_ref, bf16[2,1024,1024]{2,1,0:T(8,128)(2,1)} %bitcast.10, bf16[2,256,1024]{2,1,0:T(8,128)(2,1)} %collective-permute-done.next_ref, bf16[2,2,1024,1024]{3,2,1,0:T(8,128)(2,1)} %bitcast.14), custom_call_target="tpu_custom_call" | custom-call | flops 2147483648 | bytes 8388608 | tf_op jit(solution)/shard_map/pallas_call | solution.py:212
  34.5 0.0 collective-permute-done.2.next_ref
  34.5 5.5 %shard_map.59 = (f32[64,2048]{1,0:T(8,128)S(1)}, f32[64,2048]{1,0:T(8,128)S(1)}, bf16[128,2048]{1,0:T(8,128)(2,1)S(1)}) custom-call(s32[5]{0:T(128)S(1)} %get-tuple-element.34.pick_ref, bf16[2,1024,1024]{2,1,0:T(8,128)(2,1)} %bitcast.11, bf16[2,256,1024]{2,1,0:T(8,128)(2,1)S(1)} %collective-permute-done.2.next_ref, bf16[2,2,1024,1024]{3,2,1,0:T(8,128)(2,1)} %bitcast.15), custom_call_target="tpu_custom_call" | custom-call | flops 2147483648 | bytes 8388608 | tf_op jit(solution)/shard_map/pallas_call | solution.py:212
  40.0 3.1 %collective-permute-done.4.next_ref = bf16[2,256,1024]{2,1,0:T(8,128)(2,1)S(1)} collective-permute-done((bf16[2,256,1024]{2,1,0:T(8,128)(2,1)}, bf16[2,256,1024]{2,1,0:T(8,128)(2,1)S(1)}, u32[]{:S(2)}, u32[]{:S(2)}) %collective-permute-start.4) | collective-permute-done | bytes 1048608 | tf_op jit(solution)/shard_map/ppermute | solution.py:17
  43.1 5.5 %shard_map.60 = (f32[64,2048]{1,0:T(8,128)S(1)}, f32[64,2048]{1,0:T(8,128)S(1)}, bf16[128,2048]{1,0:T(8,128)(2,1)S(1)}) custom-call(s32[5]{0:T(128)S(1)} %get-tuple-element.39.pick_ref, bf16[2,1024,1024]{2,1,0:T(8,128)(2,1)} %bitcast.12, bf16[2,256,1024]{2,1,0:T(8,128)(2,1)S(1)} %collective-permute-done.4.next_ref, bf16[2,2,1024,1024]{3,2,1,0:T(8,128)(2,1)} %bitcast.16), custom_call_target="tpu_custom_call" | custom-call | flops 2147483648 | bytes 8388608 | tf_op jit(solution)/shard_map/pallas_call | solution.py:212
  48.5 0.1 collective-permute-start.5
  48.6 0.5 collective-permute-start.3
  49.1 0.1 collective-permute-start.1
  49.2 5.1 %collective-permute-done.6.next_ref = bf16[2,256,1024]{2,1,0:T(8,128)(2,1)S(1)} collective-permute-done((bf16[2,256,1024]{2,1,0:T(8,128)(2,1)}, bf16[2,256,1024]{2,1,0:T(8,128)(2,1)S(1)}, u32[]{:S(2)}, u32[]{:S(2)}) %collective-permute-start.6) | collective-permute-done | bytes 1048608 | tf_op jit(solution)/shard_map/ppermute | solution.py:17
  54.3 0.0 collective-permute-done.5
  54.3 0.0 collective-permute-done.3
  54.3 0.0 collective-permute-done.1
  54.4 0.1 collective-permute-start.10
  54.5 2.1 %collective-permute-start.9 = (bf16[64,2048]{1,0:T(8,128)(2,1)S(1)}, bf16[64,2048]{1,0:T(8,128)(2,1)S(1)}, u32[]{:S(2)}, u32[]{:S(2)}) collective-permute-start(bf16[64,2048]{1,0:T(8,128)(2,1)S(1)} %add_convert_fusion.4), channel_id=1, source_target_pairs={{0,2},{1,3},{2,0},{3,1},{4,6},{5,7},{6,4},{7,5},{8,10},{9,11},{10,... | collective-permute-start | bytes 786440 | tf_op jit(solution)/shard_map/ppermute | solution.py:17
  56.6 7.1 %collective-permute-done.10 = bf16[64,2048]{1,0:T(8,128)(2,1)S(1)} collective-permute-done((bf16[64,2048]{1,0:T(8,128)(2,1)S(1)}, bf16[64,2048]{1,0:T(8,128)(2,1)S(1)}, u32[]{:S(2)}, u32[]{:S(2)}) %collective-permute-start.10) | collective-permute-done | bytes 262176 | tf_op jit(solution)/shard_map/ppermute | solution.py:17
  63.7 0.1 add_convert_fusion.1
  63.8 0.1 collective-permute-start.11
  63.9 0.1 collective-permute-start.12
  64.0 5.5 %shard_map.61 = (f32[64,2048]{1,0:T(8,128)S(1)}, f32[64,2048]{1,0:T(8,128)S(1)}, bf16[128,2048]{1,0:T(8,128)(2,1)S(1)}) custom-call(s32[5]{0:T(128)S(1)} %get-tuple-element.48.pick_ref, bf16[2,1024,1024]{2,1,0:T(8,128)(2,1)} %bitcast.13, bf16[2,256,1024]{2,1,0:T(8,128)(2,1)S(1)} %collective-permute-done.6.next_ref, bf16[2,2,1024,1024]{3,2,1,0:T(8,128)(2,1)} %bitcast.17), custom_call_target="tpu_custom_call" | custom-call | flops 2147483648 | bytes 8388608 | tf_op jit(solution)/shard_map/pallas_call | solution.py:212
  69.5 0.3 collective-permute-start.7
  69.7 0.0 collective-permute-done.9
  69.7 0.5 collective-permute-done.11
  70.2 0.1 convert_add_fusion
  70.3 4.0 %collective-permute-start.14 = (bf16[64,2048]{1,0:T(8,128)(2,1)S(1)}, bf16[64,2048]{1,0:T(8,128)(2,1)S(1)}, u32[]{:S(2)}, u32[]{:S(2)}) collective-permute-start(bf16[64,2048]{1,0:T(8,128)(2,1)S(1)} %convert_add_fusion), channel_id=1, source_target_pairs={{0,8},{1,9},{2,10},{3,11},{4,12},{5,13},{6,14},{7,15},{8,0},{9,1},... | collective-permute-start | bytes 786440 | tf_op jit(solution)/shard_map/ppermute | solution.py:17
  74.3 0.0 collective-permute-done.12
  74.3 0.1 add_convert_fusion
  74.4 0.4 collective-permute-start.13
  74.8 0.0 collective-permute-done.7.core_ref
  74.8 0.1 add_convert_fusion.2
  74.8 0.0 copy-done
  74.9 0.4 collective-permute-start.8
  75.2 11.3 %collective-permute-done.14.pair_ref = bf16[64,2048]{1,0:T(8,128)(2,1)S(1)} collective-permute-done((bf16[64,2048]{1,0:T(8,128)(2,1)S(1)}, bf16[64,2048]{1,0:T(8,128)(2,1)S(1)}, u32[]{:S(2)}, u32[]{:S(2)}) %collective-permute-start.14) | collective-permute-done | bytes 262176 | tf_op jit(solution)/shard_map/ppermute | solution.py:17
  86.5 1.4 %collective-permute-done.13.near_ref = bf16[64,2048]{1,0:T(8,128)(2,1)S(1)} collective-permute-done((bf16[64,2048]{1,0:T(8,128)(2,1)S(1)}, bf16[64,2048]{1,0:T(8,128)(2,1)S(1)}, u32[]{:S(2)}, u32[]{:S(2)}) %collective-permute-start.13) | collective-permute-done | bytes 262176 | tf_op jit(solution)/shard_map/ppermute | solution.py:17
  87.9 0.0 collective-permute-done.8.across_ref
  88.0 0.7 copy-done.3
  88.6 0.1 copy-done.4
  88.8 3.4 %shard_map.62 = f32[64,2,1024]{2,1,0:T(2,128)} custom-call(f32[64,2048]{1,0:T(8,128)} %copy-done, bf16[128,2048]{1,0:T(8,128)(2,1)} %copy-done.1, bf16[64,2048]{1,0:T(8,128)(2,1)} %copy-done.4, bf16[64,2048]{1,0:T(8,128)(2,1)} %copy-done.3, bf16[64,2048]{1,0:T(8,128)(2,1)} %copy-done.2), custom_call_target="tpu_custom_call" | custom-call | flops 655360 | bytes 2097152 | tf_op jit(solution)/shard_map/pallas_call | solution.py:254
  (12 shorter events, 0.2 us)
Async XLA Ops:
  0.0 13.5 %copy-start.5 = (s32[2]{0:T(128)S(1)}, s32[2]{0:T(128)}, u32[]{:S(2)}) copy-start(s32[2]{0:T(128)} %param.8) | copy-start | bytes 28
  2.5 24.6 %collective-permute-start = (bf16[2,256,1024]{2,1,0:T(8,128)(2,1)}, bf16[2,256,1024]{2,1,0:T(8,128)(2,1)}, u32[]{:S(2)}, u32[]{:S(2)}) collective-permute-start(bf16[2,256,1024]{2,1,0:T(8,128)(2,1)} %shard_map.56), channel_id=1, source_target_pairs={{0,15},{1,0},{2,1},{3,2},{4,3},{5,4},{6,5},{7,6},{8,7},{9,8},{10,9... | collective-permute-start | bytes 3145736 | tf_op jit(solution)/shard_map/ppermute | solution.py:17
  12.2 22.4 %collective-permute-start.2 = (bf16[2,256,1024]{2,1,0:T(8,128)(2,1)}, bf16[2,256,1024]{2,1,0:T(8,128)(2,1)S(1)}, u32[]{:S(2)}, u32[]{:S(2)}) collective-permute-start(bf16[2,256,1024]{2,1,0:T(8,128)(2,1)} %get-tuple-element.36), channel_id=1, source_target_pairs={{0,15},{1,0},{2,1},{3,2},{4,3},{5,4},{6,5},{7,6},{8,7},{9,8},{10,9... | collective-permute-start | bytes 3145736 | tf_op jit(solution)/shard_map/ppermute | solution.py:17
  12.9 30.2 %collective-permute-start.4 = (bf16[2,256,1024]{2,1,0:T(8,128)(2,1)}, bf16[2,256,1024]{2,1,0:T(8,128)(2,1)S(1)}, u32[]{:S(2)}, u32[]{:S(2)}) collective-permute-start(bf16[2,256,1024]{2,1,0:T(8,128)(2,1)} %get-tuple-element.40), channel_id=1, source_target_pairs={{0,15},{1,0},{2,1},{3,2},{4,3},{5,4},{6,5},{7,6},{8,7},{9,8},{10,9... | collective-permute-start | bytes 3145736 | tf_op jit(solution)/shard_map/ppermute | solution.py:17
  13.0 41.4 %collective-permute-start.6 = (bf16[2,256,1024]{2,1,0:T(8,128)(2,1)}, bf16[2,256,1024]{2,1,0:T(8,128)(2,1)S(1)}, u32[]{:S(2)}, u32[]{:S(2)}) collective-permute-start(bf16[2,256,1024]{2,1,0:T(8,128)(2,1)} %get-tuple-element.42), channel_id=1, source_target_pairs={{0,15},{1,0},{2,1},{3,2},{4,3},{5,4},{6,5},{7,6},{8,7},{9,8},{10,9... | collective-permute-start | bytes 3145736 | tf_op jit(solution)/shard_map/ppermute | solution.py:17
  48.5 5.8 %collective-permute-start.5 = (bf16[128,2048]{1,0:T(8,128)(2,1)S(1)}, bf16[128,2048]{1,0:T(8,128)(2,1)S(1)}, u32[]{:S(2)}, u32[]{:S(2)}) collective-permute-start(bf16[128,2048]{1,0:T(8,128)(2,1)S(1)} %get-tuple-element.41), channel_id=1, source_target_pairs={{0,1},{1,0},{2,3},{3,2},{4,5},{5,4},{6,7},{7,6},{8,9},{9,8},{10,11... | collective-permute-start | bytes 1572872 | tf_op jit(solution)/shard_map/ppermute | solution.py:17
  48.6 5.7 %collective-permute-start.3 = (bf16[128,2048]{1,0:T(8,128)(2,1)S(1)}, bf16[128,2048]{1,0:T(8,128)(2,1)S(1)}, u32[]{:S(2)}, u32[]{:S(2)}) collective-permute-start(bf16[128,2048]{1,0:T(8,128)(2,1)S(1)} %get-tuple-element.37), channel_id=1, source_target_pairs={{0,1},{1,0},{2,3},{3,2},{4,5},{5,4},{6,7},{7,6},{8,9},{9,8},{10,11... | collective-permute-start | bytes 1572872 | tf_op jit(solution)/shard_map/ppermute | solution.py:17
  49.1 5.2 %collective-permute-start.1 = (bf16[128,2048]{1,0:T(8,128)(2,1)S(1)}, bf16[128,2048]{1,0:T(8,128)(2,1)S(1)}, u32[]{:S(2)}, u32[]{:S(2)}) collective-permute-start(bf16[128,2048]{1,0:T(8,128)(2,1)S(1)} %get-tuple-element.32), channel_id=1, source_target_pairs={{0,1},{1,0},{2,3},{3,2},{4,5},{5,4},{6,7},{7,6},{8,9},{9,8},{10,11... | collective-permute-start | bytes 1572872 | tf_op jit(solution)/shard_map/ppermute | solution.py:17
  54.4 9.3 %collective-permute-start.10 = (bf16[64,2048]{1,0:T(8,128)(2,1)S(1)}, bf16[64,2048]{1,0:T(8,128)(2,1)S(1)}, u32[]{:S(2)}, u32[]{:S(2)}) collective-permute-start(bf16[64,2048]{1,0:T(8,128)(2,1)S(1)} %add_convert_fusion.5), channel_id=1, source_target_pairs={{0,2},{1,3},{2,0},{3,1},{4,6},{5,7},{6,4},{7,5},{8,10},{9,11},{10,... | collective-permute-start | bytes 786440 | tf_op jit(solution)/shard_map/ppermute | solution.py:17
  54.5 15.2 %collective-permute-start.9 = (bf16[64,2048]{1,0:T(8,128)(2,1)S(1)}, bf16[64,2048]{1,0:T(8,128)(2,1)S(1)}, u32[]{:S(2)}, u32[]{:S(2)}) collective-permute-start(bf16[64,2048]{1,0:T(8,128)(2,1)S(1)} %add_convert_fusion.4), channel_id=1, source_target_pairs={{0,2},{1,3},{2,0},{3,1},{4,6},{5,7},{6,4},{7,5},{8,10},{9,11},{10,... | collective-permute-start | bytes 786440 | tf_op jit(solution)/shard_map/ppermute | solution.py:17
  63.8 6.4 %collective-permute-start.11 = (bf16[64,2048]{1,0:T(8,128)(2,1)S(1)}, bf16[64,2048]{1,0:T(8,128)(2,1)S(1)}, u32[]{:S(2)}, u32[]{:S(2)}) collective-permute-start(bf16[64,2048]{1,0:T(8,128)(2,1)S(1)} %add_convert_fusion.1), channel_id=1, source_target_pairs={{0,4},{1,5},{2,6},{3,7},{4,0},{5,1},{6,2},{7,3},{8,12},{9,13},{10,... | collective-permute-start | bytes 786440 | tf_op jit(solution)/shard_map/ppermute | solution.py:17
  63.9 10.4 %collective-permute-start.12 = (bf16[64,2048]{1,0:T(8,128)(2,1)S(1)}, bf16[64,2048]{1,0:T(8,128)(2,1)S(1)}, u32[]{:S(2)}, u32[]{:S(2)}) collective-permute-start(bf16[64,2048]{1,0:T(8,128)(2,1)S(1)} %add_convert_fusion.3), channel_id=1, source_target_pairs={{0,2},{1,3},{2,0},{3,1},{4,6},{5,7},{6,4},{7,5},{8,10},{9,11},{10,... | collective-permute-start | bytes 786440 | tf_op jit(solution)/shard_map/ppermute | solution.py:17
  69.5 5.4 %copy-start = (f32[64,2048]{1,0:T(8,128)}, f32[64,2048]{1,0:T(8,128)S(1)}, u32[]{:S(2)}) copy-start(f32[64,2048]{1,0:T(8,128)S(1)} %get-tuple-element.50.mine_ref) | copy-start | bytes 1572868
  69.5 5.3 %collective-permute-start.7 = (bf16[128,2048]{1,0:T(8,128)(2,1)S(1)}, bf16[128,2048]{1,0:T(8,128)(2,1)S(1)}, u32[]{:S(2)}, u32[]{:S(2)}) collective-permute-start(bf16[128,2048]{1,0:T(8,128)(2,1)S(1)} %get-tuple-element.51), channel_id=1, source_target_pairs={{0,1},{1,0},{2,3},{3,2},{4,5},{5,4},{6,7},{7,6},{8,9},{9,8},{10,11... | collective-permute-start | bytes 1572872 | tf_op jit(solution)/shard_map/ppermute | solution.py:17
  70.3 16.2 %collective-permute-start.14 = (bf16[64,2048]{1,0:T(8,128)(2,1)S(1)}, bf16[64,2048]{1,0:T(8,128)(2,1)S(1)}, u32[]{:S(2)}, u32[]{:S(2)}) collective-permute-start(bf16[64,2048]{1,0:T(8,128)(2,1)S(1)} %convert_add_fusion), channel_id=1, source_target_pairs={{0,8},{1,9},{2,10},{3,11},{4,12},{5,13},{6,14},{7,15},{8,0},{9,1},... | collective-permute-start | bytes 786440 | tf_op jit(solution)/shard_map/ppermute | solution.py:17
  74.4 13.5 %collective-permute-start.13 = (bf16[64,2048]{1,0:T(8,128)(2,1)S(1)}, bf16[64,2048]{1,0:T(8,128)(2,1)S(1)}, u32[]{:S(2)}, u32[]{:S(2)}) collective-permute-start(bf16[64,2048]{1,0:T(8,128)(2,1)S(1)} %add_convert_fusion), channel_id=1, source_target_pairs={{0,4},{1,5},{2,6},{3,7},{4,0},{5,1},{6,2},{7,3},{8,12},{9,13},{10,... | collective-permute-start | bytes 786440 | tf_op jit(solution)/shard_map/ppermute | solution.py:17
  74.8 13.2 %copy-start.1 = (bf16[128,2048]{1,0:T(8,128)(2,1)}, bf16[128,2048]{1,0:T(8,128)(2,1)S(1)}, u32[]{:S(2)}) copy-start(bf16[128,2048]{1,0:T(8,128)(2,1)S(1)} %collective-permute-done.7.core_ref) | copy-start | bytes 1572868
  74.9 13.1 %collective-permute-start.8 = (bf16[64,2048]{1,0:T(8,128)(2,1)S(1)}, bf16[64,2048]{1,0:T(8,128)(2,1)S(1)}, u32[]{:S(2)}, u32[]{:S(2)}) collective-permute-start(bf16[64,2048]{1,0:T(8,128)(2,1)S(1)} %add_convert_fusion.2), channel_id=1, source_target_pairs={{0,2},{1,3},{2,0},{3,1},{4,6},{5,7},{6,4},{7,5},{8,10},{9,11},{10,... | collective-permute-start | bytes 786440 | tf_op jit(solution)/shard_map/ppermute | solution.py:17
  86.5 1.4 %copy-start.2 = (bf16[64,2048]{1,0:T(8,128)(2,1)}, bf16[64,2048]{1,0:T(8,128)(2,1)S(1)}, u32[]{:S(2)}) copy-start(bf16[64,2048]{1,0:T(8,128)(2,1)S(1)} %collective-permute-done.14.pair_ref) | copy-start | bytes 786436
  87.9 0.7 copy-start.3
  87.9 0.8 copy-start.4

commit v10 on v9

--- a/solution.py
+++ b/solution.py
@@ -237,32 +237,6 @@
     )(pick, own, following, products)
 
 
-def close_kernel(factor, mine_ref, core_ref, across_ref, near_ref, pair_ref, out_ref):
-    _, modes, excitons = out_ref.shape
-    total = mine_ref[...]
-    for ref in (core_ref, across_ref, near_ref, pair_ref):
-        total = total + ref[...].astype(jnp.float32)
-    total = total * factor
-    for m in range(modes):
-        out_ref[:, m, :] = total[:, m * excitons:(m + 1) * excitons]
-
-
-def closed(mine, from_core, across, near, pair, modes, factor):
-    rows, columns = mine.shape
-    step = 16
-    part = pl.BlockSpec((step, columns), lambda i: (i, 0))
-    return pl.pallas_call(
-        functools.partial(close_kernel, factor),
-        out_shape=jax.ShapeDtypeStruct((rows, modes, columns // modes), jnp.float32),
-        grid=(rows // step,),
-        in_specs=[part] * 5,
-        out_specs=pl.BlockSpec((step, modes, columns // modes), lambda i: (i, 0, 0)),
-        cost_estimate=pl.CostEstimate(
-            flops=5 * mine.size, bytes_accessed=16 * mine.size, transcendentals=0
-        ),
-    )(mine, from_core, across, near, pair)
-
-
 def on_two_by_four(coeffs, g_cond, g_val, k_plus_q, band_first, norm_factor):
     k_local, bands_c, bands_v, excitons = coeffs.shape
     modes = g_cond.shape[1]
@@ -307,7 +281,8 @@
     send_0, send_1, send_2 = for_x(step_0, core_0), for_x(step_1, core_1), for_x(step_2, core_2)
     across_0, across_1, across_2 = from_x(send_0), from_x(send_1), from_x(send_2)
     mine_3, other_3, core_3 = rows(3, (send_0, send_1, send_2))
-    far = own_sum(step_0[0], core_0, across_0)
+    mine_0, _ = lax.optimization_barrier((step_0[0], mine_3))
+    far = own_sum(mine_0, core_0, across_0)
     far = over(far, 4)
     send_3 = for_x((mine_3, other_3), core_3)
     across_3 = from_x(send_3)
@@ -315,7 +290,8 @@
     mine_2, _ = lax.optimization_barrier((step_2[0], pair))
     pair = over(pair, 8)
     near = over(own_sum(mine_2, core_2, across_2), 4)
-    return closed(mine_3, core_3, across_3, near, pair, modes, norm_factor)
+    total = own_sum(mine_3, core_3, across_3) + near.astype(jnp.float32) + pair.astype(jnp.float32)
+    return (total * norm_factor).reshape(width // 4, modes, excitons)
 
 
 def on_any(coeffs, g_cond, g_val, k_plus_q, band_first, norm_factor):

time: 92.6 us -> 87.3 us (0.943)
  Pallas kernels: 47.3 us -> 44.3 us
  starting transfers between devices: 14.7 us -> 11.9 us
    pallas_call x1 -> x0, Pallas kernels: 3.45 us -> none  [closed(): pl.pallas_call(functools.partial(close_kernel, factor), out_shape=jax.Sha...]
    ppermute x15, starting transfers between devices: 14.7 us -> 11.9 us  [permute(): lax.ppermute(x, 'ka', [(i, j % size) for i, j in pairs if j is not None])]
    reshape x0 -> x1, local copies, waits for them, and re-layouts: none -> 1.23 us  [on_two_by_four(): return (total * norm_factor).reshape(width // 4, modes, excitons)]
  transfers between devices with their start and end apart: 15 -> 15, of which waited for: 6 -> 8; matrix products, arithmetic and copies ran while one was open for 1% -> 1% of each run, Pallas kernels for 45% -> 48%
where the time goes in v10:
time: 87.3 us; the launch traced here: 87 us
  Pallas kernels  44.3 us (51%)
  waiting for transfers between devices  28.6 us (33%)
  starting transfers between devices  11.9 us (14%)
  local copies, waits for them, and re-layouts  1.24 us (1%)
    ppermute x15, waiting for transfers between devices, permute(): lax.ppermute(x, 'ka', [(i, j % size) for i, j in pairs if j is not None])  28.6 us
    pallas_call x4, Pallas kernels, rows_of(): pl.pallas_call(rows_kernel, out_shape=[jax.ShapeDtypeStruct((width // 4,...  24.2 us
    pallas_call x1, Pallas kernels, products_of(): pl.pallas_call(products_kernel, out_shape=jax.ShapeDtypeStruct((k_local,...  13.4 us
    ppermute x15, starting transfers between devices, permute(): lax.ppermute(x, 'ka', [(i, j % size) for i, j in pairs if j is not None])  11.9 us
    pallas_call x2, Pallas kernels, turned_pieces(): pl.pallas_call(functools.partial(turn_kernel, first), out_shape=[jax.Shap...  6.78 us
  transfers between devices with their start and end apart: 15, of which 8 were waited for; matrix products, arithmetic and copies ran while one was open for 1% of the time, Pallas kernels for 48%

profile of v10, /device:TPU:0, one launch (start us, length us, event | category | flops | bytes accessed | tf_op | source)
XLA Modules:
  0.0 87.0 jit_solution(1504028282699730872)
XLA Ops:
  0.0 0.0 copy-start
  0.0 2.6 %shard_map.56 = bf16[2,256,1024]{2,1,0:T(8,128)(2,1)} custom-call(bf16[2,1024,1024]{2,1,0:T(8,128)(2,1)} %bitcast.8), custom_call_target="tpu_custom_call" | custom-call | bytes 2097152 | tf_op jit(solution)/shard_map/pallas_call | solution.py:137
  2.6 5.5 %collective-permute-start = (bf16[2,256,1024]{2,1,0:T(8,128)(2,1)}, bf16[2,256,1024]{2,1,0:T(8,128)(2,1)}, u32[]{:S(2)}, u32[]{:S(2)}) collective-permute-start(bf16[2,256,1024]{2,1,0:T(8,128)(2,1)} %shard_map.56), channel_id=1, source_target_pairs={{0,15},{1,0},{2,1},{3,2},{4,3},{5,4},{6,5},{7,6},{8,7},{9,8},{10,9... | collective-permute-start | bytes 3145736 | tf_op jit(solution)/shard_map/ppermute | solution.py:17
  8.0 4.2 %shard_map.58 = (bf16[2,256,1024]{2,1,0:T(8,128)(2,1)}, bf16[2,256,1024]{2,1,0:T(8,128)(2,1)}, bf16[2,256,1024]{2,1,0:T(8,128)(2,1)}) custom-call(bf16[2,1024,1024]{2,1,0:T(8,128)(2,1)} %bitcast.9), custom_call_target="tpu_custom_call" | custom-call | bytes 6291456 | tf_op jit(solution)/shard_map/pallas_call | solution.py:137
  12.3 0.7 collective-permute-start.2
  13.0 0.1 collective-permute-start.4
  13.1 0.6 collective-permute-start.6
  13.6 0.0 copy-done
  13.7 0.1 add_add_fusion
  13.7 13.4 %shard_map.55 = bf16[2,2,32,32,1024]{4,3,2,1,0:T(8,128)(2,1)} custom-call(s32[2,2]{1,0:T(2,128)} %first_ref.1, bf16[2,32,32,1024]{3,2,1,0:T(8,128)(2,1)} %coeffs_ref.1, bf16[2,2,32,32]{3,2,1,0:T(8,128)(2,1)} %cond_ref.1, bf16[2,2,32,32]{3,2,1,0:T(8,128)(2,1)} %val_ref.1), custom_call_target="tpu_custom_call" | custom-call | flops 6442450944 | bytes 12582912 | tf_op jit(solution)/shard_map/pallas_call | solution.py:90
  27.1 0.1 add_add_fusion.3
  27.2 0.0 collective-permute-done.next_ref
  27.2 7.7 %shard_map.57 = (f32[64,2048]{1,0:T(8,128)S(1)}, f32[64,2048]{1,0:T(8,128)S(1)}, bf16[128,2048]{1,0:T(8,128)(2,1)S(1)}) custom-call(s32[5]{0:T(128)S(1)} %get-tuple-element.31.pick_ref, bf16[2,1024,1024]{2,1,0:T(8,128)(2,1)} %bitcast.10, bf16[2,256,1024]{2,1,0:T(8,128)(2,1)} %collective-permute-done.next_ref, bf16[2,2,1024,1024]{3,2,1,0:T(8,128)(2,1)} %bitcast.14), custom_call_target="tpu_custom_call" | custom-call | flops 2147483648 | bytes 8388608 | tf_op jit(solution)/shard_map/pallas_call | solution.py:212
  34.9 0.0 collective-permute-done.2.next_ref
  34.9 5.5 %shard_map.59 = (f32[64,2048]{1,0:T(8,128)S(1)}, f32[64,2048]{1,0:T(8,128)S(1)}, bf16[128,2048]{1,0:T(8,128)(2,1)S(1)}) custom-call(s32[5]{0:T(128)S(1)} %get-tuple-element.35.pick_ref, bf16[2,1024,1024]{2,1,0:T(8,128)(2,1)} %bitcast.11, bf16[2,256,1024]{2,1,0:T(8,128)(2,1)S(1)} %collective-permute-done.2.next_ref, bf16[2,2,1024,1024]{3,2,1,0:T(8,128)(2,1)} %bitcast.15), custom_call_target="tpu_custom_call" | custom-call | flops 2147483648 | bytes 8388608 | tf_op jit(solution)/shard_map/pallas_call | solution.py:212
  40.4 2.7 %collective-permute-done.4.next_ref = bf16[2,256,1024]{2,1,0:T(8,128)(2,1)S(1)} collective-permute-done((bf16[2,256,1024]{2,1,0:T(8,128)(2,1)}, bf16[2,256,1024]{2,1,0:T(8,128)(2,1)S(1)}, u32[]{:S(2)}, u32[]{:S(2)}) %collective-permute-start.4) | collective-permute-done | bytes 1048608 | tf_op jit(solution)/shard_map/ppermute | solution.py:17
  43.1 5.5 %shard_map.60 = (f32[64,2048]{1,0:T(8,128)S(1)}, f32[64,2048]{1,0:T(8,128)S(1)}, bf16[128,2048]{1,0:T(8,128)(2,1)S(1)}) custom-call(s32[5]{0:T(128)S(1)} %get-tuple-element.40.pick_ref, bf16[2,1024,1024]{2,1,0:T(8,128)(2,1)} %bitcast.12, bf16[2,256,1024]{2,1,0:T(8,128)(2,1)S(1)} %collective-permute-done.4.next_ref, bf16[2,2,1024,1024]{3,2,1,0:T(8,128)(2,1)} %bitcast.16), custom_call_target="tpu_custom_call" | custom-call | flops 2147483648 | bytes 8388608 | tf_op jit(solution)/shard_map/pallas_call | solution.py:212
  48.6 0.1 collective-permute-start.5
  48.7 0.5 collective-permute-start.3
  49.2 0.1 collective-permute-start.1
  49.3 5.1 %collective-permute-done.6.next_ref = bf16[2,256,1024]{2,1,0:T(8,128)(2,1)S(1)} collective-permute-done((bf16[2,256,1024]{2,1,0:T(8,128)(2,1)}, bf16[2,256,1024]{2,1,0:T(8,128)(2,1)S(1)}, u32[]{:S(2)}, u32[]{:S(2)}) %collective-permute-start.6) | collective-permute-done | bytes 1048608 | tf_op jit(solution)/shard_map/ppermute | solution.py:17
  54.4 0.0 collective-permute-done.5
  54.4 0.0 collective-permute-done.3
  54.4 0.0 collective-permute-done.1
  54.4 0.1 collective-permute-start.10
  54.6 2.1 %collective-permute-start.9 = (bf16[64,2048]{1,0:T(8,128)(2,1)S(1)}, bf16[64,2048]{1,0:T(8,128)(2,1)S(1)}, u32[]{:S(2)}, u32[]{:S(2)}) collective-permute-start(bf16[64,2048]{1,0:T(8,128)(2,1)S(1)} %add_convert_fusion.4), channel_id=1, source_target_pairs={{0,2},{1,3},{2,0},{3,1},{4,6},{5,7},{6,4},{7,5},{8,10},{9,11},{10,... | collective-permute-start | bytes 786440 | tf_op jit(solution)/shard_map/ppermute | solution.py:17
  56.7 5.5 %shard_map.61 = (f32[64,2048]{1,0:T(8,128)S(1)}, f32[64,2048]{1,0:T(8,128)S(1)}, bf16[128,2048]{1,0:T(8,128)(2,1)S(1)}) custom-call(s32[5]{0:T(128)S(1)} %get-tuple-element.49.pick_ref, bf16[2,1024,1024]{2,1,0:T(8,128)(2,1)} %bitcast.13, bf16[2,256,1024]{2,1,0:T(8,128)(2,1)S(1)} %collective-permute-done.6.next_ref, bf16[2,2,1024,1024]{3,2,1,0:T(8,128)(2,1)} %bitcast.17), custom_call_target="tpu_custom_call" | custom-call | flops 2147483648 | bytes 8388608 | tf_op jit(solution)/shard_map/pallas_call | solution.py:212
  62.2 1.6 %collective-permute-done.10 = bf16[64,2048]{1,0:T(8,128)(2,1)S(1)} collective-permute-done((bf16[64,2048]{1,0:T(8,128)(2,1)S(1)}, bf16[64,2048]{1,0:T(8,128)(2,1)S(1)}, u32[]{:S(2)}, u32[]{:S(2)}) %collective-permute-start.10) | collective-permute-done | bytes 262176 | tf_op jit(solution)/shard_map/ppermute | solution.py:17
  63.8 0.1 add_convert_fusion.1
  63.8 0.1 collective-permute-start.11
  63.9 0.1 collective-permute-start.12
  64.0 0.1 collective-permute-start.7
  64.1 3.9 %collective-permute-done.9 = bf16[64,2048]{1,0:T(8,128)(2,1)S(1)} collective-permute-done((bf16[64,2048]{1,0:T(8,128)(2,1)S(1)}, bf16[64,2048]{1,0:T(8,128)(2,1)S(1)}, u32[]{:S(2)}, u32[]{:S(2)}) %collective-permute-start.9) | collective-permute-done | bytes 262176 | tf_op jit(solution)/shard_map/ppermute | solution.py:17
  68.0 2.3 %collective-permute-done.11 = bf16[64,2048]{1,0:T(8,128)(2,1)S(1)} collective-permute-done((bf16[64,2048]{1,0:T(8,128)(2,1)S(1)}, bf16[64,2048]{1,0:T(8,128)(2,1)S(1)}, u32[]{:S(2)}, u32[]{:S(2)}) %collective-permute-start.11) | collective-permute-done | bytes 262176 | tf_op jit(solution)/shard_map/ppermute | solution.py:17
  70.3 0.1 convert_add_fusion
  70.4 0.1 collective-permute-start.14
  70.5 1.8 %collective-permute-done.12 = bf16[64,2048]{1,0:T(8,128)(2,1)S(1)} collective-permute-done((bf16[64,2048]{1,0:T(8,128)(2,1)S(1)}, bf16[64,2048]{1,0:T(8,128)(2,1)S(1)}, u32[]{:S(2)}, u32[]{:S(2)}) %collective-permute-start.12) | collective-permute-done | bytes 262176 | tf_op jit(solution)/shard_map/ppermute | solution.py:17
  72.3 0.1 add_convert_fusion
  72.4 1.1 %collective-permute-start.13 = (bf16[64,2048]{1,0:T(8,128)(2,1)S(1)}, bf16[64,2048]{1,0:T(8,128)(2,1)S(1)}, u32[]{:S(2)}, u32[]{:S(2)}) collective-permute-start(bf16[64,2048]{1,0:T(8,128)(2,1)S(1)} %add_convert_fusion), channel_id=1, source_target_pairs={{0,4},{1,5},{2,6},{3,7},{4,0},{5,1},{6,2},{7,3},{8,12},{9,13},{10,... | collective-permute-start | bytes 786440 | tf_op jit(solution)/shard_map/ppermute | solution.py:17
  73.5 0.0 collective-permute-done.7
  73.6 0.8 collective-permute-start.8
  74.3 10.2 %collective-permute-done.14 = bf16[64,2048]{1,0:T(8,128)(2,1)S(1)} collective-permute-done((bf16[64,2048]{1,0:T(8,128)(2,1)S(1)}, bf16[64,2048]{1,0:T(8,128)(2,1)S(1)}, u32[]{:S(2)}, u32[]{:S(2)}) %collective-permute-start.14) | collective-permute-done | bytes 262176 | tf_op jit(solution)/shard_map/ppermute | solution.py:17
  84.5 1.1 %collective-permute-done.13 = bf16[64,2048]{1,0:T(8,128)(2,1)S(1)} collective-permute-done((bf16[64,2048]{1,0:T(8,128)(2,1)S(1)}, bf16[64,2048]{1,0:T(8,128)(2,1)S(1)}, u32[]{:S(2)}, u32[]{:S(2)}) %collective-permute-start.13) | collective-permute-done | bytes 262176 | tf_op jit(solution)/shard_map/ppermute | solution.py:17
  85.6 0.0 collective-permute-done.8
  85.6 0.2 add_multiply_fusion
  85.8 1.2 %reshape.11 = f32[64,2,1024]{2,1,0:T(2,128)} reshape(f32[64,2048]{1,0:T(8,128)S(1)} %add_multiply_fusion) | data formatting | bytes 1048576 | tf_op jit(solution)/shard_map/reshape | solution.py:294
  (5 shorter events, 0.2 us)
Async XLA Ops:
  0.0 13.7 %copy-start = (s32[2]{0:T(128)S(1)}, s32[2]{0:T(128)}, u32[]{:S(2)}) copy-start(s32[2]{0:T(128)} %param.8) | copy-start | bytes 28
  2.6 24.6 %collective-permute-start = (bf16[2,256,1024]{2,1,0:T(8,128)(2,1)}, bf16[2,256,1024]{2,1,0:T(8,128)(2,1)}, u32[]{:S(2)}, u32[]{:S(2)}) collective-permute-start(bf16[2,256,1024]{2,1,0:T(8,128)(2,1)} %shard_map.56), channel_id=1, source_target_pairs={{0,15},{1,0},{2,1},{3,2},{4,3},{5,4},{6,5},{7,6},{8,7},{9,8},{10,9... | collective-permute-start | bytes 3145736 | tf_op jit(solution)/shard_map/ppermute | solution.py:17
  12.3 22.6 %collective-permute-start.2 = (bf16[2,256,1024]{2,1,0:T(8,128)(2,1)}, bf16[2,256,1024]{2,1,0:T(8,128)(2,1)S(1)}, u32[]{:S(2)}, u32[]{:S(2)}) collective-permute-start(bf16[2,256,1024]{2,1,0:T(8,128)(2,1)} %get-tuple-element.37), channel_id=1, source_target_pairs={{0,15},{1,0},{2,1},{3,2},{4,3},{5,4},{6,5},{7,6},{8,7},{9,8},{10,9... | collective-permute-start | bytes 3145736 | tf_op jit(solution)/shard_map/ppermute | solution.py:17
  13.0 30.1 %collective-permute-start.4 = (bf16[2,256,1024]{2,1,0:T(8,128)(2,1)}, bf16[2,256,1024]{2,1,0:T(8,128)(2,1)S(1)}, u32[]{:S(2)}, u32[]{:S(2)}) collective-permute-start(bf16[2,256,1024]{2,1,0:T(8,128)(2,1)} %get-tuple-element.41), channel_id=1, source_target_pairs={{0,15},{1,0},{2,1},{3,2},{4,3},{5,4},{6,5},{7,6},{8,7},{9,8},{10,9... | collective-permute-start | bytes 3145736 | tf_op jit(solution)/shard_map/ppermute | solution.py:17
  13.1 41.3 %collective-permute-start.6 = (bf16[2,256,1024]{2,1,0:T(8,128)(2,1)}, bf16[2,256,1024]{2,1,0:T(8,128)(2,1)S(1)}, u32[]{:S(2)}, u32[]{:S(2)}) collective-permute-start(bf16[2,256,1024]{2,1,0:T(8,128)(2,1)} %get-tuple-element.43), channel_id=1, source_target_pairs={{0,15},{1,0},{2,1},{3,2},{4,3},{5,4},{6,5},{7,6},{8,7},{9,8},{10,9... | collective-permute-start | bytes 3145736 | tf_op jit(solution)/shard_map/ppermute | solution.py:17
  48.6 5.7 %collective-permute-start.5 = (bf16[128,2048]{1,0:T(8,128)(2,1)S(1)}, bf16[128,2048]{1,0:T(8,128)(2,1)S(1)}, u32[]{:S(2)}, u32[]{:S(2)}) collective-permute-start(bf16[128,2048]{1,0:T(8,128)(2,1)S(1)} %get-tuple-element.42), channel_id=1, source_target_pairs={{0,1},{1,0},{2,3},{3,2},{4,5},{5,4},{6,7},{7,6},{8,9},{9,8},{10,11... | collective-permute-start | bytes 1572872 | tf_op jit(solution)/shard_map/ppermute | solution.py:17
  48.7 5.7 %collective-permute-start.3 = (bf16[128,2048]{1,0:T(8,128)(2,1)S(1)}, bf16[128,2048]{1,0:T(8,128)(2,1)S(1)}, u32[]{:S(2)}, u32[]{:S(2)}) collective-permute-start(bf16[128,2048]{1,0:T(8,128)(2,1)S(1)} %get-tuple-element.38), channel_id=1, source_target_pairs={{0,1},{1,0},{2,3},{3,2},{4,5},{5,4},{6,7},{7,6},{8,9},{9,8},{10,11... | collective-permute-start | bytes 1572872 | tf_op jit(solution)/shard_map/ppermute | solution.py:17
  49.2 5.2 %collective-permute-start.1 = (bf16[128,2048]{1,0:T(8,128)(2,1)S(1)}, bf16[128,2048]{1,0:T(8,128)(2,1)S(1)}, u32[]{:S(2)}, u32[]{:S(2)}) collective-permute-start(bf16[128,2048]{1,0:T(8,128)(2,1)S(1)} %get-tuple-element.33), channel_id=1, source_target_pairs={{0,1},{1,0},{2,3},{3,2},{4,5},{5,4},{6,7},{7,6},{8,9},{9,8},{10,11... | collective-permute-start | bytes 1572872 | tf_op jit(solution)/shard_map/ppermute | solution.py:17
  54.4 9.3 %collective-permute-start.10 = (bf16[64,2048]{1,0:T(8,128)(2,1)S(1)}, bf16[64,2048]{1,0:T(8,128)(2,1)S(1)}, u32[]{:S(2)}, u32[]{:S(2)}) collective-permute-start(bf16[64,2048]{1,0:T(8,128)(2,1)S(1)} %add_convert_fusion.5), channel_id=1, source_target_pairs={{0,2},{1,3},{2,0},{3,1},{4,6},{5,7},{6,4},{7,5},{8,10},{9,11},{10,... | collective-permute-start | bytes 786440 | tf_op jit(solution)/shard_map/ppermute | solution.py:17
  54.6 13.4 %collective-permute-start.9 = (bf16[64,2048]{1,0:T(8,128)(2,1)S(1)}, bf16[64,2048]{1,0:T(8,128)(2,1)S(1)}, u32[]{:S(2)}, u32[]{:S(2)}) collective-permute-start(bf16[64,2048]{1,0:T(8,128)(2,1)S(1)} %add_convert_fusion.4), channel_id=1, source_target_pairs={{0,2},{1,3},{2,0},{3,1},{4,6},{5,7},{6,4},{7,5},{8,10},{9,11},{10,... | collective-permute-start | bytes 786440 | tf_op jit(solution)/shard_map/ppermute | solution.py:17
  63.8 6.4 %collective-permute-start.11 = (bf16[64,2048]{1,0:T(8,128)(2,1)S(1)}, bf16[64,2048]{1,0:T(8,128)(2,1)S(1)}, u32[]{:S(2)}, u32[]{:S(2)}) collective-permute-start(bf16[64,2048]{1,0:T(8,128)(2,1)S(1)} %add_convert_fusion.1), channel_id=1, source_target_pairs={{0,4},{1,5},{2,6},{3,7},{4,0},{5,1},{6,2},{7,3},{8,12},{9,13},{10,... | collective-permute-start | bytes 786440 | tf_op jit(solution)/shard_map/ppermute | solution.py:17
  63.9 8.4 %collective-permute-start.12 = (bf16[64,2048]{1,0:T(8,128)(2,1)S(1)}, bf16[64,2048]{1,0:T(8,128)(2,1)S(1)}, u32[]{:S(2)}, u32[]{:S(2)}) collective-permute-start(bf16[64,2048]{1,0:T(8,128)(2,1)S(1)} %add_convert_fusion.3), channel_id=1, source_target_pairs={{0,2},{1,3},{2,0},{3,1},{4,6},{5,7},{6,4},{7,5},{8,10},{9,11},{10,... | collective-permute-start | bytes 786440 | tf_op jit(solution)/shard_map/ppermute | solution.py:17
  64.0 9.5 %collective-permute-start.7 = (bf16[128,2048]{1,0:T(8,128)(2,1)S(1)}, bf16[128,2048]{1,0:T(8,128)(2,1)S(1)}, u32[]{:S(2)}, u32[]{:S(2)}) collective-permute-start(bf16[128,2048]{1,0:T(8,128)(2,1)S(1)} %get-tuple-element.52), channel_id=1, source_target_pairs={{0,1},{1,0},{2,3},{3,2},{4,5},{5,4},{6,7},{7,6},{8,9},{9,8},{10,11... | collective-permute-start | bytes 1572872 | tf_op jit(solution)/shard_map/ppermute | solution.py:17
  70.4 14.1 %collective-permute-start.14 = (bf16[64,2048]{1,0:T(8,128)(2,1)S(1)}, bf16[64,2048]{1,0:T(8,128)(2,1)S(1)}, u32[]{:S(2)}, u32[]{:S(2)}) collective-permute-start(bf16[64,2048]{1,0:T(8,128)(2,1)S(1)} %convert_add_fusion), channel_id=1, source_target_pairs={{0,8},{1,9},{2,10},{3,11},{4,12},{5,13},{6,14},{7,15},{8,0},{9,1},... | collective-permute-start | bytes 786440 | tf_op jit(solution)/shard_map/ppermute | solution.py:17
  72.4 13.2 %collective-permute-start.13 = (bf16[64,2048]{1,0:T(8,128)(2,1)S(1)}, bf16[64,2048]{1,0:T(8,128)(2,1)S(1)}, u32[]{:S(2)}, u32[]{:S(2)}) collective-permute-start(bf16[64,2048]{1,0:T(8,128)(2,1)S(1)} %add_convert_fusion), channel_id=1, source_target_pairs={{0,4},{1,5},{2,6},{3,7},{4,0},{5,1},{6,2},{7,3},{8,12},{9,13},{10,... | collective-permute-start | bytes 786440 | tf_op jit(solution)/shard_map/ppermute | solution.py:17
  73.6 12.0 %collective-permute-start.8 = (bf16[64,2048]{1,0:T(8,128)(2,1)S(1)}, bf16[64,2048]{1,0:T(8,128)(2,1)S(1)}, u32[]{:S(2)}, u32[]{:S(2)}) collective-permute-start(bf16[64,2048]{1,0:T(8,128)(2,1)S(1)} %add_convert_fusion.2), channel_id=1, source_target_pairs={{0,2},{1,3},{2,0},{3,1},{4,6},{5,7},{6,4},{7,5},{8,10},{9,11},{10,... | collective-permute-start | bytes 786440 | tf_op jit(solution)/shard_map/ppermute | solution.py:17

commit v11 on v10

--- a/solution.py
+++ b/solution.py
@@ -279,9 +279,10 @@
         (step_0[2], step_1[2], step_2[2], following[3])
     )
     send_0, send_1, send_2 = for_x(step_0, core_0), for_x(step_1, core_1), for_x(step_2, core_2)
+    mine_3, other_3, core_3 = rows(3, send_0)
+    send_1, _ = lax.optimization_barrier((send_1, mine_3))
     across_0, across_1, across_2 = from_x(send_0), from_x(send_1), from_x(send_2)
-    mine_3, other_3, core_3 = rows(3, (send_0, send_1, send_2))
-    mine_0, _ = lax.optimization_barrier((step_0[0], mine_3))
+    mine_0, _ = lax.optimization_barrier((step_0[0], send_1))
     far = own_sum(mine_0, core_0, across_0)
     far = over(far, 4)
     send_3 = for_x((mine_3, other_3), core_3)

time: 87.3 us -> 87 us (level)
  waiting for transfers between devices: 28.6 us -> 26 us
  starting transfers between devices: 11.9 us -> 14.3 us
    ppermute x15, waiting for transfers between devices: 28.6 us -> 26 us  [permute(): lax.ppermute(x, 'ka', [(i, j % size) for i, j in pairs if j is not None])]
    ppermute x15, starting transfers between devices: 11.9 us -> 14.3 us  [permute(): lax.ppermute(x, 'ka', [(i, j % size) for i, j in pairs if j is not None])]
  transfers between devices with their start and end apart: 15 -> 15, of which waited for: 8 -> 6; matrix products, arithmetic and copies ran while one was open for 1% -> 1% of each run, Pallas kernels for 48% -> 48%
where the time goes in v11:
time: 87 us; the launch traced here: 86.7 us
  Pallas kernels  44.1 us (51%)
  waiting for transfers between devices  26 us (30%)
  starting transfers between devices  14.3 us (16%)
  local copies, waits for them, and re-layouts  1.24 us (1%)
    ppermute x15, waiting for transfers between devices, permute(): lax.ppermute(x, 'ka', [(i, j % size) for i, j in pairs if j is not None])  26 us
    pallas_call x4, Pallas kernels, rows_of(): pl.pallas_call(rows_kernel, out_shape=[jax.ShapeDtypeStruct((width // 4,...  24 us
    ppermute x15, starting transfers between devices, permute(): lax.ppermute(x, 'ka', [(i, j % size) for i, j in pairs if j is not None])  14.3 us
    pallas_call x1, Pallas kernels, products_of(): pl.pallas_call(products_kernel, out_shape=jax.ShapeDtypeStruct((k_local,...  13.4 us
    pallas_call x2, Pallas kernels, turned_pieces(): pl.pallas_call(functools.partial(turn_kernel, first), out_shape=[jax.Shap...  6.78 us
  transfers between devices with their start and end apart: 15, of which 6 were waited for; matrix products, arithmetic and copies ran while one was open for 1% of the time, Pallas kernels for 48%

profile of v11, /device:TPU:0, one launch (start us, length us, event | category | flops | bytes accessed | tf_op | source)
XLA Modules:
  0.0 86.7 jit_solution(13637182485374940862)
XLA Ops:
  0.0 0.0 copy-start
  0.0 2.6 %shard_map.56 = bf16[2,256,1024]{2,1,0:T(8,128)(2,1)} custom-call(bf16[2,1024,1024]{2,1,0:T(8,128)(2,1)} %bitcast.8), custom_call_target="tpu_custom_call" | custom-call | bytes 2097152 | tf_op jit(solution)/shard_map/pallas_call | solution.py:137
  2.6 5.5 %collective-permute-start = (bf16[2,256,1024]{2,1,0:T(8,128)(2,1)}, bf16[2,256,1024]{2,1,0:T(8,128)(2,1)}, u32[]{:S(2)}, u32[]{:S(2)}) collective-permute-start(bf16[2,256,1024]{2,1,0:T(8,128)(2,1)} %shard_map.56), channel_id=1, source_target_pairs={{0,15},{1,0},{2,1},{3,2},{4,3},{5,4},{6,5},{7,6},{8,7},{9,8},{10,9... | collective-permute-start | bytes 3145736 | tf_op jit(solution)/shard_map/ppermute | solution.py:17
  8.0 4.2 %shard_map.58 = (bf16[2,256,1024]{2,1,0:T(8,128)(2,1)}, bf16[2,256,1024]{2,1,0:T(8,128)(2,1)}, bf16[2,256,1024]{2,1,0:T(8,128)(2,1)}) custom-call(bf16[2,1024,1024]{2,1,0:T(8,128)(2,1)} %bitcast.9), custom_call_target="tpu_custom_call" | custom-call | bytes 6291456 | tf_op jit(solution)/shard_map/pallas_call | solution.py:137
  12.3 0.7 collective-permute-start.2
  13.0 0.1 collective-permute-start.4
  13.1 0.6 collective-permute-start.6
  13.6 0.0 copy-done
  13.7 0.1 add_add_fusion
  13.7 13.4 %shard_map.55 = bf16[2,2,32,32,1024]{4,3,2,1,0:T(8,128)(2,1)} custom-call(s32[2,2]{1,0:T(2,128)} %first_ref.1, bf16[2,32,32,1024]{3,2,1,0:T(8,128)(2,1)} %coeffs_ref.1, bf16[2,2,32,32]{3,2,1,0:T(8,128)(2,1)} %cond_ref.1, bf16[2,2,32,32]{3,2,1,0:T(8,128)(2,1)} %val_ref.1), custom_call_target="tpu_custom_call" | custom-call | flops 6442450944 | bytes 12582912 | tf_op jit(solution)/shard_map/pallas_call | solution.py:90
  27.1 0.1 add_add_fusion.3
  27.2 0.0 collective-permute-done.next_ref
  27.2 7.5 %shard_map.57 = (f32[64,2048]{1,0:T(8,128)S(1)}, f32[64,2048]{1,0:T(8,128)S(1)}, bf16[128,2048]{1,0:T(8,128)(2,1)S(1)}) custom-call(s32[5]{0:T(128)S(1)} %get-tuple-element.32.pick_ref, bf16[2,1024,1024]{2,1,0:T(8,128)(2,1)} %bitcast.10, bf16[2,256,1024]{2,1,0:T(8,128)(2,1)} %collective-permute-done.next_ref, bf16[2,2,1024,1024]{3,2,1,0:T(8,128)(2,1)} %bitcast.14), custom_call_target="tpu_custom_call" | custom-call | flops 2147483648 | bytes 8388608 | tf_op jit(solution)/shard_map/pallas_call | solution.py:212
  34.7 0.0 collective-permute-done.2.next_ref
  34.7 5.5 %shard_map.59 = (f32[64,2048]{1,0:T(8,128)S(1)}, f32[64,2048]{1,0:T(8,128)S(1)}, bf16[128,2048]{1,0:T(8,128)(2,1)S(1)}) custom-call(s32[5]{0:T(128)S(1)} %get-tuple-element.36.pick_ref, bf16[2,1024,1024]{2,1,0:T(8,128)(2,1)} %bitcast.11, bf16[2,256,1024]{2,1,0:T(8,128)(2,1)S(1)} %collective-permute-done.2.next_ref, bf16[2,2,1024,1024]{3,2,1,0:T(8,128)(2,1)} %bitcast.15), custom_call_target="tpu_custom_call" | custom-call | flops 2147483648 | bytes 8388608 | tf_op jit(solution)/shard_map/pallas_call | solution.py:212
  40.3 2.9 %collective-permute-done.4.next_ref = bf16[2,256,1024]{2,1,0:T(8,128)(2,1)S(1)} collective-permute-done((bf16[2,256,1024]{2,1,0:T(8,128)(2,1)}, bf16[2,256,1024]{2,1,0:T(8,128)(2,1)S(1)}, u32[]{:S(2)}, u32[]{:S(2)}) %collective-permute-start.4) | collective-permute-done | bytes 1048608 | tf_op jit(solution)/shard_map/ppermute | solution.py:17
  43.1 5.5 %shard_map.60 = (f32[64,2048]{1,0:T(8,128)S(1)}, f32[64,2048]{1,0:T(8,128)S(1)}, bf16[128,2048]{1,0:T(8,128)(2,1)S(1)}) custom-call(s32[5]{0:T(128)S(1)} %get-tuple-element.41.pick_ref, bf16[2,1024,1024]{2,1,0:T(8,128)(2,1)} %bitcast.12, bf16[2,256,1024]{2,1,0:T(8,128)(2,1)S(1)} %collective-permute-done.4.next_ref, bf16[2,2,1024,1024]{3,2,1,0:T(8,128)(2,1)} %bitcast.16), custom_call_target="tpu_custom_call" | custom-call | flops 2147483648 | bytes 8388608 | tf_op jit(solution)/shard_map/pallas_call | solution.py:212
  48.6 0.1 collective-permute-start.5
  48.7 0.5 collective-permute-start.3
  49.2 0.1 collective-permute-start.1
  49.3 5.1 %collective-permute-done.6.next_ref = bf16[2,256,1024]{2,1,0:T(8,128)(2,1)S(1)} collective-permute-done((bf16[2,256,1024]{2,1,0:T(8,128)(2,1)}, bf16[2,256,1024]{2,1,0:T(8,128)(2,1)S(1)}, u32[]{:S(2)}, u32[]{:S(2)}) %collective-permute-start.6) | collective-permute-done | bytes 1048608 | tf_op jit(solution)/shard_map/ppermute | solution.py:17
  54.4 0.0 collective-permute-done.5
  54.4 0.0 collective-permute-done.3
  54.4 0.0 collective-permute-done.1
  54.4 0.1 collective-permute-start.10
  54.6 5.5 %shard_map.61 = (f32[64,2048]{1,0:T(8,128)S(1)}, f32[64,2048]{1,0:T(8,128)S(1)}, bf16[128,2048]{1,0:T(8,128)(2,1)S(1)}) custom-call(s32[5]{0:T(128)S(1)} %get-tuple-element.46.pick_ref, bf16[2,1024,1024]{2,1,0:T(8,128)(2,1)} %bitcast.13, bf16[2,256,1024]{2,1,0:T(8,128)(2,1)S(1)} %collective-permute-done.6.next_ref, bf16[2,2,1024,1024]{3,2,1,0:T(8,128)(2,1)} %bitcast.17), custom_call_target="tpu_custom_call" | custom-call | flops 2147483648 | bytes 8388608 | tf_op jit(solution)/shard_map/pallas_call | solution.py:212
  60.1 2.1 %collective-permute-start.9 = (bf16[64,2048]{1,0:T(8,128)(2,1)S(1)}, bf16[64,2048]{1,0:T(8,128)(2,1)S(1)}, u32[]{:S(2)}, u32[]{:S(2)}) collective-permute-start(bf16[64,2048]{1,0:T(8,128)(2,1)S(1)} %add_convert_fusion.3), channel_id=1, source_target_pairs={{0,2},{1,3},{2,0},{3,1},{4,6},{5,7},{6,4},{7,5},{8,10},{9,11},{10,... | collective-permute-start | bytes 786440 | tf_op jit(solution)/shard_map/ppermute | solution.py:17
  62.1 0.0 collective-permute-done.10
  62.1 0.1 add_convert_fusion.2
  62.2 0.1 collective-permute-start.11
  62.3 0.1 add_convert_fusion.1
  62.4 0.7 collective-permute-start.12
  63.1 0.0 collective-permute-start.7
  63.1 6.2 %collective-permute-done.9 = bf16[64,2048]{1,0:T(8,128)(2,1)S(1)} collective-permute-done((bf16[64,2048]{1,0:T(8,128)(2,1)S(1)}, bf16[64,2048]{1,0:T(8,128)(2,1)S(1)}, u32[]{:S(2)}, u32[]{:S(2)}) %collective-permute-start.9) | collective-permute-done | bytes 262176 | tf_op jit(solution)/shard_map/ppermute | solution.py:17
  69.3 0.0 collective-permute-done.11
  69.3 0.1 convert_add_fusion
  69.5 2.3 %collective-permute-start.14 = (bf16[64,2048]{1,0:T(8,128)(2,1)S(1)}, bf16[64,2048]{1,0:T(8,128)(2,1)S(1)}, u32[]{:S(2)}, u32[]{:S(2)}) collective-permute-start(bf16[64,2048]{1,0:T(8,128)(2,1)S(1)} %convert_add_fusion), channel_id=1, source_target_pairs={{0,8},{1,9},{2,10},{3,11},{4,12},{5,13},{6,14},{7,15},{8,0},{9,1},... | collective-permute-start | bytes 786440 | tf_op jit(solution)/shard_map/ppermute | solution.py:17
  71.8 1.9 %collective-permute-done.12 = bf16[64,2048]{1,0:T(8,128)(2,1)S(1)} collective-permute-done((bf16[64,2048]{1,0:T(8,128)(2,1)S(1)}, bf16[64,2048]{1,0:T(8,128)(2,1)S(1)}, u32[]{:S(2)}, u32[]{:S(2)}) %collective-permute-start.12) | collective-permute-done | bytes 262176 | tf_op jit(solution)/shard_map/ppermute | solution.py:17
  73.7 0.1 add_convert_fusion
  73.8 0.1 collective-permute-start.13
  73.9 0.0 collective-permute-done.7
  74.0 1.5 %collective-permute-start.8 = (bf16[64,2048]{1,0:T(8,128)(2,1)S(1)}, bf16[64,2048]{1,0:T(8,128)(2,1)S(1)}, u32[]{:S(2)}, u32[]{:S(2)}) collective-permute-start(bf16[64,2048]{1,0:T(8,128)(2,1)S(1)} %add_convert_fusion.4), channel_id=1, source_target_pairs={{0,2},{1,3},{2,0},{3,1},{4,6},{5,7},{6,4},{7,5},{8,10},{9,11},{10,... | collective-permute-start | bytes 786440 | tf_op jit(solution)/shard_map/ppermute | solution.py:17
  75.4 9.1 %collective-permute-done.14 = bf16[64,2048]{1,0:T(8,128)(2,1)S(1)} collective-permute-done((bf16[64,2048]{1,0:T(8,128)(2,1)S(1)}, bf16[64,2048]{1,0:T(8,128)(2,1)S(1)}, u32[]{:S(2)}, u32[]{:S(2)}) %collective-permute-start.14) | collective-permute-done | bytes 262176 | tf_op jit(solution)/shard_map/ppermute | solution.py:17
  84.5 0.8 collective-permute-done.13
  85.3 0.0 collective-permute-done.8
  85.3 0.2 add_multiply_fusion
  85.4 1.2 %reshape.11 = f32[64,2,1024]{2,1,0:T(2,128)} reshape(f32[64,2048]{1,0:T(8,128)S(1)} %add_multiply_fusion) | data formatting | bytes 1048576 | tf_op jit(solution)/shard_map/reshape | solution.py:295
  (4 shorter events, 0.2 us)
Async XLA Ops:
  0.0 13.7 %copy-start = (s32[2]{0:T(128)S(1)}, s32[2]{0:T(128)}, u32[]{:S(2)}) copy-start(s32[2]{0:T(128)} %param.8) | copy-start | bytes 28
  2.6 24.6 %collective-permute-start = (bf16[2,256,1024]{2,1,0:T(8,128)(2,1)}, bf16[2,256,1024]{2,1,0:T(8,128)(2,1)}, u32[]{:S(2)}, u32[]{:S(2)}) collective-permute-start(bf16[2,256,1024]{2,1,0:T(8,128)(2,1)} %shard_map.56), channel_id=1, source_target_pairs={{0,15},{1,0},{2,1},{3,2},{4,3},{5,4},{6,5},{7,6},{8,7},{9,8},{10,9... | collective-permute-start | bytes 3145736 | tf_op jit(solution)/shard_map/ppermute | solution.py:17
  12.3 22.4 %collective-permute-start.2 = (bf16[2,256,1024]{2,1,0:T(8,128)(2,1)}, bf16[2,256,1024]{2,1,0:T(8,128)(2,1)S(1)}, u32[]{:S(2)}, u32[]{:S(2)}) collective-permute-start(bf16[2,256,1024]{2,1,0:T(8,128)(2,1)} %get-tuple-element.38), channel_id=1, source_target_pairs={{0,15},{1,0},{2,1},{3,2},{4,3},{5,4},{6,5},{7,6},{8,7},{9,8},{10,9... | collective-permute-start | bytes 3145736 | tf_op jit(solution)/shard_map/ppermute | solution.py:17
  13.0 30.1 %collective-permute-start.4 = (bf16[2,256,1024]{2,1,0:T(8,128)(2,1)}, bf16[2,256,1024]{2,1,0:T(8,128)(2,1)S(1)}, u32[]{:S(2)}, u32[]{:S(2)}) collective-permute-start(bf16[2,256,1024]{2,1,0:T(8,128)(2,1)} %get-tuple-element.42), channel_id=1, source_target_pairs={{0,15},{1,0},{2,1},{3,2},{4,3},{5,4},{6,5},{7,6},{8,7},{9,8},{10,9... | collective-permute-start | bytes 3145736 | tf_op jit(solution)/shard_map/ppermute | solution.py:17
  13.1 41.3 %collective-permute-start.6 = (bf16[2,256,1024]{2,1,0:T(8,128)(2,1)}, bf16[2,256,1024]{2,1,0:T(8,128)(2,1)S(1)}, u32[]{:S(2)}, u32[]{:S(2)}) collective-permute-start(bf16[2,256,1024]{2,1,0:T(8,128)(2,1)} %get-tuple-element.44), channel_id=1, source_target_pairs={{0,15},{1,0},{2,1},{3,2},{4,3},{5,4},{6,5},{7,6},{8,7},{9,8},{10,9... | collective-permute-start | bytes 3145736 | tf_op jit(solution)/shard_map/ppermute | solution.py:17
  48.6 5.7 %collective-permute-start.5 = (bf16[128,2048]{1,0:T(8,128)(2,1)S(1)}, bf16[128,2048]{1,0:T(8,128)(2,1)S(1)}, u32[]{:S(2)}, u32[]{:S(2)}) collective-permute-start(bf16[128,2048]{1,0:T(8,128)(2,1)S(1)} %get-tuple-element.43), channel_id=1, source_target_pairs={{0,1},{1,0},{2,3},{3,2},{4,5},{5,4},{6,7},{7,6},{8,9},{9,8},{10,11... | collective-permute-start | bytes 1572872 | tf_op jit(solution)/shard_map/ppermute | solution.py:17
  48.7 5.7 %collective-permute-start.3 = (bf16[128,2048]{1,0:T(8,128)(2,1)S(1)}, bf16[128,2048]{1,0:T(8,128)(2,1)S(1)}, u32[]{:S(2)}, u32[]{:S(2)}) collective-permute-start(bf16[128,2048]{1,0:T(8,128)(2,1)S(1)} %get-tuple-element.39), channel_id=1, source_target_pairs={{0,1},{1,0},{2,3},{3,2},{4,5},{5,4},{6,7},{7,6},{8,9},{9,8},{10,11... | collective-permute-start | bytes 1572872 | tf_op jit(solution)/shard_map/ppermute | solution.py:17
  49.2 5.2 %collective-permute-start.1 = (bf16[128,2048]{1,0:T(8,128)(2,1)S(1)}, bf16[128,2048]{1,0:T(8,128)(2,1)S(1)}, u32[]{:S(2)}, u32[]{:S(2)}) collective-permute-start(bf16[128,2048]{1,0:T(8,128)(2,1)S(1)} %get-tuple-element.34), channel_id=1, source_target_pairs={{0,1},{1,0},{2,3},{3,2},{4,5},{5,4},{6,7},{7,6},{8,9},{9,8},{10,11... | collective-permute-start | bytes 1572872 | tf_op jit(solution)/shard_map/ppermute | solution.py:17
  54.4 7.7 %collective-permute-start.10 = (bf16[64,2048]{1,0:T(8,128)(2,1)S(1)}, bf16[64,2048]{1,0:T(8,128)(2,1)S(1)}, u32[]{:S(2)}, u32[]{:S(2)}) collective-permute-start(bf16[64,2048]{1,0:T(8,128)(2,1)S(1)} %add_convert_fusion.5), channel_id=1, source_target_pairs={{0,2},{1,3},{2,0},{3,1},{4,6},{5,7},{6,4},{7,5},{8,10},{9,11},{10,... | collective-permute-start | bytes 786440 | tf_op jit(solution)/shard_map/ppermute | solution.py:17
  60.1 9.3 %collective-permute-start.9 = (bf16[64,2048]{1,0:T(8,128)(2,1)S(1)}, bf16[64,2048]{1,0:T(8,128)(2,1)S(1)}, u32[]{:S(2)}, u32[]{:S(2)}) collective-permute-start(bf16[64,2048]{1,0:T(8,128)(2,1)S(1)} %add_convert_fusion.3), channel_id=1, source_target_pairs={{0,2},{1,3},{2,0},{3,1},{4,6},{5,7},{6,4},{7,5},{8,10},{9,11},{10,... | collective-permute-start | bytes 786440 | tf_op jit(solution)/shard_map/ppermute | solution.py:17
  62.2 7.1 %collective-permute-start.11 = (bf16[64,2048]{1,0:T(8,128)(2,1)S(1)}, bf16[64,2048]{1,0:T(8,128)(2,1)S(1)}, u32[]{:S(2)}, u32[]{:S(2)}) collective-permute-start(bf16[64,2048]{1,0:T(8,128)(2,1)S(1)} %add_convert_fusion.2), channel_id=1, source_target_pairs={{0,4},{1,5},{2,6},{3,7},{4,0},{5,1},{6,2},{7,3},{8,12},{9,13},{10,... | collective-permute-start | bytes 786440 | tf_op jit(solution)/shard_map/ppermute | solution.py:17
  62.4 11.3 %collective-permute-start.12 = (bf16[64,2048]{1,0:T(8,128)(2,1)S(1)}, bf16[64,2048]{1,0:T(8,128)(2,1)S(1)}, u32[]{:S(2)}, u32[]{:S(2)}) collective-permute-start(bf16[64,2048]{1,0:T(8,128)(2,1)S(1)} %add_convert_fusion.1), channel_id=1, source_target_pairs={{0,2},{1,3},{2,0},{3,1},{4,6},{5,7},{6,4},{7,5},{8,10},{9,11},{10,... | collective-permute-start | bytes 786440 | tf_op jit(solution)/shard_map/ppermute | solution.py:17
  63.1 10.8 %collective-permute-start.7 = (bf16[128,2048]{1,0:T(8,128)(2,1)S(1)}, bf16[128,2048]{1,0:T(8,128)(2,1)S(1)}, u32[]{:S(2)}, u32[]{:S(2)}) collective-permute-start(bf16[128,2048]{1,0:T(8,128)(2,1)S(1)} %get-tuple-element.49), channel_id=1, source_target_pairs={{0,1},{1,0},{2,3},{3,2},{4,5},{5,4},{6,7},{7,6},{8,9},{9,8},{10,11... | collective-permute-start | bytes 1572872 | tf_op jit(solution)/shard_map/ppermute | solution.py:17
  69.5 15.1 %collective-permute-start.14 = (bf16[64,2048]{1,0:T(8,128)(2,1)S(1)}, bf16[64,2048]{1,0:T(8,128)(2,1)S(1)}, u32[]{:S(2)}, u32[]{:S(2)}) collective-permute-start(bf16[64,2048]{1,0:T(8,128)(2,1)S(1)} %convert_add_fusion), channel_id=1, source_target_pairs={{0,8},{1,9},{2,10},{3,11},{4,12},{5,13},{6,14},{7,15},{8,0},{9,1},... | collective-permute-start | bytes 786440 | tf_op jit(solution)/shard_map/ppermute | solution.py:17
  73.8 11.5 %collective-permute-start.13 = (bf16[64,2048]{1,0:T(8,128)(2,1)S(1)}, bf16[64,2048]{1,0:T(8,128)(2,1)S(1)}, u32[]{:S(2)}, u32[]{:S(2)}) collective-permute-start(bf16[64,2048]{1,0:T(8,128)(2,1)S(1)} %add_convert_fusion), channel_id=1, source_target_pairs={{0,4},{1,5},{2,6},{3,7},{4,0},{5,1},{6,2},{7,3},{8,12},{9,13},{10,... | collective-permute-start | bytes 786440 | tf_op jit(solution)/shard_map/ppermute | solution.py:17
  74.0 11.3 %collective-permute-start.8 = (bf16[64,2048]{1,0:T(8,128)(2,1)S(1)}, bf16[64,2048]{1,0:T(8,128)(2,1)S(1)}, u32[]{:S(2)}, u32[]{:S(2)}) collective-permute-start(bf16[64,2048]{1,0:T(8,128)(2,1)S(1)} %add_convert_fusion.4), channel_id=1, source_target_pairs={{0,2},{1,3},{2,0},{3,1},{4,6},{5,7},{6,4},{7,5},{8,10},{9,11},{10,... | collective-permute-start | bytes 786440 | tf_op jit(solution)/shard_map/ppermute | solution.py:17

commit v12 on v10

--- a/solution.py
+++ b/solution.py
@@ -249,7 +249,7 @@
     pieces = turned_pieces(flat, 0, 1, width)
     rest, _ = lax.optimization_barrier((flat, pieces))
     pieces += turned_pieces(rest, 1, 3, width)
-    following = [permute(piece, lambda i: i - 1) for piece in pieces]
+    following = [permute(piece, lambda i: i - 1) for piece in pieces[:3]]
     products = products_of(coeffs, g_cond, g_val, band_first)
     products = products.reshape(k_local, modes, bands_c * bands_v, excitons)
     places = jnp.mod(k_plus_q - me * k_local, k_local * size)
@@ -274,15 +274,19 @@
 
     step_0 = rows(0, products)
     step_1 = rows(1, step_0[0])
-    step_2 = rows(2, step_1[0])
-    core_0, core_1, core_2, following[3] = lax.optimization_barrier(
-        (step_0[2], step_1[2], step_2[2], following[3])
-    )
-    send_0, send_1, send_2 = for_x(step_0, core_0), for_x(step_1, core_1), for_x(step_2, core_2)
-    across_0, across_1, across_2 = from_x(send_0), from_x(send_1), from_x(send_2)
-    mine_3, other_3, core_3 = rows(3, (send_0, send_1, send_2))
-    mine_0, _ = lax.optimization_barrier((step_0[0], mine_3))
-    far = own_sum(mine_0, core_0, across_0)
+    core_0, following[2], _ = lax.optimization_barrier((step_0[2], following[2], step_1[0]))
+    send_0 = for_x(step_0, core_0)
+    across_0 = from_x(send_0)
+    step_2 = rows(2, (step_1[0], send_0))
+    last_piece, _ = lax.optimization_barrier((pieces[3], (across_0, step_2[0])))
+    following.append(permute(last_piece, lambda i: i - 1))
+    far = own_sum(step_0[0], core_0, across_0)
+    core_1, core_2, following[3] = lax.optimization_barrier((step_1[2], step_2[2], following[3]))
+    send_1, send_2 = for_x(step_1, core_1), for_x(step_2, core_2)
+    across_1 = from_x(send_1)
+    mine_3, other_3, core_3 = rows(3, (far, send_1))
+    send_2, _ = lax.optimization_barrier((send_2, mine_3))
+    across_2 = from_x(send_2)
     far = over(far, 4)
     send_3 = for_x((mine_3, other_3), core_3)
     across_3 = from_x(send_3)

time: 87.3 us -> 102 us (1.17)
  waiting for transfers between devices: 28.6 us -> 41.5 us
  starting transfers between devices: 11.9 us -> 13.6 us
  local copies, waits for them, and re-layouts: 1.24 us -> 2.85 us
  Pallas kernels: 44.3 us -> 42.8 us
    ppermute x15, waiting for transfers between devices: 28.6 us -> 41.5 us  [permute(): lax.ppermute(x, 'ka', [(i, j % size) for i, j in pairs if j is not None])]
    ppermute x15, starting transfers between devices: 11.9 us -> 13.6 us  [permute(): lax.ppermute(x, 'ka', [(i, j % size) for i, j in pairs if j is not None])]
    unnamed x2 -> x12, local copies, waits for them, and re-layouts: 0.01 us -> 1.62 us
    pallas_call x4, Pallas kernels: 24.2 us -> 22.7 us  [rows_of(): pl.pallas_call(rows_kernel, out_shape=[jax.ShapeDtypeStruct((width // 4,...]
  transfers between devices with their start and end apart: 15 -> 15, of which waited for: 8 -> 7; matrix products, arithmetic and copies ran while one was open for 1% -> 1% of each run, Pallas kernels for 48% -> 40%
where the time goes in v12:
time: 102 us
  Pallas kernels  42.8 us (42%)
  waiting for transfers between devices  41.5 us (41%)
  starting transfers between devices  13.6 us (13%)
  local copies, waits for them, and re-layouts  2.85 us (3%)
    ppermute x15, waiting for transfers between devices, permute(): lax.ppermute(x, 'ka', [(i, j % size) for i, j in pairs if j is not None])  41.5 us
    pallas_call x4, Pallas kernels, rows_of(): pl.pallas_call(rows_kernel, out_shape=[jax.ShapeDtypeStruct((width // 4,...  22.7 us
    ppermute x15, starting transfers between devices, permute(): lax.ppermute(x, 'ka', [(i, j % size) for i, j in pairs if j is not None])  13.6 us
    pallas_call x1, Pallas kernels, products_of(): pl.pallas_call(products_kernel, out_shape=jax.ShapeDtypeStruct((k_local,...  13.4 us
    pallas_call x2, Pallas kernels, turned_pieces(): pl.pallas_call(functools.partial(turn_kernel, first), out_shape=[jax.Shap...  6.68 us
  transfers between devices with their start and end apart: 15, of which 7 were waited for; matrix products, arithmetic and copies ran while one was open for 1% of the time, Pallas kernels for 40%

profile of v12, /device:TPU:0, one launch (start us, length us, event | category | flops | bytes accessed | tf_op | source)
XLA Modules:
  0.0 101.8 jit_solution(2887441554248315529)
XLA Ops:
  0.0 2.5 %shard_map.56 = bf16[2,256,1024]{2,1,0:T(8,128)(2,1)} custom-call(bf16[2,1024,1024]{2,1,0:T(8,128)(2,1)} %bitcast.8), custom_call_target="tpu_custom_call" | custom-call | bytes 2097152 | tf_op jit(solution)/shard_map/pallas_call | solution.py:137
  2.5 5.5 %collective-permute-start = (bf16[2,256,1024]{2,1,0:T(8,128)(2,1)}, bf16[2,256,1024]{2,1,0:T(8,128)(2,1)S(1)}, u32[]{:S(2)}, u32[]{:S(2)}) collective-permute-start(bf16[2,256,1024]{2,1,0:T(8,128)(2,1)} %shard_map.56), channel_id=1, source_target_pairs={{0,15},{1,0},{2,1},{3,2},{4,3},{5,4},{6,5},{7,6},{8,7},{9,8},{10,9... | collective-permute-start | bytes 3145736 | tf_op jit(solution)/shard_map/ppermute | solution.py:17
  8.0 4.2 %shard_map.58 = (bf16[2,256,1024]{2,1,0:T(8,128)(2,1)}, bf16[2,256,1024]{2,1,0:T(8,128)(2,1)}, bf16[2,256,1024]{2,1,0:T(8,128)(2,1)}) custom-call(bf16[2,1024,1024]{2,1,0:T(8,128)(2,1)} %bitcast.9), custom_call_target="tpu_custom_call" | custom-call | bytes 6291456 | tf_op jit(solution)/shard_map/pallas_call | solution.py:137
  12.2 0.7 collective-permute-start.2
  12.9 0.1 collective-permute-start.3
  13.0 13.4 %shard_map.55 = bf16[2,2,32,32,1024]{4,3,2,1,0:T(8,128)(2,1)} custom-call(s32[2,2]{1,0:T(2,128)} %first_ref.1, bf16[2,32,32,1024]{3,2,1,0:T(8,128)(2,1)} %coeffs_ref.1, bf16[2,2,32,32]{3,2,1,0:T(8,128)(2,1)} %cond_ref.1, bf16[2,2,32,32]{3,2,1,0:T(8,128)(2,1)} %val_ref.1), custom_call_target="tpu_custom_call" | custom-call | flops 6442450944 | bytes 12582912 | tf_op jit(solution)/shard_map/pallas_call | solution.py:90
  26.4 0.1 add_add_fusion
  26.4 0.0 collective-permute-done.next_ref
  26.4 6.3 %shard_map.57 = (f32[64,2048]{1,0:T(8,128)S(1)}, f32[64,2048]{1,0:T(8,128)S(1)}, bf16[128,2048]{1,0:T(8,128)(2,1)}) custom-call(s32[5]{0:T(128)S(1)} %get-tuple-element.33.pick_ref, bf16[2,1024,1024]{2,1,0:T(8,128)(2,1)} %bitcast.10, bf16[2,256,1024]{2,1,0:T(8,128)(2,1)S(1)} %collective-permute-done.next_ref, bf16[2,2,1024,1024]{3,2,1,0:T(8,128)(2,1)} %bitcast.14), custom_call_target="tpu_custom_call" | custom-call | flops 2147483648 | bytes 8388608 | tf_op jit(solution)/shard_map/pallas_call | solution.py:212
  32.7 0.8 copy-done
  33.5 0.8 copy-done.2
  34.3 0.4 collective-permute-start.1
  34.8 0.1 add_add_fusion.3
  34.9 8.2 %collective-permute-done.3.next_ref = bf16[2,256,1024]{2,1,0:T(8,128)(2,1)S(1)} collective-permute-done((bf16[2,256,1024]{2,1,0:T(8,128)(2,1)}, bf16[2,256,1024]{2,1,0:T(8,128)(2,1)S(1)}, u32[]{:S(2)}, u32[]{:S(2)}) %collective-permute-start.3) | collective-permute-done | bytes 1048608 | tf_op jit(solution)/shard_map/ppermute | solution.py:17
  43.1 5.5 %shard_map.59 = (f32[64,2048]{1,0:T(8,128)S(1)}, f32[64,2048]{1,0:T(8,128)S(1)}, bf16[128,2048]{1,0:T(8,128)(2,1)S(1)}) custom-call(s32[5]{0:T(128)S(1)} %get-tuple-element.38.pick_ref, bf16[2,1024,1024]{2,1,0:T(8,128)(2,1)} %bitcast.11, bf16[2,256,1024]{2,1,0:T(8,128)(2,1)S(1)} %collective-permute-done.3.next_ref, bf16[2,2,1024,1024]{3,2,1,0:T(8,128)(2,1)} %bitcast.15), custom_call_target="tpu_custom_call" | custom-call | flops 2147483648 | bytes 8388608 | tf_op jit(solution)/shard_map/pallas_call | solution.py:212
  48.6 0.0 collective-permute-done.2.next_ref
  48.6 0.0 collective-permute-done.1
  48.7 0.1 collective-permute-start.4
  48.8 5.5 %shard_map.60 = (f32[64,2048]{1,0:T(8,128)S(1)}, f32[64,2048]{1,0:T(8,128)S(1)}, bf16[128,2048]{1,0:T(8,128)(2,1)S(1)}) custom-call(s32[5]{0:T(128)S(1)} %get-tuple-element.45.pick_ref, bf16[2,1024,1024]{2,1,0:T(8,128)(2,1)} %bitcast.12, bf16[2,256,1024]{2,1,0:T(8,128)(2,1)S(1)} %collective-permute-done.2.next_ref, bf16[2,2,1024,1024]{3,2,1,0:T(8,128)(2,1)} %bitcast.16), custom_call_target="tpu_custom_call" | custom-call | flops 2147483648 | bytes 8388608 | tf_op jit(solution)/shard_map/pallas_call | solution.py:212
  54.3 1.0 %collective-permute-done.4 = bf16[64,2048]{1,0:T(8,128)(2,1)S(1)} collective-permute-done((bf16[64,2048]{1,0:T(8,128)(2,1)S(1)}, bf16[64,2048]{1,0:T(8,128)(2,1)S(1)}, u32[]{:S(2)}, u32[]{:S(2)}) %collective-permute-start.4) | collective-permute-done | bytes 262176 | tf_op jit(solution)/shard_map/ppermute | solution.py:17
  55.3 3.5 %collective-permute-start.7 = (bf16[2,256,1024]{2,1,0:T(8,128)(2,1)S(1)}, bf16[2,256,1024]{2,1,0:T(8,128)(2,1)S(1)}, u32[]{:S(2)}, u32[]{:S(2)}) collective-permute-start(bf16[2,256,1024]{2,1,0:T(8,128)(2,1)S(1)} %copy-done.4), channel_id=1, source_target_pairs={{0,15},{1,0},{2,1},{3,2},{4,3},{5,4},{6,5},{7,6},{8,7},{9,8},{10,9... | collective-permute-start | bytes 3145736 | tf_op jit(solution)/shard_map/ppermute | solution.py:17
  58.8 0.0 collective-permute-start.5
  58.8 0.5 collective-permute-start.6
  59.4 0.1 convert_add_fusion.1
  59.5 0.1 collective-permute-start.11
  59.5 1.2 %collective-permute-done.5 = bf16[128,2048]{1,0:T(8,128)(2,1)S(1)} collective-permute-done((bf16[128,2048]{1,0:T(8,128)(2,1)S(1)}, bf16[128,2048]{1,0:T(8,128)(2,1)S(1)}, u32[]{:S(2)}, u32[]{:S(2)}) %collective-permute-start.5) | collective-permute-done | bytes 524320 | tf_op jit(solution)/shard_map/ppermute | solution.py:17
  60.8 0.7 collective-permute-done.6
  61.5 12.5 %collective-permute-done.7.next_ref = bf16[2,256,1024]{2,1,0:T(8,128)(2,1)S(1)} collective-permute-done((bf16[2,256,1024]{2,1,0:T(8,128)(2,1)S(1)}, bf16[2,256,1024]{2,1,0:T(8,128)(2,1)S(1)}, u32[]{:S(2)}, u32[]{:S(2)}) %collective-permute-start.7) | collective-permute-done | bytes 1048608 | tf_op jit(solution)/shard_map/ppermute | solution.py:17
  74.0 0.1 add_convert_fusion.3
  74.0 0.1 collective-permute-start.10
  74.1 0.1 add_convert_fusion.1
  74.2 5.5 %shard_map.61 = (f32[64,2048]{1,0:T(8,128)S(1)}, f32[64,2048]{1,0:T(8,128)S(1)}, bf16[128,2048]{1,0:T(8,128)(2,1)S(1)}) custom-call(s32[5]{0:T(128)S(1)} %get-tuple-element.52.pick_ref, bf16[2,1024,1024]{2,1,0:T(8,128)(2,1)} %bitcast.13, bf16[2,256,1024]{2,1,0:T(8,128)(2,1)S(1)} %collective-permute-done.7.next_ref, bf16[2,2,1024,1024]{3,2,1,0:T(8,128)(2,1)} %bitcast.17), custom_call_target="tpu_custom_call" | custom-call | flops 2147483648 | bytes 8388608 | tf_op jit(solution)/shard_map/pallas_call | solution.py:212
  79.6 2.1 %collective-permute-start.12 = (bf16[64,2048]{1,0:T(8,128)(2,1)S(1)}, bf16[64,2048]{1,0:T(8,128)(2,1)S(1)}, u32[]{:S(2)}, u32[]{:S(2)}) collective-permute-start(bf16[64,2048]{1,0:T(8,128)(2,1)S(1)} %add_convert_fusion.1), channel_id=1, source_target_pairs={{0,2},{1,3},{2,0},{3,1},{4,6},{5,7},{6,4},{7,5},{8,10},{9,11},{10,... | collective-permute-start | bytes 786440 | tf_op jit(solution)/shard_map/ppermute | solution.py:17
  81.7 0.0 collective-permute-start.8
  81.7 0.0 collective-permute-done.11
  81.7 0.0 collective-permute-done.10
  81.7 0.1 convert_add_fusion
  81.9 0.1 collective-permute-start.14
  81.9 5.9 %collective-permute-done.12 = bf16[64,2048]{1,0:T(8,128)(2,1)S(1)} collective-permute-done((bf16[64,2048]{1,0:T(8,128)(2,1)S(1)}, bf16[64,2048]{1,0:T(8,128)(2,1)S(1)}, u32[]{:S(2)}, u32[]{:S(2)}) %collective-permute-start.12) | collective-permute-done | bytes 262176 | tf_op jit(solution)/shard_map/ppermute | solution.py:17
  87.8 0.1 add_convert_fusion
  87.9 0.1 collective-permute-start.13
  88.0 0.0 collective-permute-done.8
  88.1 0.4 collective-permute-start.9
  88.4 11.9 %collective-permute-done.13 = bf16[64,2048]{1,0:T(8,128)(2,1)S(1)} collective-permute-done((bf16[64,2048]{1,0:T(8,128)(2,1)S(1)}, bf16[64,2048]{1,0:T(8,128)(2,1)S(1)}, u32[]{:S(2)}, u32[]{:S(2)}) %collective-permute-start.13) | collective-permute-done | bytes 262176 | tf_op jit(solution)/shard_map/ppermute | solution.py:17
  100.4 0.0 collective-permute-done.14
  100.4 0.0 collective-permute-done.9
  100.4 0.2 add_multiply_fusion
  100.5 1.2 %reshape.11 = f32[64,2,1024]{2,1,0:T(2,128)} reshape(f32[64,2048]{1,0:T(8,128)S(1)} %add_multiply_fusion) | data formatting | bytes 1048576 | tf_op jit(solution)/shard_map/reshape | solution.py:298
  (13 shorter events, 0.1 us)
Async XLA Ops:
  2.5 24.0 %collective-permute-start = (bf16[2,256,1024]{2,1,0:T(8,128)(2,1)}, bf16[2,256,1024]{2,1,0:T(8,128)(2,1)S(1)}, u32[]{:S(2)}, u32[]{:S(2)}) collective-permute-start(bf16[2,256,1024]{2,1,0:T(8,128)(2,1)} %shard_map.56), channel_id=1, source_target_pairs={{0,15},{1,0},{2,1},{3,2},{4,3},{5,4},{6,5},{7,6},{8,7},{9,8},{10,9... | collective-permute-start | bytes 3145736 | tf_op jit(solution)/shard_map/ppermute | solution.py:17
  12.2 36.5 %collective-permute-start.2 = (bf16[2,256,1024]{2,1,0:T(8,128)(2,1)}, bf16[2,256,1024]{2,1,0:T(8,128)(2,1)S(1)}, u32[]{:S(2)}, u32[]{:S(2)}) collective-permute-start(bf16[2,256,1024]{2,1,0:T(8,128)(2,1)} %get-tuple-element.37), channel_id=1, source_target_pairs={{0,15},{1,0},{2,1},{3,2},{4,3},{5,4},{6,5},{7,6},{8,7},{9,8},{10,9... | collective-permute-start | bytes 3145736 | tf_op jit(solution)/shard_map/ppermute | solution.py:17
  12.9 13.5 %copy-start.5 = (s32[2]{0:T(128)S(1)}, s32[2]{0:T(128)}, u32[]{:S(2)}) copy-start(s32[2]{0:T(128)} %param.8) | copy-start | bytes 28
  12.9 30.2 %collective-permute-start.3 = (bf16[2,256,1024]{2,1,0:T(8,128)(2,1)}, bf16[2,256,1024]{2,1,0:T(8,128)(2,1)S(1)}, u32[]{:S(2)}, u32[]{:S(2)}) collective-permute-start(bf16[2,256,1024]{2,1,0:T(8,128)(2,1)} %get-tuple-element.39), channel_id=1, source_target_pairs={{0,15},{1,0},{2,1},{3,2},{4,3},{5,4},{6,5},{7,6},{8,7},{9,8},{10,9... | collective-permute-start | bytes 3145736 | tf_op jit(solution)/shard_map/ppermute | solution.py:17
  32.7 0.8 copy-start
  33.5 0.8 copy-start.2
  34.3 14.3 %copy-start.3 = (f32[64,2048]{1,0:T(8,128)S(1)}, f32[64,2048]{1,0:T(8,128)}, u32[]{:S(2)}) copy-start(f32[64,2048]{1,0:T(8,128)} %copy-done.2) | copy-start | bytes 1572868
  34.3 14.3 %collective-permute-start.1 = (bf16[128,2048]{1,0:T(8,128)(2,1)}, bf16[128,2048]{1,0:T(8,128)(2,1)S(1)}, u32[]{:S(2)}, u32[]{:S(2)}) collective-permute-start(bf16[128,2048]{1,0:T(8,128)(2,1)} %get-tuple-element.35), channel_id=1, source_target_pairs={{0,1},{1,0},{2,3},{3,2},{4,5},{5,4},{6,7},{7,6},{8,9},{9,8},{10,11... | collective-permute-start | bytes 1572872 | tf_op jit(solution)/shard_map/ppermute | solution.py:17
  48.6 6.7 %copy-start.4 = (bf16[2,256,1024]{2,1,0:T(8,128)(2,1)S(1)}, bf16[2,256,1024]{2,1,0:T(8,128)(2,1)}, u32[]{:S(2)}) copy-start(bf16[2,256,1024]{2,1,0:T(8,128)(2,1)} %get-tuple-element.50) | copy-start | bytes 3145732
  48.6 10.8 %copy-start.1 = (f32[64,2048]{1,0:T(8,128)S(1)}, f32[64,2048]{1,0:T(8,128)}, u32[]{:S(2)}) copy-start(f32[64,2048]{1,0:T(8,128)} %copy-done) | copy-start | bytes 1572868
  48.7 6.6 %collective-permute-start.4 = (bf16[64,2048]{1,0:T(8,128)(2,1)S(1)}, bf16[64,2048]{1,0:T(8,128)(2,1)S(1)}, u32[]{:S(2)}, u32[]{:S(2)}) collective-permute-start(bf16[64,2048]{1,0:T(8,128)(2,1)S(1)} %add_convert_fusion.4), channel_id=1, source_target_pairs={{0,2},{1,3},{2,0},{3,1},{4,6},{5,7},{6,4},{7,5},{8,10},{9,11},{10,... | collective-permute-start | bytes 786440 | tf_op jit(solution)/shard_map/ppermute | solution.py:17
  55.3 18.7 %collective-permute-start.7 = (bf16[2,256,1024]{2,1,0:T(8,128)(2,1)S(1)}, bf16[2,256,1024]{2,1,0:T(8,128)(2,1)S(1)}, u32[]{:S(2)}, u32[]{:S(2)}) collective-permute-start(bf16[2,256,1024]{2,1,0:T(8,128)(2,1)S(1)} %copy-done.4), channel_id=1, source_target_pairs={{0,15},{1,0},{2,1},{3,2},{4,3},{5,4},{6,5},{7,6},{8,7},{9,8},{10,9... | collective-permute-start | bytes 3145736 | tf_op jit(solution)/shard_map/ppermute | solution.py:17
  58.8 1.9 %collective-permute-start.5 = (bf16[128,2048]{1,0:T(8,128)(2,1)S(1)}, bf16[128,2048]{1,0:T(8,128)(2,1)S(1)}, u32[]{:S(2)}, u32[]{:S(2)}) collective-permute-start(bf16[128,2048]{1,0:T(8,128)(2,1)S(1)} %get-tuple-element.44), channel_id=1, source_target_pairs={{0,1},{1,0},{2,3},{3,2},{4,5},{5,4},{6,7},{7,6},{8,9},{9,8},{10,11... | collective-permute-start | bytes 1572872 | tf_op jit(solution)/shard_map/ppermute | solution.py:17
  58.8 2.7 %collective-permute-start.6 = (bf16[128,2048]{1,0:T(8,128)(2,1)S(1)}, bf16[128,2048]{1,0:T(8,128)(2,1)S(1)}, u32[]{:S(2)}, u32[]{:S(2)}) collective-permute-start(bf16[128,2048]{1,0:T(8,128)(2,1)S(1)} %get-tuple-element.47), channel_id=1, source_target_pairs={{0,1},{1,0},{2,3},{3,2},{4,5},{5,4},{6,7},{7,6},{8,9},{9,8},{10,11... | collective-permute-start | bytes 1572872 | tf_op jit(solution)/shard_map/ppermute | solution.py:17
  59.5 22.3 %collective-permute-start.11 = (bf16[64,2048]{1,0:T(8,128)(2,1)S(1)}, bf16[64,2048]{1,0:T(8,128)(2,1)S(1)}, u32[]{:S(2)}, u32[]{:S(2)}) collective-permute-start(bf16[64,2048]{1,0:T(8,128)(2,1)S(1)} %convert_add_fusion.1), channel_id=1, source_target_pairs={{0,4},{1,5},{2,6},{3,7},{4,0},{5,1},{6,2},{7,3},{8,12},{9,13},{10,... | collective-permute-start | bytes 786440 | tf_op jit(solution)/shard_map/ppermute | solution.py:17
  74.0 7.7 %collective-permute-start.10 = (bf16[64,2048]{1,0:T(8,128)(2,1)S(1)}, bf16[64,2048]{1,0:T(8,128)(2,1)S(1)}, u32[]{:S(2)}, u32[]{:S(2)}) collective-permute-start(bf16[64,2048]{1,0:T(8,128)(2,1)S(1)} %add_convert_fusion.3), channel_id=1, source_target_pairs={{0,2},{1,3},{2,0},{3,1},{4,6},{5,7},{6,4},{7,5},{8,10},{9,11},{10,... | collective-permute-start | bytes 786440 | tf_op jit(solution)/shard_map/ppermute | solution.py:17
  79.6 8.2 %collective-permute-start.12 = (bf16[64,2048]{1,0:T(8,128)(2,1)S(1)}, bf16[64,2048]{1,0:T(8,128)(2,1)S(1)}, u32[]{:S(2)}, u32[]{:S(2)}) collective-permute-start(bf16[64,2048]{1,0:T(8,128)(2,1)S(1)} %add_convert_fusion.1), channel_id=1, source_target_pairs={{0,2},{1,3},{2,0},{3,1},{4,6},{5,7},{6,4},{7,5},{8,10},{9,11},{10,... | collective-permute-start | bytes 786440 | tf_op jit(solution)/shard_map/ppermute | solution.py:17
  81.7 6.3 %collective-permute-start.8 = (bf16[128,2048]{1,0:T(8,128)(2,1)S(1)}, bf16[128,2048]{1,0:T(8,128)(2,1)S(1)}, u32[]{:S(2)}, u32[]{:S(2)}) collective-permute-start(bf16[128,2048]{1,0:T(8,128)(2,1)S(1)} %get-tuple-element.55), channel_id=1, source_target_pairs={{0,1},{1,0},{2,3},{3,2},{4,5},{5,4},{6,7},{7,6},{8,9},{9,8},{10,11... | collective-permute-start | bytes 1572872 | tf_op jit(solution)/shard_map/ppermute | solution.py:17
  81.9 18.5 %collective-permute-start.14 = (bf16[64,2048]{1,0:T(8,128)(2,1)S(1)}, bf16[64,2048]{1,0:T(8,128)(2,1)S(1)}, u32[]{:S(2)}, u32[]{:S(2)}) collective-permute-start(bf16[64,2048]{1,0:T(8,128)(2,1)S(1)} %convert_add_fusion), channel_id=1, source_target_pairs={{0,8},{1,9},{2,10},{3,11},{4,12},{5,13},{6,14},{7,15},{8,0},{9,1},... | collective-permute-start | bytes 786440 | tf_op jit(solution)/shard_map/ppermute | solution.py:17
  87.9 12.4 %collective-permute-start.13 = (bf16[64,2048]{1,0:T(8,128)(2,1)S(1)}, bf16[64,2048]{1,0:T(8,128)(2,1)S(1)}, u32[]{:S(2)}, u32[]{:S(2)}) collective-permute-start(bf16[64,2048]{1,0:T(8,128)(2,1)S(1)} %add_convert_fusion), channel_id=1, source_target_pairs={{0,4},{1,5},{2,6},{3,7},{4,0},{5,1},{6,2},{7,3},{8,12},{9,13},{10,... | collective-permute-start | bytes 786440 | tf_op jit(solution)/shard_map/ppermute | solution.py:17
  88.1 12.3 %collective-permute-start.9 = (bf16[64,2048]{1,0:T(8,128)(2,1)S(1)}, bf16[64,2048]{1,0:T(8,128)(2,1)S(1)}, u32[]{:S(2)}, u32[]{:S(2)}) collective-permute-start(bf16[64,2048]{1,0:T(8,128)(2,1)S(1)} %add_convert_fusion.2), channel_id=1, source_target_pairs={{0,2},{1,3},{2,0},{3,1},{4,6},{5,7},{6,4},{7,5},{8,10},{9,11},{10,... | collective-permute-start | bytes 786440 | tf_op jit(solution)/shard_map/ppermute | solution.py:17

commit v13 on v10

--- a/solution.py
+++ b/solution.py
@@ -260,17 +260,19 @@
         mine, other, send = rows_of(pick, flat, following[step], products)
         return mine, other, permute(send, lambda i: i ^ 1)
 
-    def for_x(step, from_core):
-        return (step[1] + from_core[width // 4:].astype(jnp.float32)).astype(jnp.bfloat16)
-
-    def from_x(send):
-        return permute(send, lambda i: i ^ 2)
-
-    def own_sum(mine, from_core, across):
-        return mine + from_core[:width // 4].astype(jnp.float32) + across.astype(jnp.float32)
-
-    def over(value, bit):
-        return permute(value.astype(jnp.bfloat16), lambda i: i ^ bit)
+    half = width // 4
+
+    def summed(step, from_core):
+        from_core = from_core.astype(jnp.float32)
+        return step[0] + from_core[:half], step[1] + from_core[half:]
+
+    def over(value, bits):
+        return permute(value.astype(jnp.bfloat16), lambda i: i ^ bits)
+
+    def total_of(value, *arrived):
+        for array in arrived:
+            value = value + array.astype(jnp.float32)
+        return value
 
     step_0 = rows(0, products)
     step_1 = rows(1, step_0[0])
@@ -278,19 +280,18 @@
     core_0, core_1, core_2, following[3] = lax.optimization_barrier(
         (step_0[2], step_1[2], step_2[2], following[3])
     )
-    send_0, send_1, send_2 = for_x(step_0, core_0), for_x(step_1, core_1), for_x(step_2, core_2)
-    across_0, across_1, across_2 = from_x(send_0), from_x(send_1), from_x(send_2)
-    mine_3, other_3, core_3 = rows(3, (send_0, send_1, send_2))
-    mine_0, _ = lax.optimization_barrier((step_0[0], mine_3))
-    far = own_sum(mine_0, core_0, across_0)
-    far = over(far, 4)
-    send_3 = for_x((mine_3, other_3), core_3)
-    across_3 = from_x(send_3)
-    pair = own_sum(step_1[0], core_1, across_1) + far.astype(jnp.float32)
-    mine_2, _ = lax.optimization_barrier((step_2[0], pair))
-    pair = over(pair, 8)
-    near = over(own_sum(mine_2, core_2, across_2), 4)
-    total = own_sum(mine_3, core_3, across_3) + near.astype(jnp.float32) + pair.astype(jnp.float32)
+    mine_0, other_0 = summed(step_0, core_0)
+    mine_1, other_1 = summed(step_1, core_1)
+    mine_2, other_2 = summed(step_2, core_2)
+    sends = [value.astype(jnp.bfloat16) for value in (mine_0, other_0, other_1, mine_2, other_2)]
+    step_3 = rows(3, sends)
+    far = over(sends[0], 4), over(sends[1], 6)
+    across_1 = over(sends[2], 2)
+    near = over(sends[3], 4), over(sends[4], 6)
+    mine_1, _ = lax.optimization_barrier((mine_1, step_3[0]))
+    pair = over(total_of(mine_1, across_1, *far), 8)
+    mine_3, other_3 = summed(step_3, step_3[2])
+    total = total_of(mine_3, over(other_3, 2), pair, *near)
     return (total * norm_factor).reshape(width // 4, modes, excitons)
 
 

time: 87.3 us -> 85.8 us (0.983)
  waiting for transfers between devices: 28.6 us -> 23.7 us
  starting transfers between devices: 11.9 us -> 14.9 us
    ppermute x15, waiting for transfers between devices: 28.6 us -> 23.7 us  [permute(): lax.ppermute(x, 'ka', [(i, j % size) for i, j in pairs if j is not None])]
    ppermute x15, starting transfers between devices: 11.9 us -> 14.9 us  [permute(): lax.ppermute(x, 'ka', [(i, j % size) for i, j in pairs if j is not None])]
  transfers between devices with their start and end apart: 15 -> 15, of which waited for: 8 -> 8; matrix products, arithmetic and copies ran while one was open for 1% -> 1% of each run, Pallas kernels for 48% -> 49%
where the time goes in v13:
time: 85.8 us; the launch traced here: 85.4 us
  Pallas kernels  44 us (51%)
  waiting for transfers between devices  23.7 us (28%)
  starting transfers between devices  14.9 us (17%)
  other arithmetic  1.35 us (2%)
  local copies, waits for them, and re-layouts  1.24 us (1%)
    pallas_call x4, Pallas kernels, rows_of(): pl.pallas_call(rows_kernel, out_shape=[jax.ShapeDtypeStruct((width // 4,...  24 us
    ppermute x15, waiting for transfers between devices, permute(): lax.ppermute(x, 'ka', [(i, j % size) for i, j in pairs if j is not None])  23.7 us
    ppermute x15, starting transfers between devices, permute(): lax.ppermute(x, 'ka', [(i, j % size) for i, j in pairs if j is not None])  14.9 us
    pallas_call x1, Pallas kernels, products_of(): pl.pallas_call(products_kernel, out_shape=jax.ShapeDtypeStruct((k_local,...  13.4 us
    pallas_call x2, Pallas kernels, turned_pieces(): pl.pallas_call(functools.partial(turn_kernel, first), out_shape=[jax.Shap...  6.7 us
  transfers between devices with their start and end apart: 15, of which 8 were waited for; matrix products, arithmetic and copies ran while one was open for 1% of the time, Pallas kernels for 49%

profile of v13, /device:TPU:0, one launch (start us, length us, event | category | flops | bytes accessed | tf_op | source)
XLA Modules:
  0.0 85.4 jit_solution(1314461151659571010)
XLA Ops:
  0.0 2.5 %shard_map.56 = bf16[2,256,1024]{2,1,0:T(8,128)(2,1)} custom-call(bf16[2,1024,1024]{2,1,0:T(8,128)(2,1)} %bitcast.8), custom_call_target="tpu_custom_call" | custom-call | bytes 2097152 | tf_op jit(solution)/shard_map/pallas_call | solution.py:137
  2.5 5.5 %collective-permute-start = (bf16[2,256,1024]{2,1,0:T(8,128)(2,1)}, bf16[2,256,1024]{2,1,0:T(8,128)(2,1)}, u32[]{:S(2)}, u32[]{:S(2)}) collective-permute-start(bf16[2,256,1024]{2,1,0:T(8,128)(2,1)} %shard_map.56), channel_id=1, source_target_pairs={{0,15},{1,0},{2,1},{3,2},{4,3},{5,4},{6,5},{7,6},{8,7},{9,8},{10,9... | collective-permute-start | bytes 3145736 | tf_op jit(solution)/shard_map/ppermute | solution.py:17
  8.0 4.2 %shard_map.58 = (bf16[2,256,1024]{2,1,0:T(8,128)(2,1)}, bf16[2,256,1024]{2,1,0:T(8,128)(2,1)}, bf16[2,256,1024]{2,1,0:T(8,128)(2,1)}) custom-call(bf16[2,1024,1024]{2,1,0:T(8,128)(2,1)} %bitcast.9), custom_call_target="tpu_custom_call" | custom-call | bytes 6291456 | tf_op jit(solution)/shard_map/pallas_call | solution.py:137
  12.2 0.7 collective-permute-start.2
  12.9 0.1 collective-permute-start.4
  13.0 0.6 collective-permute-start.6
  13.6 0.1 add_add_fusion.3
  13.7 13.4 %shard_map.55 = bf16[2,2,32,32,1024]{4,3,2,1,0:T(8,128)(2,1)} custom-call(s32[2,2]{1,0:T(2,128)} %first_ref.1, bf16[2,32,32,1024]{3,2,1,0:T(8,128)(2,1)} %coeffs_ref.1, bf16[2,2,32,32]{3,2,1,0:T(8,128)(2,1)} %cond_ref.1, bf16[2,2,32,32]{3,2,1,0:T(8,128)(2,1)} %val_ref.1), custom_call_target="tpu_custom_call" | custom-call | flops 6442450944 | bytes 12582912 | tf_op jit(solution)/shard_map/pallas_call | solution.py:90
  27.1 0.1 add_add_fusion.2
  27.1 0.0 collective-permute-done.next_ref
  27.1 7.6 %shard_map.57 = (f32[64,2048]{1,0:T(8,128)S(1)}, f32[64,2048]{1,0:T(8,128)S(1)}, bf16[128,2048]{1,0:T(8,128)(2,1)S(1)}) custom-call(s32[5]{0:T(128)S(1)} %get-tuple-element.30.pick_ref, bf16[2,1024,1024]{2,1,0:T(8,128)(2,1)} %bitcast.10, bf16[2,256,1024]{2,1,0:T(8,128)(2,1)} %collective-permute-done.next_ref, bf16[2,2,1024,1024]{3,2,1,0:T(8,128)(2,1)} %bitcast.14), custom_call_target="tpu_custom_call" | custom-call | flops 2147483648 | bytes 8388608 | tf_op jit(solution)/shard_map/pallas_call | solution.py:212
  34.7 0.1 collective-permute-start.1
  34.8 5.5 %shard_map.59 = (f32[64,2048]{1,0:T(8,128)S(1)}, f32[64,2048]{1,0:T(8,128)S(1)}, bf16[128,2048]{1,0:T(8,128)(2,1)S(1)}) custom-call(s32[5]{0:T(128)S(1)} %get-tuple-element.33.pick_ref, bf16[2,1024,1024]{2,1,0:T(8,128)(2,1)} %bitcast.11, bf16[2,256,1024]{2,1,0:T(8,128)(2,1)S(1)} %collective-permute-done.2.next_ref, bf16[2,2,1024,1024]{3,2,1,0:T(8,128)(2,1)} %bitcast.15), custom_call_target="tpu_custom_call" | custom-call | flops 2147483648 | bytes 8388608 | tf_op jit(solution)/shard_map/pallas_call | solution.py:212
  40.3 0.6 collective-permute-start.3
  40.8 2.3 %collective-permute-done.4.next_ref = bf16[2,256,1024]{2,1,0:T(8,128)(2,1)S(1)} collective-permute-done((bf16[2,256,1024]{2,1,0:T(8,128)(2,1)}, bf16[2,256,1024]{2,1,0:T(8,128)(2,1)S(1)}, u32[]{:S(2)}, u32[]{:S(2)}) %collective-permute-start.4) | collective-permute-done | bytes 1048608 | tf_op jit(solution)/shard_map/ppermute | solution.py:17
  43.1 5.5 %shard_map.60 = (f32[64,2048]{1,0:T(8,128)S(1)}, f32[64,2048]{1,0:T(8,128)S(1)}, bf16[128,2048]{1,0:T(8,128)(2,1)S(1)}) custom-call(s32[5]{0:T(128)S(1)} %get-tuple-element.38.pick_ref, bf16[2,1024,1024]{2,1,0:T(8,128)(2,1)} %bitcast.12, bf16[2,256,1024]{2,1,0:T(8,128)(2,1)S(1)} %collective-permute-done.4.next_ref, bf16[2,2,1024,1024]{3,2,1,0:T(8,128)(2,1)} %bitcast.16), custom_call_target="tpu_custom_call" | custom-call | flops 2147483648 | bytes 8388608 | tf_op jit(solution)/shard_map/pallas_call | solution.py:212
  48.6 0.1 collective-permute-start.5
  48.6 5.7 %collective-permute-done.6.next_ref = bf16[2,256,1024]{2,1,0:T(8,128)(2,1)S(1)} collective-permute-done((bf16[2,256,1024]{2,1,0:T(8,128)(2,1)}, bf16[2,256,1024]{2,1,0:T(8,128)(2,1)S(1)}, u32[]{:S(2)}, u32[]{:S(2)}) %collective-permute-start.6) | collective-permute-done | bytes 1048608 | tf_op jit(solution)/shard_map/ppermute | solution.py:17
  54.3 0.0 collective-permute-done.1
  54.3 0.0 collective-permute-done.3
  54.3 0.0 collective-permute-done.5
  54.3 0.1 convert_element_type.54
  54.4 0.1 convert_element_type.57
  54.6 0.1 convert_element_type.59
  54.7 0.1 fusion.9
  54.8 0.1 collective-permute-start.11
  54.9 0.1 collective-permute-start.10
  54.9 0.3 slice_add_fusion
  55.3 3.5 %collective-permute-start.9 = (bf16[64,2048]{1,0:T(8,128)(2,1)S(1)}, bf16[64,2048]{1,0:T(8,128)(2,1)S(1)}, u32[]{:S(2)}, u32[]{:S(2)}) collective-permute-start(bf16[64,2048]{1,0:T(8,128)(2,1)S(1)} %get-tuple-element.56), channel_id=1, source_target_pairs={{0,2},{1,3},{2,0},{3,1},{4,6},{5,7},{6,4},{7,5},{8,10},{9,11},{10,... | collective-permute-start | bytes 786440 | tf_op jit(solution)/shard_map/ppermute | solution.py:17
  58.7 5.5 %shard_map.61 = (f32[64,2048]{1,0:T(8,128)S(1)}, f32[64,2048]{1,0:T(8,128)S(1)}, bf16[128,2048]{1,0:T(8,128)(2,1)S(1)}) custom-call(s32[5]{0:T(128)S(1)} %get-tuple-element.49.pick_ref, bf16[2,1024,1024]{2,1,0:T(8,128)(2,1)} %bitcast.13, bf16[2,256,1024]{2,1,0:T(8,128)(2,1)S(1)} %collective-permute-done.6.next_ref, bf16[2,2,1024,1024]{3,2,1,0:T(8,128)(2,1)} %bitcast.17), custom_call_target="tpu_custom_call" | custom-call | flops 2147483648 | bytes 8388608 | tf_op jit(solution)/shard_map/pallas_call | solution.py:212
  64.2 0.1 collective-permute-start.7
  64.3 0.2 collective-permute-start.14
  64.5 0.5 collective-permute-done.11
  65.0 0.8 collective-permute-start.13
  65.8 1.3 %collective-permute-done.10 = bf16[64,2048]{1,0:T(8,128)(2,1)S(1)} collective-permute-done((bf16[64,2048]{1,0:T(8,128)(2,1)S(1)}, bf16[64,2048]{1,0:T(8,128)(2,1)S(1)}, u32[]{:S(2)}, u32[]{:S(2)}) %collective-permute-start.10) | collective-permute-done | bytes 262176 | tf_op jit(solution)/shard_map/ppermute | solution.py:17
  67.1 0.9 %collective-permute-done.9 = bf16[64,2048]{1,0:T(8,128)(2,1)S(1)} collective-permute-done((bf16[64,2048]{1,0:T(8,128)(2,1)S(1)}, bf16[64,2048]{1,0:T(8,128)(2,1)S(1)}, u32[]{:S(2)}, u32[]{:S(2)}) %collective-permute-start.9) | collective-permute-done | bytes 262176 | tf_op jit(solution)/shard_map/ppermute | solution.py:17
  68.0 0.1 add_convert_fusion
  68.1 1.4 %collective-permute-start.12 = (bf16[64,2048]{1,0:T(8,128)(2,1)S(1)}, bf16[64,2048]{1,0:T(8,128)(2,1)S(1)}, u32[]{:S(2)}, u32[]{:S(2)}) collective-permute-start(bf16[64,2048]{1,0:T(8,128)(2,1)S(1)} %add_convert_fusion), channel_id=1, source_target_pairs={{0,8},{1,9},{2,10},{3,11},{4,12},{5,13},{6,14},{7,15},{8,0},{9,1},... | collective-permute-start | bytes 786440 | tf_op jit(solution)/shard_map/ppermute | solution.py:17
  69.5 0.0 collective-permute-done.7
  69.5 0.1 convert_element_type.62
  69.7 0.1 fusion
  69.7 1.3 %collective-permute-start.8 = (bf16[64,2048]{1,0:T(8,128)(2,1)S(1)}, bf16[64,2048]{1,0:T(8,128)(2,1)S(1)}, u32[]{:S(2)}, u32[]{:S(2)}) collective-permute-start(bf16[64,2048]{1,0:T(8,128)(2,1)S(1)} %fusion), channel_id=1, source_target_pairs={{0,2},{1,3},{2,0},{3,1},{4,6},{5,7},{6,4},{7,5},{8,10},{9,11},{10,... | collective-permute-start | bytes 786440 | tf_op jit(solution)/shard_map/ppermute | solution.py:17
  71.0 9.0 %collective-permute-done.14 = bf16[64,2048]{1,0:T(8,128)(2,1)S(1)} collective-permute-done((bf16[64,2048]{1,0:T(8,128)(2,1)S(1)}, bf16[64,2048]{1,0:T(8,128)(2,1)S(1)}, u32[]{:S(2)}, u32[]{:S(2)}) %collective-permute-start.14) | collective-permute-done | bytes 262176 | tf_op jit(solution)/shard_map/ppermute | solution.py:17
  80.0 3.7 %collective-permute-done.13 = bf16[64,2048]{1,0:T(8,128)(2,1)S(1)} collective-permute-done((bf16[64,2048]{1,0:T(8,128)(2,1)S(1)}, bf16[64,2048]{1,0:T(8,128)(2,1)S(1)}, u32[]{:S(2)}, u32[]{:S(2)}) %collective-permute-start.13) | collective-permute-done | bytes 262176 | tf_op jit(solution)/shard_map/ppermute | solution.py:17
  83.7 0.3 collective-permute-done.12
  84.0 0.0 collective-permute-done.8
  84.0 0.2 fusion.5
  84.2 1.2 %reshape.11 = f32[64,2,1024]{2,1,0:T(2,128)} reshape(f32[64,2048]{1,0:T(8,128)S(1)} %fusion.5) | data formatting | bytes 1048576 | tf_op jit(solution)/shard_map/reshape | solution.py:295
  (4 shorter events, 0.0 us)
Async XLA Ops:
  0.0 13.6 %copy-start = (s32[2]{0:T(128)S(1)}, s32[2]{0:T(128)}, u32[]{:S(2)}) copy-start(s32[2]{0:T(128)} %param.8) | copy-start | bytes 28
  2.5 24.6 %collective-permute-start = (bf16[2,256,1024]{2,1,0:T(8,128)(2,1)}, bf16[2,256,1024]{2,1,0:T(8,128)(2,1)}, u32[]{:S(2)}, u32[]{:S(2)}) collective-permute-start(bf16[2,256,1024]{2,1,0:T(8,128)(2,1)} %shard_map.56), channel_id=1, source_target_pairs={{0,15},{1,0},{2,1},{3,2},{4,3},{5,4},{6,5},{7,6},{8,7},{9,8},{10,9... | collective-permute-start | bytes 3145736 | tf_op jit(solution)/shard_map/ppermute | solution.py:17
  12.2 22.6 %collective-permute-start.2 = (bf16[2,256,1024]{2,1,0:T(8,128)(2,1)}, bf16[2,256,1024]{2,1,0:T(8,128)(2,1)S(1)}, u32[]{:S(2)}, u32[]{:S(2)}) collective-permute-start(bf16[2,256,1024]{2,1,0:T(8,128)(2,1)} %get-tuple-element.35), channel_id=1, source_target_pairs={{0,15},{1,0},{2,1},{3,2},{4,3},{5,4},{6,5},{7,6},{8,7},{9,8},{10,9... | collective-permute-start | bytes 3145736 | tf_op jit(solution)/shard_map/ppermute | solution.py:17
  12.9 30.2 %collective-permute-start.4 = (bf16[2,256,1024]{2,1,0:T(8,128)(2,1)}, bf16[2,256,1024]{2,1,0:T(8,128)(2,1)S(1)}, u32[]{:S(2)}, u32[]{:S(2)}) collective-permute-start(bf16[2,256,1024]{2,1,0:T(8,128)(2,1)} %get-tuple-element.39), channel_id=1, source_target_pairs={{0,15},{1,0},{2,1},{3,2},{4,3},{5,4},{6,5},{7,6},{8,7},{9,8},{10,9... | collective-permute-start | bytes 3145736 | tf_op jit(solution)/shard_map/ppermute | solution.py:17
  13.0 41.3 %collective-permute-start.6 = (bf16[2,256,1024]{2,1,0:T(8,128)(2,1)}, bf16[2,256,1024]{2,1,0:T(8,128)(2,1)S(1)}, u32[]{:S(2)}, u32[]{:S(2)}) collective-permute-start(bf16[2,256,1024]{2,1,0:T(8,128)(2,1)} %get-tuple-element.41), channel_id=1, source_target_pairs={{0,15},{1,0},{2,1},{3,2},{4,3},{5,4},{6,5},{7,6},{8,7},{9,8},{10,9... | collective-permute-start | bytes 3145736 | tf_op jit(solution)/shard_map/ppermute | solution.py:17
  34.7 19.6 %collective-permute-start.1 = (bf16[128,2048]{1,0:T(8,128)(2,1)S(1)}, bf16[128,2048]{1,0:T(8,128)(2,1)S(1)}, u32[]{:S(2)}, u32[]{:S(2)}) collective-permute-start(bf16[128,2048]{1,0:T(8,128)(2,1)S(1)} %get-tuple-element.32), channel_id=1, source_target_pairs={{0,1},{1,0},{2,3},{3,2},{4,5},{5,4},{6,7},{7,6},{8,9},{9,8},{10,11... | collective-permute-start | bytes 1572872 | tf_op jit(solution)/shard_map/ppermute | solution.py:17
  40.3 14.1 %collective-permute-start.3 = (bf16[128,2048]{1,0:T(8,128)(2,1)S(1)}, bf16[128,2048]{1,0:T(8,128)(2,1)S(1)}, u32[]{:S(2)}, u32[]{:S(2)}) collective-permute-start(bf16[128,2048]{1,0:T(8,128)(2,1)S(1)} %get-tuple-element.36), channel_id=1, source_target_pairs={{0,1},{1,0},{2,3},{3,2},{4,5},{5,4},{6,7},{7,6},{8,9},{9,8},{10,11... | collective-permute-start | bytes 1572872 | tf_op jit(solution)/shard_map/ppermute | solution.py:17
  48.6 5.8 %collective-permute-start.5 = (bf16[128,2048]{1,0:T(8,128)(2,1)S(1)}, bf16[128,2048]{1,0:T(8,128)(2,1)S(1)}, u32[]{:S(2)}, u32[]{:S(2)}) collective-permute-start(bf16[128,2048]{1,0:T(8,128)(2,1)S(1)} %get-tuple-element.40), channel_id=1, source_target_pairs={{0,1},{1,0},{2,3},{3,2},{4,5},{5,4},{6,7},{7,6},{8,9},{9,8},{10,11... | collective-permute-start | bytes 1572872 | tf_op jit(solution)/shard_map/ppermute | solution.py:17
  54.8 10.2 %collective-permute-start.11 = (bf16[64,2048]{1,0:T(8,128)(2,1)S(1)}, bf16[64,2048]{1,0:T(8,128)(2,1)S(1)}, u32[]{:S(2)}, u32[]{:S(2)}) collective-permute-start(bf16[64,2048]{1,0:T(8,128)(2,1)S(1)} %get-tuple-element.59), channel_id=1, source_target_pairs={{0,6},{1,7},{2,4},{3,5},{4,2},{5,3},{6,0},{7,1},{8,14},{9,15},{10,... | collective-permute-start | bytes 786440 | tf_op jit(solution)/shard_map/ppermute | solution.py:17
  54.9 12.3 %collective-permute-start.10 = (bf16[64,2048]{1,0:T(8,128)(2,1)S(1)}, bf16[64,2048]{1,0:T(8,128)(2,1)S(1)}, u32[]{:S(2)}, u32[]{:S(2)}) collective-permute-start(bf16[64,2048]{1,0:T(8,128)(2,1)S(1)} %get-tuple-element.60), channel_id=1, source_target_pairs={{0,4},{1,5},{2,6},{3,7},{4,0},{5,1},{6,2},{7,3},{8,12},{9,13},{10,... | collective-permute-start | bytes 786440 | tf_op jit(solution)/shard_map/ppermute | solution.py:17
  55.3 12.8 %collective-permute-start.9 = (bf16[64,2048]{1,0:T(8,128)(2,1)S(1)}, bf16[64,2048]{1,0:T(8,128)(2,1)S(1)}, u32[]{:S(2)}, u32[]{:S(2)}) collective-permute-start(bf16[64,2048]{1,0:T(8,128)(2,1)S(1)} %get-tuple-element.56), channel_id=1, source_target_pairs={{0,2},{1,3},{2,0},{3,1},{4,6},{5,7},{6,4},{7,5},{8,10},{9,11},{10,... | collective-permute-start | bytes 786440 | tf_op jit(solution)/shard_map/ppermute | solution.py:17
  64.2 5.4 %collective-permute-start.7 = (bf16[128,2048]{1,0:T(8,128)(2,1)S(1)}, bf16[128,2048]{1,0:T(8,128)(2,1)S(1)}, u32[]{:S(2)}, u32[]{:S(2)}) collective-permute-start(bf16[128,2048]{1,0:T(8,128)(2,1)S(1)} %get-tuple-element.52), channel_id=1, source_target_pairs={{0,1},{1,0},{2,3},{3,2},{4,5},{5,4},{6,7},{7,6},{8,9},{9,8},{10,11... | collective-permute-start | bytes 1572872 | tf_op jit(solution)/shard_map/ppermute | solution.py:17
  64.3 15.7 %collective-permute-start.14 = (bf16[64,2048]{1,0:T(8,128)(2,1)S(1)}, bf16[64,2048]{1,0:T(8,128)(2,1)S(1)}, u32[]{:S(2)}, u32[]{:S(2)}) collective-permute-start(bf16[64,2048]{1,0:T(8,128)(2,1)S(1)} %get-tuple-element.66), channel_id=1, source_target_pairs={{0,6},{1,7},{2,4},{3,5},{4,2},{5,3},{6,0},{7,1},{8,14},{9,15},{10,... | collective-permute-start | bytes 786440 | tf_op jit(solution)/shard_map/ppermute | solution.py:17
  65.0 18.7 %collective-permute-start.13 = (bf16[64,2048]{1,0:T(8,128)(2,1)S(1)}, bf16[64,2048]{1,0:T(8,128)(2,1)S(1)}, u32[]{:S(2)}, u32[]{:S(2)}) collective-permute-start(bf16[64,2048]{1,0:T(8,128)(2,1)S(1)} %get-tuple-element.65), channel_id=1, source_target_pairs={{0,4},{1,5},{2,6},{3,7},{4,0},{5,1},{6,2},{7,3},{8,12},{9,13},{10,... | collective-permute-start | bytes 786440 | tf_op jit(solution)/shard_map/ppermute | solution.py:17
  68.1 15.9 %collective-permute-start.12 = (bf16[64,2048]{1,0:T(8,128)(2,1)S(1)}, bf16[64,2048]{1,0:T(8,128)(2,1)S(1)}, u32[]{:S(2)}, u32[]{:S(2)}) collective-permute-start(bf16[64,2048]{1,0:T(8,128)(2,1)S(1)} %add_convert_fusion), channel_id=1, source_target_pairs={{0,8},{1,9},{2,10},{3,11},{4,12},{5,13},{6,14},{7,15},{8,0},{9,1},... | collective-permute-start | bytes 786440 | tf_op jit(solution)/shard_map/ppermute | solution.py:17
  69.7 14.3 %collective-permute-start.8 = (bf16[64,2048]{1,0:T(8,128)(2,1)S(1)}, bf16[64,2048]{1,0:T(8,128)(2,1)S(1)}, u32[]{:S(2)}, u32[]{:S(2)}) collective-permute-start(bf16[64,2048]{1,0:T(8,128)(2,1)S(1)} %fusion), channel_id=1, source_target_pairs={{0,2},{1,3},{2,0},{3,1},{4,6},{5,7},{6,4},{7,5},{8,10},{9,11},{10,... | collective-permute-start | bytes 786440 | tf_op jit(solution)/shard_map/ppermute | solution.py:17

commit v14 on v13

--- a/solution.py
+++ b/solution.py
@@ -283,15 +283,19 @@
     mine_0, other_0 = summed(step_0, core_0)
     mine_1, other_1 = summed(step_1, core_1)
     mine_2, other_2 = summed(step_2, core_2)
-    sends = [value.astype(jnp.bfloat16) for value in (mine_0, other_0, other_1, mine_2, other_2)]
+    sends = [value.astype(jnp.bfloat16) for value in (mine_0, other_0, other_1, other_2)]
     step_3 = rows(3, sends)
     far = over(sends[0], 4), over(sends[1], 6)
     across_1 = over(sends[2], 2)
-    near = over(sends[3], 4), over(sends[4], 6)
+    send_2, _ = lax.optimization_barrier((sends[3], step_3[0]))
+    across_2 = over(send_2, 2)
     mine_1, _ = lax.optimization_barrier((mine_1, step_3[0]))
-    pair = over(total_of(mine_1, across_1, *far), 8)
+    pair = total_of(mine_1, across_1, *far)
     mine_3, other_3 = summed(step_3, step_3[2])
-    total = total_of(mine_3, over(other_3, 2), pair, *near)
+    mine_2, _ = lax.optimization_barrier((mine_2, (pair, other_3)))
+    pair = over(pair, 8)
+    near = over(total_of(mine_2, across_2), 4)
+    total = total_of(mine_3, over(other_3, 2), pair, near)
     return (total * norm_factor).reshape(width // 4, modes, excitons)
 
 

time: 85.8 us -> 90.2 us (1.051)
  waiting for transfers between devices: 23.7 us -> 29.7 us
  starting transfers between devices: 14.9 us -> 13.2 us
    ppermute x15, waiting for transfers between devices: 23.7 us -> 29.7 us  [permute(): lax.ppermute(x, 'ka', [(i, j % size) for i, j in pairs if j is not None])]
    ppermute x15, starting transfers between devices: 14.9 us -> 13.2 us  [permute(): lax.ppermute(x, 'ka', [(i, j % size) for i, j in pairs if j is not None])]
  transfers between devices with their start and end apart: 15 -> 15, of which waited for: 8 -> 7; matrix products, arithmetic and copies ran while one was open for 1% -> 1% of each run, Pallas kernels for 49% -> 46%
where the time goes in v14:
time: 90.2 us; the launch traced here: 89.7 us
  Pallas kernels  44 us (49%)
  waiting for transfers between devices  29.7 us (33%)
  starting transfers between devices  13.2 us (15%)
  other arithmetic  1.34 us (1%)
  local copies, waits for them, and re-layouts  1.24 us (1%)
    ppermute x15, waiting for transfers between devices, permute(): lax.ppermute(x, 'ka', [(i, j % size) for i, j in pairs if j is not None])  29.7 us
    pallas_call x4, Pallas kernels, rows_of(): pl.pallas_call(rows_kernel, out_shape=[jax.ShapeDtypeStruct((width // 4,...  23.9 us
    pallas_call x1, Pallas kernels, products_of(): pl.pallas_call(products_kernel, out_shape=jax.ShapeDtypeStruct((k_local,...  13.4 us
    ppermute x15, starting transfers between devices, permute(): lax.ppermute(x, 'ka', [(i, j % size) for i, j in pairs if j is not None])  13.2 us
    pallas_call x2, Pallas kernels, turned_pieces(): pl.pallas_call(functools.partial(turn_kernel, first), out_shape=[jax.Shap...  6.7 us
  transfers between devices with their start and end apart: 15, of which 7 were waited for; matrix products, arithmetic and copies ran while one was open for 1% of the time, Pallas kernels for 46%

profile of v14, /device:TPU:0, one launch (start us, length us, event | category | flops | bytes accessed | tf_op | source)
XLA Modules:
  0.0 89.7 jit_solution(18035953942853064871)
XLA Ops:
  0.0 2.5 %shard_map.56 = bf16[2,256,1024]{2,1,0:T(8,128)(2,1)} custom-call(bf16[2,1024,1024]{2,1,0:T(8,128)(2,1)} %bitcast.8), custom_call_target="tpu_custom_call" | custom-call | bytes 2097152 | tf_op jit(solution)/shard_map/pallas_call | solution.py:137
  2.5 5.5 %collective-permute-start = (bf16[2,256,1024]{2,1,0:T(8,128)(2,1)}, bf16[2,256,1024]{2,1,0:T(8,128)(2,1)}, u32[]{:S(2)}, u32[]{:S(2)}) collective-permute-start(bf16[2,256,1024]{2,1,0:T(8,128)(2,1)} %shard_map.56), channel_id=1, source_target_pairs={{0,15},{1,0},{2,1},{3,2},{4,3},{5,4},{6,5},{7,6},{8,7},{9,8},{10,9... | collective-permute-start | bytes 3145736 | tf_op jit(solution)/shard_map/ppermute | solution.py:17
  8.0 4.2 %shard_map.58 = (bf16[2,256,1024]{2,1,0:T(8,128)(2,1)}, bf16[2,256,1024]{2,1,0:T(8,128)(2,1)}, bf16[2,256,1024]{2,1,0:T(8,128)(2,1)}) custom-call(bf16[2,1024,1024]{2,1,0:T(8,128)(2,1)} %bitcast.9), custom_call_target="tpu_custom_call" | custom-call | bytes 6291456 | tf_op jit(solution)/shard_map/pallas_call | solution.py:137
  12.2 0.7 collective-permute-start.2
  12.9 0.1 collective-permute-start.4
  13.0 0.6 collective-permute-start.6
  13.6 0.1 add_add_fusion.3
  13.7 13.4 %shard_map.55 = bf16[2,2,32,32,1024]{4,3,2,1,0:T(8,128)(2,1)} custom-call(s32[2,2]{1,0:T(2,128)} %first_ref.1, bf16[2,32,32,1024]{3,2,1,0:T(8,128)(2,1)} %coeffs_ref.1, bf16[2,2,32,32]{3,2,1,0:T(8,128)(2,1)} %cond_ref.1, bf16[2,2,32,32]{3,2,1,0:T(8,128)(2,1)} %val_ref.1), custom_call_target="tpu_custom_call" | custom-call | flops 6442450944 | bytes 12582912 | tf_op jit(solution)/shard_map/pallas_call | solution.py:90
  27.1 0.1 add_add_fusion.2
  27.1 0.0 collective-permute-done.next_ref
  27.1 7.6 %shard_map.57 = (f32[64,2048]{1,0:T(8,128)S(1)}, f32[64,2048]{1,0:T(8,128)S(1)}, bf16[128,2048]{1,0:T(8,128)(2,1)S(1)}) custom-call(s32[5]{0:T(128)S(1)} %get-tuple-element.32.pick_ref, bf16[2,1024,1024]{2,1,0:T(8,128)(2,1)} %bitcast.10, bf16[2,256,1024]{2,1,0:T(8,128)(2,1)} %collective-permute-done.next_ref, bf16[2,2,1024,1024]{3,2,1,0:T(8,128)(2,1)} %bitcast.14), custom_call_target="tpu_custom_call" | custom-call | flops 2147483648 | bytes 8388608 | tf_op jit(solution)/shard_map/pallas_call | solution.py:212
  34.7 0.0 collective-permute-done.2.next_ref
  34.7 5.5 %shard_map.59 = (f32[64,2048]{1,0:T(8,128)S(1)}, f32[64,2048]{1,0:T(8,128)S(1)}, bf16[128,2048]{1,0:T(8,128)(2,1)S(1)}) custom-call(s32[5]{0:T(128)S(1)} %get-tuple-element.35.pick_ref, bf16[2,1024,1024]{2,1,0:T(8,128)(2,1)} %bitcast.11, bf16[2,256,1024]{2,1,0:T(8,128)(2,1)S(1)} %collective-permute-done.2.next_ref, bf16[2,2,1024,1024]{3,2,1,0:T(8,128)(2,1)} %bitcast.15), custom_call_target="tpu_custom_call" | custom-call | flops 2147483648 | bytes 8388608 | tf_op jit(solution)/shard_map/pallas_call | solution.py:212
  40.2 2.9 %collective-permute-done.4.next_ref = bf16[2,256,1024]{2,1,0:T(8,128)(2,1)S(1)} collective-permute-done((bf16[2,256,1024]{2,1,0:T(8,128)(2,1)}, bf16[2,256,1024]{2,1,0:T(8,128)(2,1)S(1)}, u32[]{:S(2)}, u32[]{:S(2)}) %collective-permute-start.4) | collective-permute-done | bytes 1048608 | tf_op jit(solution)/shard_map/ppermute | solution.py:17
  43.1 5.5 %shard_map.60 = (f32[64,2048]{1,0:T(8,128)S(1)}, f32[64,2048]{1,0:T(8,128)S(1)}, bf16[128,2048]{1,0:T(8,128)(2,1)S(1)}) custom-call(s32[5]{0:T(128)S(1)} %get-tuple-element.40.pick_ref, bf16[2,1024,1024]{2,1,0:T(8,128)(2,1)} %bitcast.12, bf16[2,256,1024]{2,1,0:T(8,128)(2,1)S(1)} %collective-permute-done.4.next_ref, bf16[2,2,1024,1024]{3,2,1,0:T(8,128)(2,1)} %bitcast.16), custom_call_target="tpu_custom_call" | custom-call | flops 2147483648 | bytes 8388608 | tf_op jit(solution)/shard_map/pallas_call | solution.py:212
  48.6 0.1 collective-permute-start.5
  48.6 0.5 collective-permute-start.3
  49.1 0.1 collective-permute-start.1
  49.2 5.1 %collective-permute-done.6.next_ref = bf16[2,256,1024]{2,1,0:T(8,128)(2,1)S(1)} collective-permute-done((bf16[2,256,1024]{2,1,0:T(8,128)(2,1)}, bf16[2,256,1024]{2,1,0:T(8,128)(2,1)S(1)}, u32[]{:S(2)}, u32[]{:S(2)}) %collective-permute-start.6) | collective-permute-done | bytes 1048608 | tf_op jit(solution)/shard_map/ppermute | solution.py:17
  54.3 0.0 collective-permute-done.3
  54.3 0.0 collective-permute-done.1
  54.3 0.1 convert_element_type.59
  54.4 0.1 convert_element_type.54
  54.6 0.1 convert_element_type.57
  54.7 0.3 slice_add_fusion.1
  55.0 0.1 collective-permute-start.10
  55.1 0.1 collective-permute-start.11
  55.1 3.4 %collective-permute-start.9 = (bf16[64,2048]{1,0:T(8,128)(2,1)S(1)}, bf16[64,2048]{1,0:T(8,128)(2,1)S(1)}, u32[]{:S(2)}, u32[]{:S(2)}) collective-permute-start(bf16[64,2048]{1,0:T(8,128)(2,1)S(1)} %get-tuple-element.60), channel_id=1, source_target_pairs={{0,2},{1,3},{2,0},{3,1},{4,6},{5,7},{6,4},{7,5},{8,10},{9,11},{10,... | collective-permute-start | bytes 786440 | tf_op jit(solution)/shard_map/ppermute | solution.py:17
  58.5 0.1 slice_add_fusion
  58.7 5.5 %shard_map.61 = (f32[64,2048]{1,0:T(8,128)S(1)}, f32[64,2048]{1,0:T(8,128)S(1)}, bf16[128,2048]{1,0:T(8,128)(2,1)S(1)}) custom-call(s32[5]{0:T(128)S(1)} %get-tuple-element.50.pick_ref, bf16[2,1024,1024]{2,1,0:T(8,128)(2,1)} %bitcast.13, bf16[2,256,1024]{2,1,0:T(8,128)(2,1)S(1)} %collective-permute-done.6.next_ref, bf16[2,2,1024,1024]{3,2,1,0:T(8,128)(2,1)} %bitcast.17), custom_call_target="tpu_custom_call" | custom-call | flops 2147483648 | bytes 8388608 | tf_op jit(solution)/shard_map/pallas_call | solution.py:212
  64.1 0.1 collective-permute-start.7
  64.2 0.1 collective-permute-start.13
  64.3 0.0 collective-permute-done.10
  64.3 1.4 %collective-permute-done.11 = bf16[64,2048]{1,0:T(8,128)(2,1)S(1)} collective-permute-done((bf16[64,2048]{1,0:T(8,128)(2,1)S(1)}, bf16[64,2048]{1,0:T(8,128)(2,1)S(1)}, u32[]{:S(2)}, u32[]{:S(2)}) %collective-permute-start.11) | collective-permute-done | bytes 262176 | tf_op jit(solution)/shard_map/ppermute | solution.py:17
  65.7 5.4 %collective-permute-done.9 = bf16[64,2048]{1,0:T(8,128)(2,1)S(1)} collective-permute-done((bf16[64,2048]{1,0:T(8,128)(2,1)S(1)}, bf16[64,2048]{1,0:T(8,128)(2,1)S(1)}, u32[]{:S(2)}, u32[]{:S(2)}) %collective-permute-start.9) | collective-permute-done | bytes 262176 | tf_op jit(solution)/shard_map/ppermute | solution.py:17
  71.2 0.1 convert_add_fusion
  71.3 0.1 collective-permute-start.12
  71.4 0.0 collective-permute-done.7
  71.4 0.1 convert_element_type.61
  71.5 0.1 slice_add_fusion.2
  71.6 3.9 %collective-permute-done.13 = bf16[64,2048]{1,0:T(8,128)(2,1)S(1)} collective-permute-done((bf16[64,2048]{1,0:T(8,128)(2,1)S(1)}, bf16[64,2048]{1,0:T(8,128)(2,1)S(1)}, u32[]{:S(2)}, u32[]{:S(2)}) %collective-permute-start.13) | collective-permute-done | bytes 262176 | tf_op jit(solution)/shard_map/ppermute | solution.py:17
  75.5 1.6 %collective-permute-start.14 = (bf16[64,2048]{1,0:T(8,128)(2,1)S(1)}, bf16[64,2048]{1,0:T(8,128)(2,1)S(1)}, u32[]{:S(2)}, u32[]{:S(2)}) collective-permute-start(bf16[64,2048]{1,0:T(8,128)(2,1)S(1)} %add_convert_fusion), channel_id=1, source_target_pairs={{0,4},{1,5},{2,6},{3,7},{4,0},{5,1},{6,2},{7,3},{8,12},{9,13},{10,... | collective-permute-start | bytes 786440 | tf_op jit(solution)/shard_map/ppermute | solution.py:17
  77.1 0.3 collective-permute-start.8
  77.4 9.2 %collective-permute-done.12 = bf16[64,2048]{1,0:T(8,128)(2,1)S(1)} collective-permute-done((bf16[64,2048]{1,0:T(8,128)(2,1)S(1)}, bf16[64,2048]{1,0:T(8,128)(2,1)S(1)}, u32[]{:S(2)}, u32[]{:S(2)}) %collective-permute-start.12) | collective-permute-done | bytes 262176 | tf_op jit(solution)/shard_map/ppermute | solution.py:17
  86.7 1.6 %collective-permute-done.14 = bf16[64,2048]{1,0:T(8,128)(2,1)S(1)} collective-permute-done((bf16[64,2048]{1,0:T(8,128)(2,1)S(1)}, bf16[64,2048]{1,0:T(8,128)(2,1)S(1)}, u32[]{:S(2)}, u32[]{:S(2)}) %collective-permute-start.14) | collective-permute-done | bytes 262176 | tf_op jit(solution)/shard_map/ppermute | solution.py:17
  88.3 0.0 collective-permute-done.8
  88.3 0.1 fusion.3
  88.5 1.2 %reshape.11 = f32[64,2,1024]{2,1,0:T(2,128)} reshape(f32[64,2048]{1,0:T(8,128)S(1)} %fusion.3) | data formatting | bytes 1048576 | tf_op jit(solution)/shard_map/reshape | solution.py:299
  (5 shorter events, 0.1 us)
Async XLA Ops:
  0.0 13.6 %copy-start = (s32[2]{0:T(128)S(1)}, s32[2]{0:T(128)}, u32[]{:S(2)}) copy-start(s32[2]{0:T(128)} %param.8) | copy-start | bytes 28
  2.5 24.6 %collective-permute-start = (bf16[2,256,1024]{2,1,0:T(8,128)(2,1)}, bf16[2,256,1024]{2,1,0:T(8,128)(2,1)}, u32[]{:S(2)}, u32[]{:S(2)}) collective-permute-start(bf16[2,256,1024]{2,1,0:T(8,128)(2,1)} %shard_map.56), channel_id=1, source_target_pairs={{0,15},{1,0},{2,1},{3,2},{4,3},{5,4},{6,5},{7,6},{8,7},{9,8},{10,9... | collective-permute-start | bytes 3145736 | tf_op jit(solution)/shard_map/ppermute | solution.py:17
  12.2 22.5 %collective-permute-start.2 = (bf16[2,256,1024]{2,1,0:T(8,128)(2,1)}, bf16[2,256,1024]{2,1,0:T(8,128)(2,1)S(1)}, u32[]{:S(2)}, u32[]{:S(2)}) collective-permute-start(bf16[2,256,1024]{2,1,0:T(8,128)(2,1)} %get-tuple-element.37), channel_id=1, source_target_pairs={{0,15},{1,0},{2,1},{3,2},{4,3},{5,4},{6,5},{7,6},{8,7},{9,8},{10,9... | collective-permute-start | bytes 3145736 | tf_op jit(solution)/shard_map/ppermute | solution.py:17
  12.9 30.2 %collective-permute-start.4 = (bf16[2,256,1024]{2,1,0:T(8,128)(2,1)}, bf16[2,256,1024]{2,1,0:T(8,128)(2,1)S(1)}, u32[]{:S(2)}, u32[]{:S(2)}) collective-permute-start(bf16[2,256,1024]{2,1,0:T(8,128)(2,1)} %get-tuple-element.41), channel_id=1, source_target_pairs={{0,15},{1,0},{2,1},{3,2},{4,3},{5,4},{6,5},{7,6},{8,7},{9,8},{10,9... | collective-permute-start | bytes 3145736 | tf_op jit(solution)/shard_map/ppermute | solution.py:17
  13.0 41.3 %collective-permute-start.6 = (bf16[2,256,1024]{2,1,0:T(8,128)(2,1)}, bf16[2,256,1024]{2,1,0:T(8,128)(2,1)S(1)}, u32[]{:S(2)}, u32[]{:S(2)}) collective-permute-start(bf16[2,256,1024]{2,1,0:T(8,128)(2,1)} %get-tuple-element.43), channel_id=1, source_target_pairs={{0,15},{1,0},{2,1},{3,2},{4,3},{5,4},{6,5},{7,6},{8,7},{9,8},{10,9... | collective-permute-start | bytes 3145736 | tf_op jit(solution)/shard_map/ppermute | solution.py:17
  48.6 5.8 %collective-permute-start.5 = (bf16[128,2048]{1,0:T(8,128)(2,1)S(1)}, bf16[128,2048]{1,0:T(8,128)(2,1)S(1)}, u32[]{:S(2)}, u32[]{:S(2)}) collective-permute-start(bf16[128,2048]{1,0:T(8,128)(2,1)S(1)} %get-tuple-element.42), channel_id=1, source_target_pairs={{0,1},{1,0},{2,3},{3,2},{4,5},{5,4},{6,7},{7,6},{8,9},{9,8},{10,11... | collective-permute-start | bytes 1572872 | tf_op jit(solution)/shard_map/ppermute | solution.py:17
  48.6 5.7 %collective-permute-start.3 = (bf16[128,2048]{1,0:T(8,128)(2,1)S(1)}, bf16[128,2048]{1,0:T(8,128)(2,1)S(1)}, u32[]{:S(2)}, u32[]{:S(2)}) collective-permute-start(bf16[128,2048]{1,0:T(8,128)(2,1)S(1)} %get-tuple-element.38), channel_id=1, source_target_pairs={{0,1},{1,0},{2,3},{3,2},{4,5},{5,4},{6,7},{7,6},{8,9},{9,8},{10,11... | collective-permute-start | bytes 1572872 | tf_op jit(solution)/shard_map/ppermute | solution.py:17
  49.1 5.2 %collective-permute-start.1 = (bf16[128,2048]{1,0:T(8,128)(2,1)S(1)}, bf16[128,2048]{1,0:T(8,128)(2,1)S(1)}, u32[]{:S(2)}, u32[]{:S(2)}) collective-permute-start(bf16[128,2048]{1,0:T(8,128)(2,1)S(1)} %get-tuple-element.34), channel_id=1, source_target_pairs={{0,1},{1,0},{2,3},{3,2},{4,5},{5,4},{6,7},{7,6},{8,9},{9,8},{10,11... | collective-permute-start | bytes 1572872 | tf_op jit(solution)/shard_map/ppermute | solution.py:17
  55.0 9.3 %collective-permute-start.10 = (bf16[64,2048]{1,0:T(8,128)(2,1)S(1)}, bf16[64,2048]{1,0:T(8,128)(2,1)S(1)}, u32[]{:S(2)}, u32[]{:S(2)}) collective-permute-start(bf16[64,2048]{1,0:T(8,128)(2,1)S(1)} %get-tuple-element.69), channel_id=1, source_target_pairs={{0,4},{1,5},{2,6},{3,7},{4,0},{5,1},{6,2},{7,3},{8,12},{9,13},{10,... | collective-permute-start | bytes 786440 | tf_op jit(solution)/shard_map/ppermute | solution.py:17
  55.1 10.7 %collective-permute-start.11 = (bf16[64,2048]{1,0:T(8,128)(2,1)S(1)}, bf16[64,2048]{1,0:T(8,128)(2,1)S(1)}, u32[]{:S(2)}, u32[]{:S(2)}) collective-permute-start(bf16[64,2048]{1,0:T(8,128)(2,1)S(1)} %get-tuple-element.70), channel_id=1, source_target_pairs={{0,6},{1,7},{2,4},{3,5},{4,2},{5,3},{6,0},{7,1},{8,14},{9,15},{10,... | collective-permute-start | bytes 786440 | tf_op jit(solution)/shard_map/ppermute | solution.py:17
  55.1 16.0 %collective-permute-start.9 = (bf16[64,2048]{1,0:T(8,128)(2,1)S(1)}, bf16[64,2048]{1,0:T(8,128)(2,1)S(1)}, u32[]{:S(2)}, u32[]{:S(2)}) collective-permute-start(bf16[64,2048]{1,0:T(8,128)(2,1)S(1)} %get-tuple-element.60), channel_id=1, source_target_pairs={{0,2},{1,3},{2,0},{3,1},{4,6},{5,7},{6,4},{7,5},{8,10},{9,11},{10,... | collective-permute-start | bytes 786440 | tf_op jit(solution)/shard_map/ppermute | solution.py:17
  64.1 7.3 %collective-permute-start.7 = (bf16[128,2048]{1,0:T(8,128)(2,1)S(1)}, bf16[128,2048]{1,0:T(8,128)(2,1)S(1)}, u32[]{:S(2)}, u32[]{:S(2)}) collective-permute-start(bf16[128,2048]{1,0:T(8,128)(2,1)S(1)} %get-tuple-element.53), channel_id=1, source_target_pairs={{0,1},{1,0},{2,3},{3,2},{4,5},{5,4},{6,7},{7,6},{8,9},{9,8},{10,11... | collective-permute-start | bytes 1572872 | tf_op jit(solution)/shard_map/ppermute | solution.py:17
  64.2 11.2 %collective-permute-start.13 = (bf16[64,2048]{1,0:T(8,128)(2,1)S(1)}, bf16[64,2048]{1,0:T(8,128)(2,1)S(1)}, u32[]{:S(2)}, u32[]{:S(2)}) collective-permute-start(bf16[64,2048]{1,0:T(8,128)(2,1)S(1)} %get-tuple-element.58), channel_id=1, source_target_pairs={{0,2},{1,3},{2,0},{3,1},{4,6},{5,7},{6,4},{7,5},{8,10},{9,11},{10,... | collective-permute-start | bytes 786440 | tf_op jit(solution)/shard_map/ppermute | solution.py:17
  71.3 15.4 %collective-permute-start.12 = (bf16[64,2048]{1,0:T(8,128)(2,1)S(1)}, bf16[64,2048]{1,0:T(8,128)(2,1)S(1)}, u32[]{:S(2)}, u32[]{:S(2)}) collective-permute-start(bf16[64,2048]{1,0:T(8,128)(2,1)S(1)} %convert_add_fusion), channel_id=1, source_target_pairs={{0,8},{1,9},{2,10},{3,11},{4,12},{5,13},{6,14},{7,15},{8,0},{9,1},... | collective-permute-start | bytes 786440 | tf_op jit(solution)/shard_map/ppermute | solution.py:17
  75.5 12.8 %collective-permute-start.14 = (bf16[64,2048]{1,0:T(8,128)(2,1)S(1)}, bf16[64,2048]{1,0:T(8,128)(2,1)S(1)}, u32[]{:S(2)}, u32[]{:S(2)}) collective-permute-start(bf16[64,2048]{1,0:T(8,128)(2,1)S(1)} %add_convert_fusion), channel_id=1, source_target_pairs={{0,4},{1,5},{2,6},{3,7},{4,0},{5,1},{6,2},{7,3},{8,12},{9,13},{10,... | collective-permute-start | bytes 786440 | tf_op jit(solution)/shard_map/ppermute | solution.py:17
  77.1 11.2 %collective-permute-start.8 = (bf16[64,2048]{1,0:T(8,128)(2,1)S(1)}, bf16[64,2048]{1,0:T(8,128)(2,1)S(1)}, u32[]{:S(2)}, u32[]{:S(2)}) collective-permute-start(bf16[64,2048]{1,0:T(8,128)(2,1)S(1)} %slice_add_fusion.2), channel_id=1, source_target_pairs={{0,2},{1,3},{2,0},{3,1},{4,6},{5,7},{6,4},{7,5},{8,10},{9,11},{10,... | collective-permute-start | bytes 786440 | tf_op jit(solution)/shard_map/ppermute | solution.py:17

commit v15 on v13

--- a/solution.py
+++ b/solution.py
@@ -283,15 +283,21 @@
     mine_0, other_0 = summed(step_0, core_0)
     mine_1, other_1 = summed(step_1, core_1)
     mine_2, other_2 = summed(step_2, core_2)
-    sends = [value.astype(jnp.bfloat16) for value in (mine_0, other_0, other_1, mine_2, other_2)]
-    step_3 = rows(3, sends)
+    both = jnp.concatenate((other_1.astype(jnp.bfloat16), other_2.astype(jnp.bfloat16)))
+    sends = mine_0.astype(jnp.bfloat16), other_0.astype(jnp.bfloat16)
+    step_3 = rows(3, (both, sends))
+    across = over(both, 2)
     far = over(sends[0], 4), over(sends[1], 6)
-    across_1 = over(sends[2], 2)
-    near = over(sends[3], 4), over(sends[4], 6)
     mine_1, _ = lax.optimization_barrier((mine_1, step_3[0]))
-    pair = over(total_of(mine_1, across_1, *far), 8)
-    mine_3, other_3 = summed(step_3, step_3[2])
-    total = total_of(mine_3, over(other_3, 2), pair, *near)
+    pair = total_of(mine_1, across[:half], *far)
+    mine_2, _ = lax.optimization_barrier((mine_2, pair))
+    pair = over(pair, 8)
+    near = over(total_of(mine_2, across[half:]), 4)
+    core_3, _ = lax.optimization_barrier((step_3[2], mine_2))
+    mine_3, other_3 = summed(step_3, core_3)
+    mine_3, other_3 = lax.optimization_barrier((mine_3, other_3.astype(jnp.bfloat16)))
+    total = lax.optimization_barrier(total_of(mine_3, pair))
+    total = total_of(total, over(other_3, 2), near)
     return (total * norm_factor).reshape(width // 4, modes, excitons)
 
 

time: 85.8 us -> 88.9 us (1.036)
  waiting for transfers between devices: 23.7 us -> 26 us
    ppermute x15 -> x14, waiting for transfers between devices: 23.7 us -> 26 us  [permute(): lax.ppermute(x, 'ka', [(i, j % size) for i, j in pairs if j is not None])]
    ppermute x15 -> x14, starting transfers between devices: 14.9 us -> 15.7 us  [permute(): lax.ppermute(x, 'ka', [(i, j % size) for i, j in pairs if j is not None])]
  transfers between devices with their start and end apart: 15 -> 14, of which waited for: 8 -> 7; matrix products, arithmetic and copies ran while one was open for 1% -> 1% of each run, Pallas kernels for 49% -> 47%
where the time goes in v15:
time: 88.9 us; the launch traced here: 88.6 us
  Pallas kernels  44 us (49%)
  waiting for transfers between devices  26 us (29%)
  starting transfers between devices  15.7 us (18%)
  other arithmetic  1.48 us (2%)
  local copies, waits for them, and re-layouts  1.24 us (1%)
    ppermute x14, waiting for transfers between devices, permute(): lax.ppermute(x, 'ka', [(i, j % size) for i, j in pairs if j is not None])  26 us
    pallas_call x4, Pallas kernels, rows_of(): pl.pallas_call(rows_kernel, out_shape=[jax.ShapeDtypeStruct((width // 4,...  23.9 us
    ppermute x14, starting transfers between devices, permute(): lax.ppermute(x, 'ka', [(i, j % size) for i, j in pairs if j is not None])  15.7 us
    pallas_call x1, Pallas kernels, products_of(): pl.pallas_call(products_kernel, out_shape=jax.ShapeDtypeStruct((k_local,...  13.4 us
    pallas_call x2, Pallas kernels, turned_pieces(): pl.pallas_call(functools.partial(turn_kernel, first), out_shape=[jax.Shap...  6.69 us
  transfers between devices with their start and end apart: 14, of which 7 were waited for; matrix products, arithmetic and copies ran while one was open for 1% of the time, Pallas kernels for 47%

profile of v15, /device:TPU:0, one launch (start us, length us, event | category | flops | bytes accessed | tf_op | source)
XLA Modules:
  0.0 88.6 jit_solution(8401614382724631117)
XLA Ops:
  0.0 2.5 %shard_map.56 = bf16[2,256,1024]{2,1,0:T(8,128)(2,1)} custom-call(bf16[2,1024,1024]{2,1,0:T(8,128)(2,1)} %bitcast.8), custom_call_target="tpu_custom_call" | custom-call | bytes 2097152 | tf_op jit(solution)/shard_map/pallas_call | solution.py:137
  2.5 5.5 %collective-permute-start = (bf16[2,256,1024]{2,1,0:T(8,128)(2,1)}, bf16[2,256,1024]{2,1,0:T(8,128)(2,1)}, u32[]{:S(2)}, u32[]{:S(2)}) collective-permute-start(bf16[2,256,1024]{2,1,0:T(8,128)(2,1)} %shard_map.56), channel_id=1, source_target_pairs={{0,15},{1,0},{2,1},{3,2},{4,3},{5,4},{6,5},{7,6},{8,7},{9,8},{10,9... | collective-permute-start | bytes 3145736 | tf_op jit(solution)/shard_map/ppermute | solution.py:17
  8.0 4.2 %shard_map.58 = (bf16[2,256,1024]{2,1,0:T(8,128)(2,1)}, bf16[2,256,1024]{2,1,0:T(8,128)(2,1)}, bf16[2,256,1024]{2,1,0:T(8,128)(2,1)}) custom-call(bf16[2,1024,1024]{2,1,0:T(8,128)(2,1)} %bitcast.9), custom_call_target="tpu_custom_call" | custom-call | bytes 6291456 | tf_op jit(solution)/shard_map/pallas_call | solution.py:137
  12.2 0.7 collective-permute-start.1
  12.9 0.1 collective-permute-start.4
  13.0 0.6 collective-permute-start.6
  13.6 0.1 add_add_fusion.2
  13.7 13.4 %shard_map.55 = bf16[2,2,32,32,1024]{4,3,2,1,0:T(8,128)(2,1)} custom-call(s32[2,2]{1,0:T(2,128)} %first_ref.1, bf16[2,32,32,1024]{3,2,1,0:T(8,128)(2,1)} %coeffs_ref.1, bf16[2,2,32,32]{3,2,1,0:T(8,128)(2,1)} %cond_ref.1, bf16[2,2,32,32]{3,2,1,0:T(8,128)(2,1)} %val_ref.1), custom_call_target="tpu_custom_call" | custom-call | flops 6442450944 | bytes 12582912 | tf_op jit(solution)/shard_map/pallas_call | solution.py:90
  27.0 0.1 add_add_fusion
  27.1 0.0 collective-permute-done.next_ref
  27.1 7.4 %shard_map.57 = (f32[64,2048]{1,0:T(8,128)S(1)}, f32[64,2048]{1,0:T(8,128)S(1)}, bf16[128,2048]{1,0:T(8,128)(2,1)S(1)}) custom-call(s32[5]{0:T(128)S(1)} %get-tuple-element.34.pick_ref, bf16[2,1024,1024]{2,1,0:T(8,128)(2,1)} %bitcast.10, bf16[2,256,1024]{2,1,0:T(8,128)(2,1)} %collective-permute-done.next_ref, bf16[2,2,1024,1024]{3,2,1,0:T(8,128)(2,1)} %bitcast.14), custom_call_target="tpu_custom_call" | custom-call | flops 2147483648 | bytes 8388608 | tf_op jit(solution)/shard_map/pallas_call | solution.py:212
  34.6 0.0 collective-permute-done.1.next_ref
  34.6 5.5 %shard_map.59 = (f32[64,2048]{1,0:T(8,128)S(1)}, f32[64,2048]{1,0:T(8,128)S(1)}, bf16[128,2048]{1,0:T(8,128)(2,1)S(1)}) custom-call(s32[5]{0:T(128)S(1)} %get-tuple-element.36.pick_ref, bf16[2,1024,1024]{2,1,0:T(8,128)(2,1)} %bitcast.11, bf16[2,256,1024]{2,1,0:T(8,128)(2,1)S(1)} %collective-permute-done.1.next_ref, bf16[2,2,1024,1024]{3,2,1,0:T(8,128)(2,1)} %bitcast.15), custom_call_target="tpu_custom_call" | custom-call | flops 2147483648 | bytes 8388608 | tf_op jit(solution)/shard_map/pallas_call | solution.py:212
  40.1 3.0 %collective-permute-done.4.next_ref = bf16[2,256,1024]{2,1,0:T(8,128)(2,1)S(1)} collective-permute-done((bf16[2,256,1024]{2,1,0:T(8,128)(2,1)}, bf16[2,256,1024]{2,1,0:T(8,128)(2,1)S(1)}, u32[]{:S(2)}, u32[]{:S(2)}) %collective-permute-start.4) | collective-permute-done | bytes 1048608 | tf_op jit(solution)/shard_map/ppermute | solution.py:17
  43.1 5.5 %shard_map.60 = (f32[64,2048]{1,0:T(8,128)S(1)}, f32[64,2048]{1,0:T(8,128)S(1)}, bf16[128,2048]{1,0:T(8,128)(2,1)S(1)}) custom-call(s32[5]{0:T(128)S(1)} %get-tuple-element.43.pick_ref, bf16[2,1024,1024]{2,1,0:T(8,128)(2,1)} %bitcast.12, bf16[2,256,1024]{2,1,0:T(8,128)(2,1)S(1)} %collective-permute-done.4.next_ref, bf16[2,2,1024,1024]{3,2,1,0:T(8,128)(2,1)} %bitcast.16), custom_call_target="tpu_custom_call" | custom-call | flops 2147483648 | bytes 8388608 | tf_op jit(solution)/shard_map/pallas_call | solution.py:212
  48.6 0.1 collective-permute-start.5
  48.6 0.5 collective-permute-start.3
  49.1 0.1 collective-permute-start.2
  49.2 5.1 %collective-permute-done.6.next_ref = bf16[2,256,1024]{2,1,0:T(8,128)(2,1)S(1)} collective-permute-done((bf16[2,256,1024]{2,1,0:T(8,128)(2,1)}, bf16[2,256,1024]{2,1,0:T(8,128)(2,1)S(1)}, u32[]{:S(2)}, u32[]{:S(2)}) %collective-permute-start.6) | collective-permute-done | bytes 1048608 | tf_op jit(solution)/shard_map/ppermute | solution.py:17
  54.3 0.0 collective-permute-done.5
  54.3 0.0 collective-permute-done.3
  54.3 0.0 collective-permute-done.2
  54.3 0.1 convert_element_type.54
  54.4 0.1 convert_element_type.56
  54.5 0.2 fusion.4
  54.7 0.2 fusion.3
  54.9 0.1 collective-permute-start.8
  55.0 0.1 convert_element_type.58
  55.1 0.1 fusion.2
  55.2 0.1 collective-permute-start.9
  55.3 3.5 %collective-permute-start.10 = (bf16[64,2048]{1,0:T(8,128)(2,1)S(1)}, bf16[64,2048]{1,0:T(8,128)(2,1)S(1)}, u32[]{:S(2)}, u32[]{:S(2)}) collective-permute-start(bf16[64,2048]{1,0:T(8,128)(2,1)S(1)} %get-tuple-element.70), channel_id=1, source_target_pairs={{0,6},{1,7},{2,4},{3,5},{4,2},{5,3},{6,0},{7,1},{8,14},{9,15},{10,... | collective-permute-start | bytes 786440 | tf_op jit(solution)/shard_map/ppermute | solution.py:17
  58.8 5.5 %shard_map.61 = (f32[64,2048]{1,0:T(8,128)S(1)}, f32[64,2048]{1,0:T(8,128)S(1)}, bf16[128,2048]{1,0:T(8,128)(2,1)S(1)}) custom-call(s32[5]{0:T(128)S(1)} %get-tuple-element.52.pick_ref, bf16[2,1024,1024]{2,1,0:T(8,128)(2,1)} %bitcast.13, bf16[2,256,1024]{2,1,0:T(8,128)(2,1)S(1)} %collective-permute-done.6.next_ref, bf16[2,2,1024,1024]{3,2,1,0:T(8,128)(2,1)} %bitcast.17), custom_call_target="tpu_custom_call" | custom-call | flops 2147483648 | bytes 8388608 | tf_op jit(solution)/shard_map/pallas_call | solution.py:212
  64.2 0.1 collective-permute-start.7
  64.3 0.2 collective-permute-done.9
  64.5 4.2 %collective-permute-done.10 = bf16[64,2048]{1,0:T(8,128)(2,1)S(1)} collective-permute-done((bf16[64,2048]{1,0:T(8,128)(2,1)S(1)}, bf16[64,2048]{1,0:T(8,128)(2,1)S(1)}, u32[]{:S(2)}, u32[]{:S(2)}) %collective-permute-start.10) | collective-permute-done | bytes 262176 | tf_op jit(solution)/shard_map/ppermute | solution.py:17
  68.7 4.1 %collective-permute-done.8 = bf16[128,2048]{1,0:T(8,128)(2,1)S(1)} collective-permute-done((bf16[128,2048]{1,0:T(8,128)(2,1)S(1)}, bf16[128,2048]{1,0:T(8,128)(2,1)S(1)}, u32[]{:S(2)}, u32[]{:S(2)}) %collective-permute-start.8) | collective-permute-done | bytes 524320 | tf_op jit(solution)/shard_map/ppermute | solution.py:17
  72.7 0.1 convert_add_fusion.1
  72.9 1.7 %collective-permute-start.11 = (bf16[64,2048]{1,0:T(8,128)(2,1)S(1)}, bf16[64,2048]{1,0:T(8,128)(2,1)S(1)}, u32[]{:S(2)}, u32[]{:S(2)}) collective-permute-start(bf16[64,2048]{1,0:T(8,128)(2,1)S(1)} %convert_add_fusion.1), channel_id=1, source_target_pairs={{0,8},{1,9},{2,10},{3,11},{4,12},{5,13},{6,14},{7,15},{8,0},{9,1},... | collective-permute-start | bytes 786440 | tf_op jit(solution)/shard_map/ppermute | solution.py:17
  74.6 0.5 collective-permute-start.13
  75.1 0.0 collective-permute-done.7
  75.1 0.1 convert_element_type.64
  75.2 0.1 fusion
  75.3 2.4 %collective-permute-start.12 = (bf16[64,2048]{1,0:T(8,128)(2,1)S(1)}, bf16[64,2048]{1,0:T(8,128)(2,1)S(1)}, u32[]{:S(2)}, u32[]{:S(2)}) collective-permute-start(bf16[64,2048]{1,0:T(8,128)(2,1)S(1)} %get-tuple-element.62), channel_id=1, source_target_pairs={{0,2},{1,3},{2,0},{3,1},{4,6},{5,7},{6,4},{7,5},{8,10},{9,11},{10,... | collective-permute-start | bytes 786440 | tf_op jit(solution)/shard_map/ppermute | solution.py:17
  77.7 9.4 %collective-permute-done.11 = bf16[64,2048]{1,0:T(8,128)(2,1)S(1)} collective-permute-done((bf16[64,2048]{1,0:T(8,128)(2,1)S(1)}, bf16[64,2048]{1,0:T(8,128)(2,1)S(1)}, u32[]{:S(2)}, u32[]{:S(2)}) %collective-permute-start.11) | collective-permute-done | bytes 262176 | tf_op jit(solution)/shard_map/ppermute | solution.py:17
  87.0 0.1 convert_add_fusion
  87.1 0.1 collective-permute-done.13
  87.2 0.1 add_multiply_fusion
  87.3 1.2 %reshape.11 = f32[64,2,1024]{2,1,0:T(2,128)} reshape(f32[64,2048]{1,0:T(8,128)S(1)} %add_multiply_fusion) | data formatting | bytes 1048576 | tf_op jit(solution)/shard_map/reshape | solution.py:301
  (6 shorter events, 0.1 us)
Async XLA Ops:
  0.0 13.6 %copy-start = (s32[2]{0:T(128)S(1)}, s32[2]{0:T(128)}, u32[]{:S(2)}) copy-start(s32[2]{0:T(128)} %param.8) | copy-start | bytes 28
  2.5 24.6 %collective-permute-start = (bf16[2,256,1024]{2,1,0:T(8,128)(2,1)}, bf16[2,256,1024]{2,1,0:T(8,128)(2,1)}, u32[]{:S(2)}, u32[]{:S(2)}) collective-permute-start(bf16[2,256,1024]{2,1,0:T(8,128)(2,1)} %shard_map.56), channel_id=1, source_target_pairs={{0,15},{1,0},{2,1},{3,2},{4,3},{5,4},{6,5},{7,6},{8,7},{9,8},{10,9... | collective-permute-start | bytes 3145736 | tf_op jit(solution)/shard_map/ppermute | solution.py:17
  12.2 22.4 %collective-permute-start.1 = (bf16[2,256,1024]{2,1,0:T(8,128)(2,1)}, bf16[2,256,1024]{2,1,0:T(8,128)(2,1)S(1)}, u32[]{:S(2)}, u32[]{:S(2)}) collective-permute-start(bf16[2,256,1024]{2,1,0:T(8,128)(2,1)} %get-tuple-element.38), channel_id=1, source_target_pairs={{0,15},{1,0},{2,1},{3,2},{4,3},{5,4},{6,5},{7,6},{8,7},{9,8},{10,9... | collective-permute-start | bytes 3145736 | tf_op jit(solution)/shard_map/ppermute | solution.py:17
  12.9 30.2 %collective-permute-start.4 = (bf16[2,256,1024]{2,1,0:T(8,128)(2,1)}, bf16[2,256,1024]{2,1,0:T(8,128)(2,1)S(1)}, u32[]{:S(2)}, u32[]{:S(2)}) collective-permute-start(bf16[2,256,1024]{2,1,0:T(8,128)(2,1)} %get-tuple-element.44), channel_id=1, source_target_pairs={{0,15},{1,0},{2,1},{3,2},{4,3},{5,4},{6,5},{7,6},{8,7},{9,8},{10,9... | collective-permute-start | bytes 3145736 | tf_op jit(solution)/shard_map/ppermute | solution.py:17
  13.0 41.4 %collective-permute-start.6 = (bf16[2,256,1024]{2,1,0:T(8,128)(2,1)}, bf16[2,256,1024]{2,1,0:T(8,128)(2,1)S(1)}, u32[]{:S(2)}, u32[]{:S(2)}) collective-permute-start(bf16[2,256,1024]{2,1,0:T(8,128)(2,1)} %get-tuple-element.46), channel_id=1, source_target_pairs={{0,15},{1,0},{2,1},{3,2},{4,3},{5,4},{6,5},{7,6},{8,7},{9,8},{10,9... | collective-permute-start | bytes 3145736 | tf_op jit(solution)/shard_map/ppermute | solution.py:17
  48.6 5.8 %collective-permute-start.5 = (bf16[128,2048]{1,0:T(8,128)(2,1)S(1)}, bf16[128,2048]{1,0:T(8,128)(2,1)S(1)}, u32[]{:S(2)}, u32[]{:S(2)}) collective-permute-start(bf16[128,2048]{1,0:T(8,128)(2,1)S(1)} %get-tuple-element.45), channel_id=1, source_target_pairs={{0,1},{1,0},{2,3},{3,2},{4,5},{5,4},{6,7},{7,6},{8,9},{9,8},{10,11... | collective-permute-start | bytes 1572872 | tf_op jit(solution)/shard_map/ppermute | solution.py:17
  48.6 5.7 %collective-permute-start.3 = (bf16[128,2048]{1,0:T(8,128)(2,1)S(1)}, bf16[128,2048]{1,0:T(8,128)(2,1)S(1)}, u32[]{:S(2)}, u32[]{:S(2)}) collective-permute-start(bf16[128,2048]{1,0:T(8,128)(2,1)S(1)} %get-tuple-element.41), channel_id=1, source_target_pairs={{0,1},{1,0},{2,3},{3,2},{4,5},{5,4},{6,7},{7,6},{8,9},{9,8},{10,11... | collective-permute-start | bytes 1572872 | tf_op jit(solution)/shard_map/ppermute | solution.py:17
  49.1 5.2 %collective-permute-start.2 = (bf16[128,2048]{1,0:T(8,128)(2,1)S(1)}, bf16[128,2048]{1,0:T(8,128)(2,1)S(1)}, u32[]{:S(2)}, u32[]{:S(2)}) collective-permute-start(bf16[128,2048]{1,0:T(8,128)(2,1)S(1)} %get-tuple-element.40), channel_id=1, source_target_pairs={{0,1},{1,0},{2,3},{3,2},{4,5},{5,4},{6,7},{7,6},{8,9},{9,8},{10,11... | collective-permute-start | bytes 1572872 | tf_op jit(solution)/shard_map/ppermute | solution.py:17
  54.9 17.8 %collective-permute-start.8 = (bf16[128,2048]{1,0:T(8,128)(2,1)S(1)}, bf16[128,2048]{1,0:T(8,128)(2,1)S(1)}, u32[]{:S(2)}, u32[]{:S(2)}) collective-permute-start(bf16[128,2048]{1,0:T(8,128)(2,1)S(1)} %pad_maximum_fusion), channel_id=1, source_target_pairs={{0,2},{1,3},{2,0},{3,1},{4,6},{5,7},{6,4},{7,5},{8,10},{9,11},{10,... | collective-permute-start | bytes 1572872 | tf_op jit(solution)/shard_map/ppermute | solution.py:17
  55.2 9.3 %collective-permute-start.9 = (bf16[64,2048]{1,0:T(8,128)(2,1)S(1)}, bf16[64,2048]{1,0:T(8,128)(2,1)S(1)}, u32[]{:S(2)}, u32[]{:S(2)}) collective-permute-start(bf16[64,2048]{1,0:T(8,128)(2,1)S(1)} %get-tuple-element.69), channel_id=1, source_target_pairs={{0,4},{1,5},{2,6},{3,7},{4,0},{5,1},{6,2},{7,3},{8,12},{9,13},{10,... | collective-permute-start | bytes 786440 | tf_op jit(solution)/shard_map/ppermute | solution.py:17
  55.3 13.4 %collective-permute-start.10 = (bf16[64,2048]{1,0:T(8,128)(2,1)S(1)}, bf16[64,2048]{1,0:T(8,128)(2,1)S(1)}, u32[]{:S(2)}, u32[]{:S(2)}) collective-permute-start(bf16[64,2048]{1,0:T(8,128)(2,1)S(1)} %get-tuple-element.70), channel_id=1, source_target_pairs={{0,6},{1,7},{2,4},{3,5},{4,2},{5,3},{6,0},{7,1},{8,14},{9,15},{10,... | collective-permute-start | bytes 786440 | tf_op jit(solution)/shard_map/ppermute | solution.py:17
  64.2 10.8 %collective-permute-start.7 = (bf16[128,2048]{1,0:T(8,128)(2,1)S(1)}, bf16[128,2048]{1,0:T(8,128)(2,1)S(1)}, u32[]{:S(2)}, u32[]{:S(2)}) collective-permute-start(bf16[128,2048]{1,0:T(8,128)(2,1)S(1)} %get-tuple-element.55), channel_id=1, source_target_pairs={{0,1},{1,0},{2,3},{3,2},{4,5},{5,4},{6,7},{7,6},{8,9},{9,8},{10,11... | collective-permute-start | bytes 1572872 | tf_op jit(solution)/shard_map/ppermute | solution.py:17
  72.9 14.2 %collective-permute-start.11 = (bf16[64,2048]{1,0:T(8,128)(2,1)S(1)}, bf16[64,2048]{1,0:T(8,128)(2,1)S(1)}, u32[]{:S(2)}, u32[]{:S(2)}) collective-permute-start(bf16[64,2048]{1,0:T(8,128)(2,1)S(1)} %convert_add_fusion.1), channel_id=1, source_target_pairs={{0,8},{1,9},{2,10},{3,11},{4,12},{5,13},{6,14},{7,15},{8,0},{9,1},... | collective-permute-start | bytes 786440 | tf_op jit(solution)/shard_map/ppermute | solution.py:17
  74.6 12.6 %collective-permute-start.13 = (bf16[64,2048]{1,0:T(8,128)(2,1)S(1)}, bf16[64,2048]{1,0:T(8,128)(2,1)S(1)}, u32[]{:S(2)}, u32[]{:S(2)}) collective-permute-start(bf16[64,2048]{1,0:T(8,128)(2,1)S(1)} %add_convert_fusion), channel_id=1, source_target_pairs={{0,4},{1,5},{2,6},{3,7},{4,0},{5,1},{6,2},{7,3},{8,12},{9,13},{10,... | collective-permute-start | bytes 786440 | tf_op jit(solution)/shard_map/ppermute | solution.py:17
  75.3 11.9 %collective-permute-start.12 = (bf16[64,2048]{1,0:T(8,128)(2,1)S(1)}, bf16[64,2048]{1,0:T(8,128)(2,1)S(1)}, u32[]{:S(2)}, u32[]{:S(2)}) collective-permute-start(bf16[64,2048]{1,0:T(8,128)(2,1)S(1)} %get-tuple-element.62), channel_id=1, source_target_pairs={{0,2},{1,3},{2,0},{3,1},{4,6},{5,7},{6,4},{7,5},{8,10},{9,11},{10,... | collective-permute-start | bytes 786440 | tf_op jit(solution)/shard_map/ppermute | solution.py:17

commit v16 on v15

--- a/solution.py
+++ b/solution.py
@@ -283,16 +283,16 @@
     mine_0, other_0 = summed(step_0, core_0)
     mine_1, other_1 = summed(step_1, core_1)
     mine_2, other_2 = summed(step_2, core_2)
-    both = jnp.concatenate((other_1.astype(jnp.bfloat16), other_2.astype(jnp.bfloat16)))
-    sends = mine_0.astype(jnp.bfloat16), other_0.astype(jnp.bfloat16)
-    step_3 = rows(3, (both, sends))
-    across = over(both, 2)
+    sends = [value.astype(jnp.bfloat16) for value in (mine_0, other_0, other_1, other_2)]
+    step_3 = rows(3, sends)
+    across_1, across_2 = over(sends[2], 2), over(sends[3], 2)
     far = over(sends[0], 4), over(sends[1], 6)
     mine_1, _ = lax.optimization_barrier((mine_1, step_3[0]))
-    pair = total_of(mine_1, across[:half], *far)
+    mine_1 = total_of(mine_1, across_1)
+    pair = total_of(lax.optimization_barrier(mine_1), *far)
     mine_2, _ = lax.optimization_barrier((mine_2, pair))
     pair = over(pair, 8)
-    near = over(total_of(mine_2, across[half:]), 4)
+    near = over(total_of(mine_2, across_2), 4)
     core_3, _ = lax.optimization_barrier((step_3[2], mine_2))
     mine_3, other_3 = summed(step_3, core_3)
     mine_3, other_3 = lax.optimization_barrier((mine_3, other_3.astype(jnp.bfloat16)))

time: 88.9 us -> 88.4 us (level)
    ppermute x14 -> x15, starting transfers between devices: 15.7 us -> 15.3 us  [permute(): lax.ppermute(x, 'ka', [(i, j % size) for i, j in pairs if j is not None])]
    ppermute x14 -> x15, waiting for transfers between devices: 26 us -> 26.1 us  [permute(): lax.ppermute(x, 'ka', [(i, j % size) for i, j in pairs if j is not None])]
  transfers between devices with their start and end apart: 14 -> 15, of which waited for: 7 -> 6; matrix products, arithmetic and copies ran while one was open for 1% -> 1% of each run, Pallas kernels for 47% -> 47%
where the time goes in v16:
time: 88.4 us; the launch traced here: 88 us
  Pallas kernels  43.8 us (50%)
  waiting for transfers between devices  26.1 us (30%)
  starting transfers between devices  15.3 us (17%)
  other arithmetic  1.42 us (2%)
  local copies, waits for them, and re-layouts  1.24 us (1%)
    ppermute x15, waiting for transfers between devices, permute(): lax.ppermute(x, 'ka', [(i, j % size) for i, j in pairs if j is not None])  26.1 us
    pallas_call x4, Pallas kernels, rows_of(): pl.pallas_call(rows_kernel, out_shape=[jax.ShapeDtypeStruct((width // 4,...  23.7 us
    ppermute x15, starting transfers between devices, permute(): lax.ppermute(x, 'ka', [(i, j % size) for i, j in pairs if j is not None])  15.3 us
    pallas_call x1, Pallas kernels, products_of(): pl.pallas_call(products_kernel, out_shape=jax.ShapeDtypeStruct((k_local,...  13.4 us
    pallas_call x2, Pallas kernels, turned_pieces(): pl.pallas_call(functools.partial(turn_kernel, first), out_shape=[jax.Shap...  6.69 us
  transfers between devices with their start and end apart: 15, of which 6 were waited for; matrix products, arithmetic and copies ran while one was open for 1% of the time, Pallas kernels for 47%

profile of v16, /device:TPU:0, one launch (start us, length us, event | category | flops | bytes accessed | tf_op | source)
XLA Modules:
  0.0 88.0 jit_solution(1518371180233243180)
XLA Ops:
  0.0 2.5 %shard_map.56 = bf16[2,256,1024]{2,1,0:T(8,128)(2,1)} custom-call(bf16[2,1024,1024]{2,1,0:T(8,128)(2,1)} %bitcast.8), custom_call_target="tpu_custom_call" | custom-call | bytes 2097152 | tf_op jit(solution)/shard_map/pallas_call | solution.py:137
  2.5 5.5 %collective-permute-start = (bf16[2,256,1024]{2,1,0:T(8,128)(2,1)}, bf16[2,256,1024]{2,1,0:T(8,128)(2,1)}, u32[]{:S(2)}, u32[]{:S(2)}) collective-permute-start(bf16[2,256,1024]{2,1,0:T(8,128)(2,1)} %shard_map.56), channel_id=1, source_target_pairs={{0,15},{1,0},{2,1},{3,2},{4,3},{5,4},{6,5},{7,6},{8,7},{9,8},{10,9... | collective-permute-start | bytes 3145736 | tf_op jit(solution)/shard_map/ppermute | solution.py:17
  8.0 4.2 %shard_map.58 = (bf16[2,256,1024]{2,1,0:T(8,128)(2,1)}, bf16[2,256,1024]{2,1,0:T(8,128)(2,1)}, bf16[2,256,1024]{2,1,0:T(8,128)(2,1)}) custom-call(bf16[2,1024,1024]{2,1,0:T(8,128)(2,1)} %bitcast.9), custom_call_target="tpu_custom_call" | custom-call | bytes 6291456 | tf_op jit(solution)/shard_map/pallas_call | solution.py:137
  12.2 0.7 collective-permute-start.2
  12.9 0.1 collective-permute-start.4
  13.0 0.6 collective-permute-start.6
  13.6 0.1 add_add_fusion
  13.7 13.4 %shard_map.55 = bf16[2,2,32,32,1024]{4,3,2,1,0:T(8,128)(2,1)} custom-call(s32[2,2]{1,0:T(2,128)} %first_ref.1, bf16[2,32,32,1024]{3,2,1,0:T(8,128)(2,1)} %coeffs_ref.1, bf16[2,2,32,32]{3,2,1,0:T(8,128)(2,1)} %cond_ref.1, bf16[2,2,32,32]{3,2,1,0:T(8,128)(2,1)} %val_ref.1), custom_call_target="tpu_custom_call" | custom-call | flops 6442450944 | bytes 12582912 | tf_op jit(solution)/shard_map/pallas_call | solution.py:90
  27.0 0.1 add_add_fusion.2
  27.1 0.0 collective-permute-done.next_ref
  27.1 7.3 %shard_map.57 = (f32[64,2048]{1,0:T(8,128)S(1)}, f32[64,2048]{1,0:T(8,128)S(1)}, bf16[128,2048]{1,0:T(8,128)(2,1)S(1)}) custom-call(s32[5]{0:T(128)S(1)} %get-tuple-element.34.pick_ref, bf16[2,1024,1024]{2,1,0:T(8,128)(2,1)} %bitcast.10, bf16[2,256,1024]{2,1,0:T(8,128)(2,1)} %collective-permute-done.next_ref, bf16[2,2,1024,1024]{3,2,1,0:T(8,128)(2,1)} %bitcast.14), custom_call_target="tpu_custom_call" | custom-call | flops 2147483648 | bytes 8388608 | tf_op jit(solution)/shard_map/pallas_call | solution.py:212
  34.4 0.0 collective-permute-done.2.next_ref
  34.4 5.5 %shard_map.59 = (f32[64,2048]{1,0:T(8,128)S(1)}, f32[64,2048]{1,0:T(8,128)S(1)}, bf16[128,2048]{1,0:T(8,128)(2,1)S(1)}) custom-call(s32[5]{0:T(128)S(1)} %get-tuple-element.37.pick_ref, bf16[2,1024,1024]{2,1,0:T(8,128)(2,1)} %bitcast.11, bf16[2,256,1024]{2,1,0:T(8,128)(2,1)S(1)} %collective-permute-done.2.next_ref, bf16[2,2,1024,1024]{3,2,1,0:T(8,128)(2,1)} %bitcast.15), custom_call_target="tpu_custom_call" | custom-call | flops 2147483648 | bytes 8388608 | tf_op jit(solution)/shard_map/pallas_call | solution.py:212
  39.9 0.2 collective-permute-start.1
  40.1 0.4 collective-permute-start.3
  40.5 2.6 %collective-permute-done.4.next_ref = bf16[2,256,1024]{2,1,0:T(8,128)(2,1)S(1)} collective-permute-done((bf16[2,256,1024]{2,1,0:T(8,128)(2,1)}, bf16[2,256,1024]{2,1,0:T(8,128)(2,1)S(1)}, u32[]{:S(2)}, u32[]{:S(2)}) %collective-permute-start.4) | collective-permute-done | bytes 1048608 | tf_op jit(solution)/shard_map/ppermute | solution.py:17
  43.1 5.5 %shard_map.60 = (f32[64,2048]{1,0:T(8,128)S(1)}, f32[64,2048]{1,0:T(8,128)S(1)}, bf16[128,2048]{1,0:T(8,128)(2,1)S(1)}) custom-call(s32[5]{0:T(128)S(1)} %get-tuple-element.42.pick_ref, bf16[2,1024,1024]{2,1,0:T(8,128)(2,1)} %bitcast.12, bf16[2,256,1024]{2,1,0:T(8,128)(2,1)S(1)} %collective-permute-done.4.next_ref, bf16[2,2,1024,1024]{3,2,1,0:T(8,128)(2,1)} %bitcast.16), custom_call_target="tpu_custom_call" | custom-call | flops 2147483648 | bytes 8388608 | tf_op jit(solution)/shard_map/pallas_call | solution.py:212
  48.6 0.1 collective-permute-start.5
  48.6 5.7 %collective-permute-done.6.next_ref = bf16[2,256,1024]{2,1,0:T(8,128)(2,1)S(1)} collective-permute-done((bf16[2,256,1024]{2,1,0:T(8,128)(2,1)}, bf16[2,256,1024]{2,1,0:T(8,128)(2,1)S(1)}, u32[]{:S(2)}, u32[]{:S(2)}) %collective-permute-start.6) | collective-permute-done | bytes 1048608 | tf_op jit(solution)/shard_map/ppermute | solution.py:17
  54.3 0.0 collective-permute-done.1
  54.3 0.0 collective-permute-done.3
  54.3 0.0 collective-permute-done.5
  54.3 0.1 convert_element_type.59
  54.4 0.1 convert_element_type.57
  54.6 0.1 convert_element_type.54
  54.7 0.3 fusion.2
  55.0 0.1 collective-permute-start.10
  55.1 0.1 collective-permute-start.8
  55.1 3.4 %collective-permute-start.9 = (bf16[64,2048]{1,0:T(8,128)(2,1)S(1)}, bf16[64,2048]{1,0:T(8,128)(2,1)S(1)}, u32[]{:S(2)}, u32[]{:S(2)}) collective-permute-start(bf16[64,2048]{1,0:T(8,128)(2,1)S(1)} %get-tuple-element.76), channel_id=1, source_target_pairs={{0,4},{1,5},{2,6},{3,7},{4,0},{5,1},{6,2},{7,3},{8,12},{9,13},{10,... | collective-permute-start | bytes 786440 | tf_op jit(solution)/shard_map/ppermute | solution.py:17
  58.5 0.1 fusion.1
  58.7 0.1 collective-permute-start.13
  58.7 5.5 %shard_map.61 = (f32[64,2048]{1,0:T(8,128)S(1)}, f32[64,2048]{1,0:T(8,128)S(1)}, bf16[128,2048]{1,0:T(8,128)(2,1)S(1)}) custom-call(s32[5]{0:T(128)S(1)} %get-tuple-element.52.pick_ref, bf16[2,1024,1024]{2,1,0:T(8,128)(2,1)} %bitcast.13, bf16[2,256,1024]{2,1,0:T(8,128)(2,1)S(1)} %collective-permute-done.6.next_ref, bf16[2,2,1024,1024]{3,2,1,0:T(8,128)(2,1)} %bitcast.17), custom_call_target="tpu_custom_call" | custom-call | flops 2147483648 | bytes 8388608 | tf_op jit(solution)/shard_map/pallas_call | solution.py:212
  64.2 0.1 collective-permute-start.7
  64.3 3.9 %collective-permute-done.8 = bf16[64,2048]{1,0:T(8,128)(2,1)S(1)} collective-permute-done((bf16[64,2048]{1,0:T(8,128)(2,1)S(1)}, bf16[64,2048]{1,0:T(8,128)(2,1)S(1)}, u32[]{:S(2)}, u32[]{:S(2)}) %collective-permute-start.8) | collective-permute-done | bytes 262176 | tf_op jit(solution)/shard_map/ppermute | solution.py:17
  68.3 0.0 collective-permute-done.10
  68.3 0.0 collective-permute-done.9
  68.3 0.1 convert_add_fusion.1
  68.4 1.6 %collective-permute-start.11 = (bf16[64,2048]{1,0:T(8,128)(2,1)S(1)}, bf16[64,2048]{1,0:T(8,128)(2,1)S(1)}, u32[]{:S(2)}, u32[]{:S(2)}) collective-permute-start(bf16[64,2048]{1,0:T(8,128)(2,1)S(1)} %convert_add_fusion.1), channel_id=1, source_target_pairs={{0,8},{1,9},{2,10},{3,11},{4,12},{5,13},{6,14},{7,15},{8,0},{9,1},... | collective-permute-start | bytes 786440 | tf_op jit(solution)/shard_map/ppermute | solution.py:17
  70.0 3.9 %collective-permute-done.13 = bf16[64,2048]{1,0:T(8,128)(2,1)S(1)} collective-permute-done((bf16[64,2048]{1,0:T(8,128)(2,1)S(1)}, bf16[64,2048]{1,0:T(8,128)(2,1)S(1)}, u32[]{:S(2)}, u32[]{:S(2)}) %collective-permute-start.13) | collective-permute-done | bytes 262176 | tf_op jit(solution)/shard_map/ppermute | solution.py:17
  73.9 0.9 %collective-permute-start.14 = (bf16[64,2048]{1,0:T(8,128)(2,1)S(1)}, bf16[64,2048]{1,0:T(8,128)(2,1)S(1)}, u32[]{:S(2)}, u32[]{:S(2)}) collective-permute-start(bf16[64,2048]{1,0:T(8,128)(2,1)S(1)} %add_convert_fusion), channel_id=1, source_target_pairs={{0,4},{1,5},{2,6},{3,7},{4,0},{5,1},{6,2},{7,3},{8,12},{9,13},{10,... | collective-permute-start | bytes 786440 | tf_op jit(solution)/shard_map/ppermute | solution.py:17
  74.8 0.0 collective-permute-done.7
  74.8 0.1 convert_element_type.64
  74.9 0.1 fusion
  75.0 1.6 %collective-permute-start.12 = (bf16[64,2048]{1,0:T(8,128)(2,1)S(1)}, bf16[64,2048]{1,0:T(8,128)(2,1)S(1)}, u32[]{:S(2)}, u32[]{:S(2)}) collective-permute-start(bf16[64,2048]{1,0:T(8,128)(2,1)S(1)} %get-tuple-element.62), channel_id=1, source_target_pairs={{0,2},{1,3},{2,0},{3,1},{4,6},{5,7},{6,4},{7,5},{8,10},{9,11},{10,... | collective-permute-start | bytes 786440 | tf_op jit(solution)/shard_map/ppermute | solution.py:17
  76.6 6.8 %collective-permute-done.11 = bf16[64,2048]{1,0:T(8,128)(2,1)S(1)} collective-permute-done((bf16[64,2048]{1,0:T(8,128)(2,1)S(1)}, bf16[64,2048]{1,0:T(8,128)(2,1)S(1)}, u32[]{:S(2)}, u32[]{:S(2)}) %collective-permute-start.11) | collective-permute-done | bytes 262176 | tf_op jit(solution)/shard_map/ppermute | solution.py:17
  83.4 3.3 %collective-permute-done.14 = bf16[64,2048]{1,0:T(8,128)(2,1)S(1)} collective-permute-done((bf16[64,2048]{1,0:T(8,128)(2,1)S(1)}, bf16[64,2048]{1,0:T(8,128)(2,1)S(1)}, u32[]{:S(2)}, u32[]{:S(2)}) %collective-permute-start.14) | collective-permute-done | bytes 262176 | tf_op jit(solution)/shard_map/ppermute | solution.py:17
  86.7 0.1 add_multiply_fusion
  86.8 1.2 %reshape.11 = f32[64,2,1024]{2,1,0:T(2,128)} reshape(f32[64,2048]{1,0:T(8,128)S(1)} %add_multiply_fusion) | data formatting | bytes 1048576 | tf_op jit(solution)/shard_map/reshape | solution.py:301
  (7 shorter events, 0.2 us)
Async XLA Ops:
  0.0 13.6 %copy-start = (s32[2]{0:T(128)S(1)}, s32[2]{0:T(128)}, u32[]{:S(2)}) copy-start(s32[2]{0:T(128)} %param.8) | copy-start | bytes 28
  2.5 24.6 %collective-permute-start = (bf16[2,256,1024]{2,1,0:T(8,128)(2,1)}, bf16[2,256,1024]{2,1,0:T(8,128)(2,1)}, u32[]{:S(2)}, u32[]{:S(2)}) collective-permute-start(bf16[2,256,1024]{2,1,0:T(8,128)(2,1)} %shard_map.56), channel_id=1, source_target_pairs={{0,15},{1,0},{2,1},{3,2},{4,3},{5,4},{6,5},{7,6},{8,7},{9,8},{10,9... | collective-permute-start | bytes 3145736 | tf_op jit(solution)/shard_map/ppermute | solution.py:17
  12.2 22.2 %collective-permute-start.2 = (bf16[2,256,1024]{2,1,0:T(8,128)(2,1)}, bf16[2,256,1024]{2,1,0:T(8,128)(2,1)S(1)}, u32[]{:S(2)}, u32[]{:S(2)}) collective-permute-start(bf16[2,256,1024]{2,1,0:T(8,128)(2,1)} %get-tuple-element.39), channel_id=1, source_target_pairs={{0,15},{1,0},{2,1},{3,2},{4,3},{5,4},{6,5},{7,6},{8,7},{9,8},{10,9... | collective-permute-start | bytes 3145736 | tf_op jit(solution)/shard_map/ppermute | solution.py:17
  12.9 30.2 %collective-permute-start.4 = (bf16[2,256,1024]{2,1,0:T(8,128)(2,1)}, bf16[2,256,1024]{2,1,0:T(8,128)(2,1)S(1)}, u32[]{:S(2)}, u32[]{:S(2)}) collective-permute-start(bf16[2,256,1024]{2,1,0:T(8,128)(2,1)} %get-tuple-element.43), channel_id=1, source_target_pairs={{0,15},{1,0},{2,1},{3,2},{4,3},{5,4},{6,5},{7,6},{8,7},{9,8},{10,9... | collective-permute-start | bytes 3145736 | tf_op jit(solution)/shard_map/ppermute | solution.py:17
  13.0 41.4 %collective-permute-start.6 = (bf16[2,256,1024]{2,1,0:T(8,128)(2,1)}, bf16[2,256,1024]{2,1,0:T(8,128)(2,1)S(1)}, u32[]{:S(2)}, u32[]{:S(2)}) collective-permute-start(bf16[2,256,1024]{2,1,0:T(8,128)(2,1)} %get-tuple-element.45), channel_id=1, source_target_pairs={{0,15},{1,0},{2,1},{3,2},{4,3},{5,4},{6,5},{7,6},{8,7},{9,8},{10,9... | collective-permute-start | bytes 3145736 | tf_op jit(solution)/shard_map/ppermute | solution.py:17
  39.9 14.4 %collective-permute-start.1 = (bf16[128,2048]{1,0:T(8,128)(2,1)S(1)}, bf16[128,2048]{1,0:T(8,128)(2,1)S(1)}, u32[]{:S(2)}, u32[]{:S(2)}) collective-permute-start(bf16[128,2048]{1,0:T(8,128)(2,1)S(1)} %get-tuple-element.36), channel_id=1, source_target_pairs={{0,1},{1,0},{2,3},{3,2},{4,5},{5,4},{6,7},{7,6},{8,9},{9,8},{10,11... | collective-permute-start | bytes 1572872 | tf_op jit(solution)/shard_map/ppermute | solution.py:17
  40.1 14.2 %collective-permute-start.3 = (bf16[128,2048]{1,0:T(8,128)(2,1)S(1)}, bf16[128,2048]{1,0:T(8,128)(2,1)S(1)}, u32[]{:S(2)}, u32[]{:S(2)}) collective-permute-start(bf16[128,2048]{1,0:T(8,128)(2,1)S(1)} %get-tuple-element.40), channel_id=1, source_target_pairs={{0,1},{1,0},{2,3},{3,2},{4,5},{5,4},{6,7},{7,6},{8,9},{9,8},{10,11... | collective-permute-start | bytes 1572872 | tf_op jit(solution)/shard_map/ppermute | solution.py:17
  48.6 5.8 %collective-permute-start.5 = (bf16[128,2048]{1,0:T(8,128)(2,1)S(1)}, bf16[128,2048]{1,0:T(8,128)(2,1)S(1)}, u32[]{:S(2)}, u32[]{:S(2)}) collective-permute-start(bf16[128,2048]{1,0:T(8,128)(2,1)S(1)} %get-tuple-element.44), channel_id=1, source_target_pairs={{0,1},{1,0},{2,3},{3,2},{4,5},{5,4},{6,7},{7,6},{8,9},{9,8},{10,11... | collective-permute-start | bytes 1572872 | tf_op jit(solution)/shard_map/ppermute | solution.py:17
  55.0 13.3 %collective-permute-start.10 = (bf16[64,2048]{1,0:T(8,128)(2,1)S(1)}, bf16[64,2048]{1,0:T(8,128)(2,1)S(1)}, u32[]{:S(2)}, u32[]{:S(2)}) collective-permute-start(bf16[64,2048]{1,0:T(8,128)(2,1)S(1)} %get-tuple-element.75), channel_id=1, source_target_pairs={{0,6},{1,7},{2,4},{3,5},{4,2},{5,3},{6,0},{7,1},{8,14},{9,15},{10,... | collective-permute-start | bytes 786440 | tf_op jit(solution)/shard_map/ppermute | solution.py:17
  55.1 13.2 %collective-permute-start.8 = (bf16[64,2048]{1,0:T(8,128)(2,1)S(1)}, bf16[64,2048]{1,0:T(8,128)(2,1)S(1)}, u32[]{:S(2)}, u32[]{:S(2)}) collective-permute-start(bf16[64,2048]{1,0:T(8,128)(2,1)S(1)} %get-tuple-element.67), channel_id=1, source_target_pairs={{0,2},{1,3},{2,0},{3,1},{4,6},{5,7},{6,4},{7,5},{8,10},{9,11},{10,... | collective-permute-start | bytes 786440 | tf_op jit(solution)/shard_map/ppermute | solution.py:17
  55.1 13.1 %collective-permute-start.9 = (bf16[64,2048]{1,0:T(8,128)(2,1)S(1)}, bf16[64,2048]{1,0:T(8,128)(2,1)S(1)}, u32[]{:S(2)}, u32[]{:S(2)}) collective-permute-start(bf16[64,2048]{1,0:T(8,128)(2,1)S(1)} %get-tuple-element.76), channel_id=1, source_target_pairs={{0,4},{1,5},{2,6},{3,7},{4,0},{5,1},{6,2},{7,3},{8,12},{9,13},{10,... | collective-permute-start | bytes 786440 | tf_op jit(solution)/shard_map/ppermute | solution.py:17
  58.7 15.2 %collective-permute-start.13 = (bf16[64,2048]{1,0:T(8,128)(2,1)S(1)}, bf16[64,2048]{1,0:T(8,128)(2,1)S(1)}, u32[]{:S(2)}, u32[]{:S(2)}) collective-permute-start(bf16[64,2048]{1,0:T(8,128)(2,1)S(1)} %get-tuple-element.65), channel_id=1, source_target_pairs={{0,2},{1,3},{2,0},{3,1},{4,6},{5,7},{6,4},{7,5},{8,10},{9,11},{10,... | collective-permute-start | bytes 786440 | tf_op jit(solution)/shard_map/ppermute | solution.py:17
  64.2 10.6 %collective-permute-start.7 = (bf16[128,2048]{1,0:T(8,128)(2,1)S(1)}, bf16[128,2048]{1,0:T(8,128)(2,1)S(1)}, u32[]{:S(2)}, u32[]{:S(2)}) collective-permute-start(bf16[128,2048]{1,0:T(8,128)(2,1)S(1)} %get-tuple-element.55), channel_id=1, source_target_pairs={{0,1},{1,0},{2,3},{3,2},{4,5},{5,4},{6,7},{7,6},{8,9},{9,8},{10,11... | collective-permute-start | bytes 1572872 | tf_op jit(solution)/shard_map/ppermute | solution.py:17
  68.4 15.0 %collective-permute-start.11 = (bf16[64,2048]{1,0:T(8,128)(2,1)S(1)}, bf16[64,2048]{1,0:T(8,128)(2,1)S(1)}, u32[]{:S(2)}, u32[]{:S(2)}) collective-permute-start(bf16[64,2048]{1,0:T(8,128)(2,1)S(1)} %convert_add_fusion.1), channel_id=1, source_target_pairs={{0,8},{1,9},{2,10},{3,11},{4,12},{5,13},{6,14},{7,15},{8,0},{9,1},... | collective-permute-start | bytes 786440 | tf_op jit(solution)/shard_map/ppermute | solution.py:17
  73.9 12.8 %collective-permute-start.14 = (bf16[64,2048]{1,0:T(8,128)(2,1)S(1)}, bf16[64,2048]{1,0:T(8,128)(2,1)S(1)}, u32[]{:S(2)}, u32[]{:S(2)}) collective-permute-start(bf16[64,2048]{1,0:T(8,128)(2,1)S(1)} %add_convert_fusion), channel_id=1, source_target_pairs={{0,4},{1,5},{2,6},{3,7},{4,0},{5,1},{6,2},{7,3},{8,12},{9,13},{10,... | collective-permute-start | bytes 786440 | tf_op jit(solution)/shard_map/ppermute | solution.py:17
  75.0 11.7 %collective-permute-start.12 = (bf16[64,2048]{1,0:T(8,128)(2,1)S(1)}, bf16[64,2048]{1,0:T(8,128)(2,1)S(1)}, u32[]{:S(2)}, u32[]{:S(2)}) collective-permute-start(bf16[64,2048]{1,0:T(8,128)(2,1)S(1)} %get-tuple-element.62), channel_id=1, source_target_pairs={{0,2},{1,3},{2,0},{3,1},{4,6},{5,7},{6,4},{7,5},{8,10},{9,11},{10,... | collective-permute-start | bytes 786440 | tf_op jit(solution)/shard_map/ppermute | solution.py:17

commit v17 on v16

--- a/solution.py
+++ b/solution.py
@@ -254,11 +254,11 @@
     products = products.reshape(k_local, modes, bands_c * bands_v, excitons)
     places = jnp.mod(k_plus_q - me * k_local, k_local * size)
 
-    def rows(step, after):
+    def rows(step, after, sent=True):
         pick = jnp.concatenate((places, jnp.stack((z ^ (3 - step), core, x))))
         pick, _ = lax.optimization_barrier((pick, after))
         mine, other, send = rows_of(pick, flat, following[step], products)
-        return mine, other, permute(send, lambda i: i ^ 1)
+        return mine, other, permute(send, lambda i: i ^ 1) if sent else send
 
     half = width // 4
 
@@ -284,17 +284,21 @@
     mine_1, other_1 = summed(step_1, core_1)
     mine_2, other_2 = summed(step_2, core_2)
     sends = [value.astype(jnp.bfloat16) for value in (mine_0, other_0, other_1, other_2)]
-    step_3 = rows(3, sends)
-    across_1, across_2 = over(sends[2], 2), over(sends[3], 2)
-    far = over(sends[0], 4), over(sends[1], 6)
-    mine_1, _ = lax.optimization_barrier((mine_1, step_3[0]))
-    mine_1 = total_of(mine_1, across_1)
-    pair = total_of(lax.optimization_barrier(mine_1), *far)
+    turns = [jnp.where(core == turn, sends[2], sends[0]) for turn in range(2)]
+    arrived = [
+        permute(turns[turn], lambda i: i ^ (2 if i % 2 == turn else 4)) for turn in range(2)
+    ]
+    arrived.append(over(sends[1], 6))
+    across_2 = over(sends[3], 2)
+    mine_3, other_3, send_3 = rows(3, (turns, sends), False)
+    mine_1, _ = lax.optimization_barrier((mine_1, mine_3))
+    pair = total_of(mine_1, *arrived)
     mine_2, _ = lax.optimization_barrier((mine_2, pair))
+    send_3, _ = lax.optimization_barrier((send_3, pair))
     pair = over(pair, 8)
     near = over(total_of(mine_2, across_2), 4)
-    core_3, _ = lax.optimization_barrier((step_3[2], mine_2))
-    mine_3, other_3 = summed(step_3, core_3)
+    core_3, _ = lax.optimization_barrier((over(send_3, 1), mine_2))
+    mine_3, other_3 = summed((mine_3, other_3), core_3)
     mine_3, other_3 = lax.optimization_barrier((mine_3, other_3.astype(jnp.bfloat16)))
     total = lax.optimization_barrier(total_of(mine_3, pair))
     total = total_of(total, over(other_3, 2), near)

time: 88.4 us -> 91.6 us (1.036)
  waiting for transfers between devices: 26.1 us -> 18.4 us
  other arithmetic: 1.42 us -> 5.63 us
  local copies, waits for them, and re-layouts: 1.24 us -> 4.42 us
  Pallas kernels: 43.8 us -> 46.5 us
    ppermute x15, waiting for transfers between devices: 26.1 us -> 18.4 us  [permute(): lax.ppermute(x, 'ka', [(i, j % size) for i, j in pairs if j is not None])]
    unnamed x2 -> x24, local copies, waits for them, and re-layouts: 0.01 us -> 3.18 us
    convert_element_type x4, other arithmetic: 0.39 us -> 3.52 us  [summed(): from_core = from_core.astype(jnp.float32)]
    pallas_call x4, Pallas kernels: 23.7 us -> 26.5 us  [rows_of(): pl.pallas_call(rows_kernel, out_shape=[jax.ShapeDtypeStruct((width // 4,...]
    select_n x0 -> x2, other arithmetic: none -> 1.22 us  [on_two_by_four(): turns = [jnp.where(core == turn, sends[2], sends[0]) for turn in range(2)]]
  transfers between devices with their start and end apart: 15 -> 15, of which waited for: 6 -> 6; matrix products, arithmetic and copies ran while one was open for 1% -> 3% of each run, Pallas kernels for 47% -> 48%
where the time goes in v17:
time: 91.6 us; the launch traced here: 91.3 us
  Pallas kernels  46.5 us (51%)
  waiting for transfers between devices  18.4 us (20%)
  starting transfers between devices  16.1 us (18%)
  other arithmetic  5.63 us (6%)
  local copies, waits for them, and re-layouts  4.42 us (5%)
    pallas_call x4, Pallas kernels, rows_of(): pl.pallas_call(rows_kernel, out_shape=[jax.ShapeDtypeStruct((width // 4,...  26.5 us
    ppermute x15, waiting for transfers between devices, permute(): lax.ppermute(x, 'ka', [(i, j % size) for i, j in pairs if j is not None])  18.4 us
    ppermute x15, starting transfers between devices, permute(): lax.ppermute(x, 'ka', [(i, j % size) for i, j in pairs if j is not None])  16.1 us
    pallas_call x1, Pallas kernels, products_of(): pl.pallas_call(products_kernel, out_shape=jax.ShapeDtypeStruct((k_local,...  13.4 us
    pallas_call x2, Pallas kernels, turned_pieces(): pl.pallas_call(functools.partial(turn_kernel, first), out_shape=[jax.Shap...  6.61 us
    convert_element_type x4, other arithmetic, summed(): from_core = from_core.astype(jnp.float32)  3.52 us
    unnamed x24, local copies, waits for them, and re-layouts  3.18 us
  transfers between devices with their start and end apart: 15, of which 6 were waited for; matrix products, arithmetic and copies ran while one was open for 3% of the time, Pallas kernels for 48%

profile of v17, /device:TPU:0, one launch (start us, length us, event | category | flops | bytes accessed | tf_op | source)
XLA Modules:
  0.0 91.3 jit_solution(606720396485474473)
XLA Ops:
  0.0 2.5 %shard_map.56 = bf16[2,256,1024]{2,1,0:T(8,128)(2,1)} custom-call(bf16[2,1024,1024]{2,1,0:T(8,128)(2,1)} %bitcast.8), custom_call_target="tpu_custom_call" | custom-call | bytes 2097152 | tf_op jit(solution)/shard_map/pallas_call | solution.py:137
  2.5 5.5 %collective-permute-start = (bf16[2,256,1024]{2,1,0:T(8,128)(2,1)}, bf16[2,256,1024]{2,1,0:T(8,128)(2,1)}, u32[]{:S(2)}, u32[]{:S(2)}) collective-permute-start(bf16[2,256,1024]{2,1,0:T(8,128)(2,1)} %shard_map.56), channel_id=1, source_target_pairs={{0,15},{1,0},{2,1},{3,2},{4,3},{5,4},{6,5},{7,6},{8,7},{9,8},{10,9... | collective-permute-start | bytes 3145736 | tf_op jit(solution)/shard_map/ppermute | solution.py:17
  8.0 4.1 %shard_map.58 = (bf16[2,256,1024]{2,1,0:T(8,128)(2,1)}, bf16[2,256,1024]{2,1,0:T(8,128)(2,1)}, bf16[2,256,1024]{2,1,0:T(8,128)(2,1)}) custom-call(bf16[2,1024,1024]{2,1,0:T(8,128)(2,1)} %bitcast.9), custom_call_target="tpu_custom_call" | custom-call | bytes 6291456 | tf_op jit(solution)/shard_map/pallas_call | solution.py:137
  12.1 0.7 collective-permute-start.1
  12.8 0.1 collective-permute-start.4
  12.9 0.6 collective-permute-start.6
  13.5 0.1 add_add_fusion.2
  13.6 13.4 %shard_map.55 = bf16[2,2,32,32,1024]{4,3,2,1,0:T(8,128)(2,1)} custom-call(s32[2,2]{1,0:T(2,128)} %first_ref.1, bf16[2,32,32,1024]{3,2,1,0:T(8,128)(2,1)} %coeffs_ref.1, bf16[2,2,32,32]{3,2,1,0:T(8,128)(2,1)} %cond_ref.1, bf16[2,2,32,32]{3,2,1,0:T(8,128)(2,1)} %val_ref.1), custom_call_target="tpu_custom_call" | custom-call | flops 6442450944 | bytes 12582912 | tf_op jit(solution)/shard_map/pallas_call | solution.py:90
  27.0 0.1 add_add_fusion
  27.0 8.3 %shard_map.57 = (f32[64,2048]{1,0:T(8,128)S(1)}, f32[64,2048]{1,0:T(8,128)S(1)}, bf16[128,2048]{1,0:T(8,128)(2,1)}) custom-call(s32[5]{0:T(128)S(1)} %get-tuple-element.35.pick_ref, bf16[2,1024,1024]{2,1,0:T(8,128)(2,1)} %bitcast.10, bf16[2,256,1024]{2,1,0:T(8,128)(2,1)} %collective-permute-done.next_ref, bf16[2,2,1024,1024]{3,2,1,0:T(8,128)(2,1)} %bitcast.14), custom_call_target="tpu_custom_call" | custom-call | flops 2147483648 | bytes 8388608 | tf_op jit(solution)/shard_map/pallas_call | solution.py:212
  35.4 0.8 copy-done.2
  36.2 0.0 collective-permute-done.1.next_ref
  36.2 6.3 %shard_map.59 = (f32[64,2048]{1,0:T(8,128)S(1)}, f32[64,2048]{1,0:T(8,128)S(1)}, bf16[128,2048]{1,0:T(8,128)(2,1)}) custom-call(s32[5]{0:T(128)S(1)} %get-tuple-element.37.pick_ref, bf16[2,1024,1024]{2,1,0:T(8,128)(2,1)} %bitcast.11, bf16[2,256,1024]{2,1,0:T(8,128)(2,1)S(1)} %collective-permute-done.1.next_ref, bf16[2,2,1024,1024]{3,2,1,0:T(8,128)(2,1)} %bitcast.15), custom_call_target="tpu_custom_call" | custom-call | flops 2147483648 | bytes 8388608 | tf_op jit(solution)/shard_map/pallas_call | solution.py:212
  42.4 0.8 copy-done.10
  43.2 0.5 collective-permute-start.3
  43.7 0.0 collective-permute-done.4.next_ref
  43.7 6.3 %shard_map.60 = (f32[64,2048]{1,0:T(8,128)S(1)}, f32[64,2048]{1,0:T(8,128)S(1)}, bf16[128,2048]{1,0:T(8,128)(2,1)}) custom-call(s32[5]{0:T(128)S(1)} %get-tuple-element.44.pick_ref, bf16[2,1024,1024]{2,1,0:T(8,128)(2,1)} %bitcast.12, bf16[2,256,1024]{2,1,0:T(8,128)(2,1)S(1)} %collective-permute-done.4.next_ref, bf16[2,2,1024,1024]{3,2,1,0:T(8,128)(2,1)} %bitcast.16), custom_call_target="tpu_custom_call" | custom-call | flops 2147483648 | bytes 8388608 | tf_op jit(solution)/shard_map/pallas_call | solution.py:212
  50.1 0.8 copy-done.6
  50.9 0.8 copy-done.8
  51.6 0.1 collective-permute-start.5
  51.7 2.6 %collective-permute-done.6.next_ref = bf16[2,256,1024]{2,1,0:T(8,128)(2,1)S(1)} collective-permute-done((bf16[2,256,1024]{2,1,0:T(8,128)(2,1)}, bf16[2,256,1024]{2,1,0:T(8,128)(2,1)S(1)}, u32[]{:S(2)}, u32[]{:S(2)}) %collective-permute-start.6) | collective-permute-done | bytes 1048608 | tf_op jit(solution)/shard_map/ppermute | solution.py:17
  54.3 0.0 collective-permute-done.2
  54.3 1.1 %convert_element_type.59 = f32[128,2048]{1,0:T(8,128)S(1)} convert(bf16[128,2048]{1,0:T(8,128)(2,1)} %collective-permute-done.5) | non-fusion elementwise | flops 262144 | bytes 1572864 | tf_op jit(solution)/shard_map/convert_element_type | solution.py:266
  55.5 1.1 %convert_element_type.56 = f32[128,2048]{1,0:T(8,128)S(1)} convert(bf16[128,2048]{1,0:T(8,128)(2,1)} %collective-permute-done.2) | non-fusion elementwise | flops 262144 | bytes 1572864 | tf_op jit(solution)/shard_map/convert_element_type | solution.py:266
  56.6 0.1 fusion.2
  56.7 0.1 collective-permute-start.9
  56.8 1.1 %convert_element_type.54 = f32[128,2048]{1,0:T(8,128)S(1)} convert(bf16[128,2048]{1,0:T(8,128)(2,1)} %collective-permute-done.3) | non-fusion elementwise | flops 262144 | bytes 1572864 | tf_op jit(solution)/shard_map/convert_element_type | solution.py:266
  58.0 1.2 %broadcast_select_fusion.1 = (bf16[64,2048]{1,0:T(8,128)(2,1)S(1)}, bf16[64,2048]{1,0:T(8,128)(2,1)S(1)}, bf16[64,2048]{1,0:T(8,128)(2,1)S(1)}) fusion(pred[]{:T(512)S(6)} %eq.8, f32[64,2048]{1,0:T(8,128)S(1)} %copy-done.5, f32[128,2048]{1,0:T(8,128)S(1)} %convert_element_type.56, f32[64,2048]{1,0:T(8,128)} %copy-done.10, ...), kind=kLoop, calls=%fused_computation.18 | loop fusion | flops 655360 | bytes 2883585 | tf_op jit(solution)/shard_map/jit(_where)/select_n | solution.py:287
  59.2 2.6 %collective-permute-start.8 = (bf16[64,2048]{1,0:T(8,128)(2,1)S(1)}, bf16[64,2048]{1,0:T(8,128)(2,1)S(1)}, u32[]{:S(2)}, u32[]{:S(2)}) collective-permute-start(bf16[64,2048]{1,0:T(8,128)(2,1)S(1)} %broadcast_select_fusion), channel_id=1, source_target_pairs={{0,4},{1,3},{2,6},{3,1},{4,0},{5,7},{6,2},{7,5},{8,12},{9,11},{10,... | collective-permute-start | bytes 786440 | tf_op jit(solution)/shard_map/ppermute | solution.py:17
  61.8 0.9 collective-permute-start.7
  62.7 0.1 fusion.1
  62.9 0.1 slice_add_fusion.3
  63.0 1.2 %collective-permute-start.13 = (bf16[64,2048]{1,0:T(8,128)(2,1)S(1)}, bf16[64,2048]{1,0:T(8,128)(2,1)S(1)}, u32[]{:S(2)}, u32[]{:S(2)}) collective-permute-start(bf16[64,2048]{1,0:T(8,128)(2,1)S(1)} %get-tuple-element.70), channel_id=1, source_target_pairs={{0,2},{1,3},{2,0},{3,1},{4,6},{5,7},{6,4},{7,5},{8,10},{9,11},{10,... | collective-permute-start | bytes 786440 | tf_op jit(solution)/shard_map/ppermute | solution.py:17
  64.2 5.6 %shard_map.61 = (f32[64,2048]{1,0:T(8,128)S(1)}, f32[64,2048]{1,0:T(8,128)S(1)}, bf16[128,2048]{1,0:T(8,128)(2,1)S(1)}) custom-call(s32[5]{0:T(128)S(1)} %get-tuple-element.53.pick_ref, bf16[2,1024,1024]{2,1,0:T(8,128)(2,1)} %bitcast.13, bf16[2,256,1024]{2,1,0:T(8,128)(2,1)S(1)} %collective-permute-done.6.next_ref, bf16[2,2,1024,1024]{3,2,1,0:T(8,128)(2,1)} %bitcast.17), custom_call_target="tpu_custom_call" | custom-call | flops 2147483648 | bytes 8388608 | tf_op jit(solution)/shard_map/pallas_call | solution.py:212
  69.8 1.5 %collective-permute-done.8 = bf16[64,2048]{1,0:T(8,128)(2,1)S(1)} collective-permute-done((bf16[64,2048]{1,0:T(8,128)(2,1)S(1)}, bf16[64,2048]{1,0:T(8,128)(2,1)S(1)}, u32[]{:S(2)}, u32[]{:S(2)}) %collective-permute-start.8) | collective-permute-done | bytes 262176 | tf_op jit(solution)/shard_map/ppermute | solution.py:17
  71.3 0.5 collective-permute-done.7
  71.8 0.1 convert_add_fusion.1
  71.9 0.1 collective-permute-start.10
  72.0 1.8 %collective-permute-start.11 = (bf16[64,2048]{1,0:T(8,128)(2,1)S(1)}, bf16[64,2048]{1,0:T(8,128)(2,1)S(1)}, u32[]{:S(2)}, u32[]{:S(2)}) collective-permute-start(bf16[64,2048]{1,0:T(8,128)(2,1)S(1)} %convert_add_fusion.1), channel_id=1, source_target_pairs={{0,8},{1,9},{2,10},{3,11},{4,12},{5,13},{6,14},{7,15},{8,0},{9,1},... | collective-permute-start | bytes 786440 | tf_op jit(solution)/shard_map/ppermute | solution.py:17
  73.8 3.0 %collective-permute-done.13 = bf16[64,2048]{1,0:T(8,128)(2,1)S(1)} collective-permute-done((bf16[64,2048]{1,0:T(8,128)(2,1)S(1)}, bf16[64,2048]{1,0:T(8,128)(2,1)S(1)}, u32[]{:S(2)}, u32[]{:S(2)}) %collective-permute-start.13) | collective-permute-done | bytes 262176 | tf_op jit(solution)/shard_map/ppermute | solution.py:17
  76.9 0.4 collective-permute-start.14
  77.3 0.1 convert_element_type.64
  77.4 0.1 fusion
  77.5 1.5 %collective-permute-start.12 = (bf16[64,2048]{1,0:T(8,128)(2,1)S(1)}, bf16[64,2048]{1,0:T(8,128)(2,1)S(1)}, u32[]{:S(2)}, u32[]{:S(2)}) collective-permute-start(bf16[64,2048]{1,0:T(8,128)(2,1)S(1)} %get-tuple-element.64), channel_id=1, source_target_pairs={{0,2},{1,3},{2,0},{3,1},{4,6},{5,7},{6,4},{7,5},{8,10},{9,11},{10,... | collective-permute-start | bytes 786440 | tf_op jit(solution)/shard_map/ppermute | solution.py:17
  79.1 8.3 %collective-permute-done.11 = bf16[64,2048]{1,0:T(8,128)(2,1)S(1)} collective-permute-done((bf16[64,2048]{1,0:T(8,128)(2,1)S(1)}, bf16[64,2048]{1,0:T(8,128)(2,1)S(1)}, u32[]{:S(2)}, u32[]{:S(2)}) %collective-permute-start.11) | collective-permute-done | bytes 262176 | tf_op jit(solution)/shard_map/ppermute | solution.py:17
  87.4 2.5 %collective-permute-done.14 = bf16[64,2048]{1,0:T(8,128)(2,1)S(1)} collective-permute-done((bf16[64,2048]{1,0:T(8,128)(2,1)S(1)}, bf16[64,2048]{1,0:T(8,128)(2,1)S(1)}, u32[]{:S(2)}, u32[]{:S(2)}) %collective-permute-start.14) | collective-permute-done | bytes 262176 | tf_op jit(solution)/shard_map/ppermute | solution.py:17
  89.9 0.1 add_multiply_fusion
  90.1 1.2 %reshape.11 = f32[64,2,1024]{2,1,0:T(2,128)} reshape(f32[64,2048]{1,0:T(8,128)S(1)} %add_multiply_fusion) | data formatting | bytes 1048576 | tf_op jit(solution)/shard_map/reshape | solution.py:305
  (31 shorter events, 0.2 us)
Async XLA Ops:
  0.0 13.5 %copy-start.11 = (s32[2]{0:T(128)S(1)}, s32[2]{0:T(128)}, u32[]{:S(2)}) copy-start(s32[2]{0:T(128)} %param.8) | copy-start | bytes 28
  2.5 24.5 %collective-permute-start = (bf16[2,256,1024]{2,1,0:T(8,128)(2,1)}, bf16[2,256,1024]{2,1,0:T(8,128)(2,1)}, u32[]{:S(2)}, u32[]{:S(2)}) collective-permute-start(bf16[2,256,1024]{2,1,0:T(8,128)(2,1)} %shard_map.56), channel_id=1, source_target_pairs={{0,15},{1,0},{2,1},{3,2},{4,3},{5,4},{6,5},{7,6},{8,7},{9,8},{10,9... | collective-permute-start | bytes 3145736 | tf_op jit(solution)/shard_map/ppermute | solution.py:17
  12.1 24.1 %collective-permute-start.1 = (bf16[2,256,1024]{2,1,0:T(8,128)(2,1)}, bf16[2,256,1024]{2,1,0:T(8,128)(2,1)S(1)}, u32[]{:S(2)}, u32[]{:S(2)}) collective-permute-start(bf16[2,256,1024]{2,1,0:T(8,128)(2,1)} %get-tuple-element.39), channel_id=1, source_target_pairs={{0,15},{1,0},{2,1},{3,2},{4,3},{5,4},{6,5},{7,6},{8,7},{9,8},{10,9... | collective-permute-start | bytes 3145736 | tf_op jit(solution)/shard_map/ppermute | solution.py:17
  12.8 30.9 %collective-permute-start.4 = (bf16[2,256,1024]{2,1,0:T(8,128)(2,1)}, bf16[2,256,1024]{2,1,0:T(8,128)(2,1)S(1)}, u32[]{:S(2)}, u32[]{:S(2)}) collective-permute-start(bf16[2,256,1024]{2,1,0:T(8,128)(2,1)} %get-tuple-element.45), channel_id=1, source_target_pairs={{0,15},{1,0},{2,1},{3,2},{4,3},{5,4},{6,5},{7,6},{8,7},{9,8},{10,9... | collective-permute-start | bytes 3145736 | tf_op jit(solution)/shard_map/ppermute | solution.py:17
  12.9 41.4 %collective-permute-start.6 = (bf16[2,256,1024]{2,1,0:T(8,128)(2,1)}, bf16[2,256,1024]{2,1,0:T(8,128)(2,1)S(1)}, u32[]{:S(2)}, u32[]{:S(2)}) collective-permute-start(bf16[2,256,1024]{2,1,0:T(8,128)(2,1)} %get-tuple-element.47), channel_id=1, source_target_pairs={{0,15},{1,0},{2,1},{3,2},{4,3},{5,4},{6,5},{7,6},{8,7},{9,8},{10,9... | collective-permute-start | bytes 3145736 | tf_op jit(solution)/shard_map/ppermute | solution.py:17
  35.4 0.8 copy-start.2
  36.2 7.1 %copy-start.4 = (f32[64,2048]{1,0:T(8,128)}, f32[64,2048]{1,0:T(8,128)S(1)}, u32[]{:S(2)}) copy-start(f32[64,2048]{1,0:T(8,128)S(1)} %get-tuple-element.36) | copy-start | bytes 1572868
  42.4 0.8 copy-start.10
  43.2 6.8 %copy-start = (f32[64,2048]{1,0:T(8,128)}, f32[64,2048]{1,0:T(8,128)S(1)}, u32[]{:S(2)}) copy-start(f32[64,2048]{1,0:T(8,128)S(1)} %get-tuple-element.43) | copy-start | bytes 1572868
  43.2 11.1 %collective-permute-start.2 = (bf16[128,2048]{1,0:T(8,128)(2,1)}, bf16[128,2048]{1,0:T(8,128)(2,1)}, u32[]{:S(2)}, u32[]{:S(2)}) collective-permute-start(bf16[128,2048]{1,0:T(8,128)(2,1)} %get-tuple-element.41), channel_id=1, source_target_pairs={{0,1},{1,0},{2,3},{3,2},{4,5},{5,4},{6,7},{7,6},{8,9},{9,8},{10,11... | collective-permute-start | bytes 1572872 | tf_op jit(solution)/shard_map/ppermute | solution.py:17
  43.2 13.4 %copy-start.3 = (f32[64,2048]{1,0:T(8,128)S(1)}, f32[64,2048]{1,0:T(8,128)}, u32[]{:S(2)}) copy-start(f32[64,2048]{1,0:T(8,128)} %copy-done.2) | copy-start | bytes 1572868
  43.2 11.1 %collective-permute-start.3 = (bf16[128,2048]{1,0:T(8,128)(2,1)}, bf16[128,2048]{1,0:T(8,128)(2,1)}, u32[]{:S(2)}, u32[]{:S(2)}) collective-permute-start(bf16[128,2048]{1,0:T(8,128)(2,1)} %get-tuple-element.42), channel_id=1, source_target_pairs={{0,1},{1,0},{2,3},{3,2},{4,5},{5,4},{6,7},{7,6},{8,9},{9,8},{10,11... | collective-permute-start | bytes 1572872 | tf_op jit(solution)/shard_map/ppermute | solution.py:17
  43.7 14.2 %copy-start.5 = (f32[64,2048]{1,0:T(8,128)S(1)}, f32[64,2048]{1,0:T(8,128)}, u32[]{:S(2)}) copy-start(f32[64,2048]{1,0:T(8,128)} %copy-done.4) | copy-start | bytes 1572868
  50.1 0.8 copy-start.6
  50.9 0.8 copy-start.8
  51.6 11.1 %copy-start.7 = (f32[64,2048]{1,0:T(8,128)S(1)}, f32[64,2048]{1,0:T(8,128)}, u32[]{:S(2)}) copy-start(f32[64,2048]{1,0:T(8,128)} %copy-done.6) | copy-start | bytes 1572868
  51.6 11.2 %copy-start.1 = (f32[64,2048]{1,0:T(8,128)S(1)}, f32[64,2048]{1,0:T(8,128)}, u32[]{:S(2)}) copy-start(f32[64,2048]{1,0:T(8,128)} %copy-done) | copy-start | bytes 1572868
  51.6 2.7 %collective-permute-start.5 = (bf16[128,2048]{1,0:T(8,128)(2,1)}, bf16[128,2048]{1,0:T(8,128)(2,1)}, u32[]{:S(2)}, u32[]{:S(2)}) collective-permute-start(bf16[128,2048]{1,0:T(8,128)(2,1)} %get-tuple-element.46), channel_id=1, source_target_pairs={{0,1},{1,0},{2,3},{3,2},{4,5},{5,4},{6,7},{7,6},{8,9},{9,8},{10,11... | collective-permute-start | bytes 1572872 | tf_op jit(solution)/shard_map/ppermute | solution.py:17
  51.7 11.0 %copy-start.9 = (f32[64,2048]{1,0:T(8,128)S(1)}, f32[64,2048]{1,0:T(8,128)}, u32[]{:S(2)}) copy-start(f32[64,2048]{1,0:T(8,128)} %copy-done.8) | copy-start | bytes 1572868
  56.7 13.1 %collective-permute-start.9 = (bf16[64,2048]{1,0:T(8,128)(2,1)S(1)}, bf16[64,2048]{1,0:T(8,128)(2,1)S(1)}, u32[]{:S(2)}, u32[]{:S(2)}) collective-permute-start(bf16[64,2048]{1,0:T(8,128)(2,1)S(1)} %fusion.2), channel_id=1, source_target_pairs={{0,6},{1,7},{2,4},{3,5},{4,2},{5,3},{6,0},{7,1},{8,14},{9,15},{10,... | collective-permute-start | bytes 786440 | tf_op jit(solution)/shard_map/ppermute | solution.py:17
  59.2 12.1 %collective-permute-start.8 = (bf16[64,2048]{1,0:T(8,128)(2,1)S(1)}, bf16[64,2048]{1,0:T(8,128)(2,1)S(1)}, u32[]{:S(2)}, u32[]{:S(2)}) collective-permute-start(bf16[64,2048]{1,0:T(8,128)(2,1)S(1)} %broadcast_select_fusion), channel_id=1, source_target_pairs={{0,4},{1,3},{2,6},{3,1},{4,0},{5,7},{6,2},{7,5},{8,12},{9,11},{10,... | collective-permute-start | bytes 786440 | tf_op jit(solution)/shard_map/ppermute | solution.py:17
  61.8 10.0 %collective-permute-start.7 = (bf16[64,2048]{1,0:T(8,128)(2,1)S(1)}, bf16[64,2048]{1,0:T(8,128)(2,1)S(1)}, u32[]{:S(2)}, u32[]{:S(2)}) collective-permute-start(bf16[64,2048]{1,0:T(8,128)(2,1)S(1)} %get-tuple-element.65), channel_id=1, source_target_pairs={{0,2},{1,5},{2,0},{3,7},{4,6},{5,1},{6,4},{7,3},{8,10},{9,13},{10,... | collective-permute-start | bytes 786440 | tf_op jit(solution)/shard_map/ppermute | solution.py:17
  63.0 13.9 %collective-permute-start.13 = (bf16[64,2048]{1,0:T(8,128)(2,1)S(1)}, bf16[64,2048]{1,0:T(8,128)(2,1)S(1)}, u32[]{:S(2)}, u32[]{:S(2)}) collective-permute-start(bf16[64,2048]{1,0:T(8,128)(2,1)S(1)} %get-tuple-element.70), channel_id=1, source_target_pairs={{0,2},{1,3},{2,0},{3,1},{4,6},{5,7},{6,4},{7,5},{8,10},{9,11},{10,... | collective-permute-start | bytes 786440 | tf_op jit(solution)/shard_map/ppermute | solution.py:17
  71.9 5.4 %collective-permute-start.10 = (bf16[128,2048]{1,0:T(8,128)(2,1)S(1)}, bf16[128,2048]{1,0:T(8,128)(2,1)S(1)}, u32[]{:S(2)}, u32[]{:S(2)}) collective-permute-start(bf16[128,2048]{1,0:T(8,128)(2,1)S(1)} %get-tuple-element.58), channel_id=1, source_target_pairs={{0,1},{1,0},{2,3},{3,2},{4,5},{5,4},{6,7},{7,6},{8,9},{9,8},{10,11... | collective-permute-start | bytes 1572872 | tf_op jit(solution)/shard_map/ppermute | solution.py:17
  72.0 15.3 %collective-permute-start.11 = (bf16[64,2048]{1,0:T(8,128)(2,1)S(1)}, bf16[64,2048]{1,0:T(8,128)(2,1)S(1)}, u32[]{:S(2)}, u32[]{:S(2)}) collective-permute-start(bf16[64,2048]{1,0:T(8,128)(2,1)S(1)} %convert_add_fusion.1), channel_id=1, source_target_pairs={{0,8},{1,9},{2,10},{3,11},{4,12},{5,13},{6,14},{7,15},{8,0},{9,1},... | collective-permute-start | bytes 786440 | tf_op jit(solution)/shard_map/ppermute | solution.py:17
  76.9 13.1 %collective-permute-start.14 = (bf16[64,2048]{1,0:T(8,128)(2,1)S(1)}, bf16[64,2048]{1,0:T(8,128)(2,1)S(1)}, u32[]{:S(2)}, u32[]{:S(2)}) collective-permute-start(bf16[64,2048]{1,0:T(8,128)(2,1)S(1)} %add_convert_fusion), channel_id=1, source_target_pairs={{0,4},{1,5},{2,6},{3,7},{4,0},{5,1},{6,2},{7,3},{8,12},{9,13},{10,... | collective-permute-start | bytes 786440 | tf_op jit(solution)/shard_map/ppermute | solution.py:17
  77.5 12.4 %collective-permute-start.12 = (bf16[64,2048]{1,0:T(8,128)(2,1)S(1)}, bf16[64,2048]{1,0:T(8,128)(2,1)S(1)}, u32[]{:S(2)}, u32[]{:S(2)}) collective-permute-start(bf16[64,2048]{1,0:T(8,128)(2,1)S(1)} %get-tuple-element.64), channel_id=1, source_target_pairs={{0,2},{1,3},{2,0},{3,1},{4,6},{5,7},{6,4},{7,5},{8,10},{9,11},{10,... | collective-permute-start | bytes 786440 | tf_op jit(solution)/shard_map/ppermute | solution.py:17

commit v18 on v17

--- a/solution.py
+++ b/solution.py
@@ -237,6 +237,41 @@
     )(pick, own, following, products)
 
 
+def payloads_kernel(*refs):
+    ins, (turn_0, turn_1, cross_0, cross_2, mine_1, mine_2) = refs[:9], refs[9:]
+    half = turn_0.shape[0]
+
+    def summed(block, own):
+        rows = slice(0, half) if own else slice(half, 2 * half)
+        mine, other, core = ins[3 * block:3 * block + 3]
+        return (mine if own else other)[...] + core[rows, :].astype(jnp.float32)
+
+    straight = summed(0, True).astype(jnp.bfloat16)
+    across = summed(1, False).astype(jnp.bfloat16)
+    first = lax.axis_index("ka") & 1 == 0
+    turn_0[...] = jnp.where(first, across, straight)
+    turn_1[...] = jnp.where(first, straight, across)
+    cross_0[...] = summed(0, False).astype(jnp.bfloat16)
+    cross_2[...] = summed(2, False).astype(jnp.bfloat16)
+    mine_1[...] = summed(1, True)
+    mine_2[...] = summed(2, True)
+
+
+def payloads_of(*parts):
+    shape = parts[0].shape
+    return pl.pallas_call(
+        payloads_kernel,
+        out_shape=[jax.ShapeDtypeStruct(shape, jnp.bfloat16)] * 4
+        + [jax.ShapeDtypeStruct(shape, jnp.float32)] * 2,
+        in_specs=[pl.BlockSpec(memory_space=pltpu.VMEM)] * 9,
+        out_specs=[pl.BlockSpec(memory_space=pltpu.VMEM)] * 6,
+        compiler_params=pltpu.CompilerParams(vmem_limit_bytes=24 * MIB),
+        cost_estimate=pl.CostEstimate(
+            flops=6 * parts[0].size, bytes_accessed=26 * parts[0].size, transcendentals=0
+        ),
+    )(*parts)
+
+
 def on_two_by_four(coeffs, g_cond, g_val, k_plus_q, band_first, norm_factor):
     k_local, bands_c, bands_v, excitons = coeffs.shape
     modes = g_cond.shape[1]
@@ -280,17 +315,15 @@
     core_0, core_1, core_2, following[3] = lax.optimization_barrier(
         (step_0[2], step_1[2], step_2[2], following[3])
     )
-    mine_0, other_0 = summed(step_0, core_0)
-    mine_1, other_1 = summed(step_1, core_1)
-    mine_2, other_2 = summed(step_2, core_2)
-    sends = [value.astype(jnp.bfloat16) for value in (mine_0, other_0, other_1, other_2)]
-    turns = [jnp.where(core == turn, sends[2], sends[0]) for turn in range(2)]
+    *turns, cross_0, cross_2, mine_1, mine_2 = payloads_of(
+        *step_0[:2], core_0, *step_1[:2], core_1, *step_2[:2], core_2
+    )
     arrived = [
         permute(turns[turn], lambda i: i ^ (2 if i % 2 == turn else 4)) for turn in range(2)
     ]
-    arrived.append(over(sends[1], 6))
-    across_2 = over(sends[3], 2)
-    mine_3, other_3, send_3 = rows(3, (turns, sends), False)
+    arrived.append(over(cross_0, 6))
+    across_2 = over(cross_2, 2)
+    mine_3, other_3, send_3 = rows(3, mine_2, False)
     mine_1, _ = lax.optimization_barrier((mine_1, mine_3))
     pair = total_of(mine_1, *arrived)
     mine_2, _ = lax.optimization_barrier((mine_2, pair))

time: 91.6 us -> 88.8 us (0.969)
  waiting for transfers between devices: 18.4 us -> 27.9 us
  other arithmetic: 5.63 us -> 0.68 us
  local copies, waits for them, and re-layouts: 4.42 us -> 1.24 us
  Pallas kernels: 46.5 us -> 44.3 us
  starting transfers between devices: 16.1 us -> 14.2 us
    ppermute x15, waiting for transfers between devices: 18.4 us -> 27.9 us  [permute(): lax.ppermute(x, 'ka', [(i, j % size) for i, j in pairs if j is not None])]
    convert_element_type x4 -> x1, other arithmetic: 3.52 us -> 0.1 us  [summed(): from_core = from_core.astype(jnp.float32)]
    unnamed x24 -> x2, local copies, waits for them, and re-layouts: 3.18 us -> 0.01 us
    pallas_call x4, Pallas kernels: 26.5 us -> 23.8 us  [rows_of(): pl.pallas_call(rows_kernel, out_shape=[jax.ShapeDtypeStruct((width // 4,...]
    ppermute x15, starting transfers between devices: 16.1 us -> 14.2 us  [permute(): lax.ppermute(x, 'ka', [(i, j % size) for i, j in pairs if j is not None])]
    select_n x2 -> x0, other arithmetic: 1.22 us -> none  [on_two_by_four(): turns = [jnp.where(core == turn, sends[2], sends[0]) for turn in range(2)]]
  transfers between devices with their start and end apart: 15 -> 15, of which waited for: 6 -> 6; matrix products, arithmetic and copies ran while one was open for 3% -> 1% of each run, Pallas kernels for 48% -> 47%
where the time goes in v18:
time: 88.8 us; the launch traced here: 88.5 us
  Pallas kernels  44.3 us (50%)
  waiting for transfers between devices  27.9 us (31%)
  starting transfers between devices  14.2 us (16%)
  local copies, waits for them, and re-layouts  1.24 us (1%)
    ppermute x15, waiting for transfers between devices, permute(): lax.ppermute(x, 'ka', [(i, j % size) for i, j in pairs if j is not None])  27.9 us
    pallas_call x4, Pallas kernels, rows_of(): pl.pallas_call(rows_kernel, out_shape=[jax.ShapeDtypeStruct((width // 4,...  23.8 us
    ppermute x15, starting transfers between devices, permute(): lax.ppermute(x, 'ka', [(i, j % size) for i, j in pairs if j is not None])  14.2 us
    pallas_call x1, Pallas kernels, products_of(): pl.pallas_call(products_kernel, out_shape=jax.ShapeDtypeStruct((k_local,...  13.4 us
    pallas_call x2, Pallas kernels, turned_pieces(): pl.pallas_call(functools.partial(turn_kernel, first), out_shape=[jax.Shap...  6.78 us
  transfers between devices with their start and end apart: 15, of which 6 were waited for; matrix products, arithmetic and copies ran while one was open for 1% of the time, Pallas kernels for 47%

profile of v18, /device:TPU:0, one launch (start us, length us, event | category | flops | bytes accessed | tf_op | source)
XLA Modules:
  0.0 88.5 jit_solution(13040707733927432696)
XLA Ops:
  0.0 0.0 copy-start
  0.0 2.6 %shard_map.56 = bf16[2,256,1024]{2,1,0:T(8,128)(2,1)} custom-call(bf16[2,1024,1024]{2,1,0:T(8,128)(2,1)} %bitcast.8), custom_call_target="tpu_custom_call" | custom-call | bytes 2097152 | tf_op jit(solution)/shard_map/pallas_call | solution.py:137
  2.6 5.5 %collective-permute-start = (bf16[2,256,1024]{2,1,0:T(8,128)(2,1)}, bf16[2,256,1024]{2,1,0:T(8,128)(2,1)}, u32[]{:S(2)}, u32[]{:S(2)}) collective-permute-start(bf16[2,256,1024]{2,1,0:T(8,128)(2,1)} %shard_map.56), channel_id=1, source_target_pairs={{0,15},{1,0},{2,1},{3,2},{4,3},{5,4},{6,5},{7,6},{8,7},{9,8},{10,9... | collective-permute-start | bytes 3145736 | tf_op jit(solution)/shard_map/ppermute | solution.py:17
  8.0 4.2 %shard_map.58 = (bf16[2,256,1024]{2,1,0:T(8,128)(2,1)}, bf16[2,256,1024]{2,1,0:T(8,128)(2,1)}, bf16[2,256,1024]{2,1,0:T(8,128)(2,1)}) custom-call(bf16[2,1024,1024]{2,1,0:T(8,128)(2,1)} %bitcast.9), custom_call_target="tpu_custom_call" | custom-call | bytes 6291456 | tf_op jit(solution)/shard_map/pallas_call | solution.py:137
  12.3 0.7 collective-permute-start.2
  13.0 0.1 collective-permute-start.4
  13.1 0.6 collective-permute-start.6
  13.6 0.0 copy-done
  13.7 0.1 add_add_fusion
  13.7 13.4 %shard_map.55 = bf16[2,2,32,32,1024]{4,3,2,1,0:T(8,128)(2,1)} custom-call(s32[2,2]{1,0:T(2,128)} %first_ref.1, bf16[2,32,32,1024]{3,2,1,0:T(8,128)(2,1)} %coeffs_ref.1, bf16[2,2,32,32]{3,2,1,0:T(8,128)(2,1)} %cond_ref.1, bf16[2,2,32,32]{3,2,1,0:T(8,128)(2,1)} %val_ref.1), custom_call_target="tpu_custom_call" | custom-call | flops 6442450944 | bytes 12582912 | tf_op jit(solution)/shard_map/pallas_call | solution.py:90
  27.1 0.1 add_add_fusion.3
  27.2 0.0 collective-permute-done.next_ref
  27.2 7.4 %shard_map.57 = (f32[64,2048]{1,0:T(8,128)S(1)}, f32[64,2048]{1,0:T(8,128)S(1)}, bf16[128,2048]{1,0:T(8,128)(2,1)S(1)}) custom-call(s32[5]{0:T(128)S(1)} %get-tuple-element.41.pick_ref, bf16[2,1024,1024]{2,1,0:T(8,128)(2,1)} %bitcast.10, bf16[2,256,1024]{2,1,0:T(8,128)(2,1)} %collective-permute-done.next_ref, bf16[2,2,1024,1024]{3,2,1,0:T(8,128)(2,1)} %bitcast.14), custom_call_target="tpu_custom_call" | custom-call | flops 2147483648 | bytes 8388608 | tf_op jit(solution)/shard_map/pallas_call | solution.py:212
  34.7 0.0 collective-permute-done.2.next_ref
  34.7 5.5 %shard_map.59 = (f32[64,2048]{1,0:T(8,128)S(1)}, f32[64,2048]{1,0:T(8,128)S(1)}, bf16[128,2048]{1,0:T(8,128)(2,1)S(1)}) custom-call(s32[5]{0:T(128)S(1)} %get-tuple-element.45.pick_ref, bf16[2,1024,1024]{2,1,0:T(8,128)(2,1)} %bitcast.11, bf16[2,256,1024]{2,1,0:T(8,128)(2,1)S(1)} %collective-permute-done.2.next_ref, bf16[2,2,1024,1024]{3,2,1,0:T(8,128)(2,1)} %bitcast.15), custom_call_target="tpu_custom_call" | custom-call | flops 2147483648 | bytes 8388608 | tf_op jit(solution)/shard_map/pallas_call | solution.py:212
  40.1 3.0 %collective-permute-done.4.next_ref = bf16[2,256,1024]{2,1,0:T(8,128)(2,1)S(1)} collective-permute-done((bf16[2,256,1024]{2,1,0:T(8,128)(2,1)}, bf16[2,256,1024]{2,1,0:T(8,128)(2,1)S(1)}, u32[]{:S(2)}, u32[]{:S(2)}) %collective-permute-start.4) | collective-permute-done | bytes 1048608 | tf_op jit(solution)/shard_map/ppermute | solution.py:17
  43.1 5.5 %shard_map.60 = (f32[64,2048]{1,0:T(8,128)S(1)}, f32[64,2048]{1,0:T(8,128)S(1)}, bf16[128,2048]{1,0:T(8,128)(2,1)S(1)}) custom-call(s32[5]{0:T(128)S(1)} %get-tuple-element.50.pick_ref, bf16[2,1024,1024]{2,1,0:T(8,128)(2,1)} %bitcast.12, bf16[2,256,1024]{2,1,0:T(8,128)(2,1)S(1)} %collective-permute-done.4.next_ref, bf16[2,2,1024,1024]{3,2,1,0:T(8,128)(2,1)} %bitcast.16), custom_call_target="tpu_custom_call" | custom-call | flops 2147483648 | bytes 8388608 | tf_op jit(solution)/shard_map/pallas_call | solution.py:212
  48.6 0.1 collective-permute-start.5
  48.7 0.5 collective-permute-start.3
  49.2 0.1 collective-permute-start.1
  49.3 5.1 %collective-permute-done.6.next_ref = bf16[2,256,1024]{2,1,0:T(8,128)(2,1)S(1)} collective-permute-done((bf16[2,256,1024]{2,1,0:T(8,128)(2,1)}, bf16[2,256,1024]{2,1,0:T(8,128)(2,1)S(1)}, u32[]{:S(2)}, u32[]{:S(2)}) %collective-permute-start.6) | collective-permute-done | bytes 1048608 | tf_op jit(solution)/shard_map/ppermute | solution.py:17
  54.4 0.0 collective-permute-done.5.refs_8_
  54.4 0.0 collective-permute-done.3.refs_5_
  54.4 0.0 collective-permute-done.1.refs_2_
  54.4 0.3 shard_map.61
  54.7 0.1 collective-permute-start.7
  54.8 0.1 collective-permute-start.8
  54.9 3.4 %collective-permute-start.9 = (bf16[64,2048]{1,0:T(8,128)(2,1)S(1)}, bf16[64,2048]{1,0:T(8,128)(2,1)S(1)}, u32[]{:S(2)}, u32[]{:S(2)}) collective-permute-start(bf16[64,2048]{1,0:T(8,128)(2,1)S(1)} %get-tuple-element.69), channel_id=1, source_target_pairs={{0,6},{1,7},{2,4},{3,5},{4,2},{5,3},{6,0},{7,1},{8,14},{9,15},{10,... | collective-permute-start | bytes 786440 | tf_op jit(solution)/shard_map/ppermute | solution.py:17
  58.3 5.5 %shard_map.62 = (f32[64,2048]{1,0:T(8,128)S(1)}, f32[64,2048]{1,0:T(8,128)S(1)}, bf16[128,2048]{1,0:T(8,128)(2,1)S(1)}) custom-call(s32[5]{0:T(128)S(1)} %get-tuple-element.61.pick_ref, bf16[2,1024,1024]{2,1,0:T(8,128)(2,1)} %bitcast.13, bf16[2,256,1024]{2,1,0:T(8,128)(2,1)S(1)} %collective-permute-done.6.next_ref, bf16[2,2,1024,1024]{3,2,1,0:T(8,128)(2,1)} %bitcast.17), custom_call_target="tpu_custom_call" | custom-call | flops 2147483648 | bytes 8388608 | tf_op jit(solution)/shard_map/pallas_call | solution.py:212
  63.8 0.1 collective-permute-start.13
  63.9 5.1 %collective-permute-done.7 = bf16[64,2048]{1,0:T(8,128)(2,1)S(1)} collective-permute-done((bf16[64,2048]{1,0:T(8,128)(2,1)S(1)}, bf16[64,2048]{1,0:T(8,128)(2,1)S(1)}, u32[]{:S(2)}, u32[]{:S(2)}) %collective-permute-start.7) | collective-permute-done | bytes 262176 | tf_op jit(solution)/shard_map/ppermute | solution.py:17
  69.0 0.0 collective-permute-done.8
  69.0 0.0 collective-permute-done.9
  69.0 0.1 convert_add_fusion.1
  69.2 0.1 collective-permute-start.10
  69.2 1.4 %collective-permute-start.11 = (bf16[64,2048]{1,0:T(8,128)(2,1)S(1)}, bf16[64,2048]{1,0:T(8,128)(2,1)S(1)}, u32[]{:S(2)}, u32[]{:S(2)}) collective-permute-start(bf16[64,2048]{1,0:T(8,128)(2,1)S(1)} %convert_add_fusion.1), channel_id=1, source_target_pairs={{0,8},{1,9},{2,10},{3,11},{4,12},{5,13},{6,14},{7,15},{8,0},{9,1},... | collective-permute-start | bytes 786440 | tf_op jit(solution)/shard_map/ppermute | solution.py:17
  70.6 3.2 %collective-permute-done.13 = bf16[64,2048]{1,0:T(8,128)(2,1)S(1)} collective-permute-done((bf16[64,2048]{1,0:T(8,128)(2,1)S(1)}, bf16[64,2048]{1,0:T(8,128)(2,1)S(1)}, u32[]{:S(2)}, u32[]{:S(2)}) %collective-permute-start.13) | collective-permute-done | bytes 262176 | tf_op jit(solution)/shard_map/ppermute | solution.py:17
  73.9 1.5 %collective-permute-start.14 = (bf16[64,2048]{1,0:T(8,128)(2,1)S(1)}, bf16[64,2048]{1,0:T(8,128)(2,1)S(1)}, u32[]{:S(2)}, u32[]{:S(2)}) collective-permute-start(bf16[64,2048]{1,0:T(8,128)(2,1)S(1)} %add_convert_fusion), channel_id=1, source_target_pairs={{0,4},{1,5},{2,6},{3,7},{4,0},{5,1},{6,2},{7,3},{8,12},{9,13},{10,... | collective-permute-start | bytes 786440 | tf_op jit(solution)/shard_map/ppermute | solution.py:17
  75.4 0.0 collective-permute-done.10
  75.4 0.1 convert_element_type.36
  75.5 0.1 fusion
  75.6 0.1 collective-permute-start.12
  75.7 8.9 %collective-permute-done.11 = bf16[64,2048]{1,0:T(8,128)(2,1)S(1)} collective-permute-done((bf16[64,2048]{1,0:T(8,128)(2,1)S(1)}, bf16[64,2048]{1,0:T(8,128)(2,1)S(1)}, u32[]{:S(2)}, u32[]{:S(2)}) %collective-permute-start.11) | collective-permute-done | bytes 262176 | tf_op jit(solution)/shard_map/ppermute | solution.py:17
  84.6 2.5 %collective-permute-done.14 = bf16[64,2048]{1,0:T(8,128)(2,1)S(1)} collective-permute-done((bf16[64,2048]{1,0:T(8,128)(2,1)S(1)}, bf16[64,2048]{1,0:T(8,128)(2,1)S(1)}, u32[]{:S(2)}, u32[]{:S(2)}) %collective-permute-start.14) | collective-permute-done | bytes 262176 | tf_op jit(solution)/shard_map/ppermute | solution.py:17
  87.2 0.0 collective-permute-done.12
  87.2 0.1 add_multiply_fusion
  87.3 1.2 %reshape.11 = f32[64,2,1024]{2,1,0:T(2,128)} reshape(f32[64,2048]{1,0:T(8,128)S(1)} %add_multiply_fusion) | data formatting | bytes 1048576 | tf_op jit(solution)/shard_map/reshape | solution.py:338
  (3 shorter events, 0.1 us)
Async XLA Ops:
  0.0 13.7 %copy-start = (s32[2]{0:T(128)S(1)}, s32[2]{0:T(128)}, u32[]{:S(2)}) copy-start(s32[2]{0:T(128)} %param.8) | copy-start | bytes 28
  2.6 24.7 %collective-permute-start = (bf16[2,256,1024]{2,1,0:T(8,128)(2,1)}, bf16[2,256,1024]{2,1,0:T(8,128)(2,1)}, u32[]{:S(2)}, u32[]{:S(2)}) collective-permute-start(bf16[2,256,1024]{2,1,0:T(8,128)(2,1)} %shard_map.56), channel_id=1, source_target_pairs={{0,15},{1,0},{2,1},{3,2},{4,3},{5,4},{6,5},{7,6},{8,7},{9,8},{10,9... | collective-permute-start | bytes 3145736 | tf_op jit(solution)/shard_map/ppermute | solution.py:17
  12.3 22.4 %collective-permute-start.2 = (bf16[2,256,1024]{2,1,0:T(8,128)(2,1)}, bf16[2,256,1024]{2,1,0:T(8,128)(2,1)S(1)}, u32[]{:S(2)}, u32[]{:S(2)}) collective-permute-start(bf16[2,256,1024]{2,1,0:T(8,128)(2,1)} %get-tuple-element.47), channel_id=1, source_target_pairs={{0,15},{1,0},{2,1},{3,2},{4,3},{5,4},{6,5},{7,6},{8,7},{9,8},{10,9... | collective-permute-start | bytes 3145736 | tf_op jit(solution)/shard_map/ppermute | solution.py:17
  13.0 30.1 %collective-permute-start.4 = (bf16[2,256,1024]{2,1,0:T(8,128)(2,1)}, bf16[2,256,1024]{2,1,0:T(8,128)(2,1)S(1)}, u32[]{:S(2)}, u32[]{:S(2)}) collective-permute-start(bf16[2,256,1024]{2,1,0:T(8,128)(2,1)} %get-tuple-element.51), channel_id=1, source_target_pairs={{0,15},{1,0},{2,1},{3,2},{4,3},{5,4},{6,5},{7,6},{8,7},{9,8},{10,9... | collective-permute-start | bytes 3145736 | tf_op jit(solution)/shard_map/ppermute | solution.py:17
  13.1 41.3 %collective-permute-start.6 = (bf16[2,256,1024]{2,1,0:T(8,128)(2,1)}, bf16[2,256,1024]{2,1,0:T(8,128)(2,1)S(1)}, u32[]{:S(2)}, u32[]{:S(2)}) collective-permute-start(bf16[2,256,1024]{2,1,0:T(8,128)(2,1)} %get-tuple-element.53), channel_id=1, source_target_pairs={{0,15},{1,0},{2,1},{3,2},{4,3},{5,4},{6,5},{7,6},{8,7},{9,8},{10,9... | collective-permute-start | bytes 3145736 | tf_op jit(solution)/shard_map/ppermute | solution.py:17
  48.6 5.8 %collective-permute-start.5 = (bf16[128,2048]{1,0:T(8,128)(2,1)S(1)}, bf16[128,2048]{1,0:T(8,128)(2,1)S(1)}, u32[]{:S(2)}, u32[]{:S(2)}) collective-permute-start(bf16[128,2048]{1,0:T(8,128)(2,1)S(1)} %get-tuple-element.52), channel_id=1, source_target_pairs={{0,1},{1,0},{2,3},{3,2},{4,5},{5,4},{6,7},{7,6},{8,9},{9,8},{10,11... | collective-permute-start | bytes 1572872 | tf_op jit(solution)/shard_map/ppermute | solution.py:17
  48.7 5.7 %collective-permute-start.3 = (bf16[128,2048]{1,0:T(8,128)(2,1)S(1)}, bf16[128,2048]{1,0:T(8,128)(2,1)S(1)}, u32[]{:S(2)}, u32[]{:S(2)}) collective-permute-start(bf16[128,2048]{1,0:T(8,128)(2,1)S(1)} %get-tuple-element.48), channel_id=1, source_target_pairs={{0,1},{1,0},{2,3},{3,2},{4,5},{5,4},{6,7},{7,6},{8,9},{9,8},{10,11... | collective-permute-start | bytes 1572872 | tf_op jit(solution)/shard_map/ppermute | solution.py:17
  49.2 5.2 %collective-permute-start.1 = (bf16[128,2048]{1,0:T(8,128)(2,1)S(1)}, bf16[128,2048]{1,0:T(8,128)(2,1)S(1)}, u32[]{:S(2)}, u32[]{:S(2)}) collective-permute-start(bf16[128,2048]{1,0:T(8,128)(2,1)S(1)} %get-tuple-element.44), channel_id=1, source_target_pairs={{0,1},{1,0},{2,3},{3,2},{4,5},{5,4},{6,7},{7,6},{8,9},{9,8},{10,11... | collective-permute-start | bytes 1572872 | tf_op jit(solution)/shard_map/ppermute | solution.py:17
  54.7 14.3 %collective-permute-start.7 = (bf16[64,2048]{1,0:T(8,128)(2,1)S(1)}, bf16[64,2048]{1,0:T(8,128)(2,1)S(1)}, u32[]{:S(2)}, u32[]{:S(2)}) collective-permute-start(bf16[64,2048]{1,0:T(8,128)(2,1)S(1)} %get-tuple-element.67), channel_id=1, source_target_pairs={{0,2},{1,5},{2,0},{3,7},{4,6},{5,1},{6,4},{7,3},{8,10},{9,13},{10,... | collective-permute-start | bytes 786440 | tf_op jit(solution)/shard_map/ppermute | solution.py:17
  54.8 14.2 %collective-permute-start.8 = (bf16[64,2048]{1,0:T(8,128)(2,1)S(1)}, bf16[64,2048]{1,0:T(8,128)(2,1)S(1)}, u32[]{:S(2)}, u32[]{:S(2)}) collective-permute-start(bf16[64,2048]{1,0:T(8,128)(2,1)S(1)} %get-tuple-element.68), channel_id=1, source_target_pairs={{0,4},{1,3},{2,6},{3,1},{4,0},{5,7},{6,2},{7,5},{8,12},{9,11},{10,... | collective-permute-start | bytes 786440 | tf_op jit(solution)/shard_map/ppermute | solution.py:17
  54.9 14.1 %collective-permute-start.9 = (bf16[64,2048]{1,0:T(8,128)(2,1)S(1)}, bf16[64,2048]{1,0:T(8,128)(2,1)S(1)}, u32[]{:S(2)}, u32[]{:S(2)}) collective-permute-start(bf16[64,2048]{1,0:T(8,128)(2,1)S(1)} %get-tuple-element.69), channel_id=1, source_target_pairs={{0,6},{1,7},{2,4},{3,5},{4,2},{5,3},{6,0},{7,1},{8,14},{9,15},{10,... | collective-permute-start | bytes 786440 | tf_op jit(solution)/shard_map/ppermute | solution.py:17
  63.8 10.1 %collective-permute-start.13 = (bf16[64,2048]{1,0:T(8,128)(2,1)S(1)}, bf16[64,2048]{1,0:T(8,128)(2,1)S(1)}, u32[]{:S(2)}, u32[]{:S(2)}) collective-permute-start(bf16[64,2048]{1,0:T(8,128)(2,1)S(1)} %get-tuple-element.76), channel_id=1, source_target_pairs={{0,2},{1,3},{2,0},{3,1},{4,6},{5,7},{6,4},{7,5},{8,10},{9,11},{10,... | collective-permute-start | bytes 786440 | tf_op jit(solution)/shard_map/ppermute | solution.py:17
  69.2 6.2 %collective-permute-start.10 = (bf16[128,2048]{1,0:T(8,128)(2,1)S(1)}, bf16[128,2048]{1,0:T(8,128)(2,1)S(1)}, u32[]{:S(2)}, u32[]{:S(2)}) collective-permute-start(bf16[128,2048]{1,0:T(8,128)(2,1)S(1)} %get-tuple-element.70), channel_id=1, source_target_pairs={{0,1},{1,0},{2,3},{3,2},{4,5},{5,4},{6,7},{7,6},{8,9},{9,8},{10,11... | collective-permute-start | bytes 1572872 | tf_op jit(solution)/shard_map/ppermute | solution.py:17
  69.2 15.3 %collective-permute-start.11 = (bf16[64,2048]{1,0:T(8,128)(2,1)S(1)}, bf16[64,2048]{1,0:T(8,128)(2,1)S(1)}, u32[]{:S(2)}, u32[]{:S(2)}) collective-permute-start(bf16[64,2048]{1,0:T(8,128)(2,1)S(1)} %convert_add_fusion.1), channel_id=1, source_target_pairs={{0,8},{1,9},{2,10},{3,11},{4,12},{5,13},{6,14},{7,15},{8,0},{9,1},... | collective-permute-start | bytes 786440 | tf_op jit(solution)/shard_map/ppermute | solution.py:17
  73.9 13.3 %collective-permute-start.14 = (bf16[64,2048]{1,0:T(8,128)(2,1)S(1)}, bf16[64,2048]{1,0:T(8,128)(2,1)S(1)}, u32[]{:S(2)}, u32[]{:S(2)}) collective-permute-start(bf16[64,2048]{1,0:T(8,128)(2,1)S(1)} %add_convert_fusion), channel_id=1, source_target_pairs={{0,4},{1,5},{2,6},{3,7},{4,0},{5,1},{6,2},{7,3},{8,12},{9,13},{10,... | collective-permute-start | bytes 786440 | tf_op jit(solution)/shard_map/ppermute | solution.py:17
  75.6 11.6 %collective-permute-start.12 = (bf16[64,2048]{1,0:T(8,128)(2,1)S(1)}, bf16[64,2048]{1,0:T(8,128)(2,1)S(1)}, u32[]{:S(2)}, u32[]{:S(2)}) collective-permute-start(bf16[64,2048]{1,0:T(8,128)(2,1)S(1)} %get-tuple-element.75), channel_id=1, source_target_pairs={{0,2},{1,3},{2,0},{3,1},{4,6},{5,7},{6,4},{7,5},{8,10},{9,11},{10,... | collective-permute-start | bytes 786440 | tf_op jit(solution)/shard_map/ppermute | solution.py:17

commit v19 on v13

--- a/solution.py
+++ b/solution.py
@@ -237,6 +237,63 @@
     )(pick, own, following, products)
 
 
+def payloads_kernel(*refs):
+    ins, (far_0, far_1, across, near_0, near_1, mine_1) = refs[:9], refs[9:]
+    half = across.shape[0]
+
+    def summed(block, own):
+        mine, other, core = ins[3 * block:3 * block + 3]
+        rows = slice(0, half) if own else slice(half, 2 * half)
+        return (mine if own else other)[...] + core[rows, :].astype(jnp.float32)
+
+    far_0[...] = summed(0, True).astype(jnp.bfloat16)
+    far_1[...] = summed(0, False).astype(jnp.bfloat16)
+    across[...] = summed(1, False).astype(jnp.bfloat16)
+    near_0[...] = summed(2, True).astype(jnp.bfloat16)
+    near_1[...] = summed(2, False).astype(jnp.bfloat16)
+    mine_1[...] = summed(1, True)
+
+
+def payloads_of(*parts):
+    shape = parts[0].shape
+    return pl.pallas_call(
+        payloads_kernel,
+        out_shape=[jax.ShapeDtypeStruct(shape, jnp.bfloat16)] * 5
+        + [jax.ShapeDtypeStruct(shape, jnp.float32)],
+        in_specs=[pl.BlockSpec(memory_space=pltpu.VMEM)] * 9,
+        out_specs=[pl.BlockSpec(memory_space=pltpu.VMEM)] * 6,
+        compiler_params=pltpu.CompilerParams(vmem_limit_bytes=24 * MIB),
+        cost_estimate=pl.CostEstimate(
+            flops=6 * parts[0].size, bytes_accessed=26 * parts[0].size, transcendentals=0
+        ),
+    )(*parts)
+
+
+def close_kernel(factor, mine_ref, core_ref, *refs):
+    *parts, out_ref = refs
+    half, modes, excitons = out_ref.shape
+    for m in range(modes):
+        columns = slice(m * excitons, (m + 1) * excitons)
+        total = mine_ref[:, columns] + core_ref[:half, columns].astype(jnp.float32)
+        for ref in parts:
+            total = total + ref[:, columns].astype(jnp.float32)
+        out_ref[:, m, :] = total * factor
+
+
+def closed(modes, factor, *parts):
+    rows, columns = parts[0].shape
+    return pl.pallas_call(
+        functools.partial(close_kernel, factor),
+        out_shape=jax.ShapeDtypeStruct((rows, modes, columns // modes), jnp.float32),
+        in_specs=[pl.BlockSpec(memory_space=pltpu.VMEM)] * len(parts),
+        out_specs=pl.BlockSpec(memory_space=pltpu.VMEM),
+        compiler_params=pltpu.CompilerParams(vmem_limit_bytes=24 * MIB),
+        cost_estimate=pl.CostEstimate(
+            flops=5 * parts[0].size, bytes_accessed=16 * parts[0].size, transcendentals=0
+        ),
+    )(*parts)
+
+
 def on_two_by_four(coeffs, g_cond, g_val, k_plus_q, band_first, norm_factor):
     k_local, bands_c, bands_v, excitons = coeffs.shape
     modes = g_cond.shape[1]
@@ -262,10 +319,6 @@
 
     half = width // 4
 
-    def summed(step, from_core):
-        from_core = from_core.astype(jnp.float32)
-        return step[0] + from_core[:half], step[1] + from_core[half:]
-
     def over(value, bits):
         return permute(value.astype(jnp.bfloat16), lambda i: i ^ bits)
 
@@ -280,19 +333,18 @@
     core_0, core_1, core_2, following[3] = lax.optimization_barrier(
         (step_0[2], step_1[2], step_2[2], following[3])
     )
-    mine_0, other_0 = summed(step_0, core_0)
-    mine_1, other_1 = summed(step_1, core_1)
-    mine_2, other_2 = summed(step_2, core_2)
-    sends = [value.astype(jnp.bfloat16) for value in (mine_0, other_0, other_1, mine_2, other_2)]
+    *sends, mine_1 = payloads_of(
+        *step_0[:2], core_0, *step_1[:2], core_1, *step_2[:2], core_2
+    )
     step_3 = rows(3, sends)
     far = over(sends[0], 4), over(sends[1], 6)
     across_1 = over(sends[2], 2)
     near = over(sends[3], 4), over(sends[4], 6)
     mine_1, _ = lax.optimization_barrier((mine_1, step_3[0]))
     pair = over(total_of(mine_1, across_1, *far), 8)
-    mine_3, other_3 = summed(step_3, step_3[2])
-    total = total_of(mine_3, over(other_3, 2), pair, *near)
-    return (total * norm_factor).reshape(width // 4, modes, excitons)
+    mine_3, other_3, core_3 = step_3
+    across_3 = over(other_3 + core_3[half:].astype(jnp.float32), 2)
+    return closed(modes, norm_factor, mine_3, core_3, across_3, pair, *near)
 
 
 def on_any(coeffs, g_cond, g_val, k_plus_q, band_first, norm_factor):

time: 85.8 us -> 85.6 us (level)
  waiting for transfers between devices: 23.7 us -> 25.1 us
  local copies, waits for them, and re-layouts: 1.24 us -> 0.01 us
  Pallas kernels: 44 us -> 45.1 us
  other arithmetic: 1.35 us -> 0.33 us
    ppermute x15, waiting for transfers between devices: 23.7 us -> 25.1 us  [permute(): lax.ppermute(x, 'ka', [(i, j % size) for i, j in pairs if j is not None])]
    pallas_call x0 -> x2, Pallas kernels: none -> 1.33 us  [the longest x1 1.07 us: closed(): pl.pallas_call(functools.partial(close_kernel, factor), out_shape=jax.Sha...]
    reshape x1 -> x0, local copies, waits for them, and re-layouts: 1.23 us -> none  [on_two_by_four(): return (total * norm_factor).reshape(width // 4, modes, excitons)]
  transfers between devices with their start and end apart: 15 -> 15, of which waited for: 8 -> 7; matrix products, arithmetic and copies ran while one was open for 1% -> 0% of each run, Pallas kernels for 49% -> 48%
where the time goes in v19:
time: 85.6 us; the launch traced here: 85.3 us
  Pallas kernels  45.1 us (53%)
  waiting for transfers between devices  25.1 us (29%)
  starting transfers between devices  14.5 us (17%)
    ppermute x15, waiting for transfers between devices, permute(): lax.ppermute(x, 'ka', [(i, j % size) for i, j in pairs if j is not None])  25.1 us
    pallas_call x4, Pallas kernels, rows_of(): pl.pallas_call(rows_kernel, out_shape=[jax.ShapeDtypeStruct((width // 4,...  23.8 us
    ppermute x15, starting transfers between devices, permute(): lax.ppermute(x, 'ka', [(i, j % size) for i, j in pairs if j is not None])  14.5 us
    pallas_call x1, Pallas kernels, products_of(): pl.pallas_call(products_kernel, out_shape=jax.ShapeDtypeStruct((k_local,...  13.4 us
    pallas_call x2, Pallas kernels, turned_pieces(): pl.pallas_call(functools.partial(turn_kernel, first), out_shape=[jax.Shap...  6.69 us
  transfers between devices with their start and end apart: 15, of which 7 were waited for; matrix products, arithmetic and copies ran while one was open for 0% of the time, Pallas kernels for 48%

profile of v19, /device:TPU:0, one launch (start us, length us, event | category | flops | bytes accessed | tf_op | source)
XLA Modules:
  0.0 85.3 jit_solution(14385564617791549869)
XLA Ops:
  0.0 0.0 copy-start
  0.0 2.5 %shard_map.56 = bf16[2,256,1024]{2,1,0:T(8,128)(2,1)} custom-call(bf16[2,1024,1024]{2,1,0:T(8,128)(2,1)} %bitcast.8), custom_call_target="tpu_custom_call" | custom-call | bytes 2097152 | tf_op jit(solution)/shard_map/pallas_call | solution.py:137
  2.5 5.5 %collective-permute-start = (bf16[2,256,1024]{2,1,0:T(8,128)(2,1)}, bf16[2,256,1024]{2,1,0:T(8,128)(2,1)}, u32[]{:S(2)}, u32[]{:S(2)}) collective-permute-start(bf16[2,256,1024]{2,1,0:T(8,128)(2,1)} %shard_map.56), channel_id=1, source_target_pairs={{0,15},{1,0},{2,1},{3,2},{4,3},{5,4},{6,5},{7,6},{8,7},{9,8},{10,9... | collective-permute-start | bytes 3145736 | tf_op jit(solution)/shard_map/ppermute | solution.py:17
  8.0 4.2 %shard_map.58 = (bf16[2,256,1024]{2,1,0:T(8,128)(2,1)}, bf16[2,256,1024]{2,1,0:T(8,128)(2,1)}, bf16[2,256,1024]{2,1,0:T(8,128)(2,1)}) custom-call(bf16[2,1024,1024]{2,1,0:T(8,128)(2,1)} %bitcast.9), custom_call_target="tpu_custom_call" | custom-call | bytes 6291456 | tf_op jit(solution)/shard_map/pallas_call | solution.py:137
  12.2 0.7 collective-permute-start.2
  12.9 0.1 collective-permute-start.4
  13.0 0.6 collective-permute-start.6
  13.6 0.0 copy-done
  13.6 0.1 add_add_fusion.3
  13.7 13.4 %shard_map.55 = bf16[2,2,32,32,1024]{4,3,2,1,0:T(8,128)(2,1)} custom-call(s32[2,2]{1,0:T(2,128)} %first_ref.1, bf16[2,32,32,1024]{3,2,1,0:T(8,128)(2,1)} %coeffs_ref.1, bf16[2,2,32,32]{3,2,1,0:T(8,128)(2,1)} %cond_ref.1, bf16[2,2,32,32]{3,2,1,0:T(8,128)(2,1)} %val_ref.1), custom_call_target="tpu_custom_call" | custom-call | flops 6442450944 | bytes 12582912 | tf_op jit(solution)/shard_map/pallas_call | solution.py:90
  27.0 0.1 add_add_fusion.2
  27.1 0.0 collective-permute-done.next_ref
  27.1 7.3 %shard_map.57 = (f32[64,2048]{1,0:T(8,128)S(1)}, f32[64,2048]{1,0:T(8,128)S(1)}, bf16[128,2048]{1,0:T(8,128)(2,1)S(1)}) custom-call(s32[5]{0:T(128)S(1)} %get-tuple-element.36.pick_ref, bf16[2,1024,1024]{2,1,0:T(8,128)(2,1)} %bitcast.10, bf16[2,256,1024]{2,1,0:T(8,128)(2,1)} %collective-permute-done.next_ref, bf16[2,2,1024,1024]{3,2,1,0:T(8,128)(2,1)} %bitcast.14), custom_call_target="tpu_custom_call" | custom-call | flops 2147483648 | bytes 8388608 | tf_op jit(solution)/shard_map/pallas_call | solution.py:212
  34.4 0.0 collective-permute-done.2.next_ref
  34.4 5.5 %shard_map.59 = (f32[64,2048]{1,0:T(8,128)S(1)}, f32[64,2048]{1,0:T(8,128)S(1)}, bf16[128,2048]{1,0:T(8,128)(2,1)S(1)}) custom-call(s32[5]{0:T(128)S(1)} %get-tuple-element.40.pick_ref, bf16[2,1024,1024]{2,1,0:T(8,128)(2,1)} %bitcast.11, bf16[2,256,1024]{2,1,0:T(8,128)(2,1)S(1)} %collective-permute-done.2.next_ref, bf16[2,2,1024,1024]{3,2,1,0:T(8,128)(2,1)} %bitcast.15), custom_call_target="tpu_custom_call" | custom-call | flops 2147483648 | bytes 8388608 | tf_op jit(solution)/shard_map/pallas_call | solution.py:212
  40.0 3.1 %collective-permute-done.4.next_ref = bf16[2,256,1024]{2,1,0:T(8,128)(2,1)S(1)} collective-permute-done((bf16[2,256,1024]{2,1,0:T(8,128)(2,1)}, bf16[2,256,1024]{2,1,0:T(8,128)(2,1)S(1)}, u32[]{:S(2)}, u32[]{:S(2)}) %collective-permute-start.4) | collective-permute-done | bytes 1048608 | tf_op jit(solution)/shard_map/ppermute | solution.py:17
  43.1 5.5 %shard_map.60 = (f32[64,2048]{1,0:T(8,128)S(1)}, f32[64,2048]{1,0:T(8,128)S(1)}, bf16[128,2048]{1,0:T(8,128)(2,1)S(1)}) custom-call(s32[5]{0:T(128)S(1)} %get-tuple-element.45.pick_ref, bf16[2,1024,1024]{2,1,0:T(8,128)(2,1)} %bitcast.12, bf16[2,256,1024]{2,1,0:T(8,128)(2,1)S(1)} %collective-permute-done.4.next_ref, bf16[2,2,1024,1024]{3,2,1,0:T(8,128)(2,1)} %bitcast.16), custom_call_target="tpu_custom_call" | custom-call | flops 2147483648 | bytes 8388608 | tf_op jit(solution)/shard_map/pallas_call | solution.py:212
  48.6 0.1 collective-permute-start.5
  48.6 0.5 collective-permute-start.3
  49.1 0.1 collective-permute-start.1
  49.2 5.2 %collective-permute-done.6.next_ref = bf16[2,256,1024]{2,1,0:T(8,128)(2,1)S(1)} collective-permute-done((bf16[2,256,1024]{2,1,0:T(8,128)(2,1)}, bf16[2,256,1024]{2,1,0:T(8,128)(2,1)S(1)}, u32[]{:S(2)}, u32[]{:S(2)}) %collective-permute-start.6) | collective-permute-done | bytes 1048608 | tf_op jit(solution)/shard_map/ppermute | solution.py:17
  54.4 0.0 collective-permute-done.5.refs_8_
  54.4 0.0 collective-permute-done.3.refs_5_
  54.4 0.0 collective-permute-done.1.refs_2_
  54.4 0.3 shard_map.61
  54.7 0.1 collective-permute-start.10
  54.8 0.1 collective-permute-start.11
  54.8 3.4 %collective-permute-start.9 = (bf16[64,2048]{1,0:T(8,128)(2,1)S(1)}, bf16[64,2048]{1,0:T(8,128)(2,1)S(1)}, u32[]{:S(2)}, u32[]{:S(2)}) collective-permute-start(bf16[64,2048]{1,0:T(8,128)(2,1)S(1)} %get-tuple-element.57), channel_id=1, source_target_pairs={{0,2},{1,3},{2,0},{3,1},{4,6},{5,7},{6,4},{7,5},{8,10},{9,11},{10,... | collective-permute-start | bytes 786440 | tf_op jit(solution)/shard_map/ppermute | solution.py:17
  58.2 5.5 %shard_map.62 = (f32[64,2048]{1,0:T(8,128)S(1)}, f32[64,2048]{1,0:T(8,128)S(1)}, bf16[128,2048]{1,0:T(8,128)(2,1)S(1)}) custom-call(s32[5]{0:T(128)S(1)} %get-tuple-element.60.pick_ref, bf16[2,1024,1024]{2,1,0:T(8,128)(2,1)} %bitcast.13, bf16[2,256,1024]{2,1,0:T(8,128)(2,1)S(1)} %collective-permute-done.6.next_ref, bf16[2,2,1024,1024]{3,2,1,0:T(8,128)(2,1)} %bitcast.17), custom_call_target="tpu_custom_call" | custom-call | flops 2147483648 | bytes 8388608 | tf_op jit(solution)/shard_map/pallas_call | solution.py:212
  63.7 0.1 collective-permute-start.7
  63.8 0.2 collective-permute-start.13
  63.9 0.0 collective-permute-done.10
  64.0 1.4 %collective-permute-start.14 = (bf16[64,2048]{1,0:T(8,128)(2,1)S(1)}, bf16[64,2048]{1,0:T(8,128)(2,1)S(1)}, u32[]{:S(2)}, u32[]{:S(2)}) collective-permute-start(bf16[64,2048]{1,0:T(8,128)(2,1)S(1)} %get-tuple-element.59), channel_id=1, source_target_pairs={{0,6},{1,7},{2,4},{3,5},{4,2},{5,3},{6,0},{7,1},{8,14},{9,15},{10,... | collective-permute-start | bytes 786440 | tf_op jit(solution)/shard_map/ppermute | solution.py:17
  65.3 0.9 %collective-permute-done.11 = bf16[64,2048]{1,0:T(8,128)(2,1)S(1)} collective-permute-done((bf16[64,2048]{1,0:T(8,128)(2,1)S(1)}, bf16[64,2048]{1,0:T(8,128)(2,1)S(1)}, u32[]{:S(2)}, u32[]{:S(2)}) %collective-permute-start.11) | collective-permute-done | bytes 262176 | tf_op jit(solution)/shard_map/ppermute | solution.py:17
  66.2 3.2 %collective-permute-done.9 = bf16[64,2048]{1,0:T(8,128)(2,1)S(1)} collective-permute-done((bf16[64,2048]{1,0:T(8,128)(2,1)S(1)}, bf16[64,2048]{1,0:T(8,128)(2,1)S(1)}, u32[]{:S(2)}, u32[]{:S(2)}) %collective-permute-start.9) | collective-permute-done | bytes 262176 | tf_op jit(solution)/shard_map/ppermute | solution.py:17
  69.4 0.1 add_convert_fusion
  69.6 1.4 %collective-permute-start.12 = (bf16[64,2048]{1,0:T(8,128)(2,1)S(1)}, bf16[64,2048]{1,0:T(8,128)(2,1)S(1)}, u32[]{:S(2)}, u32[]{:S(2)}) collective-permute-start(bf16[64,2048]{1,0:T(8,128)(2,1)S(1)} %add_convert_fusion), channel_id=1, source_target_pairs={{0,8},{1,9},{2,10},{3,11},{4,12},{5,13},{6,14},{7,15},{8,0},{9,1},... | collective-permute-start | bytes 786440 | tf_op jit(solution)/shard_map/ppermute | solution.py:17
  71.0 0.0 collective-permute-done.7.core_ref
  71.0 0.5 collective-permute-start.8
  71.5 1.5 %collective-permute-done.13.refs_2_ = bf16[64,2048]{1,0:T(8,128)(2,1)S(1)} collective-permute-done((bf16[64,2048]{1,0:T(8,128)(2,1)S(1)}, bf16[64,2048]{1,0:T(8,128)(2,1)S(1)}, u32[]{:S(2)}, u32[]{:S(2)}) %collective-permute-start.13) | collective-permute-done | bytes 262176 | tf_op jit(solution)/shard_map/ppermute | solution.py:17
  73.0 10.5 %collective-permute-done.14.refs_3_ = bf16[64,2048]{1,0:T(8,128)(2,1)S(1)} collective-permute-done((bf16[64,2048]{1,0:T(8,128)(2,1)S(1)}, bf16[64,2048]{1,0:T(8,128)(2,1)S(1)}, u32[]{:S(2)}, u32[]{:S(2)}) %collective-permute-start.14) | collective-permute-done | bytes 262176 | tf_op jit(solution)/shard_map/ppermute | solution.py:17
  83.4 0.0 collective-permute-done.12.refs_1_
  83.4 0.8 collective-permute-done.8.refs_0_
  84.2 1.1 %shard_map.63 = f32[64,2,1024]{2,1,0:T(2,128)} custom-call(f32[64,2048]{1,0:T(8,128)S(1)} %get-tuple-element.62.mine_ref, bf16[128,2048]{1,0:T(8,128)(2,1)S(1)} %collective-permute-done.7.core_ref, bf16[64,2048]{1,0:T(8,128)(2,1)S(1)} %collective-permute-done.8.refs_0_, bf16[64,2048]{1,0:T(8,128)(2,1)S(1)} %collective-permute-done.12.refs_1_, ...), custom_call_target="tpu_custom_call" | custom-call | flops 655360 | bytes 2097152 | tf_op jit(solution)/shard_map/pallas_call | solution.py:285
  (2 shorter events, 0.1 us)
Async XLA Ops:
  0.0 13.6 %copy-start = (s32[2]{0:T(128)S(1)}, s32[2]{0:T(128)}, u32[]{:S(2)}) copy-start(s32[2]{0:T(128)} %param.8) | copy-start | bytes 28
  2.5 24.6 %collective-permute-start = (bf16[2,256,1024]{2,1,0:T(8,128)(2,1)}, bf16[2,256,1024]{2,1,0:T(8,128)(2,1)}, u32[]{:S(2)}, u32[]{:S(2)}) collective-permute-start(bf16[2,256,1024]{2,1,0:T(8,128)(2,1)} %shard_map.56), channel_id=1, source_target_pairs={{0,15},{1,0},{2,1},{3,2},{4,3},{5,4},{6,5},{7,6},{8,7},{9,8},{10,9... | collective-permute-start | bytes 3145736 | tf_op jit(solution)/shard_map/ppermute | solution.py:17
  12.2 22.2 %collective-permute-start.2 = (bf16[2,256,1024]{2,1,0:T(8,128)(2,1)}, bf16[2,256,1024]{2,1,0:T(8,128)(2,1)S(1)}, u32[]{:S(2)}, u32[]{:S(2)}) collective-permute-start(bf16[2,256,1024]{2,1,0:T(8,128)(2,1)} %get-tuple-element.42), channel_id=1, source_target_pairs={{0,15},{1,0},{2,1},{3,2},{4,3},{5,4},{6,5},{7,6},{8,7},{9,8},{10,9... | collective-permute-start | bytes 3145736 | tf_op jit(solution)/shard_map/ppermute | solution.py:17
  12.9 30.2 %collective-permute-start.4 = (bf16[2,256,1024]{2,1,0:T(8,128)(2,1)}, bf16[2,256,1024]{2,1,0:T(8,128)(2,1)S(1)}, u32[]{:S(2)}, u32[]{:S(2)}) collective-permute-start(bf16[2,256,1024]{2,1,0:T(8,128)(2,1)} %get-tuple-element.46), channel_id=1, source_target_pairs={{0,15},{1,0},{2,1},{3,2},{4,3},{5,4},{6,5},{7,6},{8,7},{9,8},{10,9... | collective-permute-start | bytes 3145736 | tf_op jit(solution)/shard_map/ppermute | solution.py:17
  13.0 41.4 %collective-permute-start.6 = (bf16[2,256,1024]{2,1,0:T(8,128)(2,1)}, bf16[2,256,1024]{2,1,0:T(8,128)(2,1)S(1)}, u32[]{:S(2)}, u32[]{:S(2)}) collective-permute-start(bf16[2,256,1024]{2,1,0:T(8,128)(2,1)} %get-tuple-element.48), channel_id=1, source_target_pairs={{0,15},{1,0},{2,1},{3,2},{4,3},{5,4},{6,5},{7,6},{8,7},{9,8},{10,9... | collective-permute-start | bytes 3145736 | tf_op jit(solution)/shard_map/ppermute | solution.py:17
  48.6 5.8 %collective-permute-start.5 = (bf16[128,2048]{1,0:T(8,128)(2,1)S(1)}, bf16[128,2048]{1,0:T(8,128)(2,1)S(1)}, u32[]{:S(2)}, u32[]{:S(2)}) collective-permute-start(bf16[128,2048]{1,0:T(8,128)(2,1)S(1)} %get-tuple-element.47), channel_id=1, source_target_pairs={{0,1},{1,0},{2,3},{3,2},{4,5},{5,4},{6,7},{7,6},{8,9},{9,8},{10,11... | collective-permute-start | bytes 1572872 | tf_op jit(solution)/shard_map/ppermute | solution.py:17
  48.6 5.8 %collective-permute-start.3 = (bf16[128,2048]{1,0:T(8,128)(2,1)S(1)}, bf16[128,2048]{1,0:T(8,128)(2,1)S(1)}, u32[]{:S(2)}, u32[]{:S(2)}) collective-permute-start(bf16[128,2048]{1,0:T(8,128)(2,1)S(1)} %get-tuple-element.43), channel_id=1, source_target_pairs={{0,1},{1,0},{2,3},{3,2},{4,5},{5,4},{6,7},{7,6},{8,9},{9,8},{10,11... | collective-permute-start | bytes 1572872 | tf_op jit(solution)/shard_map/ppermute | solution.py:17
  49.1 5.3 %collective-permute-start.1 = (bf16[128,2048]{1,0:T(8,128)(2,1)S(1)}, bf16[128,2048]{1,0:T(8,128)(2,1)S(1)}, u32[]{:S(2)}, u32[]{:S(2)}) collective-permute-start(bf16[128,2048]{1,0:T(8,128)(2,1)S(1)} %get-tuple-element.39), channel_id=1, source_target_pairs={{0,1},{1,0},{2,3},{3,2},{4,5},{5,4},{6,7},{7,6},{8,9},{9,8},{10,11... | collective-permute-start | bytes 1572872 | tf_op jit(solution)/shard_map/ppermute | solution.py:17
  54.7 9.3 %collective-permute-start.10 = (bf16[64,2048]{1,0:T(8,128)(2,1)S(1)}, bf16[64,2048]{1,0:T(8,128)(2,1)S(1)}, u32[]{:S(2)}, u32[]{:S(2)}) collective-permute-start(bf16[64,2048]{1,0:T(8,128)(2,1)S(1)} %get-tuple-element.55), channel_id=1, source_target_pairs={{0,4},{1,5},{2,6},{3,7},{4,0},{5,1},{6,2},{7,3},{8,12},{9,13},{10,... | collective-permute-start | bytes 786440 | tf_op jit(solution)/shard_map/ppermute | solution.py:17
  54.8 11.5 %collective-permute-start.11 = (bf16[64,2048]{1,0:T(8,128)(2,1)S(1)}, bf16[64,2048]{1,0:T(8,128)(2,1)S(1)}, u32[]{:S(2)}, u32[]{:S(2)}) collective-permute-start(bf16[64,2048]{1,0:T(8,128)(2,1)S(1)} %get-tuple-element.56), channel_id=1, source_target_pairs={{0,6},{1,7},{2,4},{3,5},{4,2},{5,3},{6,0},{7,1},{8,14},{9,15},{10,... | collective-permute-start | bytes 786440 | tf_op jit(solution)/shard_map/ppermute | solution.py:17
  54.8 14.6 %collective-permute-start.9 = (bf16[64,2048]{1,0:T(8,128)(2,1)S(1)}, bf16[64,2048]{1,0:T(8,128)(2,1)S(1)}, u32[]{:S(2)}, u32[]{:S(2)}) collective-permute-start(bf16[64,2048]{1,0:T(8,128)(2,1)S(1)} %get-tuple-element.57), channel_id=1, source_target_pairs={{0,2},{1,3},{2,0},{3,1},{4,6},{5,7},{6,4},{7,5},{8,10},{9,11},{10,... | collective-permute-start | bytes 786440 | tf_op jit(solution)/shard_map/ppermute | solution.py:17
  63.7 7.3 %collective-permute-start.7 = (bf16[128,2048]{1,0:T(8,128)(2,1)S(1)}, bf16[128,2048]{1,0:T(8,128)(2,1)S(1)}, u32[]{:S(2)}, u32[]{:S(2)}) collective-permute-start(bf16[128,2048]{1,0:T(8,128)(2,1)S(1)} %get-tuple-element.63), channel_id=1, source_target_pairs={{0,1},{1,0},{2,3},{3,2},{4,5},{5,4},{6,7},{7,6},{8,9},{9,8},{10,11... | collective-permute-start | bytes 1572872 | tf_op jit(solution)/shard_map/ppermute | solution.py:17
  63.8 9.2 %collective-permute-start.13 = (bf16[64,2048]{1,0:T(8,128)(2,1)S(1)}, bf16[64,2048]{1,0:T(8,128)(2,1)S(1)}, u32[]{:S(2)}, u32[]{:S(2)}) collective-permute-start(bf16[64,2048]{1,0:T(8,128)(2,1)S(1)} %get-tuple-element.58), channel_id=1, source_target_pairs={{0,4},{1,5},{2,6},{3,7},{4,0},{5,1},{6,2},{7,3},{8,12},{9,13},{10,... | collective-permute-start | bytes 786440 | tf_op jit(solution)/shard_map/ppermute | solution.py:17
  64.0 19.5 %collective-permute-start.14 = (bf16[64,2048]{1,0:T(8,128)(2,1)S(1)}, bf16[64,2048]{1,0:T(8,128)(2,1)S(1)}, u32[]{:S(2)}, u32[]{:S(2)}) collective-permute-start(bf16[64,2048]{1,0:T(8,128)(2,1)S(1)} %get-tuple-element.59), channel_id=1, source_target_pairs={{0,6},{1,7},{2,4},{3,5},{4,2},{5,3},{6,0},{7,1},{8,14},{9,15},{10,... | collective-permute-start | bytes 786440 | tf_op jit(solution)/shard_map/ppermute | solution.py:17
  69.6 13.9 %collective-permute-start.12 = (bf16[64,2048]{1,0:T(8,128)(2,1)S(1)}, bf16[64,2048]{1,0:T(8,128)(2,1)S(1)}, u32[]{:S(2)}, u32[]{:S(2)}) collective-permute-start(bf16[64,2048]{1,0:T(8,128)(2,1)S(1)} %add_convert_fusion), channel_id=1, source_target_pairs={{0,8},{1,9},{2,10},{3,11},{4,12},{5,13},{6,14},{7,15},{8,0},{9,1},... | collective-permute-start | bytes 786440 | tf_op jit(solution)/shard_map/ppermute | solution.py:17
  71.0 13.2 %collective-permute-start.8 = (bf16[64,2048]{1,0:T(8,128)(2,1)S(1)}, bf16[64,2048]{1,0:T(8,128)(2,1)S(1)}, u32[]{:S(2)}, u32[]{:S(2)}) collective-permute-start(bf16[64,2048]{1,0:T(8,128)(2,1)S(1)} %add_convert_fusion.1), channel_id=1, source_target_pairs={{0,2},{1,3},{2,0},{3,1},{4,6},{5,7},{6,4},{7,5},{8,10},{9,11},{10,... | collective-permute-start | bytes 786440 | tf_op jit(solution)/shard_map/ppermute | solution.py:17

commit v20 on v19

--- a/solution.py
+++ b/solution.py
@@ -238,17 +238,20 @@
 
 
 def payloads_kernel(*refs):
-    ins, (far_0, far_1, across, near_0, near_1, mine_1) = refs[:9], refs[9:]
-    half = across.shape[0]
+    ins, (turn_0, turn_1, far_1, near_0, near_1, mine_1) = refs[:9], refs[9:]
+    half = turn_0.shape[0]
 
     def summed(block, own):
         mine, other, core = ins[3 * block:3 * block + 3]
         rows = slice(0, half) if own else slice(half, 2 * half)
         return (mine if own else other)[...] + core[rows, :].astype(jnp.float32)
 
-    far_0[...] = summed(0, True).astype(jnp.bfloat16)
+    far_0 = summed(0, True).astype(jnp.bfloat16)
+    across = summed(1, False).astype(jnp.bfloat16)
+    first = lax.axis_index("ka") & 1 == 0
+    turn_0[...] = jnp.where(first, across, far_0)
+    turn_1[...] = jnp.where(first, far_0, across)
     far_1[...] = summed(0, False).astype(jnp.bfloat16)
-    across[...] = summed(1, False).astype(jnp.bfloat16)
     near_0[...] = summed(2, True).astype(jnp.bfloat16)
     near_1[...] = summed(2, False).astype(jnp.bfloat16)
     mine_1[...] = summed(1, True)
@@ -337,11 +340,13 @@
         *step_0[:2], core_0, *step_1[:2], core_1, *step_2[:2], core_2
     )
     step_3 = rows(3, sends)
-    far = over(sends[0], 4), over(sends[1], 6)
-    across_1 = over(sends[2], 2)
+    arrived = [
+        permute(sends[turn], lambda i: i ^ (2 if i % 2 == turn else 4)) for turn in range(2)
+    ]
+    arrived.append(over(sends[2], 6))
     near = over(sends[3], 4), over(sends[4], 6)
     mine_1, _ = lax.optimization_barrier((mine_1, step_3[0]))
-    pair = over(total_of(mine_1, across_1, *far), 8)
+    pair = over(total_of(mine_1, *arrived), 8)
     mine_3, other_3, core_3 = step_3
     across_3 = over(other_3 + core_3[half:].astype(jnp.float32), 2)
     return closed(modes, norm_factor, mine_3, core_3, across_3, pair, *near)

time: 85.6 us -> 86.3 us (level)
  waiting for transfers between devices: 25.1 us -> 27.7 us
  starting transfers between devices: 14.5 us -> 12.3 us
    ppermute x15, waiting for transfers between devices: 25.1 us -> 27.7 us  [permute(): lax.ppermute(x, 'ka', [(i, j % size) for i, j in pairs if j is not None])]
    ppermute x15, starting transfers between devices: 14.5 us -> 12.3 us  [permute(): lax.ppermute(x, 'ka', [(i, j % size) for i, j in pairs if j is not None])]
  transfers between devices with their start and end apart: 15 -> 15, of which waited for: 7 -> 6; matrix products, arithmetic and copies ran while one was open for 0% -> 0% of each run, Pallas kernels for 48% -> 48%
where the time goes in v20:
time: 86.3 us; the launch traced here: 85.9 us
  Pallas kernels  45.4 us (53%)
  waiting for transfers between devices  27.7 us (32%)
  starting transfers between devices  12.3 us (14%)
    ppermute x15, waiting for transfers between devices, permute(): lax.ppermute(x, 'ka', [(i, j % size) for i, j in pairs if j is not None])  27.7 us
    pallas_call x4, Pallas kernels, rows_of(): pl.pallas_call(rows_kernel, out_shape=[jax.ShapeDtypeStruct((width // 4,...  23.9 us
    pallas_call x1, Pallas kernels, products_of(): pl.pallas_call(products_kernel, out_shape=jax.ShapeDtypeStruct((k_local,...  13.4 us
    ppermute x15, starting transfers between devices, permute(): lax.ppermute(x, 'ka', [(i, j % size) for i, j in pairs if j is not None])  12.3 us
    pallas_call x2, Pallas kernels, turned_pieces(): pl.pallas_call(functools.partial(turn_kernel, first), out_shape=[jax.Shap...  6.69 us
  transfers between devices with their start and end apart: 15, of which 6 were waited for; matrix products, arithmetic and copies ran while one was open for 0% of the time, Pallas kernels for 48%

profile of v20, /device:TPU:0, one launch (start us, length us, event | category | flops | bytes accessed | tf_op | source)
XLA Modules:
  0.0 85.9 jit_solution(12814707720828428034)
XLA Ops:
  0.0 0.0 copy-start
  0.0 2.5 %shard_map.56 = bf16[2,256,1024]{2,1,0:T(8,128)(2,1)} custom-call(bf16[2,1024,1024]{2,1,0:T(8,128)(2,1)} %bitcast.8), custom_call_target="tpu_custom_call" | custom-call | bytes 2097152 | tf_op jit(solution)/shard_map/pallas_call | solution.py:137
  2.5 5.5 %collective-permute-start = (bf16[2,256,1024]{2,1,0:T(8,128)(2,1)}, bf16[2,256,1024]{2,1,0:T(8,128)(2,1)}, u32[]{:S(2)}, u32[]{:S(2)}) collective-permute-start(bf16[2,256,1024]{2,1,0:T(8,128)(2,1)} %shard_map.56), channel_id=1, source_target_pairs={{0,15},{1,0},{2,1},{3,2},{4,3},{5,4},{6,5},{7,6},{8,7},{9,8},{10,9... | collective-permute-start | bytes 3145736 | tf_op jit(solution)/shard_map/ppermute | solution.py:17
  8.0 4.2 %shard_map.58 = (bf16[2,256,1024]{2,1,0:T(8,128)(2,1)}, bf16[2,256,1024]{2,1,0:T(8,128)(2,1)}, bf16[2,256,1024]{2,1,0:T(8,128)(2,1)}) custom-call(bf16[2,1024,1024]{2,1,0:T(8,128)(2,1)} %bitcast.9), custom_call_target="tpu_custom_call" | custom-call | bytes 6291456 | tf_op jit(solution)/shard_map/pallas_call | solution.py:137
  12.2 0.7 collective-permute-start.2
  12.9 0.1 collective-permute-start.4
  13.0 0.6 collective-permute-start.6
  13.6 0.0 copy-done
  13.6 0.1 add_add_fusion.3
  13.7 13.4 %shard_map.55 = bf16[2,2,32,32,1024]{4,3,2,1,0:T(8,128)(2,1)} custom-call(s32[2,2]{1,0:T(2,128)} %first_ref.1, bf16[2,32,32,1024]{3,2,1,0:T(8,128)(2,1)} %coeffs_ref.1, bf16[2,2,32,32]{3,2,1,0:T(8,128)(2,1)} %cond_ref.1, bf16[2,2,32,32]{3,2,1,0:T(8,128)(2,1)} %val_ref.1), custom_call_target="tpu_custom_call" | custom-call | flops 6442450944 | bytes 12582912 | tf_op jit(solution)/shard_map/pallas_call | solution.py:90
  27.0 0.1 add_add_fusion.2
  27.1 0.0 collective-permute-done.next_ref
  27.1 7.5 %shard_map.57 = (f32[64,2048]{1,0:T(8,128)S(1)}, f32[64,2048]{1,0:T(8,128)S(1)}, bf16[128,2048]{1,0:T(8,128)(2,1)S(1)}) custom-call(s32[5]{0:T(128)S(1)} %get-tuple-element.36.pick_ref, bf16[2,1024,1024]{2,1,0:T(8,128)(2,1)} %bitcast.10, bf16[2,256,1024]{2,1,0:T(8,128)(2,1)} %collective-permute-done.next_ref, bf16[2,2,1024,1024]{3,2,1,0:T(8,128)(2,1)} %bitcast.14), custom_call_target="tpu_custom_call" | custom-call | flops 2147483648 | bytes 8388608 | tf_op jit(solution)/shard_map/pallas_call | solution.py:212
  34.6 0.0 collective-permute-done.2.next_ref
  34.6 5.5 %shard_map.59 = (f32[64,2048]{1,0:T(8,128)S(1)}, f32[64,2048]{1,0:T(8,128)S(1)}, bf16[128,2048]{1,0:T(8,128)(2,1)S(1)}) custom-call(s32[5]{0:T(128)S(1)} %get-tuple-element.40.pick_ref, bf16[2,1024,1024]{2,1,0:T(8,128)(2,1)} %bitcast.11, bf16[2,256,1024]{2,1,0:T(8,128)(2,1)S(1)} %collective-permute-done.2.next_ref, bf16[2,2,1024,1024]{3,2,1,0:T(8,128)(2,1)} %bitcast.15), custom_call_target="tpu_custom_call" | custom-call | flops 2147483648 | bytes 8388608 | tf_op jit(solution)/shard_map/pallas_call | solution.py:212
  40.1 2.9 %collective-permute-done.4.next_ref = bf16[2,256,1024]{2,1,0:T(8,128)(2,1)S(1)} collective-permute-done((bf16[2,256,1024]{2,1,0:T(8,128)(2,1)}, bf16[2,256,1024]{2,1,0:T(8,128)(2,1)S(1)}, u32[]{:S(2)}, u32[]{:S(2)}) %collective-permute-start.4) | collective-permute-done | bytes 1048608 | tf_op jit(solution)/shard_map/ppermute | solution.py:17
  43.1 5.5 %shard_map.60 = (f32[64,2048]{1,0:T(8,128)S(1)}, f32[64,2048]{1,0:T(8,128)S(1)}, bf16[128,2048]{1,0:T(8,128)(2,1)S(1)}) custom-call(s32[5]{0:T(128)S(1)} %get-tuple-element.45.pick_ref, bf16[2,1024,1024]{2,1,0:T(8,128)(2,1)} %bitcast.12, bf16[2,256,1024]{2,1,0:T(8,128)(2,1)S(1)} %collective-permute-done.4.next_ref, bf16[2,2,1024,1024]{3,2,1,0:T(8,128)(2,1)} %bitcast.16), custom_call_target="tpu_custom_call" | custom-call | flops 2147483648 | bytes 8388608 | tf_op jit(solution)/shard_map/pallas_call | solution.py:212
  48.6 0.1 collective-permute-start.5
  48.6 0.5 collective-permute-start.3
  49.1 0.1 collective-permute-start.1
  49.2 5.2 %collective-permute-done.6.next_ref = bf16[2,256,1024]{2,1,0:T(8,128)(2,1)S(1)} collective-permute-done((bf16[2,256,1024]{2,1,0:T(8,128)(2,1)}, bf16[2,256,1024]{2,1,0:T(8,128)(2,1)S(1)}, u32[]{:S(2)}, u32[]{:S(2)}) %collective-permute-start.6) | collective-permute-done | bytes 1048608 | tf_op jit(solution)/shard_map/ppermute | solution.py:17
  54.4 0.0 collective-permute-done.5.refs_8_
  54.4 0.0 collective-permute-done.3.refs_5_
  54.4 0.0 collective-permute-done.1.refs_2_
  54.4 0.3 shard_map.61
  54.7 0.1 collective-permute-start.9
  54.8 0.1 collective-permute-start.10
  54.8 3.4 %collective-permute-start.11 = (bf16[64,2048]{1,0:T(8,128)(2,1)S(1)}, bf16[64,2048]{1,0:T(8,128)(2,1)S(1)}, u32[]{:S(2)}, u32[]{:S(2)}) collective-permute-start(bf16[64,2048]{1,0:T(8,128)(2,1)S(1)} %get-tuple-element.57), channel_id=1, source_target_pairs={{0,6},{1,7},{2,4},{3,5},{4,2},{5,3},{6,0},{7,1},{8,14},{9,15},{10,... | collective-permute-start | bytes 786440 | tf_op jit(solution)/shard_map/ppermute | solution.py:17
  58.2 5.5 %shard_map.62 = (f32[64,2048]{1,0:T(8,128)S(1)}, f32[64,2048]{1,0:T(8,128)S(1)}, bf16[128,2048]{1,0:T(8,128)(2,1)S(1)}) custom-call(s32[5]{0:T(128)S(1)} %get-tuple-element.60.pick_ref, bf16[2,1024,1024]{2,1,0:T(8,128)(2,1)} %bitcast.13, bf16[2,256,1024]{2,1,0:T(8,128)(2,1)S(1)} %collective-permute-done.6.next_ref, bf16[2,2,1024,1024]{3,2,1,0:T(8,128)(2,1)} %bitcast.17), custom_call_target="tpu_custom_call" | custom-call | flops 2147483648 | bytes 8388608 | tf_op jit(solution)/shard_map/pallas_call | solution.py:212
  63.7 0.1 collective-permute-start.7
  63.8 0.1 collective-permute-start.13
  63.9 2.9 %collective-permute-done.9 = bf16[64,2048]{1,0:T(8,128)(2,1)S(1)} collective-permute-done((bf16[64,2048]{1,0:T(8,128)(2,1)S(1)}, bf16[64,2048]{1,0:T(8,128)(2,1)S(1)}, u32[]{:S(2)}, u32[]{:S(2)}) %collective-permute-start.9) | collective-permute-done | bytes 262176 | tf_op jit(solution)/shard_map/ppermute | solution.py:17
  66.8 0.0 collective-permute-start.14
  66.8 0.0 collective-permute-done.10
  66.8 2.8 %collective-permute-done.11 = bf16[64,2048]{1,0:T(8,128)(2,1)S(1)} collective-permute-done((bf16[64,2048]{1,0:T(8,128)(2,1)S(1)}, bf16[64,2048]{1,0:T(8,128)(2,1)S(1)}, u32[]{:S(2)}, u32[]{:S(2)}) %collective-permute-start.11) | collective-permute-done | bytes 262176 | tf_op jit(solution)/shard_map/ppermute | solution.py:17
  69.6 0.1 add_convert_fusion
  69.7 0.1 collective-permute-start.12
  69.8 0.0 collective-permute-done.7.core_ref
  69.8 1.1 %collective-permute-start.8 = (bf16[64,2048]{1,0:T(8,128)(2,1)S(1)}, bf16[64,2048]{1,0:T(8,128)(2,1)S(1)}, u32[]{:S(2)}, u32[]{:S(2)}) collective-permute-start(bf16[64,2048]{1,0:T(8,128)(2,1)S(1)} %add_convert_fusion.1), channel_id=1, source_target_pairs={{0,2},{1,3},{2,0},{3,1},{4,6},{5,7},{6,4},{7,5},{8,10},{9,11},{10,... | collective-permute-start | bytes 786440 | tf_op jit(solution)/shard_map/ppermute | solution.py:17
  70.9 7.7 %collective-permute-done.13.refs_2_ = bf16[64,2048]{1,0:T(8,128)(2,1)S(1)} collective-permute-done((bf16[64,2048]{1,0:T(8,128)(2,1)S(1)}, bf16[64,2048]{1,0:T(8,128)(2,1)S(1)}, u32[]{:S(2)}, u32[]{:S(2)}) %collective-permute-start.13) | collective-permute-done | bytes 262176 | tf_op jit(solution)/shard_map/ppermute | solution.py:17
  78.6 6.3 %collective-permute-done.14.refs_3_ = bf16[64,2048]{1,0:T(8,128)(2,1)S(1)} collective-permute-done((bf16[64,2048]{1,0:T(8,128)(2,1)S(1)}, bf16[64,2048]{1,0:T(8,128)(2,1)S(1)}, u32[]{:S(2)}, u32[]{:S(2)}) %collective-permute-start.14) | collective-permute-done | bytes 262176 | tf_op jit(solution)/shard_map/ppermute | solution.py:17
  84.9 0.0 collective-permute-done.12.refs_1_
  84.9 0.0 collective-permute-done.8.refs_0_
  84.9 1.1 %shard_map.63 = f32[64,2,1024]{2,1,0:T(2,128)} custom-call(f32[64,2048]{1,0:T(8,128)S(1)} %get-tuple-element.62.mine_ref, bf16[128,2048]{1,0:T(8,128)(2,1)S(1)} %collective-permute-done.7.core_ref, bf16[64,2048]{1,0:T(8,128)(2,1)S(1)} %collective-permute-done.8.refs_0_, bf16[64,2048]{1,0:T(8,128)(2,1)S(1)} %collective-permute-done.12.refs_1_, ...), custom_call_target="tpu_custom_call" | custom-call | flops 655360 | bytes 2097152 | tf_op jit(solution)/shard_map/pallas_call | solution.py:288
  (2 shorter events, 0.1 us)
Async XLA Ops:
  0.0 13.6 %copy-start = (s32[2]{0:T(128)S(1)}, s32[2]{0:T(128)}, u32[]{:S(2)}) copy-start(s32[2]{0:T(128)} %param.8) | copy-start | bytes 28
  2.5 24.6 %collective-permute-start = (bf16[2,256,1024]{2,1,0:T(8,128)(2,1)}, bf16[2,256,1024]{2,1,0:T(8,128)(2,1)}, u32[]{:S(2)}, u32[]{:S(2)}) collective-permute-start(bf16[2,256,1024]{2,1,0:T(8,128)(2,1)} %shard_map.56), channel_id=1, source_target_pairs={{0,15},{1,0},{2,1},{3,2},{4,3},{5,4},{6,5},{7,6},{8,7},{9,8},{10,9... | collective-permute-start | bytes 3145736 | tf_op jit(solution)/shard_map/ppermute | solution.py:17
  12.2 22.4 %collective-permute-start.2 = (bf16[2,256,1024]{2,1,0:T(8,128)(2,1)}, bf16[2,256,1024]{2,1,0:T(8,128)(2,1)S(1)}, u32[]{:S(2)}, u32[]{:S(2)}) collective-permute-start(bf16[2,256,1024]{2,1,0:T(8,128)(2,1)} %get-tuple-element.42), channel_id=1, source_target_pairs={{0,15},{1,0},{2,1},{3,2},{4,3},{5,4},{6,5},{7,6},{8,7},{9,8},{10,9... | collective-permute-start | bytes 3145736 | tf_op jit(solution)/shard_map/ppermute | solution.py:17
  12.9 30.2 %collective-permute-start.4 = (bf16[2,256,1024]{2,1,0:T(8,128)(2,1)}, bf16[2,256,1024]{2,1,0:T(8,128)(2,1)S(1)}, u32[]{:S(2)}, u32[]{:S(2)}) collective-permute-start(bf16[2,256,1024]{2,1,0:T(8,128)(2,1)} %get-tuple-element.46), channel_id=1, source_target_pairs={{0,15},{1,0},{2,1},{3,2},{4,3},{5,4},{6,5},{7,6},{8,7},{9,8},{10,9... | collective-permute-start | bytes 3145736 | tf_op jit(solution)/shard_map/ppermute | solution.py:17
  13.0 41.4 %collective-permute-start.6 = (bf16[2,256,1024]{2,1,0:T(8,128)(2,1)}, bf16[2,256,1024]{2,1,0:T(8,128)(2,1)S(1)}, u32[]{:S(2)}, u32[]{:S(2)}) collective-permute-start(bf16[2,256,1024]{2,1,0:T(8,128)(2,1)} %get-tuple-element.48), channel_id=1, source_target_pairs={{0,15},{1,0},{2,1},{3,2},{4,3},{5,4},{6,5},{7,6},{8,7},{9,8},{10,9... | collective-permute-start | bytes 3145736 | tf_op jit(solution)/shard_map/ppermute | solution.py:17
  48.6 5.8 %collective-permute-start.5 = (bf16[128,2048]{1,0:T(8,128)(2,1)S(1)}, bf16[128,2048]{1,0:T(8,128)(2,1)S(1)}, u32[]{:S(2)}, u32[]{:S(2)}) collective-permute-start(bf16[128,2048]{1,0:T(8,128)(2,1)S(1)} %get-tuple-element.47), channel_id=1, source_target_pairs={{0,1},{1,0},{2,3},{3,2},{4,5},{5,4},{6,7},{7,6},{8,9},{9,8},{10,11... | collective-permute-start | bytes 1572872 | tf_op jit(solution)/shard_map/ppermute | solution.py:17
  48.6 5.7 %collective-permute-start.3 = (bf16[128,2048]{1,0:T(8,128)(2,1)S(1)}, bf16[128,2048]{1,0:T(8,128)(2,1)S(1)}, u32[]{:S(2)}, u32[]{:S(2)}) collective-permute-start(bf16[128,2048]{1,0:T(8,128)(2,1)S(1)} %get-tuple-element.43), channel_id=1, source_target_pairs={{0,1},{1,0},{2,3},{3,2},{4,5},{5,4},{6,7},{7,6},{8,9},{9,8},{10,11... | collective-permute-start | bytes 1572872 | tf_op jit(solution)/shard_map/ppermute | solution.py:17
  49.1 5.2 %collective-permute-start.1 = (bf16[128,2048]{1,0:T(8,128)(2,1)S(1)}, bf16[128,2048]{1,0:T(8,128)(2,1)S(1)}, u32[]{:S(2)}, u32[]{:S(2)}) collective-permute-start(bf16[128,2048]{1,0:T(8,128)(2,1)S(1)} %get-tuple-element.39), channel_id=1, source_target_pairs={{0,1},{1,0},{2,3},{3,2},{4,5},{5,4},{6,7},{7,6},{8,9},{9,8},{10,11... | collective-permute-start | bytes 1572872 | tf_op jit(solution)/shard_map/ppermute | solution.py:17
  54.7 12.1 %collective-permute-start.9 = (bf16[64,2048]{1,0:T(8,128)(2,1)S(1)}, bf16[64,2048]{1,0:T(8,128)(2,1)S(1)}, u32[]{:S(2)}, u32[]{:S(2)}) collective-permute-start(bf16[64,2048]{1,0:T(8,128)(2,1)S(1)} %get-tuple-element.55), channel_id=1, source_target_pairs={{0,2},{1,5},{2,0},{3,7},{4,6},{5,1},{6,4},{7,3},{8,10},{9,13},{10,... | collective-permute-start | bytes 786440 | tf_op jit(solution)/shard_map/ppermute | solution.py:17
  54.8 12.0 %collective-permute-start.10 = (bf16[64,2048]{1,0:T(8,128)(2,1)S(1)}, bf16[64,2048]{1,0:T(8,128)(2,1)S(1)}, u32[]{:S(2)}, u32[]{:S(2)}) collective-permute-start(bf16[64,2048]{1,0:T(8,128)(2,1)S(1)} %get-tuple-element.56), channel_id=1, source_target_pairs={{0,4},{1,3},{2,6},{3,1},{4,0},{5,7},{6,2},{7,5},{8,12},{9,11},{10,... | collective-permute-start | bytes 786440 | tf_op jit(solution)/shard_map/ppermute | solution.py:17
  54.8 14.7 %collective-permute-start.11 = (bf16[64,2048]{1,0:T(8,128)(2,1)S(1)}, bf16[64,2048]{1,0:T(8,128)(2,1)S(1)}, u32[]{:S(2)}, u32[]{:S(2)}) collective-permute-start(bf16[64,2048]{1,0:T(8,128)(2,1)S(1)} %get-tuple-element.57), channel_id=1, source_target_pairs={{0,6},{1,7},{2,4},{3,5},{4,2},{5,3},{6,0},{7,1},{8,14},{9,15},{10,... | collective-permute-start | bytes 786440 | tf_op jit(solution)/shard_map/ppermute | solution.py:17
  63.7 6.1 %collective-permute-start.7 = (bf16[128,2048]{1,0:T(8,128)(2,1)S(1)}, bf16[128,2048]{1,0:T(8,128)(2,1)S(1)}, u32[]{:S(2)}, u32[]{:S(2)}) collective-permute-start(bf16[128,2048]{1,0:T(8,128)(2,1)S(1)} %get-tuple-element.63), channel_id=1, source_target_pairs={{0,1},{1,0},{2,3},{3,2},{4,5},{5,4},{6,7},{7,6},{8,9},{9,8},{10,11... | collective-permute-start | bytes 1572872 | tf_op jit(solution)/shard_map/ppermute | solution.py:17
  63.8 14.8 %collective-permute-start.13 = (bf16[64,2048]{1,0:T(8,128)(2,1)S(1)}, bf16[64,2048]{1,0:T(8,128)(2,1)S(1)}, u32[]{:S(2)}, u32[]{:S(2)}) collective-permute-start(bf16[64,2048]{1,0:T(8,128)(2,1)S(1)} %get-tuple-element.58), channel_id=1, source_target_pairs={{0,4},{1,5},{2,6},{3,7},{4,0},{5,1},{6,2},{7,3},{8,12},{9,13},{10,... | collective-permute-start | bytes 786440 | tf_op jit(solution)/shard_map/ppermute | solution.py:17
  66.8 18.1 %collective-permute-start.14 = (bf16[64,2048]{1,0:T(8,128)(2,1)S(1)}, bf16[64,2048]{1,0:T(8,128)(2,1)S(1)}, u32[]{:S(2)}, u32[]{:S(2)}) collective-permute-start(bf16[64,2048]{1,0:T(8,128)(2,1)S(1)} %get-tuple-element.59), channel_id=1, source_target_pairs={{0,6},{1,7},{2,4},{3,5},{4,2},{5,3},{6,0},{7,1},{8,14},{9,15},{10,... | collective-permute-start | bytes 786440 | tf_op jit(solution)/shard_map/ppermute | solution.py:17
  69.7 15.2 %collective-permute-start.12 = (bf16[64,2048]{1,0:T(8,128)(2,1)S(1)}, bf16[64,2048]{1,0:T(8,128)(2,1)S(1)}, u32[]{:S(2)}, u32[]{:S(2)}) collective-permute-start(bf16[64,2048]{1,0:T(8,128)(2,1)S(1)} %add_convert_fusion), channel_id=1, source_target_pairs={{0,8},{1,9},{2,10},{3,11},{4,12},{5,13},{6,14},{7,15},{8,0},{9,1},... | collective-permute-start | bytes 786440 | tf_op jit(solution)/shard_map/ppermute | solution.py:17
  69.8 15.1 %collective-permute-start.8 = (bf16[64,2048]{1,0:T(8,128)(2,1)S(1)}, bf16[64,2048]{1,0:T(8,128)(2,1)S(1)}, u32[]{:S(2)}, u32[]{:S(2)}) collective-permute-start(bf16[64,2048]{1,0:T(8,128)(2,1)S(1)} %add_convert_fusion.1), channel_id=1, source_target_pairs={{0,2},{1,3},{2,0},{3,1},{4,6},{5,7},{6,4},{7,5},{8,10},{9,11},{10,... | collective-permute-start | bytes 786440 | tf_op jit(solution)/shard_map/ppermute | solution.py:17

commit v21 on v19

--- a/solution.py
+++ b/solution.py
@@ -111,14 +111,52 @@
     )(band_first, coeffs, g_cond, g_val)
 
 
-def turn_kernel(first, coeffs_ref, *refs):
+def columns_of(step, width):
+    size = lax.axis_size("ka")
+    behind_z = lax.shift_right_logical(lax.rem(lax.axis_index("ka") + size - 1, size), 2)
+    return pl.ds(pl.multiple_of((behind_z ^ (3 - step)) * width, width), width)
+
+
+def cut_kernel(coeffs_ref, out_ref, sems):
+    k_local, parts = sems.shape
+    _, depth, width = out_ref.shape
+    columns, count = columns_of(0, width), depth // parts
+    copies = []
+    for k in range(k_local):
+        for p in range(parts):
+            rows = pl.ds(p * count, count)
+            copies.append(
+                pltpu.make_async_copy(
+                    coeffs_ref.at[k, rows, columns], out_ref.at[k, rows], sems.at[k, p]
+                )
+            )
+    for copy in copies:
+        copy.start()
+    for copy in copies:
+        copy.wait()
+
+
+def cut_piece(flat, width):
+    k_local, depth, _ = flat.shape
+    return pl.pallas_call(
+        cut_kernel,
+        out_shape=jax.ShapeDtypeStruct((k_local, depth, width), jnp.bfloat16),
+        in_specs=[pl.BlockSpec(memory_space=pl.ANY)],
+        out_specs=pl.BlockSpec(memory_space=pl.ANY),
+        scratch_shapes=[pltpu.SemaphoreType.DMA((k_local, 4))],
+        compiler_params=pltpu.CompilerParams(vmem_limit_bytes=60 * MIB),
+        cost_estimate=pl.CostEstimate(
+            flops=0, bytes_accessed=4 * k_local * depth * width, transcendentals=0
+        ),
+    )(flat)
+
+
+def turn_kernel(coeffs_ref, *refs):
     *out_refs, held, sems = refs
     pieces, k_local, parts, rows, width = held.shape
-    size = lax.axis_size("ka")
-    behind_z = lax.shift_right_logical(lax.rem(lax.axis_index("ka") + size - 1, size), 2)
 
     def copy(i, k, p):
-        columns = pl.ds(pl.multiple_of((behind_z ^ (3 - first - i)) * width, width), width)
+        columns = columns_of(1 + i, width)
         source = coeffs_ref.at[k, pl.ds(p * rows, rows), columns]
         return pltpu.make_async_copy(source, held.at[i, k, p], sems.at[i, k, p])
 
@@ -131,11 +169,11 @@
         out_refs[i][k, :, p * rows:(p + 1) * rows] = held[i, k, p].T
 
 
-def turned_pieces(flat, first, pieces, width):
+def turned_pieces(flat, pieces, width):
     k_local, depth, _ = flat.shape
     parts = 2
     return pl.pallas_call(
-        functools.partial(turn_kernel, first),
+        turn_kernel,
         out_shape=[jax.ShapeDtypeStruct((k_local, width, depth), jnp.bfloat16)] * pieces,
         in_specs=[pl.BlockSpec(memory_space=pl.ANY)],
         out_specs=[pl.BlockSpec(memory_space=pltpu.VMEM)] * pieces,
@@ -150,7 +188,7 @@
     )(flat)
 
 
-def rows_kernel(pick_ref, own_ref, next_ref, right_ref, mine_ref, other_ref, send_ref, *refs):
+def rows_kernel(turned, pick_ref, own_ref, next_ref, right_ref, mine_ref, other_ref, send_ref, *refs):
     own_held, next_held, held, left, own_sems, next_sems, sems = refs
     k_local, depth, width = own_held.shape
     tiles, _, _, tile = held.shape
@@ -187,7 +225,7 @@
 
         @pl.when(jnp.logical_not(near[k]))
         def _():
-            left[:, k * depth:(k + 1) * depth] = next_held[k]
+            left[:, k * depth:(k + 1) * depth] = next_held[k] if turned else next_held[k].T
 
     for t in range(tiles):
         for k in range(k_local):
@@ -204,13 +242,14 @@
         send_ref[width // 4:, place] = jnp.where(core == 0, other[1], other[0]).astype(jnp.bfloat16)
 
 
-def rows_of(pick, own, following, products):
-    k_local, width, depth = following.shape
+def rows_of(pick, own, following, products, turned):
+    k_local, depth = own.shape[:2]
+    width = following.shape[1 if turned else 2]
     modes, excitons = products.shape[1], products.shape[3]
     columns, tile = modes * excitons, 512
     tiles = columns // tile
     return pl.pallas_call(
-        rows_kernel,
+        functools.partial(rows_kernel, turned),
         out_shape=[
             jax.ShapeDtypeStruct((width // 4, columns), jnp.float32),
             jax.ShapeDtypeStruct((width // 4, columns), jnp.float32),
@@ -221,7 +260,7 @@
         out_specs=[pl.BlockSpec(memory_space=pltpu.VMEM)] * 3,
         scratch_shapes=[
             pltpu.VMEM((k_local, depth, width), jnp.bfloat16),
-            pltpu.VMEM((k_local, width, depth), jnp.bfloat16),
+            pltpu.VMEM(following.shape, jnp.bfloat16),
             pltpu.VMEM((tiles, k_local, depth, tile), jnp.bfloat16),
             pltpu.VMEM((width, k_local * depth), jnp.bfloat16),
             pltpu.SemaphoreType.DMA((k_local,)),
@@ -303,9 +342,9 @@
     core, x, z = me & 1, me >> 1 & 1, me >> 2
     flat = coeffs.reshape(k_local, bands_c * bands_v, excitons)
 
-    pieces = turned_pieces(flat, 0, 1, width)
+    pieces = [cut_piece(flat, width)]
     rest, _ = lax.optimization_barrier((flat, pieces))
-    pieces += turned_pieces(rest, 1, 3, width)
+    pieces += turned_pieces(rest, 3, width)
     following = [permute(piece, lambda i: i - 1) for piece in pieces]
     products = products_of(coeffs, g_cond, g_val, band_first)
     products = products.reshape(k_local, modes, bands_c * bands_v, excitons)
@@ -314,7 +353,7 @@
     def rows(step, after):
         pick = jnp.concatenate((places, jnp.stack((z ^ (3 - step), core, x))))
         pick, _ = lax.optimization_barrier((pick, after))
-        mine, other, send = rows_of(pick, flat, following[step], products)
+        mine, other, send = rows_of(pick, flat, following[step], products, step > 0)
         return mine, other, permute(send, lambda i: i ^ 1)
 
     half = width // 4

time: 85.6 us -> 116 us (1.36)
  Pallas kernels: 45.1 us -> 75.7 us
    pallas_call x6, Pallas kernels: 30.4 us -> 61.1 us  [the longest x1 32.9 us: cut_piece(): pl.pallas_call(cut_kernel, out_shape=jax.ShapeDtypeStruct((k_local, depth...]
  transfers between devices with their start and end apart: 15 -> 15, of which waited for: 7 -> 7; matrix products, arithmetic and copies ran while one was open for 0% -> 0% of each run, Pallas kernels for 48% -> 36%
where the time goes in v21:
time: 116 us
  Pallas kernels  75.7 us (65%)
  waiting for transfers between devices  25 us (22%)
  starting transfers between devices  14.5 us (12%)
    pallas_call x1, Pallas kernels, cut_piece(): pl.pallas_call(cut_kernel, out_shape=jax.ShapeDtypeStruct((k_local, depth...  32.9 us
    ppermute x15, waiting for transfers between devices, permute(): lax.ppermute(x, 'ka', [(i, j % size) for i, j in pairs if j is not None])  25 us
    pallas_call x4, Pallas kernels, rows_of(): pl.pallas_call(functools.partial(rows_kernel, turned), out_shape=[jax.Sha...  23.9 us
    ppermute x15, starting transfers between devices, permute(): lax.ppermute(x, 'ka', [(i, j % size) for i, j in pairs if j is not None])  14.5 us
    pallas_call x1, Pallas kernels, products_of(): pl.pallas_call(products_kernel, out_shape=jax.ShapeDtypeStruct((k_local,...  13.4 us
    pallas_call x1, Pallas kernels, turned_pieces(): pl.pallas_call(turn_kernel, out_shape=[jax.ShapeDtypeStruct((k_local, wid...  4.19 us
  transfers between devices with their start and end apart: 15, of which 7 were waited for; matrix products, arithmetic and copies ran while one was open for 0% of the time, Pallas kernels for 36%

profile of v21, /device:TPU:0, one launch (start us, length us, event | category | flops | bytes accessed | tf_op | source)
XLA Modules:
  0.0 115.7 jit_solution(15982985516384655358)
XLA Ops:
  0.0 0.0 copy-start
  0.0 32.9 %shard_map.56 = bf16[2,1024,256]{2,1,0:T(8,128)(2,1)} custom-call(bf16[2,1024,1024]{2,1,0:T(8,128)(2,1)} %bitcast.8), custom_call_target="tpu_custom_call" | custom-call | bytes 2097152 | tf_op jit(solution)/shard_map/pallas_call | solution.py:141
  32.9 5.5 %collective-permute-start = (bf16[2,1024,256]{2,1,0:T(8,128)(2,1)}, bf16[2,1024,256]{2,1,0:T(8,128)(2,1)}, u32[]{:S(2)}, u32[]{:S(2)}) collective-permute-start(bf16[2,1024,256]{2,1,0:T(8,128)(2,1)} %shard_map.56), channel_id=1, source_target_pairs={{0,15},{1,0},{2,1},{3,2},{4,3},{5,4},{6,5},{7,6},{8,7},{9,8},{10,9... | collective-permute-start | bytes 3145736 | tf_op jit(solution)/shard_map/ppermute | solution.py:17
  38.4 4.2 %shard_map.58 = (bf16[2,256,1024]{2,1,0:T(8,128)(2,1)}, bf16[2,256,1024]{2,1,0:T(8,128)(2,1)}, bf16[2,256,1024]{2,1,0:T(8,128)(2,1)}) custom-call(bf16[2,1024,1024]{2,1,0:T(8,128)(2,1)} %bitcast.9), custom_call_target="tpu_custom_call" | custom-call | bytes 6291456 | tf_op jit(solution)/shard_map/pallas_call | solution.py:175
  42.6 0.7 collective-permute-start.2
  43.3 0.1 collective-permute-start.4
  43.4 0.6 collective-permute-start.6
  44.0 0.0 copy-done
  44.0 0.1 add_add_fusion.3
  44.1 13.4 %shard_map.55 = bf16[2,2,32,32,1024]{4,3,2,1,0:T(8,128)(2,1)} custom-call(s32[2,2]{1,0:T(2,128)} %first_ref.1, bf16[2,32,32,1024]{3,2,1,0:T(8,128)(2,1)} %coeffs_ref.1, bf16[2,2,32,32]{3,2,1,0:T(8,128)(2,1)} %cond_ref.1, bf16[2,2,32,32]{3,2,1,0:T(8,128)(2,1)} %val_ref.1), custom_call_target="tpu_custom_call" | custom-call | flops 6442450944 | bytes 12582912 | tf_op jit(solution)/shard_map/pallas_call | solution.py:90
  57.5 0.1 add_add_fusion.2
  57.5 0.0 collective-permute-done.next_ref
  57.5 7.4 %shard_map.57 = (f32[64,2048]{1,0:T(8,128)S(1)}, f32[64,2048]{1,0:T(8,128)S(1)}, bf16[128,2048]{1,0:T(8,128)(2,1)S(1)}) custom-call(s32[5]{0:T(128)S(1)} %get-tuple-element.36.pick_ref, bf16[2,1024,1024]{2,1,0:T(8,128)(2,1)} %bitcast.10, bf16[2,1024,256]{2,1,0:T(8,128)(2,1)} %collective-permute-done.next_ref, bf16[2,2,1024,1024]{3,2,1,0:T(8,128)(2,1)} %bitcast.14), custom_call_target="tpu_custom_call" | custom-call | flops 2147483648 | bytes 8388608 | tf_op jit(solution)/shard_map/pallas_call | solution.py:251
  65.0 0.0 collective-permute-done.2.next_ref
  65.0 5.5 %shard_map.59 = (f32[64,2048]{1,0:T(8,128)S(1)}, f32[64,2048]{1,0:T(8,128)S(1)}, bf16[128,2048]{1,0:T(8,128)(2,1)S(1)}) custom-call(s32[5]{0:T(128)S(1)} %get-tuple-element.40.pick_ref, bf16[2,1024,1024]{2,1,0:T(8,128)(2,1)} %bitcast.11, bf16[2,256,1024]{2,1,0:T(8,128)(2,1)S(1)} %collective-permute-done.2.next_ref, bf16[2,2,1024,1024]{3,2,1,0:T(8,128)(2,1)} %bitcast.15), custom_call_target="tpu_custom_call" | custom-call | flops 2147483648 | bytes 8388608 | tf_op jit(solution)/shard_map/pallas_call | solution.py:251
  70.5 3.0 %collective-permute-done.4.next_ref = bf16[2,256,1024]{2,1,0:T(8,128)(2,1)S(1)} collective-permute-done((bf16[2,256,1024]{2,1,0:T(8,128)(2,1)}, bf16[2,256,1024]{2,1,0:T(8,128)(2,1)S(1)}, u32[]{:S(2)}, u32[]{:S(2)}) %collective-permute-start.4) | collective-permute-done | bytes 1048608 | tf_op jit(solution)/shard_map/ppermute | solution.py:17
  73.5 5.5 %shard_map.60 = (f32[64,2048]{1,0:T(8,128)S(1)}, f32[64,2048]{1,0:T(8,128)S(1)}, bf16[128,2048]{1,0:T(8,128)(2,1)S(1)}) custom-call(s32[5]{0:T(128)S(1)} %get-tuple-element.45.pick_ref, bf16[2,1024,1024]{2,1,0:T(8,128)(2,1)} %bitcast.12, bf16[2,256,1024]{2,1,0:T(8,128)(2,1)S(1)} %collective-permute-done.4.next_ref, bf16[2,2,1024,1024]{3,2,1,0:T(8,128)(2,1)} %bitcast.16), custom_call_target="tpu_custom_call" | custom-call | flops 2147483648 | bytes 8388608 | tf_op jit(solution)/shard_map/pallas_call | solution.py:251
  79.0 0.1 collective-permute-start.5
  79.1 0.5 collective-permute-start.3
  79.6 0.1 collective-permute-start.1
  79.7 5.2 %collective-permute-done.6.next_ref = bf16[2,256,1024]{2,1,0:T(8,128)(2,1)S(1)} collective-permute-done((bf16[2,256,1024]{2,1,0:T(8,128)(2,1)}, bf16[2,256,1024]{2,1,0:T(8,128)(2,1)S(1)}, u32[]{:S(2)}, u32[]{:S(2)}) %collective-permute-start.6) | collective-permute-done | bytes 1048608 | tf_op jit(solution)/shard_map/ppermute | solution.py:17
  84.8 0.0 collective-permute-done.5.refs_8_
  84.8 0.0 collective-permute-done.3.refs_5_
  84.9 0.0 collective-permute-done.1.refs_2_
  84.9 0.3 shard_map.61
  85.1 0.1 collective-permute-start.10
  85.2 0.1 collective-permute-start.11
  85.3 3.4 %collective-permute-start.9 = (bf16[64,2048]{1,0:T(8,128)(2,1)S(1)}, bf16[64,2048]{1,0:T(8,128)(2,1)S(1)}, u32[]{:S(2)}, u32[]{:S(2)}) collective-permute-start(bf16[64,2048]{1,0:T(8,128)(2,1)S(1)} %get-tuple-element.57), channel_id=1, source_target_pairs={{0,2},{1,3},{2,0},{3,1},{4,6},{5,7},{6,4},{7,5},{8,10},{9,11},{10,... | collective-permute-start | bytes 786440 | tf_op jit(solution)/shard_map/ppermute | solution.py:17
  88.7 5.5 %shard_map.62 = (f32[64,2048]{1,0:T(8,128)S(1)}, f32[64,2048]{1,0:T(8,128)S(1)}, bf16[128,2048]{1,0:T(8,128)(2,1)S(1)}) custom-call(s32[5]{0:T(128)S(1)} %get-tuple-element.60.pick_ref, bf16[2,1024,1024]{2,1,0:T(8,128)(2,1)} %bitcast.13, bf16[2,256,1024]{2,1,0:T(8,128)(2,1)S(1)} %collective-permute-done.6.next_ref, bf16[2,2,1024,1024]{3,2,1,0:T(8,128)(2,1)} %bitcast.17), custom_call_target="tpu_custom_call" | custom-call | flops 2147483648 | bytes 8388608 | tf_op jit(solution)/shard_map/pallas_call | solution.py:251
  94.2 0.1 collective-permute-start.7
  94.2 0.1 collective-permute-start.13
  94.4 0.0 collective-permute-done.10
  94.4 1.4 %collective-permute-start.14 = (bf16[64,2048]{1,0:T(8,128)(2,1)S(1)}, bf16[64,2048]{1,0:T(8,128)(2,1)S(1)}, u32[]{:S(2)}, u32[]{:S(2)}) collective-permute-start(bf16[64,2048]{1,0:T(8,128)(2,1)S(1)} %get-tuple-element.59), channel_id=1, source_target_pairs={{0,6},{1,7},{2,4},{3,5},{4,2},{5,3},{6,0},{7,1},{8,14},{9,15},{10,... | collective-permute-start | bytes 786440 | tf_op jit(solution)/shard_map/ppermute | solution.py:17
  95.8 0.9 collective-permute-done.11
  96.7 3.2 %collective-permute-done.9 = bf16[64,2048]{1,0:T(8,128)(2,1)S(1)} collective-permute-done((bf16[64,2048]{1,0:T(8,128)(2,1)S(1)}, bf16[64,2048]{1,0:T(8,128)(2,1)S(1)}, u32[]{:S(2)}, u32[]{:S(2)}) %collective-permute-start.9) | collective-permute-done | bytes 262176 | tf_op jit(solution)/shard_map/ppermute | solution.py:17
  99.9 0.1 add_convert_fusion
  100.0 1.4 %collective-permute-start.12 = (bf16[64,2048]{1,0:T(8,128)(2,1)S(1)}, bf16[64,2048]{1,0:T(8,128)(2,1)S(1)}, u32[]{:S(2)}, u32[]{:S(2)}) collective-permute-start(bf16[64,2048]{1,0:T(8,128)(2,1)S(1)} %add_convert_fusion), channel_id=1, source_target_pairs={{0,8},{1,9},{2,10},{3,11},{4,12},{5,13},{6,14},{7,15},{8,0},{9,1},... | collective-permute-start | bytes 786440 | tf_op jit(solution)/shard_map/ppermute | solution.py:17
  101.4 0.0 collective-permute-done.7.core_ref
  101.5 0.5 collective-permute-start.8
  101.9 1.5 %collective-permute-done.13.refs_2_ = bf16[64,2048]{1,0:T(8,128)(2,1)S(1)} collective-permute-done((bf16[64,2048]{1,0:T(8,128)(2,1)S(1)}, bf16[64,2048]{1,0:T(8,128)(2,1)S(1)}, u32[]{:S(2)}, u32[]{:S(2)}) %collective-permute-start.13) | collective-permute-done | bytes 262176 | tf_op jit(solution)/shard_map/ppermute | solution.py:17
  103.4 10.5 %collective-permute-done.14.refs_3_ = bf16[64,2048]{1,0:T(8,128)(2,1)S(1)} collective-permute-done((bf16[64,2048]{1,0:T(8,128)(2,1)S(1)}, bf16[64,2048]{1,0:T(8,128)(2,1)S(1)}, u32[]{:S(2)}, u32[]{:S(2)}) %collective-permute-start.14) | collective-permute-done | bytes 262176 | tf_op jit(solution)/shard_map/ppermute | solution.py:17
  113.9 0.0 collective-permute-done.12.refs_1_
  113.9 0.8 collective-permute-done.8.refs_0_
  114.6 1.1 shard_map.63
  (2 shorter events, 0.1 us)
Async XLA Ops:
  0.0 44.0 %copy-start = (s32[2]{0:T(128)S(1)}, s32[2]{0:T(128)}, u32[]{:S(2)}) copy-start(s32[2]{0:T(128)} %param.8) | copy-start | bytes 28
  32.9 24.6 %collective-permute-start = (bf16[2,1024,256]{2,1,0:T(8,128)(2,1)}, bf16[2,1024,256]{2,1,0:T(8,128)(2,1)}, u32[]{:S(2)}, u32[]{:S(2)}) collective-permute-start(bf16[2,1024,256]{2,1,0:T(8,128)(2,1)} %shard_map.56), channel_id=1, source_target_pairs={{0,15},{1,0},{2,1},{3,2},{4,3},{5,4},{6,5},{7,6},{8,7},{9,8},{10,9... | collective-permute-start | bytes 3145736 | tf_op jit(solution)/shard_map/ppermute | solution.py:17
  42.6 22.4 %collective-permute-start.2 = (bf16[2,256,1024]{2,1,0:T(8,128)(2,1)}, bf16[2,256,1024]{2,1,0:T(8,128)(2,1)S(1)}, u32[]{:S(2)}, u32[]{:S(2)}) collective-permute-start(bf16[2,256,1024]{2,1,0:T(8,128)(2,1)} %get-tuple-element.42), channel_id=1, source_target_pairs={{0,15},{1,0},{2,1},{3,2},{4,3},{5,4},{6,5},{7,6},{8,7},{9,8},{10,9... | collective-permute-start | bytes 3145736 | tf_op jit(solution)/shard_map/ppermute | solution.py:17
  43.3 30.2 %collective-permute-start.4 = (bf16[2,256,1024]{2,1,0:T(8,128)(2,1)}, bf16[2,256,1024]{2,1,0:T(8,128)(2,1)S(1)}, u32[]{:S(2)}, u32[]{:S(2)}) collective-permute-start(bf16[2,256,1024]{2,1,0:T(8,128)(2,1)} %get-tuple-element.46), channel_id=1, source_target_pairs={{0,15},{1,0},{2,1},{3,2},{4,3},{5,4},{6,5},{7,6},{8,7},{9,8},{10,9... | collective-permute-start | bytes 3145736 | tf_op jit(solution)/shard_map/ppermute | solution.py:17
  43.4 41.4 %collective-permute-start.6 = (bf16[2,256,1024]{2,1,0:T(8,128)(2,1)}, bf16[2,256,1024]{2,1,0:T(8,128)(2,1)S(1)}, u32[]{:S(2)}, u32[]{:S(2)}) collective-permute-start(bf16[2,256,1024]{2,1,0:T(8,128)(2,1)} %get-tuple-element.48), channel_id=1, source_target_pairs={{0,15},{1,0},{2,1},{3,2},{4,3},{5,4},{6,5},{7,6},{8,7},{9,8},{10,9... | collective-permute-start | bytes 3145736 | tf_op jit(solution)/shard_map/ppermute | solution.py:17
  79.0 5.8 %collective-permute-start.5 = (bf16[128,2048]{1,0:T(8,128)(2,1)S(1)}, bf16[128,2048]{1,0:T(8,128)(2,1)S(1)}, u32[]{:S(2)}, u32[]{:S(2)}) collective-permute-start(bf16[128,2048]{1,0:T(8,128)(2,1)S(1)} %get-tuple-element.47), channel_id=1, source_target_pairs={{0,1},{1,0},{2,3},{3,2},{4,5},{5,4},{6,7},{7,6},{8,9},{9,8},{10,11... | collective-permute-start | bytes 1572872 | tf_op jit(solution)/shard_map/ppermute | solution.py:17
  79.1 5.8 %collective-permute-start.3 = (bf16[128,2048]{1,0:T(8,128)(2,1)S(1)}, bf16[128,2048]{1,0:T(8,128)(2,1)S(1)}, u32[]{:S(2)}, u32[]{:S(2)}) collective-permute-start(bf16[128,2048]{1,0:T(8,128)(2,1)S(1)} %get-tuple-element.43), channel_id=1, source_target_pairs={{0,1},{1,0},{2,3},{3,2},{4,5},{5,4},{6,7},{7,6},{8,9},{9,8},{10,11... | collective-permute-start | bytes 1572872 | tf_op jit(solution)/shard_map/ppermute | solution.py:17
  79.6 5.3 %collective-permute-start.1 = (bf16[128,2048]{1,0:T(8,128)(2,1)S(1)}, bf16[128,2048]{1,0:T(8,128)(2,1)S(1)}, u32[]{:S(2)}, u32[]{:S(2)}) collective-permute-start(bf16[128,2048]{1,0:T(8,128)(2,1)S(1)} %get-tuple-element.39), channel_id=1, source_target_pairs={{0,1},{1,0},{2,3},{3,2},{4,5},{5,4},{6,7},{7,6},{8,9},{9,8},{10,11... | collective-permute-start | bytes 1572872 | tf_op jit(solution)/shard_map/ppermute | solution.py:17
  85.1 9.3 %collective-permute-start.10 = (bf16[64,2048]{1,0:T(8,128)(2,1)S(1)}, bf16[64,2048]{1,0:T(8,128)(2,1)S(1)}, u32[]{:S(2)}, u32[]{:S(2)}) collective-permute-start(bf16[64,2048]{1,0:T(8,128)(2,1)S(1)} %get-tuple-element.55), channel_id=1, source_target_pairs={{0,4},{1,5},{2,6},{3,7},{4,0},{5,1},{6,2},{7,3},{8,12},{9,13},{10,... | collective-permute-start | bytes 786440 | tf_op jit(solution)/shard_map/ppermute | solution.py:17
  85.2 11.5 %collective-permute-start.11 = (bf16[64,2048]{1,0:T(8,128)(2,1)S(1)}, bf16[64,2048]{1,0:T(8,128)(2,1)S(1)}, u32[]{:S(2)}, u32[]{:S(2)}) collective-permute-start(bf16[64,2048]{1,0:T(8,128)(2,1)S(1)} %get-tuple-element.56), channel_id=1, source_target_pairs={{0,6},{1,7},{2,4},{3,5},{4,2},{5,3},{6,0},{7,1},{8,14},{9,15},{10,... | collective-permute-start | bytes 786440 | tf_op jit(solution)/shard_map/ppermute | solution.py:17
  85.3 14.6 %collective-permute-start.9 = (bf16[64,2048]{1,0:T(8,128)(2,1)S(1)}, bf16[64,2048]{1,0:T(8,128)(2,1)S(1)}, u32[]{:S(2)}, u32[]{:S(2)}) collective-permute-start(bf16[64,2048]{1,0:T(8,128)(2,1)S(1)} %get-tuple-element.57), channel_id=1, source_target_pairs={{0,2},{1,3},{2,0},{3,1},{4,6},{5,7},{6,4},{7,5},{8,10},{9,11},{10,... | collective-permute-start | bytes 786440 | tf_op jit(solution)/shard_map/ppermute | solution.py:17
  94.2 7.3 %collective-permute-start.7 = (bf16[128,2048]{1,0:T(8,128)(2,1)S(1)}, bf16[128,2048]{1,0:T(8,128)(2,1)S(1)}, u32[]{:S(2)}, u32[]{:S(2)}) collective-permute-start(bf16[128,2048]{1,0:T(8,128)(2,1)S(1)} %get-tuple-element.63), channel_id=1, source_target_pairs={{0,1},{1,0},{2,3},{3,2},{4,5},{5,4},{6,7},{7,6},{8,9},{9,8},{10,11... | collective-permute-start | bytes 1572872 | tf_op jit(solution)/shard_map/ppermute | solution.py:17
  94.2 9.2 %collective-permute-start.13 = (bf16[64,2048]{1,0:T(8,128)(2,1)S(1)}, bf16[64,2048]{1,0:T(8,128)(2,1)S(1)}, u32[]{:S(2)}, u32[]{:S(2)}) collective-permute-start(bf16[64,2048]{1,0:T(8,128)(2,1)S(1)} %get-tuple-element.58), channel_id=1, source_target_pairs={{0,4},{1,5},{2,6},{3,7},{4,0},{5,1},{6,2},{7,3},{8,12},{9,13},{10,... | collective-permute-start | bytes 786440 | tf_op jit(solution)/shard_map/ppermute | solution.py:17
  94.4 19.5 %collective-permute-start.14 = (bf16[64,2048]{1,0:T(8,128)(2,1)S(1)}, bf16[64,2048]{1,0:T(8,128)(2,1)S(1)}, u32[]{:S(2)}, u32[]{:S(2)}) collective-permute-start(bf16[64,2048]{1,0:T(8,128)(2,1)S(1)} %get-tuple-element.59), channel_id=1, source_target_pairs={{0,6},{1,7},{2,4},{3,5},{4,2},{5,3},{6,0},{7,1},{8,14},{9,15},{10,... | collective-permute-start | bytes 786440 | tf_op jit(solution)/shard_map/ppermute | solution.py:17
  100.0 13.9 %collective-permute-start.12 = (bf16[64,2048]{1,0:T(8,128)(2,1)S(1)}, bf16[64,2048]{1,0:T(8,128)(2,1)S(1)}, u32[]{:S(2)}, u32[]{:S(2)}) collective-permute-start(bf16[64,2048]{1,0:T(8,128)(2,1)S(1)} %add_convert_fusion), channel_id=1, source_target_pairs={{0,8},{1,9},{2,10},{3,11},{4,12},{5,13},{6,14},{7,15},{8,0},{9,1},... | collective-permute-start | bytes 786440 | tf_op jit(solution)/shard_map/ppermute | solution.py:17
  101.5 13.2 %collective-permute-start.8 = (bf16[64,2048]{1,0:T(8,128)(2,1)S(1)}, bf16[64,2048]{1,0:T(8,128)(2,1)S(1)}, u32[]{:S(2)}, u32[]{:S(2)}) collective-permute-start(bf16[64,2048]{1,0:T(8,128)(2,1)S(1)} %add_convert_fusion.1), channel_id=1, source_target_pairs={{0,2},{1,3},{2,0},{3,1},{4,6},{5,7},{6,4},{7,5},{8,10},{9,11},{10,... | collective-permute-start | bytes 786440 | tf_op jit(solution)/shard_map/ppermute | solution.py:17

commit v22 on v21

--- a/solution.py
+++ b/solution.py
@@ -117,33 +117,41 @@
     return pl.ds(pl.multiple_of((behind_z ^ (3 - step)) * width, width), width)
 
 
-def cut_kernel(coeffs_ref, out_ref, sems):
-    k_local, parts = sems.shape
-    _, depth, width = out_ref.shape
-    columns, count = columns_of(0, width), depth // parts
-    copies = []
-    for k in range(k_local):
-        for p in range(parts):
-            rows = pl.ds(p * count, count)
-            copies.append(
-                pltpu.make_async_copy(
-                    coeffs_ref.at[k, rows, columns], out_ref.at[k, rows], sems.at[k, p]
-                )
-            )
-    for copy in copies:
-        copy.start()
-    for copy in copies:
-        copy.wait()
+def cut_kernel(coeffs_ref, out_ref, held, sems, out_sems):
+    k_local, parts, rows, width = held.shape
+    columns = columns_of(0, width)
+    steps = [(k, p) for k in range(k_local) for p in range(parts)]
+
+    def copy_in(k, p):
+        source = coeffs_ref.at[k, pl.ds(p * rows, rows), columns]
+        return pltpu.make_async_copy(source, held.at[k, p], sems.at[k, p])
+
+    def copy_out(k, p):
+        target = out_ref.at[k, pl.ds(p * rows, rows)]
+        return pltpu.make_async_copy(held.at[k, p], target, out_sems.at[k, p])
+
+    for step in steps:
+        copy_in(*step).start()
+    for step in steps:
+        copy_in(*step).wait()
+        copy_out(*step).start()
+    for step in steps:
+        copy_out(*step).wait()
 
 
 def cut_piece(flat, width):
     k_local, depth, _ = flat.shape
+    parts = 4
     return pl.pallas_call(
         cut_kernel,
         out_shape=jax.ShapeDtypeStruct((k_local, depth, width), jnp.bfloat16),
         in_specs=[pl.BlockSpec(memory_space=pl.ANY)],
         out_specs=pl.BlockSpec(memory_space=pl.ANY),
-        scratch_shapes=[pltpu.SemaphoreType.DMA((k_local, 4))],
+        scratch_shapes=[
+            pltpu.VMEM((k_local, parts, depth // parts, width), jnp.bfloat16),
+            pltpu.SemaphoreType.DMA((k_local, parts)),
+            pltpu.SemaphoreType.DMA((k_local, parts)),
+        ],
         compiler_params=pltpu.CompilerParams(vmem_limit_bytes=60 * MIB),
         cost_estimate=pl.CostEstimate(
             flops=0, bytes_accessed=4 * k_local * depth * width, transcendentals=0

time: 116 us -> 85.2 us (0.73)
  Pallas kernels: 75.7 us -> 45.1 us
    pallas_call x1, Pallas kernels: 32.9 us -> 2.13 us  [cut_piece(): pl.pallas_call(cut_kernel, out_shape=jax.ShapeDtypeStruct((k_local, depth...]
  transfers between devices with their start and end apart: 15 -> 15, of which waited for: 7 -> 7; matrix products, arithmetic and copies ran while one was open for 0% -> 0% of each run, Pallas kernels for 36% -> 49%
where the time goes in v22:
time: 85.2 us; the launch traced here: 84.9 us
  Pallas kernels  45.1 us (53%)
  waiting for transfers between devices  24.6 us (29%)
  starting transfers between devices  14.7 us (17%)
    ppermute x15, waiting for transfers between devices, permute(): lax.ppermute(x, 'ka', [(i, j % size) for i, j in pairs if j is not None])  24.6 us
    pallas_call x4, Pallas kernels, rows_of(): pl.pallas_call(functools.partial(rows_kernel, turned), out_shape=[jax.Sha...  24.1 us
    ppermute x15, starting transfers between devices, permute(): lax.ppermute(x, 'ka', [(i, j % size) for i, j in pairs if j is not None])  14.7 us
    pallas_call x1, Pallas kernels, products_of(): pl.pallas_call(products_kernel, out_shape=jax.ShapeDtypeStruct((k_local,...  13.4 us
    pallas_call x1, Pallas kernels, turned_pieces(): pl.pallas_call(turn_kernel, out_shape=[jax.ShapeDtypeStruct((k_local, wid...  4.19 us
    pallas_call x1, Pallas kernels, cut_piece(): pl.pallas_call(cut_kernel, out_shape=jax.ShapeDtypeStruct((k_local, depth...  2.13 us
  transfers between devices with their start and end apart: 15, of which 7 were waited for; matrix products, arithmetic and copies ran while one was open for 0% of the time, Pallas kernels for 49%

profile of v22, /device:TPU:0, one launch (start us, length us, event | category | flops | bytes accessed | tf_op | source)
XLA Modules:
  0.0 84.9 jit_solution(10839870466262055601)
XLA Ops:
  0.0 0.0 copy-start
  0.0 2.1 %shard_map.56 = bf16[2,1024,256]{2,1,0:T(8,128)(2,1)} custom-call(bf16[2,1024,1024]{2,1,0:T(8,128)(2,1)} %bitcast.8), custom_call_target="tpu_custom_call" | custom-call | bytes 2097152 | tf_op jit(solution)/shard_map/pallas_call | solution.py:145
  2.1 5.5 %collective-permute-start = (bf16[2,1024,256]{2,1,0:T(8,128)(2,1)}, bf16[2,1024,256]{2,1,0:T(8,128)(2,1)}, u32[]{:S(2)}, u32[]{:S(2)}) collective-permute-start(bf16[2,1024,256]{2,1,0:T(8,128)(2,1)} %shard_map.56), channel_id=1, source_target_pairs={{0,15},{1,0},{2,1},{3,2},{4,3},{5,4},{6,5},{7,6},{8,7},{9,8},{10,9... | collective-permute-start | bytes 3145736 | tf_op jit(solution)/shard_map/ppermute | solution.py:17
  7.6 4.2 %shard_map.58 = (bf16[2,256,1024]{2,1,0:T(8,128)(2,1)}, bf16[2,256,1024]{2,1,0:T(8,128)(2,1)}, bf16[2,256,1024]{2,1,0:T(8,128)(2,1)}) custom-call(bf16[2,1024,1024]{2,1,0:T(8,128)(2,1)} %bitcast.9), custom_call_target="tpu_custom_call" | custom-call | bytes 6291456 | tf_op jit(solution)/shard_map/pallas_call | solution.py:183
  11.8 0.7 collective-permute-start.2
  12.5 0.1 collective-permute-start.4
  12.6 0.6 collective-permute-start.6
  13.2 0.0 copy-done
  13.2 0.1 add_add_fusion.3
  13.3 13.4 %shard_map.55 = bf16[2,2,32,32,1024]{4,3,2,1,0:T(8,128)(2,1)} custom-call(s32[2,2]{1,0:T(2,128)} %first_ref.1, bf16[2,32,32,1024]{3,2,1,0:T(8,128)(2,1)} %coeffs_ref.1, bf16[2,2,32,32]{3,2,1,0:T(8,128)(2,1)} %cond_ref.1, bf16[2,2,32,32]{3,2,1,0:T(8,128)(2,1)} %val_ref.1), custom_call_target="tpu_custom_call" | custom-call | flops 6442450944 | bytes 12582912 | tf_op jit(solution)/shard_map/pallas_call | solution.py:90
  26.7 0.1 add_add_fusion.2
  26.7 0.0 collective-permute-done.next_ref
  26.7 7.6 %shard_map.57 = (f32[64,2048]{1,0:T(8,128)S(1)}, f32[64,2048]{1,0:T(8,128)S(1)}, bf16[128,2048]{1,0:T(8,128)(2,1)S(1)}) custom-call(s32[5]{0:T(128)S(1)} %get-tuple-element.36.pick_ref, bf16[2,1024,1024]{2,1,0:T(8,128)(2,1)} %bitcast.10, bf16[2,1024,256]{2,1,0:T(8,128)(2,1)} %collective-permute-done.next_ref, bf16[2,2,1024,1024]{3,2,1,0:T(8,128)(2,1)} %bitcast.14), custom_call_target="tpu_custom_call" | custom-call | flops 2147483648 | bytes 8388608 | tf_op jit(solution)/shard_map/pallas_call | solution.py:259
  34.4 0.0 collective-permute-done.2.next_ref
  34.4 5.5 %shard_map.59 = (f32[64,2048]{1,0:T(8,128)S(1)}, f32[64,2048]{1,0:T(8,128)S(1)}, bf16[128,2048]{1,0:T(8,128)(2,1)S(1)}) custom-call(s32[5]{0:T(128)S(1)} %get-tuple-element.40.pick_ref, bf16[2,1024,1024]{2,1,0:T(8,128)(2,1)} %bitcast.11, bf16[2,256,1024]{2,1,0:T(8,128)(2,1)S(1)} %collective-permute-done.2.next_ref, bf16[2,2,1024,1024]{3,2,1,0:T(8,128)(2,1)} %bitcast.15), custom_call_target="tpu_custom_call" | custom-call | flops 2147483648 | bytes 8388608 | tf_op jit(solution)/shard_map/pallas_call | solution.py:259
  39.9 2.8 %collective-permute-done.4.next_ref = bf16[2,256,1024]{2,1,0:T(8,128)(2,1)S(1)} collective-permute-done((bf16[2,256,1024]{2,1,0:T(8,128)(2,1)}, bf16[2,256,1024]{2,1,0:T(8,128)(2,1)S(1)}, u32[]{:S(2)}, u32[]{:S(2)}) %collective-permute-start.4) | collective-permute-done | bytes 1048608 | tf_op jit(solution)/shard_map/ppermute | solution.py:17
  42.7 5.5 %shard_map.60 = (f32[64,2048]{1,0:T(8,128)S(1)}, f32[64,2048]{1,0:T(8,128)S(1)}, bf16[128,2048]{1,0:T(8,128)(2,1)S(1)}) custom-call(s32[5]{0:T(128)S(1)} %get-tuple-element.45.pick_ref, bf16[2,1024,1024]{2,1,0:T(8,128)(2,1)} %bitcast.12, bf16[2,256,1024]{2,1,0:T(8,128)(2,1)S(1)} %collective-permute-done.4.next_ref, bf16[2,2,1024,1024]{3,2,1,0:T(8,128)(2,1)} %bitcast.16), custom_call_target="tpu_custom_call" | custom-call | flops 2147483648 | bytes 8388608 | tf_op jit(solution)/shard_map/pallas_call | solution.py:259
  48.2 0.1 collective-permute-start.5
  48.3 0.5 collective-permute-start.3
  48.8 0.1 collective-permute-start.1
  48.9 5.2 %collective-permute-done.6.next_ref = bf16[2,256,1024]{2,1,0:T(8,128)(2,1)S(1)} collective-permute-done((bf16[2,256,1024]{2,1,0:T(8,128)(2,1)}, bf16[2,256,1024]{2,1,0:T(8,128)(2,1)S(1)}, u32[]{:S(2)}, u32[]{:S(2)}) %collective-permute-start.6) | collective-permute-done | bytes 1048608 | tf_op jit(solution)/shard_map/ppermute | solution.py:17
  54.0 0.0 collective-permute-done.5.refs_8_
  54.0 0.0 collective-permute-done.3.refs_5_
  54.1 0.0 collective-permute-done.1.refs_2_
  54.1 0.3 shard_map.61
  54.3 0.1 collective-permute-start.10
  54.4 0.1 collective-permute-start.11
  54.5 3.4 %collective-permute-start.9 = (bf16[64,2048]{1,0:T(8,128)(2,1)S(1)}, bf16[64,2048]{1,0:T(8,128)(2,1)S(1)}, u32[]{:S(2)}, u32[]{:S(2)}) collective-permute-start(bf16[64,2048]{1,0:T(8,128)(2,1)S(1)} %get-tuple-element.57), channel_id=1, source_target_pairs={{0,2},{1,3},{2,0},{3,1},{4,6},{5,7},{6,4},{7,5},{8,10},{9,11},{10,... | collective-permute-start | bytes 786440 | tf_op jit(solution)/shard_map/ppermute | solution.py:17
  57.9 5.5 %shard_map.62 = (f32[64,2048]{1,0:T(8,128)S(1)}, f32[64,2048]{1,0:T(8,128)S(1)}, bf16[128,2048]{1,0:T(8,128)(2,1)S(1)}) custom-call(s32[5]{0:T(128)S(1)} %get-tuple-element.60.pick_ref, bf16[2,1024,1024]{2,1,0:T(8,128)(2,1)} %bitcast.13, bf16[2,256,1024]{2,1,0:T(8,128)(2,1)S(1)} %collective-permute-done.6.next_ref, bf16[2,2,1024,1024]{3,2,1,0:T(8,128)(2,1)} %bitcast.17), custom_call_target="tpu_custom_call" | custom-call | flops 2147483648 | bytes 8388608 | tf_op jit(solution)/shard_map/pallas_call | solution.py:259
  63.4 0.1 collective-permute-start.7
  63.4 0.2 collective-permute-start.13
  63.6 0.0 collective-permute-done.10
  63.6 1.4 %collective-permute-start.14 = (bf16[64,2048]{1,0:T(8,128)(2,1)S(1)}, bf16[64,2048]{1,0:T(8,128)(2,1)S(1)}, u32[]{:S(2)}, u32[]{:S(2)}) collective-permute-start(bf16[64,2048]{1,0:T(8,128)(2,1)S(1)} %get-tuple-element.59), channel_id=1, source_target_pairs={{0,6},{1,7},{2,4},{3,5},{4,2},{5,3},{6,0},{7,1},{8,14},{9,15},{10,... | collective-permute-start | bytes 786440 | tf_op jit(solution)/shard_map/ppermute | solution.py:17
  65.0 0.9 %collective-permute-done.11 = bf16[64,2048]{1,0:T(8,128)(2,1)S(1)} collective-permute-done((bf16[64,2048]{1,0:T(8,128)(2,1)S(1)}, bf16[64,2048]{1,0:T(8,128)(2,1)S(1)}, u32[]{:S(2)}, u32[]{:S(2)}) %collective-permute-start.11) | collective-permute-done | bytes 262176 | tf_op jit(solution)/shard_map/ppermute | solution.py:17
  65.9 3.2 %collective-permute-done.9 = bf16[64,2048]{1,0:T(8,128)(2,1)S(1)} collective-permute-done((bf16[64,2048]{1,0:T(8,128)(2,1)S(1)}, bf16[64,2048]{1,0:T(8,128)(2,1)S(1)}, u32[]{:S(2)}, u32[]{:S(2)}) %collective-permute-start.9) | collective-permute-done | bytes 262176 | tf_op jit(solution)/shard_map/ppermute | solution.py:17
  69.1 0.1 add_convert_fusion
  69.2 1.5 %collective-permute-start.12 = (bf16[64,2048]{1,0:T(8,128)(2,1)S(1)}, bf16[64,2048]{1,0:T(8,128)(2,1)S(1)}, u32[]{:S(2)}, u32[]{:S(2)}) collective-permute-start(bf16[64,2048]{1,0:T(8,128)(2,1)S(1)} %add_convert_fusion), channel_id=1, source_target_pairs={{0,8},{1,9},{2,10},{3,11},{4,12},{5,13},{6,14},{7,15},{8,0},{9,1},... | collective-permute-start | bytes 786440 | tf_op jit(solution)/shard_map/ppermute | solution.py:17
  70.7 0.0 collective-permute-done.7.core_ref
  70.8 0.5 collective-permute-start.8
  71.3 1.3 %collective-permute-done.13.refs_2_ = bf16[64,2048]{1,0:T(8,128)(2,1)S(1)} collective-permute-done((bf16[64,2048]{1,0:T(8,128)(2,1)S(1)}, bf16[64,2048]{1,0:T(8,128)(2,1)S(1)}, u32[]{:S(2)}, u32[]{:S(2)}) %collective-permute-start.13) | collective-permute-done | bytes 262176 | tf_op jit(solution)/shard_map/ppermute | solution.py:17
  72.6 10.5 %collective-permute-done.14.refs_3_ = bf16[64,2048]{1,0:T(8,128)(2,1)S(1)} collective-permute-done((bf16[64,2048]{1,0:T(8,128)(2,1)S(1)}, bf16[64,2048]{1,0:T(8,128)(2,1)S(1)}, u32[]{:S(2)}, u32[]{:S(2)}) %collective-permute-start.14) | collective-permute-done | bytes 262176 | tf_op jit(solution)/shard_map/ppermute | solution.py:17
  83.1 0.0 collective-permute-done.12.refs_1_
  83.1 0.8 collective-permute-done.8.refs_0_
  83.8 1.1 %shard_map.63 = f32[64,2,1024]{2,1,0:T(2,128)} custom-call(f32[64,2048]{1,0:T(8,128)S(1)} %get-tuple-element.62.mine_ref, bf16[128,2048]{1,0:T(8,128)(2,1)S(1)} %collective-permute-done.7.core_ref, bf16[64,2048]{1,0:T(8,128)(2,1)S(1)} %collective-permute-done.8.refs_0_, bf16[64,2048]{1,0:T(8,128)(2,1)S(1)} %collective-permute-done.12.refs_1_, ...), custom_call_target="tpu_custom_call" | custom-call | flops 655360 | bytes 2097152 | tf_op jit(solution)/shard_map/pallas_call | solution.py:332
  (2 shorter events, 0.1 us)
Async XLA Ops:
  0.0 13.2 %copy-start = (s32[2]{0:T(128)S(1)}, s32[2]{0:T(128)}, u32[]{:S(2)}) copy-start(s32[2]{0:T(128)} %param.8) | copy-start | bytes 28
  2.1 24.6 %collective-permute-start = (bf16[2,1024,256]{2,1,0:T(8,128)(2,1)}, bf16[2,1024,256]{2,1,0:T(8,128)(2,1)}, u32[]{:S(2)}, u32[]{:S(2)}) collective-permute-start(bf16[2,1024,256]{2,1,0:T(8,128)(2,1)} %shard_map.56), channel_id=1, source_target_pairs={{0,15},{1,0},{2,1},{3,2},{4,3},{5,4},{6,5},{7,6},{8,7},{9,8},{10,9... | collective-permute-start | bytes 3145736 | tf_op jit(solution)/shard_map/ppermute | solution.py:17
  11.8 22.6 %collective-permute-start.2 = (bf16[2,256,1024]{2,1,0:T(8,128)(2,1)}, bf16[2,256,1024]{2,1,0:T(8,128)(2,1)S(1)}, u32[]{:S(2)}, u32[]{:S(2)}) collective-permute-start(bf16[2,256,1024]{2,1,0:T(8,128)(2,1)} %get-tuple-element.42), channel_id=1, source_target_pairs={{0,15},{1,0},{2,1},{3,2},{4,3},{5,4},{6,5},{7,6},{8,7},{9,8},{10,9... | collective-permute-start | bytes 3145736 | tf_op jit(solution)/shard_map/ppermute | solution.py:17
  12.5 30.2 %collective-permute-start.4 = (bf16[2,256,1024]{2,1,0:T(8,128)(2,1)}, bf16[2,256,1024]{2,1,0:T(8,128)(2,1)S(1)}, u32[]{:S(2)}, u32[]{:S(2)}) collective-permute-start(bf16[2,256,1024]{2,1,0:T(8,128)(2,1)} %get-tuple-element.46), channel_id=1, source_target_pairs={{0,15},{1,0},{2,1},{3,2},{4,3},{5,4},{6,5},{7,6},{8,7},{9,8},{10,9... | collective-permute-start | bytes 3145736 | tf_op jit(solution)/shard_map/ppermute | solution.py:17
  12.6 41.4 %collective-permute-start.6 = (bf16[2,256,1024]{2,1,0:T(8,128)(2,1)}, bf16[2,256,1024]{2,1,0:T(8,128)(2,1)S(1)}, u32[]{:S(2)}, u32[]{:S(2)}) collective-permute-start(bf16[2,256,1024]{2,1,0:T(8,128)(2,1)} %get-tuple-element.48), channel_id=1, source_target_pairs={{0,15},{1,0},{2,1},{3,2},{4,3},{5,4},{6,5},{7,6},{8,7},{9,8},{10,9... | collective-permute-start | bytes 3145736 | tf_op jit(solution)/shard_map/ppermute | solution.py:17
  48.2 5.8 %collective-permute-start.5 = (bf16[128,2048]{1,0:T(8,128)(2,1)S(1)}, bf16[128,2048]{1,0:T(8,128)(2,1)S(1)}, u32[]{:S(2)}, u32[]{:S(2)}) collective-permute-start(bf16[128,2048]{1,0:T(8,128)(2,1)S(1)} %get-tuple-element.47), channel_id=1, source_target_pairs={{0,1},{1,0},{2,3},{3,2},{4,5},{5,4},{6,7},{7,6},{8,9},{9,8},{10,11... | collective-permute-start | bytes 1572872 | tf_op jit(solution)/shard_map/ppermute | solution.py:17
  48.3 5.8 %collective-permute-start.3 = (bf16[128,2048]{1,0:T(8,128)(2,1)S(1)}, bf16[128,2048]{1,0:T(8,128)(2,1)S(1)}, u32[]{:S(2)}, u32[]{:S(2)}) collective-permute-start(bf16[128,2048]{1,0:T(8,128)(2,1)S(1)} %get-tuple-element.43), channel_id=1, source_target_pairs={{0,1},{1,0},{2,3},{3,2},{4,5},{5,4},{6,7},{7,6},{8,9},{9,8},{10,11... | collective-permute-start | bytes 1572872 | tf_op jit(solution)/shard_map/ppermute | solution.py:17
  48.8 5.3 %collective-permute-start.1 = (bf16[128,2048]{1,0:T(8,128)(2,1)S(1)}, bf16[128,2048]{1,0:T(8,128)(2,1)S(1)}, u32[]{:S(2)}, u32[]{:S(2)}) collective-permute-start(bf16[128,2048]{1,0:T(8,128)(2,1)S(1)} %get-tuple-element.39), channel_id=1, source_target_pairs={{0,1},{1,0},{2,3},{3,2},{4,5},{5,4},{6,7},{7,6},{8,9},{9,8},{10,11... | collective-permute-start | bytes 1572872 | tf_op jit(solution)/shard_map/ppermute | solution.py:17
  54.3 9.3 %collective-permute-start.10 = (bf16[64,2048]{1,0:T(8,128)(2,1)S(1)}, bf16[64,2048]{1,0:T(8,128)(2,1)S(1)}, u32[]{:S(2)}, u32[]{:S(2)}) collective-permute-start(bf16[64,2048]{1,0:T(8,128)(2,1)S(1)} %get-tuple-element.55), channel_id=1, source_target_pairs={{0,4},{1,5},{2,6},{3,7},{4,0},{5,1},{6,2},{7,3},{8,12},{9,13},{10,... | collective-permute-start | bytes 786440 | tf_op jit(solution)/shard_map/ppermute | solution.py:17
  54.4 11.5 %collective-permute-start.11 = (bf16[64,2048]{1,0:T(8,128)(2,1)S(1)}, bf16[64,2048]{1,0:T(8,128)(2,1)S(1)}, u32[]{:S(2)}, u32[]{:S(2)}) collective-permute-start(bf16[64,2048]{1,0:T(8,128)(2,1)S(1)} %get-tuple-element.56), channel_id=1, source_target_pairs={{0,6},{1,7},{2,4},{3,5},{4,2},{5,3},{6,0},{7,1},{8,14},{9,15},{10,... | collective-permute-start | bytes 786440 | tf_op jit(solution)/shard_map/ppermute | solution.py:17
  54.5 14.6 %collective-permute-start.9 = (bf16[64,2048]{1,0:T(8,128)(2,1)S(1)}, bf16[64,2048]{1,0:T(8,128)(2,1)S(1)}, u32[]{:S(2)}, u32[]{:S(2)}) collective-permute-start(bf16[64,2048]{1,0:T(8,128)(2,1)S(1)} %get-tuple-element.57), channel_id=1, source_target_pairs={{0,2},{1,3},{2,0},{3,1},{4,6},{5,7},{6,4},{7,5},{8,10},{9,11},{10,... | collective-permute-start | bytes 786440 | tf_op jit(solution)/shard_map/ppermute | solution.py:17
  63.4 7.4 %collective-permute-start.7 = (bf16[128,2048]{1,0:T(8,128)(2,1)S(1)}, bf16[128,2048]{1,0:T(8,128)(2,1)S(1)}, u32[]{:S(2)}, u32[]{:S(2)}) collective-permute-start(bf16[128,2048]{1,0:T(8,128)(2,1)S(1)} %get-tuple-element.63), channel_id=1, source_target_pairs={{0,1},{1,0},{2,3},{3,2},{4,5},{5,4},{6,7},{7,6},{8,9},{9,8},{10,11... | collective-permute-start | bytes 1572872 | tf_op jit(solution)/shard_map/ppermute | solution.py:17
  63.4 9.2 %collective-permute-start.13 = (bf16[64,2048]{1,0:T(8,128)(2,1)S(1)}, bf16[64,2048]{1,0:T(8,128)(2,1)S(1)}, u32[]{:S(2)}, u32[]{:S(2)}) collective-permute-start(bf16[64,2048]{1,0:T(8,128)(2,1)S(1)} %get-tuple-element.58), channel_id=1, source_target_pairs={{0,4},{1,5},{2,6},{3,7},{4,0},{5,1},{6,2},{7,3},{8,12},{9,13},{10,... | collective-permute-start | bytes 786440 | tf_op jit(solution)/shard_map/ppermute | solution.py:17
  63.6 19.5 %collective-permute-start.14 = (bf16[64,2048]{1,0:T(8,128)(2,1)S(1)}, bf16[64,2048]{1,0:T(8,128)(2,1)S(1)}, u32[]{:S(2)}, u32[]{:S(2)}) collective-permute-start(bf16[64,2048]{1,0:T(8,128)(2,1)S(1)} %get-tuple-element.59), channel_id=1, source_target_pairs={{0,6},{1,7},{2,4},{3,5},{4,2},{5,3},{6,0},{7,1},{8,14},{9,15},{10,... | collective-permute-start | bytes 786440 | tf_op jit(solution)/shard_map/ppermute | solution.py:17
  69.2 13.9 %collective-permute-start.12 = (bf16[64,2048]{1,0:T(8,128)(2,1)S(1)}, bf16[64,2048]{1,0:T(8,128)(2,1)S(1)}, u32[]{:S(2)}, u32[]{:S(2)}) collective-permute-start(bf16[64,2048]{1,0:T(8,128)(2,1)S(1)} %add_convert_fusion), channel_id=1, source_target_pairs={{0,8},{1,9},{2,10},{3,11},{4,12},{5,13},{6,14},{7,15},{8,0},{9,1},... | collective-permute-start | bytes 786440 | tf_op jit(solution)/shard_map/ppermute | solution.py:17
  70.8 13.1 %collective-permute-start.8 = (bf16[64,2048]{1,0:T(8,128)(2,1)S(1)}, bf16[64,2048]{1,0:T(8,128)(2,1)S(1)}, u32[]{:S(2)}, u32[]{:S(2)}) collective-permute-start(bf16[64,2048]{1,0:T(8,128)(2,1)S(1)} %add_convert_fusion.1), channel_id=1, source_target_pairs={{0,2},{1,3},{2,0},{3,1},{4,6},{5,7},{6,4},{7,5},{8,10},{9,11},{10,... | collective-permute-start | bytes 786440 | tf_op jit(solution)/shard_map/ppermute | solution.py:17

commit v23 on v22

--- a/solution.py
+++ b/solution.py
@@ -285,17 +285,20 @@
 
 
 def payloads_kernel(*refs):
-    ins, (far_0, far_1, across, near_0, near_1, mine_1) = refs[:9], refs[9:]
-    half = across.shape[0]
+    ins, (turn_0, turn_1, far_0, near_0, near_1, mine_1) = refs[:9], refs[9:]
+    half = turn_0.shape[0]
 
     def summed(block, own):
         mine, other, core = ins[3 * block:3 * block + 3]
         rows = slice(0, half) if own else slice(half, 2 * half)
         return (mine if own else other)[...] + core[rows, :].astype(jnp.float32)
 
+    far_1 = summed(0, False).astype(jnp.bfloat16)
+    across = summed(1, False).astype(jnp.bfloat16)
+    first = lax.axis_index("ka") & 1 == 0
+    turn_0[...] = jnp.where(first, across, far_1)
+    turn_1[...] = jnp.where(first, far_1, across)
     far_0[...] = summed(0, True).astype(jnp.bfloat16)
-    far_1[...] = summed(0, False).astype(jnp.bfloat16)
-    across[...] = summed(1, False).astype(jnp.bfloat16)
     near_0[...] = summed(2, True).astype(jnp.bfloat16)
     near_1[...] = summed(2, False).astype(jnp.bfloat16)
     mine_1[...] = summed(1, True)
@@ -384,11 +387,13 @@
         *step_0[:2], core_0, *step_1[:2], core_1, *step_2[:2], core_2
     )
     step_3 = rows(3, sends)
-    far = over(sends[0], 4), over(sends[1], 6)
-    across_1 = over(sends[2], 2)
+    arrived = [
+        permute(sends[turn], lambda i: i ^ (2 if i % 2 == turn else 6)) for turn in range(2)
+    ]
+    arrived.append(over(sends[2], 4))
     near = over(sends[3], 4), over(sends[4], 6)
     mine_1, _ = lax.optimization_barrier((mine_1, step_3[0]))
-    pair = over(total_of(mine_1, across_1, *far), 8)
+    pair = over(total_of(mine_1, *arrived), 8)
     mine_3, other_3, core_3 = step_3
     across_3 = over(other_3 + core_3[half:].astype(jnp.float32), 2)
     return closed(modes, norm_factor, mine_3, core_3, across_3, pair, *near)

time: 85.2 us -> 86.2 us (1.012)
  waiting for transfers between devices: 24.6 us -> 26.7 us
  starting transfers between devices: 14.7 us -> 13.7 us
    ppermute x15, waiting for transfers between devices: 24.6 us -> 26.7 us  [permute(): lax.ppermute(x, 'ka', [(i, j % size) for i, j in pairs if j is not None])]
    ppermute x15, starting transfers between devices: 14.7 us -> 13.7 us  [permute(): lax.ppermute(x, 'ka', [(i, j % size) for i, j in pairs if j is not None])]
  transfers between devices with their start and end apart: 15 -> 15, of which waited for: 7 -> 7; matrix products, arithmetic and copies ran while one was open for 0% -> 0% of each run, Pallas kernels for 49% -> 48%
where the time goes in v23:
time: 86.2 us; the launch traced here: 85.9 us
  Pallas kernels  45 us (52%)
  waiting for transfers between devices  26.7 us (31%)
  starting transfers between devices  13.7 us (16%)
    ppermute x15, waiting for transfers between devices, permute(): lax.ppermute(x, 'ka', [(i, j % size) for i, j in pairs if j is not None])  26.7 us
    pallas_call x4, Pallas kernels, rows_of(): pl.pallas_call(functools.partial(rows_kernel, turned), out_shape=[jax.Sha...  23.9 us
    ppermute x15, starting transfers between devices, permute(): lax.ppermute(x, 'ka', [(i, j % size) for i, j in pairs if j is not None])  13.7 us
    pallas_call x1, Pallas kernels, products_of(): pl.pallas_call(products_kernel, out_shape=jax.ShapeDtypeStruct((k_local,...  13.4 us
    pallas_call x1, Pallas kernels, turned_pieces(): pl.pallas_call(turn_kernel, out_shape=[jax.ShapeDtypeStruct((k_local, wid...  4.19 us
    pallas_call x1, Pallas kernels, cut_piece(): pl.pallas_call(cut_kernel, out_shape=jax.ShapeDtypeStruct((k_local, depth...  2.13 us
  transfers between devices with their start and end apart: 15, of which 7 were waited for; matrix products, arithmetic and copies ran while one was open for 0% of the time, Pallas kernels for 48%

profile of v23, /device:TPU:0, one launch (start us, length us, event | category | flops | bytes accessed | tf_op | source)
XLA Modules:
  0.0 85.9 jit_solution(704596093033871605)
XLA Ops:
  0.0 0.0 copy-start
  0.0 2.1 %shard_map.56 = bf16[2,1024,256]{2,1,0:T(8,128)(2,1)} custom-call(bf16[2,1024,1024]{2,1,0:T(8,128)(2,1)} %bitcast.8), custom_call_target="tpu_custom_call" | custom-call | bytes 2097152 | tf_op jit(solution)/shard_map/pallas_call | solution.py:145
  2.1 5.5 %collective-permute-start = (bf16[2,1024,256]{2,1,0:T(8,128)(2,1)}, bf16[2,1024,256]{2,1,0:T(8,128)(2,1)}, u32[]{:S(2)}, u32[]{:S(2)}) collective-permute-start(bf16[2,1024,256]{2,1,0:T(8,128)(2,1)} %shard_map.56), channel_id=1, source_target_pairs={{0,15},{1,0},{2,1},{3,2},{4,3},{5,4},{6,5},{7,6},{8,7},{9,8},{10,9... | collective-permute-start | bytes 3145736 | tf_op jit(solution)/shard_map/ppermute | solution.py:17
  7.6 4.2 %shard_map.58 = (bf16[2,256,1024]{2,1,0:T(8,128)(2,1)}, bf16[2,256,1024]{2,1,0:T(8,128)(2,1)}, bf16[2,256,1024]{2,1,0:T(8,128)(2,1)}) custom-call(bf16[2,1024,1024]{2,1,0:T(8,128)(2,1)} %bitcast.9), custom_call_target="tpu_custom_call" | custom-call | bytes 6291456 | tf_op jit(solution)/shard_map/pallas_call | solution.py:183
  11.8 0.7 collective-permute-start.2
  12.5 0.1 collective-permute-start.4
  12.6 0.6 collective-permute-start.6
  13.2 0.0 copy-done
  13.2 0.1 add_add_fusion.3
  13.3 13.4 %shard_map.55 = bf16[2,2,32,32,1024]{4,3,2,1,0:T(8,128)(2,1)} custom-call(s32[2,2]{1,0:T(2,128)} %first_ref.1, bf16[2,32,32,1024]{3,2,1,0:T(8,128)(2,1)} %coeffs_ref.1, bf16[2,2,32,32]{3,2,1,0:T(8,128)(2,1)} %cond_ref.1, bf16[2,2,32,32]{3,2,1,0:T(8,128)(2,1)} %val_ref.1), custom_call_target="tpu_custom_call" | custom-call | flops 6442450944 | bytes 12582912 | tf_op jit(solution)/shard_map/pallas_call | solution.py:90
  26.7 0.1 add_add_fusion.2
  26.7 0.0 collective-permute-done.next_ref
  26.7 7.4 %shard_map.57 = (f32[64,2048]{1,0:T(8,128)S(1)}, f32[64,2048]{1,0:T(8,128)S(1)}, bf16[128,2048]{1,0:T(8,128)(2,1)S(1)}) custom-call(s32[5]{0:T(128)S(1)} %get-tuple-element.36.pick_ref, bf16[2,1024,1024]{2,1,0:T(8,128)(2,1)} %bitcast.10, bf16[2,1024,256]{2,1,0:T(8,128)(2,1)} %collective-permute-done.next_ref, bf16[2,2,1024,1024]{3,2,1,0:T(8,128)(2,1)} %bitcast.14), custom_call_target="tpu_custom_call" | custom-call | flops 2147483648 | bytes 8388608 | tf_op jit(solution)/shard_map/pallas_call | solution.py:259
  34.2 0.0 collective-permute-done.2.next_ref
  34.2 5.5 %shard_map.59 = (f32[64,2048]{1,0:T(8,128)S(1)}, f32[64,2048]{1,0:T(8,128)S(1)}, bf16[128,2048]{1,0:T(8,128)(2,1)S(1)}) custom-call(s32[5]{0:T(128)S(1)} %get-tuple-element.40.pick_ref, bf16[2,1024,1024]{2,1,0:T(8,128)(2,1)} %bitcast.11, bf16[2,256,1024]{2,1,0:T(8,128)(2,1)S(1)} %collective-permute-done.2.next_ref, bf16[2,2,1024,1024]{3,2,1,0:T(8,128)(2,1)} %bitcast.15), custom_call_target="tpu_custom_call" | custom-call | flops 2147483648 | bytes 8388608 | tf_op jit(solution)/shard_map/pallas_call | solution.py:259
  39.8 3.0 %collective-permute-done.4.next_ref = bf16[2,256,1024]{2,1,0:T(8,128)(2,1)S(1)} collective-permute-done((bf16[2,256,1024]{2,1,0:T(8,128)(2,1)}, bf16[2,256,1024]{2,1,0:T(8,128)(2,1)S(1)}, u32[]{:S(2)}, u32[]{:S(2)}) %collective-permute-start.4) | collective-permute-done | bytes 1048608 | tf_op jit(solution)/shard_map/ppermute | solution.py:17
  42.7 5.5 %shard_map.60 = (f32[64,2048]{1,0:T(8,128)S(1)}, f32[64,2048]{1,0:T(8,128)S(1)}, bf16[128,2048]{1,0:T(8,128)(2,1)S(1)}) custom-call(s32[5]{0:T(128)S(1)} %get-tuple-element.45.pick_ref, bf16[2,1024,1024]{2,1,0:T(8,128)(2,1)} %bitcast.12, bf16[2,256,1024]{2,1,0:T(8,128)(2,1)S(1)} %collective-permute-done.4.next_ref, bf16[2,2,1024,1024]{3,2,1,0:T(8,128)(2,1)} %bitcast.16), custom_call_target="tpu_custom_call" | custom-call | flops 2147483648 | bytes 8388608 | tf_op jit(solution)/shard_map/pallas_call | solution.py:259
  48.2 0.1 collective-permute-start.5
  48.3 0.5 collective-permute-start.3
  48.8 0.1 collective-permute-start.1
  48.9 5.1 %collective-permute-done.6.next_ref = bf16[2,256,1024]{2,1,0:T(8,128)(2,1)S(1)} collective-permute-done((bf16[2,256,1024]{2,1,0:T(8,128)(2,1)}, bf16[2,256,1024]{2,1,0:T(8,128)(2,1)S(1)}, u32[]{:S(2)}, u32[]{:S(2)}) %collective-permute-start.6) | collective-permute-done | bytes 1048608 | tf_op jit(solution)/shard_map/ppermute | solution.py:17
  54.0 0.0 collective-permute-done.5.refs_8_
  54.0 0.0 collective-permute-done.3.refs_5_
  54.0 0.0 collective-permute-done.1.refs_2_
  54.0 0.3 shard_map.61
  54.3 0.1 collective-permute-start.9
  54.3 0.1 collective-permute-start.10
  54.4 3.4 %collective-permute-start.11 = (bf16[64,2048]{1,0:T(8,128)(2,1)S(1)}, bf16[64,2048]{1,0:T(8,128)(2,1)S(1)}, u32[]{:S(2)}, u32[]{:S(2)}) collective-permute-start(bf16[64,2048]{1,0:T(8,128)(2,1)S(1)} %get-tuple-element.57), channel_id=1, source_target_pairs={{0,4},{1,5},{2,6},{3,7},{4,0},{5,1},{6,2},{7,3},{8,12},{9,13},{10,... | collective-permute-start | bytes 786440 | tf_op jit(solution)/shard_map/ppermute | solution.py:17
  57.8 5.5 %shard_map.62 = (f32[64,2048]{1,0:T(8,128)S(1)}, f32[64,2048]{1,0:T(8,128)S(1)}, bf16[128,2048]{1,0:T(8,128)(2,1)S(1)}) custom-call(s32[5]{0:T(128)S(1)} %get-tuple-element.60.pick_ref, bf16[2,1024,1024]{2,1,0:T(8,128)(2,1)} %bitcast.13, bf16[2,256,1024]{2,1,0:T(8,128)(2,1)S(1)} %collective-permute-done.6.next_ref, bf16[2,2,1024,1024]{3,2,1,0:T(8,128)(2,1)} %bitcast.17), custom_call_target="tpu_custom_call" | custom-call | flops 2147483648 | bytes 8388608 | tf_op jit(solution)/shard_map/pallas_call | solution.py:259
  63.3 0.1 collective-permute-start.7
  63.4 0.1 collective-permute-start.13
  63.5 4.0 %collective-permute-done.9 = bf16[64,2048]{1,0:T(8,128)(2,1)S(1)} collective-permute-done((bf16[64,2048]{1,0:T(8,128)(2,1)S(1)}, bf16[64,2048]{1,0:T(8,128)(2,1)S(1)}, u32[]{:S(2)}, u32[]{:S(2)}) %collective-permute-start.9) | collective-permute-done | bytes 262176 | tf_op jit(solution)/shard_map/ppermute | solution.py:17
  67.5 0.0 collective-permute-start.14
  67.5 0.0 collective-permute-done.10
  67.5 1.4 %collective-permute-done.11 = bf16[64,2048]{1,0:T(8,128)(2,1)S(1)} collective-permute-done((bf16[64,2048]{1,0:T(8,128)(2,1)S(1)}, bf16[64,2048]{1,0:T(8,128)(2,1)S(1)}, u32[]{:S(2)}, u32[]{:S(2)}) %collective-permute-start.11) | collective-permute-done | bytes 262176 | tf_op jit(solution)/shard_map/ppermute | solution.py:17
  68.9 0.1 add_convert_fusion
  69.0 2.0 %collective-permute-start.12 = (bf16[64,2048]{1,0:T(8,128)(2,1)S(1)}, bf16[64,2048]{1,0:T(8,128)(2,1)S(1)}, u32[]{:S(2)}, u32[]{:S(2)}) collective-permute-start(bf16[64,2048]{1,0:T(8,128)(2,1)S(1)} %add_convert_fusion), channel_id=1, source_target_pairs={{0,8},{1,9},{2,10},{3,11},{4,12},{5,13},{6,14},{7,15},{8,0},{9,1},... | collective-permute-start | bytes 786440 | tf_op jit(solution)/shard_map/ppermute | solution.py:17
  71.0 0.0 collective-permute-done.7.core_ref
  71.0 0.6 collective-permute-start.8
  71.6 8.5 %collective-permute-done.13.refs_2_ = bf16[64,2048]{1,0:T(8,128)(2,1)S(1)} collective-permute-done((bf16[64,2048]{1,0:T(8,128)(2,1)S(1)}, bf16[64,2048]{1,0:T(8,128)(2,1)S(1)}, u32[]{:S(2)}, u32[]{:S(2)}) %collective-permute-start.13) | collective-permute-done | bytes 262176 | tf_op jit(solution)/shard_map/ppermute | solution.py:17
  80.1 4.4 %collective-permute-done.14.refs_3_ = bf16[64,2048]{1,0:T(8,128)(2,1)S(1)} collective-permute-done((bf16[64,2048]{1,0:T(8,128)(2,1)S(1)}, bf16[64,2048]{1,0:T(8,128)(2,1)S(1)}, u32[]{:S(2)}, u32[]{:S(2)}) %collective-permute-start.14) | collective-permute-done | bytes 262176 | tf_op jit(solution)/shard_map/ppermute | solution.py:17
  84.5 0.0 collective-permute-done.12.refs_1_
  84.5 0.3 collective-permute-done.8.refs_0_
  84.8 1.1 %shard_map.63 = f32[64,2,1024]{2,1,0:T(2,128)} custom-call(f32[64,2048]{1,0:T(8,128)S(1)} %get-tuple-element.62.mine_ref, bf16[128,2048]{1,0:T(8,128)(2,1)S(1)} %collective-permute-done.7.core_ref, bf16[64,2048]{1,0:T(8,128)(2,1)S(1)} %collective-permute-done.8.refs_0_, bf16[64,2048]{1,0:T(8,128)(2,1)S(1)} %collective-permute-done.12.refs_1_, ...), custom_call_target="tpu_custom_call" | custom-call | flops 655360 | bytes 2097152 | tf_op jit(solution)/shard_map/pallas_call | solution.py:335
  (2 shorter events, 0.1 us)
Async XLA Ops:
  0.0 13.2 %copy-start = (s32[2]{0:T(128)S(1)}, s32[2]{0:T(128)}, u32[]{:S(2)}) copy-start(s32[2]{0:T(128)} %param.8) | copy-start | bytes 28
  2.1 24.6 %collective-permute-start = (bf16[2,1024,256]{2,1,0:T(8,128)(2,1)}, bf16[2,1024,256]{2,1,0:T(8,128)(2,1)}, u32[]{:S(2)}, u32[]{:S(2)}) collective-permute-start(bf16[2,1024,256]{2,1,0:T(8,128)(2,1)} %shard_map.56), channel_id=1, source_target_pairs={{0,15},{1,0},{2,1},{3,2},{4,3},{5,4},{6,5},{7,6},{8,7},{9,8},{10,9... | collective-permute-start | bytes 3145736 | tf_op jit(solution)/shard_map/ppermute | solution.py:17
  11.8 22.4 %collective-permute-start.2 = (bf16[2,256,1024]{2,1,0:T(8,128)(2,1)}, bf16[2,256,1024]{2,1,0:T(8,128)(2,1)S(1)}, u32[]{:S(2)}, u32[]{:S(2)}) collective-permute-start(bf16[2,256,1024]{2,1,0:T(8,128)(2,1)} %get-tuple-element.42), channel_id=1, source_target_pairs={{0,15},{1,0},{2,1},{3,2},{4,3},{5,4},{6,5},{7,6},{8,7},{9,8},{10,9... | collective-permute-start | bytes 3145736 | tf_op jit(solution)/shard_map/ppermute | solution.py:17
  12.5 30.2 %collective-permute-start.4 = (bf16[2,256,1024]{2,1,0:T(8,128)(2,1)}, bf16[2,256,1024]{2,1,0:T(8,128)(2,1)S(1)}, u32[]{:S(2)}, u32[]{:S(2)}) collective-permute-start(bf16[2,256,1024]{2,1,0:T(8,128)(2,1)} %get-tuple-element.46), channel_id=1, source_target_pairs={{0,15},{1,0},{2,1},{3,2},{4,3},{5,4},{6,5},{7,6},{8,7},{9,8},{10,9... | collective-permute-start | bytes 3145736 | tf_op jit(solution)/shard_map/ppermute | solution.py:17
  12.6 41.3 %collective-permute-start.6 = (bf16[2,256,1024]{2,1,0:T(8,128)(2,1)}, bf16[2,256,1024]{2,1,0:T(8,128)(2,1)S(1)}, u32[]{:S(2)}, u32[]{:S(2)}) collective-permute-start(bf16[2,256,1024]{2,1,0:T(8,128)(2,1)} %get-tuple-element.48), channel_id=1, source_target_pairs={{0,15},{1,0},{2,1},{3,2},{4,3},{5,4},{6,5},{7,6},{8,7},{9,8},{10,9... | collective-permute-start | bytes 3145736 | tf_op jit(solution)/shard_map/ppermute | solution.py:17
  48.2 5.8 %collective-permute-start.5 = (bf16[128,2048]{1,0:T(8,128)(2,1)S(1)}, bf16[128,2048]{1,0:T(8,128)(2,1)S(1)}, u32[]{:S(2)}, u32[]{:S(2)}) collective-permute-start(bf16[128,2048]{1,0:T(8,128)(2,1)S(1)} %get-tuple-element.47), channel_id=1, source_target_pairs={{0,1},{1,0},{2,3},{3,2},{4,5},{5,4},{6,7},{7,6},{8,9},{9,8},{10,11... | collective-permute-start | bytes 1572872 | tf_op jit(solution)/shard_map/ppermute | solution.py:17
  48.3 5.7 %collective-permute-start.3 = (bf16[128,2048]{1,0:T(8,128)(2,1)S(1)}, bf16[128,2048]{1,0:T(8,128)(2,1)S(1)}, u32[]{:S(2)}, u32[]{:S(2)}) collective-permute-start(bf16[128,2048]{1,0:T(8,128)(2,1)S(1)} %get-tuple-element.43), channel_id=1, source_target_pairs={{0,1},{1,0},{2,3},{3,2},{4,5},{5,4},{6,7},{7,6},{8,9},{9,8},{10,11... | collective-permute-start | bytes 1572872 | tf_op jit(solution)/shard_map/ppermute | solution.py:17
  48.8 5.2 %collective-permute-start.1 = (bf16[128,2048]{1,0:T(8,128)(2,1)S(1)}, bf16[128,2048]{1,0:T(8,128)(2,1)S(1)}, u32[]{:S(2)}, u32[]{:S(2)}) collective-permute-start(bf16[128,2048]{1,0:T(8,128)(2,1)S(1)} %get-tuple-element.39), channel_id=1, source_target_pairs={{0,1},{1,0},{2,3},{3,2},{4,5},{5,4},{6,7},{7,6},{8,9},{9,8},{10,11... | collective-permute-start | bytes 1572872 | tf_op jit(solution)/shard_map/ppermute | solution.py:17
  54.3 13.2 %collective-permute-start.9 = (bf16[64,2048]{1,0:T(8,128)(2,1)S(1)}, bf16[64,2048]{1,0:T(8,128)(2,1)S(1)}, u32[]{:S(2)}, u32[]{:S(2)}) collective-permute-start(bf16[64,2048]{1,0:T(8,128)(2,1)S(1)} %get-tuple-element.55), channel_id=1, source_target_pairs={{0,2},{1,7},{2,0},{3,5},{4,6},{5,3},{6,4},{7,1},{8,10},{9,15},{10,... | collective-permute-start | bytes 786440 | tf_op jit(solution)/shard_map/ppermute | solution.py:17
  54.3 13.2 %collective-permute-start.10 = (bf16[64,2048]{1,0:T(8,128)(2,1)S(1)}, bf16[64,2048]{1,0:T(8,128)(2,1)S(1)}, u32[]{:S(2)}, u32[]{:S(2)}) collective-permute-start(bf16[64,2048]{1,0:T(8,128)(2,1)S(1)} %get-tuple-element.56), channel_id=1, source_target_pairs={{0,6},{1,3},{2,4},{3,1},{4,2},{5,7},{6,0},{7,5},{8,14},{9,11},{10,... | collective-permute-start | bytes 786440 | tf_op jit(solution)/shard_map/ppermute | solution.py:17
  54.4 14.4 %collective-permute-start.11 = (bf16[64,2048]{1,0:T(8,128)(2,1)S(1)}, bf16[64,2048]{1,0:T(8,128)(2,1)S(1)}, u32[]{:S(2)}, u32[]{:S(2)}) collective-permute-start(bf16[64,2048]{1,0:T(8,128)(2,1)S(1)} %get-tuple-element.57), channel_id=1, source_target_pairs={{0,4},{1,5},{2,6},{3,7},{4,0},{5,1},{6,2},{7,3},{8,12},{9,13},{10,... | collective-permute-start | bytes 786440 | tf_op jit(solution)/shard_map/ppermute | solution.py:17
  63.3 7.7 %collective-permute-start.7 = (bf16[128,2048]{1,0:T(8,128)(2,1)S(1)}, bf16[128,2048]{1,0:T(8,128)(2,1)S(1)}, u32[]{:S(2)}, u32[]{:S(2)}) collective-permute-start(bf16[128,2048]{1,0:T(8,128)(2,1)S(1)} %get-tuple-element.63), channel_id=1, source_target_pairs={{0,1},{1,0},{2,3},{3,2},{4,5},{5,4},{6,7},{7,6},{8,9},{9,8},{10,11... | collective-permute-start | bytes 1572872 | tf_op jit(solution)/shard_map/ppermute | solution.py:17
  63.4 16.7 %collective-permute-start.13 = (bf16[64,2048]{1,0:T(8,128)(2,1)S(1)}, bf16[64,2048]{1,0:T(8,128)(2,1)S(1)}, u32[]{:S(2)}, u32[]{:S(2)}) collective-permute-start(bf16[64,2048]{1,0:T(8,128)(2,1)S(1)} %get-tuple-element.58), channel_id=1, source_target_pairs={{0,4},{1,5},{2,6},{3,7},{4,0},{5,1},{6,2},{7,3},{8,12},{9,13},{10,... | collective-permute-start | bytes 786440 | tf_op jit(solution)/shard_map/ppermute | solution.py:17
  67.5 17.0 %collective-permute-start.14 = (bf16[64,2048]{1,0:T(8,128)(2,1)S(1)}, bf16[64,2048]{1,0:T(8,128)(2,1)S(1)}, u32[]{:S(2)}, u32[]{:S(2)}) collective-permute-start(bf16[64,2048]{1,0:T(8,128)(2,1)S(1)} %get-tuple-element.59), channel_id=1, source_target_pairs={{0,6},{1,7},{2,4},{3,5},{4,2},{5,3},{6,0},{7,1},{8,14},{9,15},{10,... | collective-permute-start | bytes 786440 | tf_op jit(solution)/shard_map/ppermute | solution.py:17
  69.0 15.5 %collective-permute-start.12 = (bf16[64,2048]{1,0:T(8,128)(2,1)S(1)}, bf16[64,2048]{1,0:T(8,128)(2,1)S(1)}, u32[]{:S(2)}, u32[]{:S(2)}) collective-permute-start(bf16[64,2048]{1,0:T(8,128)(2,1)S(1)} %add_convert_fusion), channel_id=1, source_target_pairs={{0,8},{1,9},{2,10},{3,11},{4,12},{5,13},{6,14},{7,15},{8,0},{9,1},... | collective-permute-start | bytes 786440 | tf_op jit(solution)/shard_map/ppermute | solution.py:17
  71.0 13.8 %collective-permute-start.8 = (bf16[64,2048]{1,0:T(8,128)(2,1)S(1)}, bf16[64,2048]{1,0:T(8,128)(2,1)S(1)}, u32[]{:S(2)}, u32[]{:S(2)}) collective-permute-start(bf16[64,2048]{1,0:T(8,128)(2,1)S(1)} %add_convert_fusion.1), channel_id=1, source_target_pairs={{0,2},{1,3},{2,0},{3,1},{4,6},{5,7},{6,4},{7,5},{8,10},{9,11},{10,... | collective-permute-start | bytes 786440 | tf_op jit(solution)/shard_map/ppermute | solution.py:17

commit v24 on v23

--- a/solution.py
+++ b/solution.py
@@ -391,9 +391,11 @@
         permute(sends[turn], lambda i: i ^ (2 if i % 2 == turn else 6)) for turn in range(2)
     ]
     arrived.append(over(sends[2], 4))
-    near = over(sends[3], 4), over(sends[4], 6)
     mine_1, _ = lax.optimization_barrier((mine_1, step_3[0]))
-    pair = over(total_of(mine_1, *arrived), 8)
+    pair = total_of(mine_1, *arrived)
+    cross_2, _ = lax.optimization_barrier((sends[4], pair))
+    pair = over(pair, 8)
+    near = over(sends[3], 4), over(cross_2, 6)
     mine_3, other_3, core_3 = step_3
     across_3 = over(other_3 + core_3[half:].astype(jnp.float32), 2)
     return closed(modes, norm_factor, mine_3, core_3, across_3, pair, *near)

time: 86.2 us -> 87.1 us (1.010)
  no operation moved by 1% of the time
where the time goes in v24:
time: 87.1 us; the launch traced here: 86.8 us
  Pallas kernels  44.9 us (52%)
  waiting for transfers between devices  27 us (31%)
  starting transfers between devices  14.5 us (17%)
    ppermute x15, waiting for transfers between devices, permute(): lax.ppermute(x, 'ka', [(i, j % size) for i, j in pairs if j is not None])  27 us
    pallas_call x4, Pallas kernels, rows_of(): pl.pallas_call(functools.partial(rows_kernel, turned), out_shape=[jax.Sha...  23.8 us
    ppermute x15, starting transfers between devices, permute(): lax.ppermute(x, 'ka', [(i, j % size) for i, j in pairs if j is not None])  14.5 us
    pallas_call x1, Pallas kernels, products_of(): pl.pallas_call(products_kernel, out_shape=jax.ShapeDtypeStruct((k_local,...  13.4 us
    pallas_call x1, Pallas kernels, turned_pieces(): pl.pallas_call(turn_kernel, out_shape=[jax.ShapeDtypeStruct((k_local, wid...  4.19 us
    pallas_call x1, Pallas kernels, cut_piece(): pl.pallas_call(cut_kernel, out_shape=jax.ShapeDtypeStruct((k_local, depth...  2.13 us
  transfers between devices with their start and end apart: 15, of which 7 were waited for; matrix products, arithmetic and copies ran while one was open for 0% of the time, Pallas kernels for 48%

profile of v24, /device:TPU:0, one launch (start us, length us, event | category | flops | bytes accessed | tf_op | source)
XLA Modules:
  0.0 86.8 jit_solution(12426211628386477176)
XLA Ops:
  0.0 0.0 copy-start
  0.0 2.1 %shard_map.56 = bf16[2,1024,256]{2,1,0:T(8,128)(2,1)} custom-call(bf16[2,1024,1024]{2,1,0:T(8,128)(2,1)} %bitcast.8), custom_call_target="tpu_custom_call" | custom-call | bytes 2097152 | tf_op jit(solution)/shard_map/pallas_call | solution.py:145
  2.1 5.5 %collective-permute-start = (bf16[2,1024,256]{2,1,0:T(8,128)(2,1)}, bf16[2,1024,256]{2,1,0:T(8,128)(2,1)}, u32[]{:S(2)}, u32[]{:S(2)}) collective-permute-start(bf16[2,1024,256]{2,1,0:T(8,128)(2,1)} %shard_map.56), channel_id=1, source_target_pairs={{0,15},{1,0},{2,1},{3,2},{4,3},{5,4},{6,5},{7,6},{8,7},{9,8},{10,9... | collective-permute-start | bytes 3145736 | tf_op jit(solution)/shard_map/ppermute | solution.py:17
  7.6 4.2 %shard_map.58 = (bf16[2,256,1024]{2,1,0:T(8,128)(2,1)}, bf16[2,256,1024]{2,1,0:T(8,128)(2,1)}, bf16[2,256,1024]{2,1,0:T(8,128)(2,1)}) custom-call(bf16[2,1024,1024]{2,1,0:T(8,128)(2,1)} %bitcast.9), custom_call_target="tpu_custom_call" | custom-call | bytes 6291456 | tf_op jit(solution)/shard_map/pallas_call | solution.py:183
  11.8 0.7 collective-permute-start.2
  12.5 0.1 collective-permute-start.4
  12.6 0.6 collective-permute-start.6
  13.2 0.0 copy-done
  13.2 0.1 add_add_fusion.3
  13.3 13.4 %shard_map.55 = bf16[2,2,32,32,1024]{4,3,2,1,0:T(8,128)(2,1)} custom-call(s32[2,2]{1,0:T(2,128)} %first_ref.1, bf16[2,32,32,1024]{3,2,1,0:T(8,128)(2,1)} %coeffs_ref.1, bf16[2,2,32,32]{3,2,1,0:T(8,128)(2,1)} %cond_ref.1, bf16[2,2,32,32]{3,2,1,0:T(8,128)(2,1)} %val_ref.1), custom_call_target="tpu_custom_call" | custom-call | flops 6442450944 | bytes 12582912 | tf_op jit(solution)/shard_map/pallas_call | solution.py:90
  26.7 0.1 add_add_fusion.2
  26.7 0.0 collective-permute-done.next_ref
  26.7 7.4 %shard_map.57 = (f32[64,2048]{1,0:T(8,128)S(1)}, f32[64,2048]{1,0:T(8,128)S(1)}, bf16[128,2048]{1,0:T(8,128)(2,1)S(1)}) custom-call(s32[5]{0:T(128)S(1)} %get-tuple-element.37.pick_ref, bf16[2,1024,1024]{2,1,0:T(8,128)(2,1)} %bitcast.10, bf16[2,1024,256]{2,1,0:T(8,128)(2,1)} %collective-permute-done.next_ref, bf16[2,2,1024,1024]{3,2,1,0:T(8,128)(2,1)} %bitcast.14), custom_call_target="tpu_custom_call" | custom-call | flops 2147483648 | bytes 8388608 | tf_op jit(solution)/shard_map/pallas_call | solution.py:259
  34.2 0.0 collective-permute-done.2.next_ref
  34.2 5.5 %shard_map.59 = (f32[64,2048]{1,0:T(8,128)S(1)}, f32[64,2048]{1,0:T(8,128)S(1)}, bf16[128,2048]{1,0:T(8,128)(2,1)S(1)}) custom-call(s32[5]{0:T(128)S(1)} %get-tuple-element.41.pick_ref, bf16[2,1024,1024]{2,1,0:T(8,128)(2,1)} %bitcast.11, bf16[2,256,1024]{2,1,0:T(8,128)(2,1)S(1)} %collective-permute-done.2.next_ref, bf16[2,2,1024,1024]{3,2,1,0:T(8,128)(2,1)} %bitcast.15), custom_call_target="tpu_custom_call" | custom-call | flops 2147483648 | bytes 8388608 | tf_op jit(solution)/shard_map/pallas_call | solution.py:259
  39.7 3.0 %collective-permute-done.4.next_ref = bf16[2,256,1024]{2,1,0:T(8,128)(2,1)S(1)} collective-permute-done((bf16[2,256,1024]{2,1,0:T(8,128)(2,1)}, bf16[2,256,1024]{2,1,0:T(8,128)(2,1)S(1)}, u32[]{:S(2)}, u32[]{:S(2)}) %collective-permute-start.4) | collective-permute-done | bytes 1048608 | tf_op jit(solution)/shard_map/ppermute | solution.py:17
  42.7 5.5 %shard_map.60 = (f32[64,2048]{1,0:T(8,128)S(1)}, f32[64,2048]{1,0:T(8,128)S(1)}, bf16[128,2048]{1,0:T(8,128)(2,1)S(1)}) custom-call(s32[5]{0:T(128)S(1)} %get-tuple-element.46.pick_ref, bf16[2,1024,1024]{2,1,0:T(8,128)(2,1)} %bitcast.12, bf16[2,256,1024]{2,1,0:T(8,128)(2,1)S(1)} %collective-permute-done.4.next_ref, bf16[2,2,1024,1024]{3,2,1,0:T(8,128)(2,1)} %bitcast.16), custom_call_target="tpu_custom_call" | custom-call | flops 2147483648 | bytes 8388608 | tf_op jit(solution)/shard_map/pallas_call | solution.py:259
  48.2 0.1 collective-permute-start.5
  48.3 0.5 collective-permute-start.3
  48.8 0.1 collective-permute-start.1
  48.8 5.1 %collective-permute-done.6.next_ref = bf16[2,256,1024]{2,1,0:T(8,128)(2,1)S(1)} collective-permute-done((bf16[2,256,1024]{2,1,0:T(8,128)(2,1)}, bf16[2,256,1024]{2,1,0:T(8,128)(2,1)S(1)}, u32[]{:S(2)}, u32[]{:S(2)}) %collective-permute-start.6) | collective-permute-done | bytes 1048608 | tf_op jit(solution)/shard_map/ppermute | solution.py:17
  54.0 0.0 collective-permute-done.5.refs_8_
  54.0 0.0 collective-permute-done.3.refs_5_
  54.0 0.0 collective-permute-done.1.refs_2_
  54.0 0.3 shard_map.61
  54.3 0.1 collective-permute-start.9
  54.3 0.1 collective-permute-start.10
  54.4 3.4 %collective-permute-start.11 = (bf16[64,2048]{1,0:T(8,128)(2,1)S(1)}, bf16[64,2048]{1,0:T(8,128)(2,1)S(1)}, u32[]{:S(2)}, u32[]{:S(2)}) collective-permute-start(bf16[64,2048]{1,0:T(8,128)(2,1)S(1)} %get-tuple-element.58), channel_id=1, source_target_pairs={{0,4},{1,5},{2,6},{3,7},{4,0},{5,1},{6,2},{7,3},{8,12},{9,13},{10,... | collective-permute-start | bytes 786440 | tf_op jit(solution)/shard_map/ppermute | solution.py:17
  57.8 5.5 %shard_map.62 = (f32[64,2048]{1,0:T(8,128)S(1)}, f32[64,2048]{1,0:T(8,128)S(1)}, bf16[128,2048]{1,0:T(8,128)(2,1)S(1)}) custom-call(s32[5]{0:T(128)S(1)} %get-tuple-element.61.pick_ref, bf16[2,1024,1024]{2,1,0:T(8,128)(2,1)} %bitcast.13, bf16[2,256,1024]{2,1,0:T(8,128)(2,1)S(1)} %collective-permute-done.6.next_ref, bf16[2,2,1024,1024]{3,2,1,0:T(8,128)(2,1)} %bitcast.17), custom_call_target="tpu_custom_call" | custom-call | flops 2147483648 | bytes 8388608 | tf_op jit(solution)/shard_map/pallas_call | solution.py:259
  63.3 0.1 collective-permute-start.7
  63.4 0.1 collective-permute-start.13
  63.5 4.0 %collective-permute-done.9 = bf16[64,2048]{1,0:T(8,128)(2,1)S(1)} collective-permute-done((bf16[64,2048]{1,0:T(8,128)(2,1)S(1)}, bf16[64,2048]{1,0:T(8,128)(2,1)S(1)}, u32[]{:S(2)}, u32[]{:S(2)}) %collective-permute-start.9) | collective-permute-done | bytes 262176 | tf_op jit(solution)/shard_map/ppermute | solution.py:17
  67.5 0.0 collective-permute-done.10
  67.5 1.4 %collective-permute-done.11 = bf16[64,2048]{1,0:T(8,128)(2,1)S(1)} collective-permute-done((bf16[64,2048]{1,0:T(8,128)(2,1)S(1)}, bf16[64,2048]{1,0:T(8,128)(2,1)S(1)}, u32[]{:S(2)}, u32[]{:S(2)}) %collective-permute-start.11) | collective-permute-done | bytes 262176 | tf_op jit(solution)/shard_map/ppermute | solution.py:17
  68.9 0.1 convert_add_fusion
  69.0 1.8 %collective-permute-start.12 = (bf16[64,2048]{1,0:T(8,128)(2,1)S(1)}, bf16[64,2048]{1,0:T(8,128)(2,1)S(1)}, u32[]{:S(2)}, u32[]{:S(2)}) collective-permute-start(bf16[64,2048]{1,0:T(8,128)(2,1)S(1)} %convert_add_fusion), channel_id=1, source_target_pairs={{0,8},{1,9},{2,10},{3,11},{4,12},{5,13},{6,14},{7,15},{8,0},{9,1},... | collective-permute-start | bytes 786440 | tf_op jit(solution)/shard_map/ppermute | solution.py:17
  70.8 0.6 collective-permute-start.14
  71.4 0.0 collective-permute-done.7.core_ref
  71.4 0.9 collective-permute-start.8
  72.3 4.8 %collective-permute-done.13.refs_2_ = bf16[64,2048]{1,0:T(8,128)(2,1)S(1)} collective-permute-done((bf16[64,2048]{1,0:T(8,128)(2,1)S(1)}, bf16[64,2048]{1,0:T(8,128)(2,1)S(1)}, u32[]{:S(2)}, u32[]{:S(2)}) %collective-permute-start.13) | collective-permute-done | bytes 262176 | tf_op jit(solution)/shard_map/ppermute | solution.py:17
  77.2 7.3 %collective-permute-done.14.refs_3_ = bf16[64,2048]{1,0:T(8,128)(2,1)S(1)} collective-permute-done((bf16[64,2048]{1,0:T(8,128)(2,1)S(1)}, bf16[64,2048]{1,0:T(8,128)(2,1)S(1)}, u32[]{:S(2)}, u32[]{:S(2)}) %collective-permute-start.14) | collective-permute-done | bytes 262176 | tf_op jit(solution)/shard_map/ppermute | solution.py:17
  84.5 0.0 collective-permute-done.12.refs_1_
  84.5 1.2 %collective-permute-done.8.refs_0_ = bf16[64,2048]{1,0:T(8,128)(2,1)S(1)} collective-permute-done((bf16[64,2048]{1,0:T(8,128)(2,1)S(1)}, bf16[64,2048]{1,0:T(8,128)(2,1)S(1)}, u32[]{:S(2)}, u32[]{:S(2)}) %collective-permute-start.8) | collective-permute-done | bytes 262176 | tf_op jit(solution)/shard_map/ppermute | solution.py:17
  85.7 1.1 %shard_map.63 = f32[64,2,1024]{2,1,0:T(2,128)} custom-call(f32[64,2048]{1,0:T(8,128)S(1)} %get-tuple-element.63.mine_ref, bf16[128,2048]{1,0:T(8,128)(2,1)S(1)} %collective-permute-done.7.core_ref, bf16[64,2048]{1,0:T(8,128)(2,1)S(1)} %collective-permute-done.8.refs_0_, bf16[64,2048]{1,0:T(8,128)(2,1)S(1)} %collective-permute-done.12.refs_1_, ...), custom_call_target="tpu_custom_call" | custom-call | flops 655360 | bytes 2097152 | tf_op jit(solution)/shard_map/pallas_call | solution.py:335
  (2 shorter events, 0.1 us)
Async XLA Ops:
  0.0 13.2 %copy-start = (s32[2]{0:T(128)S(1)}, s32[2]{0:T(128)}, u32[]{:S(2)}) copy-start(s32[2]{0:T(128)} %param.8) | copy-start | bytes 28
  2.1 24.6 %collective-permute-start = (bf16[2,1024,256]{2,1,0:T(8,128)(2,1)}, bf16[2,1024,256]{2,1,0:T(8,128)(2,1)}, u32[]{:S(2)}, u32[]{:S(2)}) collective-permute-start(bf16[2,1024,256]{2,1,0:T(8,128)(2,1)} %shard_map.56), channel_id=1, source_target_pairs={{0,15},{1,0},{2,1},{3,2},{4,3},{5,4},{6,5},{7,6},{8,7},{9,8},{10,9... | collective-permute-start | bytes 3145736 | tf_op jit(solution)/shard_map/ppermute | solution.py:17
  11.8 22.4 %collective-permute-start.2 = (bf16[2,256,1024]{2,1,0:T(8,128)(2,1)}, bf16[2,256,1024]{2,1,0:T(8,128)(2,1)S(1)}, u32[]{:S(2)}, u32[]{:S(2)}) collective-permute-start(bf16[2,256,1024]{2,1,0:T(8,128)(2,1)} %get-tuple-element.43), channel_id=1, source_target_pairs={{0,15},{1,0},{2,1},{3,2},{4,3},{5,4},{6,5},{7,6},{8,7},{9,8},{10,9... | collective-permute-start | bytes 3145736 | tf_op jit(solution)/shard_map/ppermute | solution.py:17
  12.5 30.2 %collective-permute-start.4 = (bf16[2,256,1024]{2,1,0:T(8,128)(2,1)}, bf16[2,256,1024]{2,1,0:T(8,128)(2,1)S(1)}, u32[]{:S(2)}, u32[]{:S(2)}) collective-permute-start(bf16[2,256,1024]{2,1,0:T(8,128)(2,1)} %get-tuple-element.47), channel_id=1, source_target_pairs={{0,15},{1,0},{2,1},{3,2},{4,3},{5,4},{6,5},{7,6},{8,7},{9,8},{10,9... | collective-permute-start | bytes 3145736 | tf_op jit(solution)/shard_map/ppermute | solution.py:17
  12.6 41.3 %collective-permute-start.6 = (bf16[2,256,1024]{2,1,0:T(8,128)(2,1)}, bf16[2,256,1024]{2,1,0:T(8,128)(2,1)S(1)}, u32[]{:S(2)}, u32[]{:S(2)}) collective-permute-start(bf16[2,256,1024]{2,1,0:T(8,128)(2,1)} %get-tuple-element.49), channel_id=1, source_target_pairs={{0,15},{1,0},{2,1},{3,2},{4,3},{5,4},{6,5},{7,6},{8,7},{9,8},{10,9... | collective-permute-start | bytes 3145736 | tf_op jit(solution)/shard_map/ppermute | solution.py:17
  48.2 5.8 %collective-permute-start.5 = (bf16[128,2048]{1,0:T(8,128)(2,1)S(1)}, bf16[128,2048]{1,0:T(8,128)(2,1)S(1)}, u32[]{:S(2)}, u32[]{:S(2)}) collective-permute-start(bf16[128,2048]{1,0:T(8,128)(2,1)S(1)} %get-tuple-element.48), channel_id=1, source_target_pairs={{0,1},{1,0},{2,3},{3,2},{4,5},{5,4},{6,7},{7,6},{8,9},{9,8},{10,11... | collective-permute-start | bytes 1572872 | tf_op jit(solution)/shard_map/ppermute | solution.py:17
  48.3 5.7 %collective-permute-start.3 = (bf16[128,2048]{1,0:T(8,128)(2,1)S(1)}, bf16[128,2048]{1,0:T(8,128)(2,1)S(1)}, u32[]{:S(2)}, u32[]{:S(2)}) collective-permute-start(bf16[128,2048]{1,0:T(8,128)(2,1)S(1)} %get-tuple-element.44), channel_id=1, source_target_pairs={{0,1},{1,0},{2,3},{3,2},{4,5},{5,4},{6,7},{7,6},{8,9},{9,8},{10,11... | collective-permute-start | bytes 1572872 | tf_op jit(solution)/shard_map/ppermute | solution.py:17
  48.8 5.2 %collective-permute-start.1 = (bf16[128,2048]{1,0:T(8,128)(2,1)S(1)}, bf16[128,2048]{1,0:T(8,128)(2,1)S(1)}, u32[]{:S(2)}, u32[]{:S(2)}) collective-permute-start(bf16[128,2048]{1,0:T(8,128)(2,1)S(1)} %get-tuple-element.40), channel_id=1, source_target_pairs={{0,1},{1,0},{2,3},{3,2},{4,5},{5,4},{6,7},{7,6},{8,9},{9,8},{10,11... | collective-permute-start | bytes 1572872 | tf_op jit(solution)/shard_map/ppermute | solution.py:17
  54.3 13.2 %collective-permute-start.9 = (bf16[64,2048]{1,0:T(8,128)(2,1)S(1)}, bf16[64,2048]{1,0:T(8,128)(2,1)S(1)}, u32[]{:S(2)}, u32[]{:S(2)}) collective-permute-start(bf16[64,2048]{1,0:T(8,128)(2,1)S(1)} %get-tuple-element.56), channel_id=1, source_target_pairs={{0,2},{1,7},{2,0},{3,5},{4,6},{5,3},{6,4},{7,1},{8,10},{9,15},{10,... | collective-permute-start | bytes 786440 | tf_op jit(solution)/shard_map/ppermute | solution.py:17
  54.3 13.1 %collective-permute-start.10 = (bf16[64,2048]{1,0:T(8,128)(2,1)S(1)}, bf16[64,2048]{1,0:T(8,128)(2,1)S(1)}, u32[]{:S(2)}, u32[]{:S(2)}) collective-permute-start(bf16[64,2048]{1,0:T(8,128)(2,1)S(1)} %get-tuple-element.57), channel_id=1, source_target_pairs={{0,6},{1,3},{2,4},{3,1},{4,2},{5,7},{6,0},{7,5},{8,14},{9,11},{10,... | collective-permute-start | bytes 786440 | tf_op jit(solution)/shard_map/ppermute | solution.py:17
  54.4 14.4 %collective-permute-start.11 = (bf16[64,2048]{1,0:T(8,128)(2,1)S(1)}, bf16[64,2048]{1,0:T(8,128)(2,1)S(1)}, u32[]{:S(2)}, u32[]{:S(2)}) collective-permute-start(bf16[64,2048]{1,0:T(8,128)(2,1)S(1)} %get-tuple-element.58), channel_id=1, source_target_pairs={{0,4},{1,5},{2,6},{3,7},{4,0},{5,1},{6,2},{7,3},{8,12},{9,13},{10,... | collective-permute-start | bytes 786440 | tf_op jit(solution)/shard_map/ppermute | solution.py:17
  63.3 8.1 %collective-permute-start.7 = (bf16[128,2048]{1,0:T(8,128)(2,1)S(1)}, bf16[128,2048]{1,0:T(8,128)(2,1)S(1)}, u32[]{:S(2)}, u32[]{:S(2)}) collective-permute-start(bf16[128,2048]{1,0:T(8,128)(2,1)S(1)} %get-tuple-element.64), channel_id=1, source_target_pairs={{0,1},{1,0},{2,3},{3,2},{4,5},{5,4},{6,7},{7,6},{8,9},{9,8},{10,11... | collective-permute-start | bytes 1572872 | tf_op jit(solution)/shard_map/ppermute | solution.py:17
  63.4 13.8 %collective-permute-start.13 = (bf16[64,2048]{1,0:T(8,128)(2,1)S(1)}, bf16[64,2048]{1,0:T(8,128)(2,1)S(1)}, u32[]{:S(2)}, u32[]{:S(2)}) collective-permute-start(bf16[64,2048]{1,0:T(8,128)(2,1)S(1)} %get-tuple-element.59), channel_id=1, source_target_pairs={{0,4},{1,5},{2,6},{3,7},{4,0},{5,1},{6,2},{7,3},{8,12},{9,13},{10,... | collective-permute-start | bytes 786440 | tf_op jit(solution)/shard_map/ppermute | solution.py:17
  69.0 15.5 %collective-permute-start.12 = (bf16[64,2048]{1,0:T(8,128)(2,1)S(1)}, bf16[64,2048]{1,0:T(8,128)(2,1)S(1)}, u32[]{:S(2)}, u32[]{:S(2)}) collective-permute-start(bf16[64,2048]{1,0:T(8,128)(2,1)S(1)} %convert_add_fusion), channel_id=1, source_target_pairs={{0,8},{1,9},{2,10},{3,11},{4,12},{5,13},{6,14},{7,15},{8,0},{9,1},... | collective-permute-start | bytes 786440 | tf_op jit(solution)/shard_map/ppermute | solution.py:17
  70.8 13.7 %collective-permute-start.14 = (bf16[64,2048]{1,0:T(8,128)(2,1)S(1)}, bf16[64,2048]{1,0:T(8,128)(2,1)S(1)}, u32[]{:S(2)}, u32[]{:S(2)}) collective-permute-start(bf16[64,2048]{1,0:T(8,128)(2,1)S(1)} %get-tuple-element.68), channel_id=1, source_target_pairs={{0,6},{1,7},{2,4},{3,5},{4,2},{5,3},{6,0},{7,1},{8,14},{9,15},{10,... | collective-permute-start | bytes 786440 | tf_op jit(solution)/shard_map/ppermute | solution.py:17
  71.4 14.3 %collective-permute-start.8 = (bf16[64,2048]{1,0:T(8,128)(2,1)S(1)}, bf16[64,2048]{1,0:T(8,128)(2,1)S(1)}, u32[]{:S(2)}, u32[]{:S(2)}) collective-permute-start(bf16[64,2048]{1,0:T(8,128)(2,1)S(1)} %add_convert_fusion), channel_id=1, source_target_pairs={{0,2},{1,3},{2,0},{3,1},{4,6},{5,7},{6,4},{7,5},{8,10},{9,11},{10,... | collective-permute-start | bytes 786440 | tf_op jit(solution)/shard_map/ppermute | solution.py:17

commit v25 on v22

--- a/solution.py
+++ b/solution.py
@@ -388,7 +388,8 @@
     across_1 = over(sends[2], 2)
     near = over(sends[3], 4), over(sends[4], 6)
     mine_1, _ = lax.optimization_barrier((mine_1, step_3[0]))
-    pair = over(total_of(mine_1, across_1, *far), 8)
+    mine_1 = lax.optimization_barrier(total_of(mine_1, across_1))
+    pair = over(total_of(mine_1, *far), 8)
     mine_3, other_3, core_3 = step_3
     across_3 = over(other_3 + core_3[half:].astype(jnp.float32), 2)
     return closed(modes, norm_factor, mine_3, core_3, across_3, pair, *near)

time: 85.2 us -> 86 us (level)
  waiting for transfers between devices: 24.6 us -> 27.1 us
  starting transfers between devices: 14.7 us -> 12.8 us
    ppermute x15, waiting for transfers between devices: 24.6 us -> 27.1 us  [permute(): lax.ppermute(x, 'ka', [(i, j % size) for i, j in pairs if j is not None])]
    ppermute x15, starting transfers between devices: 14.7 us -> 12.8 us  [permute(): lax.ppermute(x, 'ka', [(i, j % size) for i, j in pairs if j is not None])]
  transfers between devices with their start and end apart: 15 -> 15, of which waited for: 7 -> 5; matrix products, arithmetic and copies ran while one was open for 0% -> 0% of each run, Pallas kernels for 49% -> 49%
where the time goes in v25:
time: 86 us; the launch traced here: 85.6 us
  Pallas kernels  45.1 us (52%)
  waiting for transfers between devices  27.1 us (32%)
  starting transfers between devices  12.8 us (15%)
    ppermute x15, waiting for transfers between devices, permute(): lax.ppermute(x, 'ka', [(i, j % size) for i, j in pairs if j is not None])  27.1 us
    pallas_call x4, Pallas kernels, rows_of(): pl.pallas_call(functools.partial(rows_kernel, turned), out_shape=[jax.Sha...  24.1 us
    pallas_call x1, Pallas kernels, products_of(): pl.pallas_call(products_kernel, out_shape=jax.ShapeDtypeStruct((k_local,...  13.4 us
    ppermute x15, starting transfers between devices, permute(): lax.ppermute(x, 'ka', [(i, j % size) for i, j in pairs if j is not None])  12.8 us
    pallas_call x1, Pallas kernels, turned_pieces(): pl.pallas_call(turn_kernel, out_shape=[jax.ShapeDtypeStruct((k_local, wid...  4.19 us
    pallas_call x1, Pallas kernels, cut_piece(): pl.pallas_call(cut_kernel, out_shape=jax.ShapeDtypeStruct((k_local, depth...  2.13 us
  transfers between devices with their start and end apart: 15, of which 5 were waited for; matrix products, arithmetic and copies ran while one was open for 0% of the time, Pallas kernels for 49%

profile of v25, /device:TPU:0, one launch (start us, length us, event | category | flops | bytes accessed | tf_op | source)
XLA Modules:
  0.0 85.6 jit_solution(17633864491135797225)
XLA Ops:
  0.0 0.0 copy-start
  0.0 2.1 %shard_map.56 = bf16[2,1024,256]{2,1,0:T(8,128)(2,1)} custom-call(bf16[2,1024,1024]{2,1,0:T(8,128)(2,1)} %bitcast.8), custom_call_target="tpu_custom_call" | custom-call | bytes 2097152 | tf_op jit(solution)/shard_map/pallas_call | solution.py:145
  2.1 5.5 %collective-permute-start = (bf16[2,1024,256]{2,1,0:T(8,128)(2,1)}, bf16[2,1024,256]{2,1,0:T(8,128)(2,1)}, u32[]{:S(2)}, u32[]{:S(2)}) collective-permute-start(bf16[2,1024,256]{2,1,0:T(8,128)(2,1)} %shard_map.56), channel_id=1, source_target_pairs={{0,15},{1,0},{2,1},{3,2},{4,3},{5,4},{6,5},{7,6},{8,7},{9,8},{10,9... | collective-permute-start | bytes 3145736 | tf_op jit(solution)/shard_map/ppermute | solution.py:17
  7.6 4.2 %shard_map.58 = (bf16[2,256,1024]{2,1,0:T(8,128)(2,1)}, bf16[2,256,1024]{2,1,0:T(8,128)(2,1)}, bf16[2,256,1024]{2,1,0:T(8,128)(2,1)}) custom-call(bf16[2,1024,1024]{2,1,0:T(8,128)(2,1)} %bitcast.9), custom_call_target="tpu_custom_call" | custom-call | bytes 6291456 | tf_op jit(solution)/shard_map/pallas_call | solution.py:183
  11.8 0.7 collective-permute-start.2
  12.5 0.1 collective-permute-start.4
  12.6 0.6 collective-permute-start.6
  13.2 0.0 copy-done
  13.2 0.1 add_add_fusion.3
  13.3 13.4 %shard_map.55 = bf16[2,2,32,32,1024]{4,3,2,1,0:T(8,128)(2,1)} custom-call(s32[2,2]{1,0:T(2,128)} %first_ref.1, bf16[2,32,32,1024]{3,2,1,0:T(8,128)(2,1)} %coeffs_ref.1, bf16[2,2,32,32]{3,2,1,0:T(8,128)(2,1)} %cond_ref.1, bf16[2,2,32,32]{3,2,1,0:T(8,128)(2,1)} %val_ref.1), custom_call_target="tpu_custom_call" | custom-call | flops 6442450944 | bytes 12582912 | tf_op jit(solution)/shard_map/pallas_call | solution.py:90
  26.7 0.1 add_add_fusion.2
  26.7 0.0 collective-permute-done.next_ref
  26.7 7.6 %shard_map.57 = (f32[64,2048]{1,0:T(8,128)S(1)}, f32[64,2048]{1,0:T(8,128)S(1)}, bf16[128,2048]{1,0:T(8,128)(2,1)S(1)}) custom-call(s32[5]{0:T(128)S(1)} %get-tuple-element.36.pick_ref, bf16[2,1024,1024]{2,1,0:T(8,128)(2,1)} %bitcast.10, bf16[2,1024,256]{2,1,0:T(8,128)(2,1)} %collective-permute-done.next_ref, bf16[2,2,1024,1024]{3,2,1,0:T(8,128)(2,1)} %bitcast.14), custom_call_target="tpu_custom_call" | custom-call | flops 2147483648 | bytes 8388608 | tf_op jit(solution)/shard_map/pallas_call | solution.py:259
  34.4 0.0 collective-permute-done.2.next_ref
  34.4 5.5 %shard_map.59 = (f32[64,2048]{1,0:T(8,128)S(1)}, f32[64,2048]{1,0:T(8,128)S(1)}, bf16[128,2048]{1,0:T(8,128)(2,1)S(1)}) custom-call(s32[5]{0:T(128)S(1)} %get-tuple-element.40.pick_ref, bf16[2,1024,1024]{2,1,0:T(8,128)(2,1)} %bitcast.11, bf16[2,256,1024]{2,1,0:T(8,128)(2,1)S(1)} %collective-permute-done.2.next_ref, bf16[2,2,1024,1024]{3,2,1,0:T(8,128)(2,1)} %bitcast.15), custom_call_target="tpu_custom_call" | custom-call | flops 2147483648 | bytes 8388608 | tf_op jit(solution)/shard_map/pallas_call | solution.py:259
  39.9 2.8 %collective-permute-done.4.next_ref = bf16[2,256,1024]{2,1,0:T(8,128)(2,1)S(1)} collective-permute-done((bf16[2,256,1024]{2,1,0:T(8,128)(2,1)}, bf16[2,256,1024]{2,1,0:T(8,128)(2,1)S(1)}, u32[]{:S(2)}, u32[]{:S(2)}) %collective-permute-start.4) | collective-permute-done | bytes 1048608 | tf_op jit(solution)/shard_map/ppermute | solution.py:17
  42.7 5.5 %shard_map.60 = (f32[64,2048]{1,0:T(8,128)S(1)}, f32[64,2048]{1,0:T(8,128)S(1)}, bf16[128,2048]{1,0:T(8,128)(2,1)S(1)}) custom-call(s32[5]{0:T(128)S(1)} %get-tuple-element.45.pick_ref, bf16[2,1024,1024]{2,1,0:T(8,128)(2,1)} %bitcast.12, bf16[2,256,1024]{2,1,0:T(8,128)(2,1)S(1)} %collective-permute-done.4.next_ref, bf16[2,2,1024,1024]{3,2,1,0:T(8,128)(2,1)} %bitcast.16), custom_call_target="tpu_custom_call" | custom-call | flops 2147483648 | bytes 8388608 | tf_op jit(solution)/shard_map/pallas_call | solution.py:259
  48.2 0.1 collective-permute-start.5
  48.3 0.5 collective-permute-start.3
  48.8 0.1 collective-permute-start.1
  48.9 5.1 %collective-permute-done.6.next_ref = bf16[2,256,1024]{2,1,0:T(8,128)(2,1)S(1)} collective-permute-done((bf16[2,256,1024]{2,1,0:T(8,128)(2,1)}, bf16[2,256,1024]{2,1,0:T(8,128)(2,1)S(1)}, u32[]{:S(2)}, u32[]{:S(2)}) %collective-permute-start.6) | collective-permute-done | bytes 1048608 | tf_op jit(solution)/shard_map/ppermute | solution.py:17
  54.0 0.0 collective-permute-done.5.refs_8_
  54.0 0.0 collective-permute-done.3.refs_5_
  54.0 0.0 collective-permute-done.1.refs_2_
  54.0 0.3 shard_map.61
  54.2 0.1 collective-permute-start.9
  54.3 0.1 collective-permute-start.10
  54.4 3.4 %collective-permute-start.11 = (bf16[64,2048]{1,0:T(8,128)(2,1)S(1)}, bf16[64,2048]{1,0:T(8,128)(2,1)S(1)}, u32[]{:S(2)}, u32[]{:S(2)}) collective-permute-start(bf16[64,2048]{1,0:T(8,128)(2,1)S(1)} %get-tuple-element.56), channel_id=1, source_target_pairs={{0,6},{1,7},{2,4},{3,5},{4,2},{5,3},{6,0},{7,1},{8,14},{9,15},{10,... | collective-permute-start | bytes 786440 | tf_op jit(solution)/shard_map/ppermute | solution.py:17
  57.8 0.0 collective-permute-start.13
  57.8 1.5 %collective-permute-start.14 = (bf16[64,2048]{1,0:T(8,128)(2,1)S(1)}, bf16[64,2048]{1,0:T(8,128)(2,1)S(1)}, u32[]{:S(2)}, u32[]{:S(2)}) collective-permute-start(bf16[64,2048]{1,0:T(8,128)(2,1)S(1)} %get-tuple-element.59), channel_id=1, source_target_pairs={{0,6},{1,7},{2,4},{3,5},{4,2},{5,3},{6,0},{7,1},{8,14},{9,15},{10,... | collective-permute-start | bytes 786440 | tf_op jit(solution)/shard_map/ppermute | solution.py:17
  59.3 5.5 %shard_map.62 = (f32[64,2048]{1,0:T(8,128)S(1)}, f32[64,2048]{1,0:T(8,128)S(1)}, bf16[128,2048]{1,0:T(8,128)(2,1)S(1)}) custom-call(s32[5]{0:T(128)S(1)} %get-tuple-element.60.pick_ref, bf16[2,1024,1024]{2,1,0:T(8,128)(2,1)} %bitcast.13, bf16[2,256,1024]{2,1,0:T(8,128)(2,1)S(1)} %collective-permute-done.6.next_ref, bf16[2,2,1024,1024]{3,2,1,0:T(8,128)(2,1)} %bitcast.17), custom_call_target="tpu_custom_call" | custom-call | flops 2147483648 | bytes 8388608 | tf_op jit(solution)/shard_map/pallas_call | solution.py:259
  64.8 0.0 collective-permute-done.9
  64.8 0.1 collective-permute-start.7
  64.9 0.0 collective-permute-done.10
  65.0 5.7 %collective-permute-done.11 = bf16[64,2048]{1,0:T(8,128)(2,1)S(1)} collective-permute-done((bf16[64,2048]{1,0:T(8,128)(2,1)S(1)}, bf16[64,2048]{1,0:T(8,128)(2,1)S(1)}, u32[]{:S(2)}, u32[]{:S(2)}) %collective-permute-start.11) | collective-permute-done | bytes 262176 | tf_op jit(solution)/shard_map/ppermute | solution.py:17
  70.6 0.1 add_convert_fusion
  70.7 0.1 collective-permute-start.12
  70.8 0.0 collective-permute-done.7.core_ref
  70.8 0.1 add_convert_fusion.1
  70.9 0.1 collective-permute-start.8
  71.0 9.5 %collective-permute-done.13.refs_2_ = bf16[64,2048]{1,0:T(8,128)(2,1)S(1)} collective-permute-done((bf16[64,2048]{1,0:T(8,128)(2,1)S(1)}, bf16[64,2048]{1,0:T(8,128)(2,1)S(1)}, u32[]{:S(2)}, u32[]{:S(2)}) %collective-permute-start.13) | collective-permute-done | bytes 262176 | tf_op jit(solution)/shard_map/ppermute | solution.py:17
  80.4 4.1 %collective-permute-done.14.refs_3_ = bf16[64,2048]{1,0:T(8,128)(2,1)S(1)} collective-permute-done((bf16[64,2048]{1,0:T(8,128)(2,1)S(1)}, bf16[64,2048]{1,0:T(8,128)(2,1)S(1)}, u32[]{:S(2)}, u32[]{:S(2)}) %collective-permute-start.14) | collective-permute-done | bytes 262176 | tf_op jit(solution)/shard_map/ppermute | solution.py:17
  84.6 0.0 collective-permute-done.12.refs_1_
  84.6 0.0 collective-permute-done.8.refs_0_
  84.6 1.1 %shard_map.63 = f32[64,2,1024]{2,1,0:T(2,128)} custom-call(f32[64,2048]{1,0:T(8,128)S(1)} %get-tuple-element.62.mine_ref, bf16[128,2048]{1,0:T(8,128)(2,1)S(1)} %collective-permute-done.7.core_ref, bf16[64,2048]{1,0:T(8,128)(2,1)S(1)} %collective-permute-done.8.refs_0_, bf16[64,2048]{1,0:T(8,128)(2,1)S(1)} %collective-permute-done.12.refs_1_, ...), custom_call_target="tpu_custom_call" | custom-call | flops 655360 | bytes 2097152 | tf_op jit(solution)/shard_map/pallas_call | solution.py:332
  (2 shorter events, 0.1 us)
Async XLA Ops:
  0.0 13.2 %copy-start = (s32[2]{0:T(128)S(1)}, s32[2]{0:T(128)}, u32[]{:S(2)}) copy-start(s32[2]{0:T(128)} %param.8) | copy-start | bytes 28
  2.1 24.6 %collective-permute-start = (bf16[2,1024,256]{2,1,0:T(8,128)(2,1)}, bf16[2,1024,256]{2,1,0:T(8,128)(2,1)}, u32[]{:S(2)}, u32[]{:S(2)}) collective-permute-start(bf16[2,1024,256]{2,1,0:T(8,128)(2,1)} %shard_map.56), channel_id=1, source_target_pairs={{0,15},{1,0},{2,1},{3,2},{4,3},{5,4},{6,5},{7,6},{8,7},{9,8},{10,9... | collective-permute-start | bytes 3145736 | tf_op jit(solution)/shard_map/ppermute | solution.py:17
  11.8 22.6 %collective-permute-start.2 = (bf16[2,256,1024]{2,1,0:T(8,128)(2,1)}, bf16[2,256,1024]{2,1,0:T(8,128)(2,1)S(1)}, u32[]{:S(2)}, u32[]{:S(2)}) collective-permute-start(bf16[2,256,1024]{2,1,0:T(8,128)(2,1)} %get-tuple-element.42), channel_id=1, source_target_pairs={{0,15},{1,0},{2,1},{3,2},{4,3},{5,4},{6,5},{7,6},{8,7},{9,8},{10,9... | collective-permute-start | bytes 3145736 | tf_op jit(solution)/shard_map/ppermute | solution.py:17
  12.5 30.2 %collective-permute-start.4 = (bf16[2,256,1024]{2,1,0:T(8,128)(2,1)}, bf16[2,256,1024]{2,1,0:T(8,128)(2,1)S(1)}, u32[]{:S(2)}, u32[]{:S(2)}) collective-permute-start(bf16[2,256,1024]{2,1,0:T(8,128)(2,1)} %get-tuple-element.46), channel_id=1, source_target_pairs={{0,15},{1,0},{2,1},{3,2},{4,3},{5,4},{6,5},{7,6},{8,7},{9,8},{10,9... | collective-permute-start | bytes 3145736 | tf_op jit(solution)/shard_map/ppermute | solution.py:17
  12.6 41.3 %collective-permute-start.6 = (bf16[2,256,1024]{2,1,0:T(8,128)(2,1)}, bf16[2,256,1024]{2,1,0:T(8,128)(2,1)S(1)}, u32[]{:S(2)}, u32[]{:S(2)}) collective-permute-start(bf16[2,256,1024]{2,1,0:T(8,128)(2,1)} %get-tuple-element.48), channel_id=1, source_target_pairs={{0,15},{1,0},{2,1},{3,2},{4,3},{5,4},{6,5},{7,6},{8,7},{9,8},{10,9... | collective-permute-start | bytes 3145736 | tf_op jit(solution)/shard_map/ppermute | solution.py:17
  48.2 5.8 %collective-permute-start.5 = (bf16[128,2048]{1,0:T(8,128)(2,1)S(1)}, bf16[128,2048]{1,0:T(8,128)(2,1)S(1)}, u32[]{:S(2)}, u32[]{:S(2)}) collective-permute-start(bf16[128,2048]{1,0:T(8,128)(2,1)S(1)} %get-tuple-element.47), channel_id=1, source_target_pairs={{0,1},{1,0},{2,3},{3,2},{4,5},{5,4},{6,7},{7,6},{8,9},{9,8},{10,11... | collective-permute-start | bytes 1572872 | tf_op jit(solution)/shard_map/ppermute | solution.py:17
  48.3 5.7 %collective-permute-start.3 = (bf16[128,2048]{1,0:T(8,128)(2,1)S(1)}, bf16[128,2048]{1,0:T(8,128)(2,1)S(1)}, u32[]{:S(2)}, u32[]{:S(2)}) collective-permute-start(bf16[128,2048]{1,0:T(8,128)(2,1)S(1)} %get-tuple-element.43), channel_id=1, source_target_pairs={{0,1},{1,0},{2,3},{3,2},{4,5},{5,4},{6,7},{7,6},{8,9},{9,8},{10,11... | collective-permute-start | bytes 1572872 | tf_op jit(solution)/shard_map/ppermute | solution.py:17
  48.8 5.2 %collective-permute-start.1 = (bf16[128,2048]{1,0:T(8,128)(2,1)S(1)}, bf16[128,2048]{1,0:T(8,128)(2,1)S(1)}, u32[]{:S(2)}, u32[]{:S(2)}) collective-permute-start(bf16[128,2048]{1,0:T(8,128)(2,1)S(1)} %get-tuple-element.39), channel_id=1, source_target_pairs={{0,1},{1,0},{2,3},{3,2},{4,5},{5,4},{6,7},{7,6},{8,9},{9,8},{10,11... | collective-permute-start | bytes 1572872 | tf_op jit(solution)/shard_map/ppermute | solution.py:17
  54.2 10.6 %collective-permute-start.9 = (bf16[64,2048]{1,0:T(8,128)(2,1)S(1)}, bf16[64,2048]{1,0:T(8,128)(2,1)S(1)}, u32[]{:S(2)}, u32[]{:S(2)}) collective-permute-start(bf16[64,2048]{1,0:T(8,128)(2,1)S(1)} %get-tuple-element.57), channel_id=1, source_target_pairs={{0,2},{1,3},{2,0},{3,1},{4,6},{5,7},{6,4},{7,5},{8,10},{9,11},{10,... | collective-permute-start | bytes 786440 | tf_op jit(solution)/shard_map/ppermute | solution.py:17
  54.3 10.6 %collective-permute-start.10 = (bf16[64,2048]{1,0:T(8,128)(2,1)S(1)}, bf16[64,2048]{1,0:T(8,128)(2,1)S(1)}, u32[]{:S(2)}, u32[]{:S(2)}) collective-permute-start(bf16[64,2048]{1,0:T(8,128)(2,1)S(1)} %get-tuple-element.55), channel_id=1, source_target_pairs={{0,4},{1,5},{2,6},{3,7},{4,0},{5,1},{6,2},{7,3},{8,12},{9,13},{10,... | collective-permute-start | bytes 786440 | tf_op jit(solution)/shard_map/ppermute | solution.py:17
  54.4 16.2 %collective-permute-start.11 = (bf16[64,2048]{1,0:T(8,128)(2,1)S(1)}, bf16[64,2048]{1,0:T(8,128)(2,1)S(1)}, u32[]{:S(2)}, u32[]{:S(2)}) collective-permute-start(bf16[64,2048]{1,0:T(8,128)(2,1)S(1)} %get-tuple-element.56), channel_id=1, source_target_pairs={{0,6},{1,7},{2,4},{3,5},{4,2},{5,3},{6,0},{7,1},{8,14},{9,15},{10,... | collective-permute-start | bytes 786440 | tf_op jit(solution)/shard_map/ppermute | solution.py:17
  57.8 22.7 %collective-permute-start.13 = (bf16[64,2048]{1,0:T(8,128)(2,1)S(1)}, bf16[64,2048]{1,0:T(8,128)(2,1)S(1)}, u32[]{:S(2)}, u32[]{:S(2)}) collective-permute-start(bf16[64,2048]{1,0:T(8,128)(2,1)S(1)} %get-tuple-element.58), channel_id=1, source_target_pairs={{0,4},{1,5},{2,6},{3,7},{4,0},{5,1},{6,2},{7,3},{8,12},{9,13},{10,... | collective-permute-start | bytes 786440 | tf_op jit(solution)/shard_map/ppermute | solution.py:17
  57.8 26.8 %collective-permute-start.14 = (bf16[64,2048]{1,0:T(8,128)(2,1)S(1)}, bf16[64,2048]{1,0:T(8,128)(2,1)S(1)}, u32[]{:S(2)}, u32[]{:S(2)}) collective-permute-start(bf16[64,2048]{1,0:T(8,128)(2,1)S(1)} %get-tuple-element.59), channel_id=1, source_target_pairs={{0,6},{1,7},{2,4},{3,5},{4,2},{5,3},{6,0},{7,1},{8,14},{9,15},{10,... | collective-permute-start | bytes 786440 | tf_op jit(solution)/shard_map/ppermute | solution.py:17
  64.8 6.0 %collective-permute-start.7 = (bf16[128,2048]{1,0:T(8,128)(2,1)S(1)}, bf16[128,2048]{1,0:T(8,128)(2,1)S(1)}, u32[]{:S(2)}, u32[]{:S(2)}) collective-permute-start(bf16[128,2048]{1,0:T(8,128)(2,1)S(1)} %get-tuple-element.63), channel_id=1, source_target_pairs={{0,1},{1,0},{2,3},{3,2},{4,5},{5,4},{6,7},{7,6},{8,9},{9,8},{10,11... | collective-permute-start | bytes 1572872 | tf_op jit(solution)/shard_map/ppermute | solution.py:17
  70.7 13.8 %collective-permute-start.12 = (bf16[64,2048]{1,0:T(8,128)(2,1)S(1)}, bf16[64,2048]{1,0:T(8,128)(2,1)S(1)}, u32[]{:S(2)}, u32[]{:S(2)}) collective-permute-start(bf16[64,2048]{1,0:T(8,128)(2,1)S(1)} %add_convert_fusion), channel_id=1, source_target_pairs={{0,8},{1,9},{2,10},{3,11},{4,12},{5,13},{6,14},{7,15},{8,0},{9,1},... | collective-permute-start | bytes 786440 | tf_op jit(solution)/shard_map/ppermute | solution.py:17
  70.9 13.7 %collective-permute-start.8 = (bf16[64,2048]{1,0:T(8,128)(2,1)S(1)}, bf16[64,2048]{1,0:T(8,128)(2,1)S(1)}, u32[]{:S(2)}, u32[]{:S(2)}) collective-permute-start(bf16[64,2048]{1,0:T(8,128)(2,1)S(1)} %add_convert_fusion.1), channel_id=1, source_target_pairs={{0,2},{1,3},{2,0},{3,1},{4,6},{5,7},{6,4},{7,5},{8,10},{9,11},{10,... | collective-permute-start | bytes 786440 | tf_op jit(solution)/shard_map/ppermute | solution.py:17
